TPU v7x, 32 devices: a whole 2x2x4 slice. The times are simulated.
32 devices in a mesh: station: 4 (over z), band: 4 (over y, x), tm: 2 (over core).
Axes of the slice: x: 2, y: 2, z: 4, core: 2. Of those that a mesh axis runs over, the one named last changes fastest.
Arguments:
- volts: bfloat16 [2, 4, 1024, 36864], P(None, 'band', 'station', 'tm'), may hold values from -300 to 300
- flagged: int32 [4, 36], replicated, may hold values from 0 to 143, as said below
Outputs:
- visibilities: float32 [4, 16, 2, 1024, 1024], P('band', 'station', None, 'tm')
Inputs may be any that keep to these rules, and one draw needn't show every extreme that they name: `flagged`: each coarse channel's list holds fine channels 0 and 143, a run of 18 consecutive fine channels (counted cyclically), and further channels; entries may repeat.
All inputs are finite; a program needn't handle non-finite values.
Results may differ from a plain program's by a relative error of at most 0.0041.
Values may be sent and summed in bfloat16 or wider, within the bound.
No kernel may reach another device: no remote copies, remote signals or barrier semaphores. Data moves between devices by JAX's collectives and lax.ppermute only.
A program may use at most 192 MiB of HBM per device.

v0:
```python
import math

import jax
import jax.numpy as jnp
from jax import lax
from jax.sharding import PartitionSpec as P

SUBBAND_COUNT = 144
TAPS = 12
GROUP = 9


def passed_along(value, axis, steps):
    count = lax.axis_size(axis)
    leading, last = (max(0, -steps), min(count, count - steps))
    return lax.ppermute(value, axis, [(source, source + steps) for source in range(leading, last)])


def window_table():
    total = TAPS * SUBBAND_COUNT
    place = jnp.arange(total, dtype=jnp.float32)
    shape = jnp.sinc((place - total / 2.0 + 0.5) / SUBBAND_COUNT)
    taper = 0.5 - 0.5 * jnp.cos(2.0 * math.pi * (place + 0.5) / total)
    return (shape * taper).reshape(TAPS, SUBBAND_COUNT)


def rotation_factor_table():
    left = jnp.arange(SUBBAND_COUNT, dtype=jnp.int32)[:, None]
    right = jnp.arange(SUBBAND_COUNT, dtype=jnp.int32)[None, :]
    angle = 2.0 * math.pi * (left * right % SUBBAND_COUNT).astype(jnp.float32) / SUBBAND_COUNT
    cosines = jnp.cos(angle)
    sines = jnp.sin(angle)
    upper = jnp.stack([cosines, -sines], 1)
    lower = jnp.stack([sines, cosines], 1)
    return jnp.concatenate([upper, lower], 0).astype(jnp.bfloat16)


def pair_products(left, right):
    swapped = jnp.stack([left[..., 1, :], -left[..., 0, :]], 4)
    real = jnp.einsum("cgfird,cgfjrd->icgj", left, right, preferred_element_type=jnp.float32)
    imag = jnp.einsum("cgfird,cgfjrd->icgj", swapped, right, preferred_element_type=jnp.float32)
    return jnp.stack([real, imag], 3)


def shards(volts, flagged):
    coarse_dev = volts.shape[1]
    inputs_dev = volts.shape[2]
    spec_count = volts.shape[3] // SUBBAND_COUNT
    frames_all = spec_count * lax.axis_size("tm")
    frames = volts.reshape(2, coarse_dev, inputs_dev, spec_count, SUBBAND_COUNT)
    history = passed_along(frames[:, :, :, spec_count - (TAPS - 1) :, :], "tm", 1)
    padded = jnp.concatenate([history, frames], 3)
    window = window_table()
    filtered = jnp.zeros((2, coarse_dev, inputs_dev, spec_count, SUBBAND_COUNT), jnp.float32)
    for tap in range(TAPS):
        filtered = filtered + window[tap][None, None, None, None, :] * padded[
            :, :, :, tap : tap + spec_count, :
        ].astype(jnp.float32)
    filtered = filtered.astype(jnp.bfloat16)
    joined_spectra = jnp.concatenate([filtered[0], filtered[1]], -1)
    spectra = jnp.einsum(
        "nqvx,xdl->nlqdv",
        joined_spectra,
        rotation_factor_table(),
        preferred_element_type=jnp.float32,
    ).astype(jnp.bfloat16)
    fine_ids = jnp.arange(SUBBAND_COUNT, dtype=jnp.int32)
    keep_all = jnp.all(flagged[:, :, None] != fine_ids[None, None, :], axis=1).astype(jnp.float32)
    kept_total = jnp.sum(keep_all)
    keep_mine = lax.dynamic_slice_in_dim(
        keep_all, lax.axis_index("band") * coarse_dev, coarse_dev, 0
    )
    values = spectra.astype(jnp.float32)
    local_power = jnp.sum(values * values * keep_mine[:, :, None, None, None], axis=(0, 1, 3, 4))
    band_total = lax.psum(local_power, ("band", "tm"))
    scale_mine = lax.rsqrt(band_total / (frames_all * kept_total) + 1e-06)
    scales = lax.all_gather(scale_mine, "station", axis=0, tiled=True)
    received = lax.all_to_all(spectra, "station", split_axis=1, concat_axis=2, tiled=True)
    fine_dev = received.shape[1]
    inputs_all = received.shape[2]
    keep_owned = lax.dynamic_slice_in_dim(
        keep_mine, lax.axis_index("station") * fine_dev, fine_dev, 1
    )
    groups_dev = fine_dev // GROUP
    masked = received * keep_owned[:, :, None, None, None].astype(jnp.bfloat16)
    blocks = masked.reshape(coarse_dev, groups_dev, GROUP, inputs_all, 2, spec_count)
    rows = inputs_all // lax.axis_size("tm")
    leading_offset = lax.axis_index("tm") * rows
    summed = lax.psum_scatter(pair_products(blocks, blocks), "tm", scatter_dimension=0, tiled=True)
    counts = keep_owned.reshape(coarse_dev, groups_dev, GROUP).sum(-1)
    denom = frames_all * jnp.maximum(counts, 1.0)
    row_scales = lax.dynamic_slice_in_dim(scales, leading_offset, rows, 0)
    pair_scales = row_scales[:, None] * scales[None, :]
    ordered = jnp.transpose(summed, (1, 2, 3, 0, 4))
    return ordered * pair_scales[None, None, None, :, :] / denom[:, :, None, None, None]


def solution(mesh):
    placed = (P(None, "band", "station", "tm"), P())
    return jax.shard_map(
        shards,
        mesh=mesh,
        in_specs=placed,
        out_specs=P("band", "station", None, "tm", None),
        check_vma=False,
    )
```

profile of v0, /device:TPU:11, one launch (start us, length us, event | category | flops | bytes accessed | tf_op | source)
XLA Modules:
  0.0 938.5 jit_solution(17748221120323980399)
XLA Ops:
  6.5 24.7 %copy.51 = bf16[2,1,256,18432]{2,3,0,1:T(8,128)(2,1)} copy(bf16[2,1,256,18432]{3,2,1,0:T(8,128)(2,1)} %param.2) | data formatting | bytes 37748736 | tf_op args[0]
  31.2 1.5 slice_bitcast_fusion.2
  32.7 0.0 copy-start.3
  32.7 1.3 collective-permute-start
  34.0 26.6 %copy.54 = bf16[2,1,256,128,144]{3,4,2,1,0:T(8,128)(2,1)} copy(bf16[2,1,256,128,144]{2,4,3,0,1:T(8,128)(2,1)} %bitcast.62) | data formatting | bytes 37748736 | tf_op jit(solution)/shard_map/reshape | solution.py:50
  60.6 0.0 copy-done.3
  60.6 0.1 copy.58
  60.7 0.1 fusion.38
  60.9 0.0 copy-start.1
  60.9 0.6 copy-done.1
  61.4 0.1 fusion.43
  61.5 0.6 fusion.36
  62.1 0.6 negate_convert_fusion
  62.7 0.1 fusion.71
  62.8 0.0 collective-permute-done
  62.8 14.7 %copy.53 = bf16[2,1,256,11,144]{3,4,2,1,0:T(8,128)(2,1)} copy(bf16[2,1,256,11,144]{2,4,3,1,0:T(8,128)(2,1)S(1)} %collective-permute-done) | data formatting | bytes 3244032 | tf_op jit(solution)/shard_map/ppermute | solution.py:16
  77.5 191.4 %add_convert_fusion = bf16[2,1,256,128,144]{3,4,2,1,0:T(8,128)(2,1)} fusion(bf16[2,1,256,128,144]{3,4,2,1,0:T(8,128)(2,1)} %copy.54, bf16[2,1,256,11,144]{3,4,2,1,0:T(8,128)(2,1)} %copy.53, f32[144]{0:T(256)S(1)} %get-tuple-element.10, f32[144]{0:T(256)S(1)} %get-tuple-element.11, f32[144]{0:T(256)S(1)} %get-tuple-element.12, f32[144]{0:T(256)S(1)} %get-tuple-element.13, ...), kind=kLoop, calls=%fused_computation.21 | loop fusion | flops 651165696 | bytes 39377664 | tf_op jit(solution)/shard_map/convert_element_type | solution.py:59
  268.9 14.4 %slice_bitcast_fusion.1 = (bf16[1,256,128,144]{2,3,1,0:T(8,128)(2,1)}, bf16[1,256,128,144]{2,3,1,0:T(8,128)(2,1)}) fusion(bf16[2,1,256,128,144]{3,4,2,1,0:T(8,128)(2,1)} %add_convert_fusion), kind=kLoop, calls=%fused_computation.50 | loop fusion | bytes 37748736 | tf_op jit(solution)/shard_map/squeeze | solution.py:60
  283.3 19.6 %multiply_reduce_fusion = (f32[256]{0:T(256)}, bf16[1,144,256,2,128]{4,1,2,3,0:T(8,128)(2,1)}) fusion(f32[144]{0:T(256)S(1)} %bitcast.69, bf16[1,256,128,144]{2,3,1,0:T(8,128)(2,1)} %get-tuple-element.8, bf16[1,256,128,144]{2,3,1,0:T(8,128)(2,1)} %get-tuple-element.7, bf16[144,1,144]{0,2,1:T(8,128)(2,1)S(1)} %get-tuple-element.26, ...), kind=kOutput, calls=%fused_computation.20 | convolution fusion | flops 5521416192 | bytes 37874752 | tf_op jit(solution)/shard_map/nqvx,xdl->nlqdv/dot_general | solution.py:61
  302.9 20.0 %copy.56 = bf16[1,144,256,2,128]{4,2,3,0,1:T(8,128)(2,1)} copy(bf16[1,144,256,2,128]{4,1,2,3,0:T(8,128)(2,1)} %get-tuple-element.24) | data formatting | bytes 37748736 | tf_op jit(solution)/shard_map/convert_element_type | solution.py:66
  322.9 7.5 all-to-all-start
  330.4 0.0 reduce-scatter.2.cloned.1.call-start
  330.4 0.1 dynamic-slice_reduce_fusion
  330.5 0.1 broadcast_in_dim.7
  330.5 0.1 fusion.72
  330.7 0.1 copy.62
  330.8 403.1 %all-to-all-done = bf16[1,144,256,2,128]{4,2,3,0,1:T(8,128)(2,1)} async-done(((bf16[1,144,256,2,128]{4,2,3,0,1:T(8,128)(2,1)}), bf16[1,144,256,2,128]{4,2,3,0,1:T(8,128)(2,1)}, u32[]{:S(2)}, u32[]{:S(2)}) %all-to-all-start) | async-done | bytes 18874400 | tf_op jit(solution)/shard_map/all_to_all | solution.py:78
  733.9 9.3 copy.57
  743.2 0.0 copy-start
  743.2 6.8 copy_multiply_fusion
  750.1 5.2 copy-done
  755.3 14.8 %fusion.70 = (bf16[1,4,9,1024,1,128]{5,3,4,1,2,0:T(8,128)(2,1)}, bf16[1,4,9,1024,1,128]{5,3,4,1,2,0:T(8,128)(2,1)}) fusion(bf16[1,4,9,1024,2,128]{5,3,4,1,2,0:T(8,128)(2,1)} %copy_multiply_fusion), kind=kLoop, calls=%fused_computation.120 | loop fusion | flops 4718592 | bytes 37748736 | tf_op jit(solution)/shard_map/slice | solution.py:39
  770.1 30.0 %fusion.19 = f32[1024,1,4,1,1024]{0,4,2,3,1:T(8,128)} fusion(bf16[4,9,1024,2,128]{4,2,3,1,0:T(8,128)(2,1)} %bitcast.64, bf16[4,9]{1,0:T(4,128)(2,1)S(1)} %get-tuple-element.22), kind=kOutput, calls=%fused_computation.52 | convolution fusion | flops 19336790016 | bytes 35651656 | tf_op jit(solution)/shard_map/cgfird,cgfjrd->icgj/dot_general | solution.py:40
  800.1 29.9 %fusion.22 = f32[1024,1,4,1,1024]{0,4,2,3,1:T(8,128)} fusion(bf16[1,4,9,1024,1,128]{5,3,4,1,2,0:T(8,128)(2,1)} %get-tuple-element.6, bf16[1,4,9,1024,1,128]{5,3,4,1,2,0:T(8,128)(2,1)} %get-tuple-element.5, bf16[4,9,1024,2,128]{4,2,3,1,0:T(8,128)(2,1)} %bitcast.65, bf16[4,9]{1,0:T(4,128)(2,1)S(1)} %get-tuple-element.22), kind=kOutput, calls=%fused_computation.53 | convolution fusion | flops 19346227200 | bytes 54526024 | tf_op jit(solution)/shard_map/cgfird,cgfjrd->icgj/dot_general | solution.py:41
  830.0 23.5 %pad_maximum_fusion = f32[1024,1,4,2,1024]{0,4,2,3,1:T(8,128)} fusion(f32[1024,1,4,1,1024]{0,4,2,3,1:T(8,128)} %fusion.22, f32[1024,1,4,1,1024]{0,4,2,3,1:T(8,128)} %fusion.19), kind=kLoop, calls=%fused_computation.22 | loop fusion | flops 8388608 | bytes 67108864 | tf_op jit(solution)/shard_map/stack | solution.py:42
  853.5 0.0 copy-start.2
  853.5 0.0 copy-start.4
  853.5 0.0 reduce-scatter.2.cloned.1.call-update
  853.5 0.6 copy-done.2
  854.1 0.6 convert_reduce_fusion
  855.4 0.0 copy-done.4
  855.4 11.9 %psum.7 = f32[256]{0:T(256)S(1)} all-reduce(f32[256]{0:T(256)S(1)} %copy-done.4), channel_id=1, replica_groups=mesh['station'=4,'band'=4,'tm'=2] {'band','tm'}, use_global_device_ids=true, to_apply=%region_3.4 | all-reduce | flops 256 | bytes 2048 | tf_op jit(solution)/shard_map/psum | solution.py:75
  867.3 9.0 all-gather
  876.4 0.1 dynamic_slice.11
  876.5 0.2 broadcast_multiply_fusion.1
  876.7 26.3 %reduce-scatter.2.cloned.1.call-done = f32[512,1,4,2,1024]{0,4,2,3,1:T(8,128)} async-done(((f32[1024,1,4,2,1024]{0,4,2,3,1:T(8,128)}), f32[512,1,4,2,1024]{0,4,2,3,1:T(8,128)}) %reduce-scatter.2.cloned.1.call-update) | async-done | bytes 16777232 | tf_op jit(solution)/shard_map/reduce_scatter | solution.py:89
  902.9 12.4 %divide_bitcast_fusion = f32[1,4,2,512,1024]{3,4,1,2,0:T(8,128)} fusion(f32[512,1,4,2,1024]{0,4,2,3,1:T(8,128)} %reduce-scatter.2.cloned.1.call-done, f32[4]{0:T(128)S(1)} %maximum_multiply_fusion, f32[512,1024]{0,1:T(8,128)S(1)} %broadcast_multiply_fusion.1), kind=kLoop, calls=%fused_computation.44 | loop fusion | flops 8388608 | bytes 35651600 | tf_op jit(solution)/shard_map/div | solution.py:95
  915.4 16.3 %copy.65 = f32[1,4,2,512,1024]{4,3,2,1,0:T(8,128)} copy(f32[1,4,2,512,1024]{3,4,1,2,0:T(8,128)} %divide_bitcast_fusion) | data formatting | bytes 33554432 | tf_op jit(solution)/shard_map/div | solution.py:95
  (4 shorter events, 0.0 us)
Async XLA Ops:
  32.7 27.9 %copy-start.3 = (s32[4,36]{1,0:T(4,128)S(1)}, s32[4,36]{1,0:T(4,128)}, u32[]{:S(2)}) copy-start(s32[4,36]{1,0:T(4,128)} %param.3) | copy-start | bytes 1732
  32.7 30.1 %collective-permute-start = (bf16[2,1,256,11,144]{2,4,3,1,0:T(8,128)(2,1)S(1)}, bf16[2,1,256,11,144]{2,4,3,1,0:T(8,128)(2,1)S(1)}, u32[]{:S(2)}, u32[]{:S(2)}) collective-permute-start(bf16[2,1,256,11,144]{2,4,3,1,0:T(8,128)(2,1)S(1)} %slice_bitcast_fusion.2), channel_id=1, source_target_pairs={{0,1},{2,3},{4,5},{6,7},{8,9},{10,11},{12,13},{14,15},{16,17},{18,... | collective-permute-start | bytes 4866056 | tf_op jit(solution)/shard_map/ppermute | solution.py:16
  60.9 0.6 copy-start.1
  322.9 411.0 %all-to-all-start = ((bf16[1,144,256,2,128]{4,2,3,0,1:T(8,128)(2,1)}), bf16[1,144,256,2,128]{4,2,3,0,1:T(8,128)(2,1)}, u32[]{:S(2)}, u32[]{:S(2)}) async-start(bf16[1,144,256,2,128]{4,2,3,0,1:T(8,128)(2,1)} %copy.56), calls=%async_computation | async-start | bytes 37748736 | tf_op jit(solution)/shard_map/all_to_all | solution.py:78
  330.4 572.6 %reduce-scatter.2.cloned.1.call-start = ((), (), s32[]{:S(2)}) async-start(), calls=%async_computation.2 | async-start | bytes 50331648 | tf_op jit(solution)/shard_map/reduce_scatter | solution.py:89
  743.2 12.1 %copy-start = (bf16[1,36,4,256,2,128]{5,3,2,4,1,0:T(8,128)(2,1)}, bf16[1,36,4,256,2,128]{5,3,2,4,1,0:T(8,128)(2,1)S(1)}, u32[]{:S(2)}) copy-start(bf16[1,36,4,256,2,128]{5,3,2,4,1,0:T(8,128)(2,1)S(1)} %copy.57) | copy-start | bytes 56623108
  853.5 0.7 copy-start.2
  853.5 1.9 copy-start.4
Sparse Core Ops, SparseCore 0:
  853.6 49.2 reduce-scatter.1
where the time goes:
time: 941 us; the launch traced here: 939 us
  waiting for transfers between devices  429 us (46%)
  other arithmetic  251 us (27%)
  local copies, waits for them, and re-layouts  135 us (14%)
  matrix products  79.5 us (8%)
  blocking collectives  21 us (2%)
  between operations  14.2 us (2%)
    all_to_all x1, waiting for transfers between devices, shards(): lax.all_to_all(spectra, 'station', split_axis=1, concat_axis=2, tiled=True)  403 us
    convert_element_type x1, other arithmetic, shards(): filtered = filtered.astype(jnp.bfloat16)  191 us
    unnamed x12, local copies, waits for them, and re-layouts  31.2 us
    dot_general x1, matrix products, pair_products(): jnp.einsum('cgfird,cgfjrd->icgj', left, right, preferred_element_type=jnp...  30 us
    dot_general x1, matrix products, pair_products(): jnp.einsum('cgfird,cgfjrd->icgj', swapped, right, preferred_element_type=...  29.9 us
    reshape x1, local copies, waits for them, and re-layouts, shards(): frames = volts.reshape(2, coarse_dev, inputs_dev, spec_count, SUBBAND_COUNT)  26.6 us
    reduce_scatter x1, waiting for transfers between devices, shards(): lax.psum_scatter(pair_products(blocks, blocks), 'tm', scatter_dimension=0...  26.3 us
    another operation x1, other arithmetic, pair_products(): return jnp.stack([real, imag], 3)  23.5 us
  transfers between devices with their start and end apart: 3, of which 2 were waited for; matrix products, arithmetic and copies ran while one was open for 3% of the time, Pallas kernels for 0%

commit v1 on v0

v1 whole, which is shorter than its diff:
```python
import functools
import math

import jax
import jax.numpy as jnp
import numpy as np
from jax import lax
from jax.experimental import pallas as pl
from jax.experimental.pallas import tpu as pltpu
from jax.sharding import PartitionSpec as P

SUBBAND_COUNT = 144
TAPS = 12
GROUP = 9
BLOCK = 16
FIRST = 1
SPREAD = BLOCK + 1
VMEM = 48 * 1024 * 1024


def window_values():
    total = TAPS * SUBBAND_COUNT
    place = np.arange(total, dtype=np.float64)
    shape = np.sinc((place - total / 2.0 + 0.5) / SUBBAND_COUNT)
    taper = 0.5 - 0.5 * np.cos(2.0 * math.pi * (place + 0.5) / total)
    return (shape * taper).reshape(TAPS, SUBBAND_COUNT).astype(np.float32)


def twiddle_values():
    f = np.arange(SUBBAND_COUNT, dtype=np.int64)[:, None]
    n = np.arange(SUBBAND_COUNT, dtype=np.int64)[None, :]
    angle = 2.0 * math.pi * (f * n % SUBBAND_COUNT) / SUBBAND_COUNT
    cosines, sines = np.cos(angle), np.sin(angle)
    real = np.concatenate([cosines, sines], 1)
    imag = np.concatenate([-sines, cosines], 1)
    return np.stack([real, imag], 1).astype(np.float32)


def front_kernel(splits, owners, keep_ref, hist_ref, volts_ref, window_ref, table_ref, *rest):
    outs, power_ref = rest[: owners * splits], rest[owners * splits]
    ring, filt, spread = rest[owners * splits + 1 :]
    step = pl.program_id(0)
    now = lax.rem(step, 2)
    before = 1 - now
    inputs = ring.shape[-1]
    tiles = inputs // 128
    span = BLOCK * SUBBAND_COUNT

    def turn(ref, slot):
        def columns(c, _):
            at = pl.multiple_of(c * 128, 128)
            for part in range(2):
                ring[slot, part, pl.ds(at, 128), :] = ref[part, 0, :, pl.ds(at, 128)].T
            return 0

        lax.fori_loop(0, span // 128, columns, 0)

    @pl.when(step == 0)
    def _():
        turn(hist_ref, 1)
        power_ref[...] = jnp.zeros_like(power_ref)

    turn(volts_ref, now)

    def filter_rows(j, _):
        base = pl.multiple_of(j * 16, 16)
        for tile in range(tiles):
            lanes = pl.ds(tile * 128, 128)
            weights = [window_ref[k, pl.ds(base, 16), :] for k in range(TAPS)]
            for part in range(2):
                samples = []
                for t in range(1 - TAPS, BLOCK):
                    slot, frame = (now, t) if t >= 0 else (before, BLOCK + t)
                    at = pl.multiple_of(frame * SUBBAND_COUNT + base, 16)
                    samples.append(ring[slot, part, pl.ds(at, 16), lanes].astype(jnp.float32))
                for t in range(BLOCK):
                    total = weights[0] * samples[t]
                    for k in range(1, TAPS):
                        total = total + weights[k] * samples[t + k]
                    at = pl.multiple_of(part * SUBBAND_COUNT + base, 16)
                    filt[t, pl.ds(at, 16), lanes] = total.astype(jnp.bfloat16)
        return 0

    lax.fori_loop(0, SUBBAND_COUNT // 16, filter_rows, 0)

    def transform(t, _):
        result = jnp.dot(table_ref[...], filt[t], preferred_element_type=jnp.float32)
        for tile in range(tiles):
            spread[tile, pl.ds(t, 2 * SUBBAND_COUNT, stride=SPREAD), :] = result[
                :, tile * 128 : (tile + 1) * 128
            ]
        return 0

    lax.fori_loop(0, BLOCK, transform, 0)

    groups = SUBBAND_COUNT // owners // GROUP
    power = [jnp.zeros((BLOCK, 128), jnp.float32) for _ in range(tiles)]
    for d in range(owners):
        for j in range(groups):
            out = outs[d * splits + j] if splits > 1 else outs[d]
            place = 0 if splits > 1 else j

            def channel(f, power, d=d, j=j, out=out, place=place):
                keep = keep_ref[(d * groups + j) * GROUP + f]
                power = list(power)
                for part in range(2):
                    row = ((d * groups + j) * 2 + part) * GROUP + f
                    for tile in range(tiles):
                        value = spread[tile, pl.ds(row * SPREAD, BLOCK), :] * keep
                        value = value.astype(jnp.bfloat16)
                        out[place, part, f, :, tile * 128 : (tile + 1) * 128] = value
                        value = value.astype(jnp.float32)
                        power[tile] = power[tile] + value * value
                return tuple(power)

            power = lax.fori_loop(0, GROUP, channel, tuple(power))
    for tile in range(tiles):
        power_ref[:, tile * 128 : (tile + 1) * 128] += power[tile]


def front(volts, hist, hist_block, first, steps, splits, owners, keep, window, table):
    inputs = volts.shape[2]
    span = BLOCK * SUBBAND_COUNT
    groups = SUBBAND_COUNT // owners // GROUP
    each = groups // splits
    frames = steps * BLOCK
    outs = [
        jax.ShapeDtypeStruct((each, 2, GROUP, frames, inputs), jnp.bfloat16)
        for _ in range(owners * splits)
    ]
    out_specs = [
        pl.BlockSpec((each, 2, GROUP, BLOCK, inputs), lambda s: (0, 0, 0, s, 0))
        for _ in range(owners * splits)
    ]
    outs.append(jax.ShapeDtypeStruct((BLOCK, inputs), jnp.float32))
    out_specs.append(pl.BlockSpec((BLOCK, inputs), lambda s: (0, 0)))
    macs = 2 * SUBBAND_COUNT * frames * inputs * 2 * SUBBAND_COUNT
    result = pl.pallas_call(
        functools.partial(front_kernel, splits, owners),
        grid=(steps,),
        out_shape=outs,
        in_specs=[
            pl.BlockSpec(memory_space=pltpu.SMEM),
            pl.BlockSpec((2, 1, inputs, span), lambda s: (0, 0, 0, hist_block)),
            pl.BlockSpec((2, 1, inputs, span), lambda s: (0, 0, 0, first + s)),
            pl.BlockSpec(window.shape, lambda s: (0, 0, 0)),
            pl.BlockSpec(table.shape, lambda s: (0, 0)),
        ],
        out_specs=out_specs,
        scratch_shapes=[
            pltpu.VMEM((2, 2, span, inputs), jnp.bfloat16),
            pltpu.VMEM((BLOCK, 2 * SUBBAND_COUNT, inputs), jnp.bfloat16),
            pltpu.VMEM((inputs // 128, 2 * SUBBAND_COUNT * SPREAD, 128), jnp.float32),
        ],
        compiler_params=pltpu.CompilerParams(vmem_limit_bytes=VMEM),
        cost_estimate=pl.CostEstimate(
            flops=2 * macs * 4, bytes_accessed=2 * frames * SUBBAND_COUNT * inputs * 8, transcendentals=0
        ),
        name="front",
    )(keep, hist, volts, window, table)
    return result[:-1], result[-1]


def after_kernel(value_ref, other_ref, out_ref):
    pass


def after(value, other):
    anywhere = pl.BlockSpec(memory_space=pl.ANY)
    return pl.pallas_call(
        after_kernel,
        out_shape=jax.ShapeDtypeStruct(value.shape, value.dtype),
        in_specs=[anywhere, anywhere],
        out_specs=anywhere,
        input_output_aliases={0: 0},
        cost_estimate=pl.CostEstimate(flops=0, bytes_accessed=0, transcendentals=0),
        name="after",
    )(value, other)


def correlate_kernel(owners, group, place_ref, *rest):
    early, late = rest[:owners], rest[owners : 2 * owners]
    out_ref, held, turned, sems = rest[2 * owners :]
    me, half = place_ref[0], place_ref[1]
    column = pl.program_id(0)
    per_half = turned.shape[0]
    lead = early[0].shape[2]

    @pl.when(column == 0)
    def _():
        copies = []
        for d in range(owners):
            source = lax.rem(me - d + owners, owners)
            copies.append(
                pltpu.make_async_copy(
                    early[d].at[group], held.at[source, :, pl.ds(0, lead)], sems.at[0, d]
                )
            )
            copies.append(
                pltpu.make_async_copy(
                    late[d].at[0],
                    held.at[source, :, pl.ds(lead, late[d].shape[2])],
                    sems.at[1, d],
                )
            )
        for copy in copies:
            copy.start()
        for copy in copies:
            copy.wait()
        for r in range(per_half):
            for part in range(2):
                turned[r, part] = held[half * per_half + r, part].T

    real, imag = held[column, 0], held[column, 1]
    width = real.shape[1]
    dot = functools.partial(jnp.dot, preferred_element_type=jnp.float32)
    for r in range(per_half):
        rows = slice(r * width, (r + 1) * width)
        out_ref[0, rows, :] = (dot(turned[r, 0], real) + dot(turned[r, 1], imag)).astype(out_ref.dtype)
        out_ref[1, rows, :] = (dot(turned[r, 1], real) - dot(turned[r, 0], imag)).astype(out_ref.dtype)


def correlate(place, early, late, group, dtype):
    owners = len(early)
    inputs = late[0].shape[-1]
    depth = early[0].shape[2] + late[0].shape[2]
    rows = owners // 2 * inputs
    anywhere = pl.BlockSpec(memory_space=pl.ANY)
    return pl.pallas_call(
        functools.partial(correlate_kernel, owners, group),
        grid=(owners,),
        out_shape=jax.ShapeDtypeStruct((2, rows, owners * inputs), dtype),
        in_specs=[pl.BlockSpec(memory_space=pltpu.SMEM)] + [anywhere] * (2 * owners),
        out_specs=pl.BlockSpec((2, rows, inputs), lambda b: (0, 0, b)),
        scratch_shapes=[
            pltpu.VMEM((owners, 2, depth, inputs), jnp.bfloat16),
            pltpu.VMEM((owners // 2, 2, inputs, depth), jnp.bfloat16),
            pltpu.SemaphoreType.DMA((2, owners)),
        ],
        compiler_params=pltpu.CompilerParams(vmem_limit_bytes=VMEM),
        cost_estimate=pl.CostEstimate(
            flops=8 * rows * owners * inputs * depth,
            bytes_accessed=owners * 4 * depth * inputs + 8 * rows * owners * inputs,
            transcendentals=0,
        ),
        name="correlate",
    )(place, *early, *late)


def equalize_kernel(rows_ref, columns_ref, mine_ref, theirs_ref, *rest):
    out_ref = rest[-1]
    scale = rows_ref[...] * columns_ref[...]
    for part in range(2):
        total = mine_ref[part] + theirs_ref[part].astype(jnp.float32)
        out_ref[0, part] = total * scale


def equalize(row_scales, column_scales, mine, theirs, out, group, groups):
    rows, columns = mine.shape[1:]
    block = rows // 4
    specs = [
        pl.BlockSpec((block, 1), lambda r: (r, 0)),
        pl.BlockSpec((1, columns), lambda r: (0, 0)),
        pl.BlockSpec((2, block, columns), lambda r: (0, r, 0)),
        pl.BlockSpec((2, block, columns), lambda r: (0, r, 0)),
    ]
    operands = [row_scales, column_scales, mine, theirs]
    aliases = {}
    if out is not None:
        specs.append(pl.BlockSpec(memory_space=pl.ANY))
        operands.append(out)
        aliases = {4: 0}
    return pl.pallas_call(
        equalize_kernel,
        grid=(rows // block,),
        out_shape=jax.ShapeDtypeStruct((groups, 2, rows, columns), jnp.float32),
        in_specs=specs,
        out_specs=pl.BlockSpec((1, 2, block, columns), lambda r: (group, 0, r, 0)),
        input_output_aliases=aliases,
        compiler_params=pltpu.CompilerParams(vmem_limit_bytes=VMEM),
        cost_estimate=pl.CostEstimate(
            flops=6 * rows * columns, bytes_accessed=20 * rows * columns, transcendentals=0
        ),
        name="equalize",
    )(*operands)


def shift(value, d):
    count = lax.axis_size("station")
    return lax.ppermute(value, "station", [(s, (s + d) % count) for s in range(count)])


def passed_on(value):
    count = lax.axis_size("tm")
    return lax.ppermute(value, "tm", [(s, s + 1) for s in range(count - 1)])


def keep_table(flagged):
    fine = jnp.arange(SUBBAND_COUNT, dtype=jnp.int32)
    return jnp.all(flagged[:, :, None] != fine[None, None, :], axis=1).astype(jnp.float32)


def pipelined(volts, flagged):
    owners = lax.axis_size("station")
    me = lax.axis_index("station")
    half = lax.axis_index("tm")
    inputs = volts.shape[2]
    frames = volts.shape[3] // SUBBAND_COUNT
    frames_all = frames * lax.axis_size("tm")
    fine = SUBBAND_COUNT // owners
    groups = fine // GROUP
    blocks = frames // BLOCK
    span = BLOCK * SUBBAND_COUNT

    keep_all = keep_table(flagged)
    keep_mine = lax.dynamic_index_in_dim(keep_all, lax.axis_index("band"), 0, keepdims=False)
    twice = jnp.concatenate([keep_mine, keep_mine])
    keep_ahead = lax.dynamic_slice_in_dim(twice, me * fine, SUBBAND_COUNT, 0)

    rows = twiddle_values().reshape(owners, groups, GROUP, 2, 2 * SUBBAND_COUNT)
    rows = rows.transpose(0, 1, 3, 2, 4).reshape(2 * SUBBAND_COUNT, 2 * SUBBAND_COUNT)
    rows = jnp.asarray(np.concatenate([rows, rows], 0)).astype(jnp.bfloat16)
    table = lax.dynamic_slice_in_dim(rows, me * 2 * fine, 2 * SUBBAND_COUNT, 0)
    window = jnp.broadcast_to(
        jnp.asarray(window_values())[:, :, None], (TAPS, SUBBAND_COUNT, 128)
    )

    halo = passed_on(volts[:, :, :, (blocks - 1) * span :])
    rest = blocks - FIRST
    early, power_a = front(volts, volts, rest - 1, rest, FIRST, 1, owners, keep_ahead, window, table)
    late, power_b = front(volts, halo, 0, 0, rest, groups, owners, keep_ahead, window, table)

    early = [x.reshape(groups, 2, GROUP * FIRST * BLOCK, inputs) for x in early]
    late = [x.reshape(1, 2, GROUP * rest * BLOCK, inputs) for x in late]
    late = [[late[d * groups + j] for d in range(owners)] for j in range(groups)]

    sent = [early[0]] + [shift(early[d], d) for d in range(1, owners)]
    arrived = []
    for j in range(groups):
        gate = sent if j == 1 else arrived[j - 2] if j > 1 else None
        got = [late[j][0]]
        for d in range(1, owners):
            value = late[j][d]
            if gate is not None:
                value = after(value, gate[d])
            got.append(shift(value, d))
        arrived.append(got)

    local = jnp.sum(power_a + power_b, axis=0)
    total = lax.psum(local, ("band", "tm"))
    scale = lax.rsqrt(total / (frames_all * jnp.sum(keep_all)) + 1e-06)
    scales = lax.all_gather(scale, "station", axis=0, tiled=True)
    kept = lax.dynamic_slice_in_dim(keep_mine, me * fine, fine, 0)
    counts = kept.reshape(groups, GROUP).sum(-1)
    denom = frames_all * jnp.maximum(counts, 1.0)
    per_half = scales.shape[0] // 2
    row_scales = lax.dynamic_slice_in_dim(scales, half * per_half, per_half, 0)

    other = [(0, 1), (1, 0)]
    send_place = jnp.stack([me, 1 - half]).astype(jnp.int32)
    mine_place = jnp.stack([me, half]).astype(jnp.int32)
    out = None
    for j in range(groups):
        theirs = correlate(send_place, sent, arrived[j], j, jnp.bfloat16)
        theirs = lax.ppermute(theirs, "tm", other)
        mine = correlate(mine_place, sent, arrived[j], j, jnp.float32)
        out = equalize(
            (row_scales / denom[j])[:, None], scales[None, :], mine, theirs, out, j, groups
        )
    return out[None]


def twiddle_table():
    values = twiddle_values().transpose(2, 1, 0)
    return jnp.asarray(values).astype(jnp.bfloat16)


def pair_products(left, right):
    swapped = jnp.stack([left[..., 1, :], -left[..., 0, :]], 4)
    real = jnp.einsum("cgfird,cgfjrd->icgj", left, right, preferred_element_type=jnp.float32)
    imag = jnp.einsum("cgfird,cgfjrd->icgj", swapped, right, preferred_element_type=jnp.float32)
    return jnp.stack([real, imag], 3)


def plain(volts, flagged):
    coarse_dev = volts.shape[1]
    inputs_dev = volts.shape[2]
    spec_count = volts.shape[3] // SUBBAND_COUNT
    frames_all = spec_count * lax.axis_size("tm")
    frames = volts.reshape(2, coarse_dev, inputs_dev, spec_count, SUBBAND_COUNT)
    history = passed_on(frames[:, :, :, spec_count - (TAPS - 1) :, :])
    padded = jnp.concatenate([history, frames], 3)
    window = jnp.asarray(window_values())
    filtered = jnp.zeros((2, coarse_dev, inputs_dev, spec_count, SUBBAND_COUNT), jnp.float32)
    for tap in range(TAPS):
        filtered = filtered + window[tap] * padded[:, :, :, tap : tap + spec_count, :].astype(
            jnp.float32
        )
    filtered = filtered.astype(jnp.bfloat16)
    joined = jnp.concatenate([filtered[0], filtered[1]], -1)
    spectra = jnp.einsum(
        "nqvx,xdl->nlqdv", joined, twiddle_table(), preferred_element_type=jnp.float32
    ).astype(jnp.bfloat16)
    keep_all = keep_table(flagged)
    keep_mine = lax.dynamic_slice_in_dim(
        keep_all, lax.axis_index("band") * coarse_dev, coarse_dev, 0
    )
    values = spectra.astype(jnp.float32)
    local = jnp.sum(values * values * keep_mine[:, :, None, None, None], axis=(0, 1, 3, 4))
    total = lax.psum(local, ("band", "tm"))
    scale = lax.rsqrt(total / (frames_all * jnp.sum(keep_all)) + 1e-06)
    scales = lax.all_gather(scale, "station", axis=0, tiled=True)
    received = lax.all_to_all(spectra, "station", split_axis=1, concat_axis=2, tiled=True)
    fine_dev = received.shape[1]
    inputs_all = received.shape[2]
    kept = lax.dynamic_slice_in_dim(keep_mine, lax.axis_index("station") * fine_dev, fine_dev, 1)
    groups_dev = fine_dev // GROUP
    masked = received * kept[:, :, None, None, None].astype(jnp.bfloat16)
    blocks = masked.reshape(coarse_dev, groups_dev, GROUP, inputs_all, 2, spec_count)
    rows = inputs_all // lax.axis_size("tm")
    summed = lax.psum_scatter(pair_products(blocks, blocks), "tm", scatter_dimension=0, tiled=True)
    counts = kept.reshape(coarse_dev, groups_dev, GROUP).sum(-1)
    denom = frames_all * jnp.maximum(counts, 1.0)
    row_scales = lax.dynamic_slice_in_dim(scales, lax.axis_index("tm") * rows, rows, 0)
    pairs = row_scales[:, None] * scales[None, :]
    ordered = jnp.transpose(summed, (1, 2, 3, 0, 4))
    return ordered * pairs[None, None, None, :, :] / denom[:, :, None, None, None]


def shards(volts, flagged):
    owners = lax.axis_size("station")
    frames = volts.shape[3] // SUBBAND_COUNT
    fits = (
        volts.shape[1] == 1
        and volts.shape[2] % 128 == 0
        and owners % 2 == 0
        and (SUBBAND_COUNT // owners) % GROUP == 0
        and lax.axis_size("tm") == 2
        and frames % BLOCK == 0
        and frames // BLOCK > FIRST
    )
    return (pipelined if fits else plain)(volts, flagged)


def solution(mesh):
    placed = (P(None, "band", "station", "tm"), P())
    return jax.shard_map(
        shards,
        mesh=mesh,
        in_specs=placed,
        out_specs=P("band", "station", None, "tm", None),
        check_vma=False,
    )
```

time: 941 us -> 590 us (0.63)
  waiting for transfers between devices: 429 us -> 170 us
  other arithmetic: 251 us -> 3.62 us
  Pallas kernels: 0 us -> 212 us
  local copies, waits for them, and re-layouts: 135 us -> 22.6 us
  matrix products: 79.5 us -> 0 us
  starting transfers between devices: 8.75 us -> 85.7 us
  blocking collectives: 21 us -> 88.9 us
  between operations: 14.2 us -> 1.08 us
    all_to_all x1 -> x0, waiting for transfers between devices: 403 us -> none  [shards(): lax.all_to_all(spectra, 'station', split_axis=1, concat_axis=2, tiled=True)]
    pallas_call x0 -> x23, Pallas kernels: none -> 212 us  [the longest x2 106 us: front(): pl.pallas_call(functools.partial(front_kernel, splits, owners), grid=(ste...]
    convert_element_type x2 -> x1, other arithmetic: 191 us -> 0.01 us  [keep_table(): jnp.all(flagged[:, :, None] != fine[None, None, :], axis=1)]
    ppermute x1 -> x20, waiting for transfers between devices: 0.01 us -> 170 us  [the longest x15 170 us: shift(): lax.ppermute(value, 'station', [(s, (s + d) % count) for s in range(count)])]
    ppermute x1 -> x20, starting transfers between devices: 1.29 us -> 85.7 us  [the longest x15 72.9 us: shift(): lax.ppermute(value, 'station', [(s, (s + d) % count) for s in range(count)])]
    dot_general x3 -> x0, matrix products: 79.5 us -> none  [the longest x1 30 us: pair_products(): jnp.einsum('cgfird,cgfjrd->icgj', left, right, preferred_element_type=jnp...]
    psum x1, blocking collectives: 11.9 us -> 81.8 us  [pipelined(): total = lax.psum(local, ('band', 'tm'))]
    reshape x1, local copies, waits for them, and re-layouts: 26.6 us -> 0.08 us  [pipelined(): counts = kept.reshape(groups, GROUP).sum(-1)]
  transfers between devices with their start and end apart: 3 -> 20, of which waited for: 2 -> 5; matrix products, arithmetic and copies ran while one was open for 3% -> 1% of each run, Pallas kernels for 0% -> 35%
where the time goes in v1:
time: 590 us; the launch traced here: 584 us
  Pallas kernels  212 us (36%)
  waiting for transfers between devices  170 us (29%)
  blocking collectives  88.9 us (15%)
  starting transfers between devices  85.7 us (15%)
  local copies, waits for them, and re-layouts  22.6 us (4%)
    ppermute x15, waiting for transfers between devices, shift(): lax.ppermute(value, 'station', [(s, (s + d) % count) for s in range(count)])  170 us
    pallas_call x2, Pallas kernels, front(): pl.pallas_call(functools.partial(front_kernel, splits, owners), grid=(ste...  106 us
    pallas_call x8, Pallas kernels, correlate(): pl.pallas_call(functools.partial(correlate_kernel, owners, group), grid=(...  85.7 us
    psum x1, blocking collectives, pipelined(): total = lax.psum(local, ('band', 'tm'))  81.8 us
    ppermute x15, starting transfers between devices, shift(): lax.ppermute(value, 'station', [(s, (s + d) % count) for s in range(count)])  72.9 us
    pallas_call x4, Pallas kernels, equalize(): pl.pallas_call(equalize_kernel, grid=(rows // block,), out_shape=jax.Shap...  20.7 us
    unnamed x77, local copies, waits for them, and re-layouts  17.5 us
  transfers between devices with their start and end apart: 20, of which 5 were waited for; matrix products, arithmetic and copies ran while one was open for 1% of the time, Pallas kernels for 35%

profile of v1, /device:TPU:11, one launch (start us, length us, event | category | flops | bytes accessed | tf_op | source)
XLA Modules:
  0.0 583.5 jit_solution(6915215213019597333)
XLA Ops:
  0.0 3.3 slice.15
  3.3 1.3 collective-permute-start
  5.3 16.0 %front.2 = (bf16[4,2,9,16,256]{4,3,2,1,0:T(8,128)(2,1)S(1)}, bf16[4,2,9,16,256]{4,3,2,1,0:T(8,128)(2,1)S(1)}, bf16[4,2,9,16,256]{4,3,2,1,0:T(8,128)(2,1)S(1)}, b...) custom-call(f32[144]{0:T(256)S(1)} %dynamic_slice.17.keep_ref, bf16[2,1,256,18432]{3,2,1,0:T(8,128)(2,1)} %volts_ref.3, ...), custom_call_target="tpu_custom_call" | custom-call | flops 2717908992 | bytes 9437184 | tf_op jit(solution)/shard_map/front/pallas_call | solution.py:138
  21.3 2.4 collective-permute-start.2
  23.9 89.6 %front.3 = (bf16[1,2,9,112,256]{4,3,2,1,0:T(8,128)(2,1)S(1)}, bf16[1,2,9,112,256]{4,3,2,1,0:T(8,128)(2,1)S(1)}, bf16[1,2,9,112,256]{4,3,2,1,0:T(8,128)(2,1)S(1)}...) custom-call(f32[144]{0:T(256)S(1)} %dynamic_slice.17.keep_ref, ...), custom_call_target="tpu_custom_call" | custom-call | flops 19025362944 | bytes 66060288 | tf_op jit(solution)/shard_map/front/pallas_call | solution.py:138
  113.5 1.0 copy-done.22
  114.5 1.0 copy-done.25
  115.4 1.0 copy-done.28
  116.4 1.0 copy-done.31
  118.3 1.1 collective-permute-start.8
  120.2 1.4 collective-permute-start.6
  121.6 77.3 %collective-permute-done.1.other_ref.rest_1_ = bf16[4,2,144,256]{3,2,1,0:T(8,128)(2,1)S(1)} collective-permute-done((bf16[4,2,144,256]{3,2,1,0:T(8,128)(2,1)S(1)}, bf16[4,2,144,256]{3,2,1,0:T(8,128)(2,1)S(1)}, u32[]{:S(2)}, u32[]{:S(2)}) %collective-permute-start.1) | collective-permute-done | bytes 589856 | tf_op jit(solution)/shard_map/ppermute | solution.py:290
  199.7 2.2 collective-permute-start.4
  202.0 1.3 collective-permute-start.13
  203.4 60.7 %collective-permute-start.9 = (bf16[1,2,1008,256]{3,2,1,0:T(8,128)(2,1)}, bf16[1,2,1008,256]{3,2,1,0:T(8,128)(2,1)}, u32[]{:S(2)}, u32[]{:S(2)}) collective-permute-start(bf16[1,2,1008,256]{3,2,1,0:T(8,128)(2,1)} %after.14), channel_id=1, source_target_pairs={{0,24},{8,0},{16,8},{24,16},{1,25},{9,1},{17,9},{25,17},{2,26},{10... | collective-permute-start | bytes 3096584 | tf_op jit(solution)/shard_map/ppermute | solution.py:290
  265.9 1.0 copy-done.3
  267.9 81.8 %psum.7 = f32[256]{0:T(256)S(1)} all-reduce(f32[256]{0:T(256)S(1)} %add_reduce_fusion), channel_id=1, replica_groups=mesh['station'=4,'band'=4,'tm'=2] {'band','tm'}, use_global_device_ids=true, to_apply=%region_2.3 | all-reduce | flops 256 | bytes 2048 | tf_op jit(solution)/shard_map/psum | solution.py:350
  349.7 7.0 %collective-permute-done.13.other_ref.rest_6_ = bf16[1,2,1008,256]{3,2,1,0:T(8,128)(2,1)} collective-permute-done((bf16[1,2,1008,256]{3,2,1,0:T(8,128)(2,1)}, bf16[1,2,1008,256]{3,2,1,0:T(8,128)(2,1)}, u32[]{:S(2)}, u32[]{:S(2)}) %collective-permute-start.13) | collective-permute-done | bytes 1032224 | tf_op jit(solution)/shard_map/ppermute | solution.py:290
  356.8 3.2 collective-permute-start.14
  360.0 58.0 %collective-permute-done.9.rest_7_ = bf16[1,2,1008,256]{3,2,1,0:T(8,128)(2,1)} collective-permute-done((bf16[1,2,1008,256]{3,2,1,0:T(8,128)(2,1)}, bf16[1,2,1008,256]{3,2,1,0:T(8,128)(2,1)}, u32[]{:S(2)}, u32[]{:S(2)}) %collective-permute-start.9) | collective-permute-done | bytes 1032224 | tf_op jit(solution)/shard_map/ppermute | solution.py:290
  418.0 1.1 copy-done.20
  419.1 1.2 copy-done.32
  420.3 10.6 %correlate.15 = bf16[2,512,1024]{2,1,0:T(8,128)(2,1)} custom-call(s32[2]{0:T(128)S(1)} %pad_add_fusion.1.place_ref, bf16[4,2,144,256]{3,2,1,0:T(8,128)(2,1)S(1)} %bitcast.41, bf16[4,2,144,256]{3,2,1,0:T(8,128)(2,1)S(1)} %copy-done.16, bf16[4,2,144,256]{3,2,1,0:T(8,128)(2,1)S(1)} %copy-done.10, bf16[4,2,144,256]{3,2,1,0:T(8,128)(2,1)S(1)} %copy-done.13, ...), custom_call_target="tpu_custom_call" | custom-call | flops 4831838208 | bytes 8912896 | tf_op jit(solution)/shard_map/correlate/pallas_call | solution.py:229
  430.9 10.6 %correlate.13 = bf16[2,512,1024]{2,1,0:T(8,128)(2,1)} custom-call(s32[2]{0:T(128)S(1)} %pad_add_fusion.1.place_ref, bf16[4,2,144,256]{3,2,1,0:T(8,128)(2,1)S(1)} %bitcast.42, bf16[4,2,144,256]{3,2,1,0:T(8,128)(2,1)S(1)} %copy-done.16, bf16[4,2,144,256]{3,2,1,0:T(8,128)(2,1)S(1)} %copy-done.10, bf16[4,2,144,256]{3,2,1,0:T(8,128)(2,1)S(1)} %copy-done.13, ...), custom_call_target="tpu_custom_call" | custom-call | flops 4831838208 | bytes 8912896 | tf_op jit(solution)/shard_map/correlate/pallas_call | solution.py:229
  441.5 7.7 %collective-permute-start.18 = (bf16[2,512,1024]{2,1,0:T(8,128)(2,1)}, bf16[2,512,1024]{2,1,0:T(8,128)(2,1)}, u32[]{:S(2)}, u32[]{:S(2)}) collective-permute-start(bf16[2,512,1024]{2,1,0:T(8,128)(2,1)} %correlate.13), channel_id=1, source_target_pairs={{0,1},{1,0},{2,3},{3,2},{4,5},{5,4},{6,7},{7,6},{8,9},{9,8},{10,11... | collective-permute-start | bytes 6291464 | tf_op jit(solution)/shard_map/ppermute | solution.py:365
  449.3 10.7 %correlate.9 = bf16[2,512,1024]{2,1,0:T(8,128)(2,1)} custom-call(s32[2]{0:T(128)S(1)} %pad_add_fusion.1.place_ref, bf16[4,2,144,256]{3,2,1,0:T(8,128)(2,1)S(1)} %bitcast.43, bf16[4,2,144,256]{3,2,1,0:T(8,128)(2,1)S(1)} %copy-done.17, bf16[4,2,144,256]{3,2,1,0:T(8,128)(2,1)S(1)} %copy-done.10, bf16[4,2,144,256]{3,2,1,0:T(8,128)(2,1)S(1)} %copy-done.13, ...), custom_call_target="tpu_custom_call" | custom-call | flops 4831838208 | bytes 8912896 | tf_op jit(solution)/shard_map/correlate/pallas_call | solution.py:229
  460.0 7.4 %collective-permute-done.12.rest_5_ = bf16[1,2,1008,256]{3,2,1,0:T(8,128)(2,1)} collective-permute-done((bf16[1,2,1008,256]{3,2,1,0:T(8,128)(2,1)}, bf16[1,2,1008,256]{3,2,1,0:T(8,128)(2,1)}, u32[]{:S(2)}, u32[]{:S(2)}) %collective-permute-start.12) | collective-permute-done | bytes 1032224 | tf_op jit(solution)/shard_map/ppermute | solution.py:290
  467.4 2.3 collective-permute-start.10
  469.6 19.8 %collective-permute-done.14.rest_6_ = bf16[1,2,1008,256]{3,2,1,0:T(8,128)(2,1)} collective-permute-done((bf16[1,2,1008,256]{3,2,1,0:T(8,128)(2,1)}, bf16[1,2,1008,256]{3,2,1,0:T(8,128)(2,1)}, u32[]{:S(2)}, u32[]{:S(2)}) %collective-permute-start.14) | collective-permute-done | bytes 1032224 | tf_op jit(solution)/shard_map/ppermute | solution.py:290
  489.5 1.0 copy-done.37
  490.4 10.6 %correlate.11 = bf16[2,512,1024]{2,1,0:T(8,128)(2,1)} custom-call(s32[2]{0:T(128)S(1)} %pad_add_fusion.1.place_ref, bf16[4,2,144,256]{3,2,1,0:T(8,128)(2,1)S(1)} %bitcast.44, bf16[4,2,144,256]{3,2,1,0:T(8,128)(2,1)S(1)} %copy-done.17, bf16[4,2,144,256]{3,2,1,0:T(8,128)(2,1)S(1)} %copy-done.10, bf16[4,2,144,256]{3,2,1,0:T(8,128)(2,1)S(1)} %copy-done.13, ...), custom_call_target="tpu_custom_call" | custom-call | flops 4831838208 | bytes 8912896 | tf_op jit(solution)/shard_map/correlate/pallas_call | solution.py:229
  501.0 1.4 collective-permute-start.17
  502.4 7.1 %all-gather = f32[4,1,256]{2,1,0:T(1,128)S(1)} all-gather(f32[1,1,256]{2,1,0:T(1,128)S(1)} %bitcast.73), channel_id=1, replica_groups=mesh['station'=4,'band'=4,'tm'=2] {'station'}, dimensions={0}, use_global_device_ids=true | all-gather | bytes 5120 | tf_op jit(solution)/shard_map/all_gather | solution.py:352
  509.5 2.5 broadcast_divide_fusion
  512.6 1.2 copy-done.8
  513.9 1.1 copy-done.11
  514.9 1.1 copy-done.14
  516.0 1.1 copy-done.18
  517.0 1.1 copy-done.21
  518.1 1.2 copy-done.33
  519.3 10.8 %correlate.14.mine_ref = f32[2,512,1024]{2,1,0:T(8,128)} custom-call(s32[2]{0:T(128)S(1)} %pad_add_fusion.place_ref, bf16[4,2,144,256]{3,2,1,0:T(8,128)(2,1)S(1)} %bitcast.45, bf16[4,2,144,256]{3,2,1,0:T(8,128)(2,1)S(1)} %copy-done.18, bf16[4,2,144,256]{3,2,1,0:T(8,128)(2,1)S(1)} %copy-done.11, bf16[4,2,144,256]{3,2,1,0:T(8,128)(2,1)S(1)} %copy-done.14, ...), custom_call_target="tpu_custom_call" | custom-call | flops 4831838208 | bytes 8912896 | tf_op jit(solution)/shard_map/correlate/pallas_call | solution.py:229
  530.2 10.8 %correlate.12.mine_ref = f32[2,512,1024]{2,1,0:T(8,128)} custom-call(s32[2]{0:T(128)S(1)} %pad_add_fusion.place_ref, bf16[4,2,144,256]{3,2,1,0:T(8,128)(2,1)S(1)} %bitcast.46, bf16[4,2,144,256]{3,2,1,0:T(8,128)(2,1)S(1)} %copy-done.18, bf16[4,2,144,256]{3,2,1,0:T(8,128)(2,1)S(1)} %copy-done.11, bf16[4,2,144,256]{3,2,1,0:T(8,128)(2,1)S(1)} %copy-done.14, ...), custom_call_target="tpu_custom_call" | custom-call | flops 4831838208 | bytes 8912896 | tf_op jit(solution)/shard_map/correlate/pallas_call | solution.py:229
  541.0 10.9 %correlate.10.mine_ref = f32[2,512,1024]{2,1,0:T(8,128)} custom-call(s32[2]{0:T(128)S(1)} %pad_add_fusion.place_ref, bf16[4,2,144,256]{3,2,1,0:T(8,128)(2,1)S(1)} %bitcast.47, bf16[4,2,144,256]{3,2,1,0:T(8,128)(2,1)S(1)} %copy-done.18, bf16[4,2,144,256]{3,2,1,0:T(8,128)(2,1)S(1)} %copy-done.11, bf16[4,2,144,256]{3,2,1,0:T(8,128)(2,1)S(1)} %copy-done.14, ...), custom_call_target="tpu_custom_call" | custom-call | flops 4831838208 | bytes 8912896 | tf_op jit(solution)/shard_map/correlate/pallas_call | solution.py:229
  551.9 10.8 %correlate.8.mine_ref = f32[2,512,1024]{2,1,0:T(8,128)} custom-call(s32[2]{0:T(128)S(1)} %pad_add_fusion.place_ref, bf16[4,2,144,256]{3,2,1,0:T(8,128)(2,1)S(1)} %bitcast.48, bf16[4,2,144,256]{3,2,1,0:T(8,128)(2,1)S(1)} %copy-done.18, bf16[4,2,144,256]{3,2,1,0:T(8,128)(2,1)S(1)} %copy-done.11, bf16[4,2,144,256]{3,2,1,0:T(8,128)(2,1)S(1)} %copy-done.14, ...), custom_call_target="tpu_custom_call" | custom-call | flops 4831838208 | bytes 8912896 | tf_op jit(solution)/shard_map/correlate/pallas_call | solution.py:229
  562.8 4.9 equalize.4.rest_0_
  567.7 5.3 equalize.5.rest_0_
  572.9 5.3 equalize.6.rest_0_
  578.2 5.3 equalize.7
  (117 shorter events, 6.5 us)
Async XLA Ops:
  0.0 5.0 copy-start.34
  0.0 5.0 copy-start.35
  0.0 4.6 copy-start.36
  3.3 20.6 %collective-permute-start = (bf16[2,1,256,2304]{3,2,1,0:T(8,128)(2,1)}, bf16[2,1,256,2304]{3,2,1,0:T(8,128)(2,1)}, u32[]{:S(2)}, u32[]{:S(2)}) collective-permute-start(bf16[2,1,256,2304]{3,2,1,0:T(8,128)(2,1)} %slice.15), channel_id=1, source_target_pairs={{0,1},{2,3},{4,5},{6,7},{8,9},{10,11},{12,13},{14,15},{16,17},{18,... | collective-permute-start | bytes 7077896 | tf_op jit(solution)/shard_map/ppermute | solution.py:295
  21.3 92.2 %copy-start.19 = (bf16[4,2,9,16,256]{4,3,2,1,0:T(8,128)(2,1)}, bf16[4,2,9,16,256]{4,3,2,1,0:T(8,128)(2,1)S(1)}, u32[]{:S(2)}) copy-start(bf16[4,2,9,16,256]{4,3,2,1,0:T(8,128)(2,1)S(1)} %get-tuple-element.29) | copy-start | bytes 1769476
  21.3 98.0 %collective-permute-start.2 = (bf16[4,2,144,256]{3,2,1,0:T(8,128)(2,1)S(1)}, bf16[4,2,144,256]{3,2,1,0:T(8,128)(2,1)S(1)}, u32[]{:S(2)}, u32[]{:S(2)}) collective-permute-start(bf16[4,2,144,256]{3,2,1,0:T(8,128)(2,1)S(1)} %bitcast.50), channel_id=1, source_target_pairs={{0,16},{8,24},{16,0},{24,8},{1,17},{9,25},{17,1},{25,9},{2,18},{10... | collective-permute-start | bytes 1769480 | tf_op jit(solution)/shard_map/ppermute | solution.py:290
  23.7 93.7 %collective-permute-start.3 = (bf16[4,2,144,256]{3,2,1,0:T(8,128)(2,1)S(1)}, bf16[4,2,144,256]{3,2,1,0:T(8,128)(2,1)S(1)}, u32[]{:S(2)}, u32[]{:S(2)}) collective-permute-start(bf16[4,2,144,256]{3,2,1,0:T(8,128)(2,1)S(1)} %bitcast.51), channel_id=1, source_target_pairs={{0,24},{8,0},{16,8},{24,16},{1,25},{9,1},{17,9},{25,17},{2,26},{10... | collective-permute-start | bytes 1769480 | tf_op jit(solution)/shard_map/ppermute | solution.py:290
  118.3 85.0 %collective-permute-start.8 = (bf16[1,2,1008,256]{3,2,1,0:T(8,128)(2,1)}, bf16[1,2,1008,256]{3,2,1,0:T(8,128)(2,1)}, u32[]{:S(2)}, u32[]{:S(2)}) collective-permute-start(bf16[1,2,1008,256]{3,2,1,0:T(8,128)(2,1)} %after.13), channel_id=1, source_target_pairs={{0,24},{8,0},{16,8},{24,16},{1,25},{9,1},{17,9},{25,17},{2,26},{10... | collective-permute-start | bytes 3096584 | tf_op jit(solution)/shard_map/ppermute | solution.py:290
  120.2 83.2 %collective-permute-start.6 = (bf16[1,2,1008,256]{3,2,1,0:T(8,128)(2,1)}, bf16[1,2,1008,256]{3,2,1,0:T(8,128)(2,1)S(1)}, u32[]{:S(2)}, u32[]{:S(2)}) collective-permute-start(bf16[1,2,1008,256]{3,2,1,0:T(8,128)(2,1)} %after.11), channel_id=1, source_target_pairs={{0,16},{8,24},{16,0},{24,8},{1,17},{9,25},{17,1},{25,9},{2,18},{10... | collective-permute-start | bytes 3096584 | tf_op jit(solution)/shard_map/ppermute | solution.py:290
  121.6 77.3 %collective-permute-start.1 = (bf16[4,2,144,256]{3,2,1,0:T(8,128)(2,1)S(1)}, bf16[4,2,144,256]{3,2,1,0:T(8,128)(2,1)S(1)}, u32[]{:S(2)}, u32[]{:S(2)}) collective-permute-start(bf16[4,2,144,256]{3,2,1,0:T(8,128)(2,1)S(1)} %bitcast.49), channel_id=1, source_target_pairs={{0,8},{8,16},{16,24},{24,0},{1,9},{9,17},{17,25},{25,1},{2,10},{10... | collective-permute-start | bytes 1769480 | tf_op jit(solution)/shard_map/ppermute | solution.py:290
  199.7 66.1 %collective-permute-start.4 = (bf16[1,2,1008,256]{3,2,1,0:T(8,128)(2,1)}, bf16[1,2,1008,256]{3,2,1,0:T(8,128)(2,1)S(1)}, u32[]{:S(2)}, u32[]{:S(2)}) collective-permute-start(bf16[1,2,1008,256]{3,2,1,0:T(8,128)(2,1)} %after.9), channel_id=1, source_target_pairs={{0,8},{8,16},{16,24},{24,0},{1,9},{9,17},{17,25},{25,1},{2,10},{10... | collective-permute-start | bytes 3096584 | tf_op jit(solution)/shard_map/ppermute | solution.py:290
  201.9 65.0 %collective-permute-start.11 = (bf16[1,2,1008,256]{3,2,1,0:T(8,128)(2,1)}, bf16[1,2,1008,256]{3,2,1,0:T(8,128)(2,1)S(1)}, u32[]{:S(2)}, u32[]{:S(2)}) collective-permute-start(bf16[1,2,1008,256]{3,2,1,0:T(8,128)(2,1)} %bitcast.77), channel_id=1, source_target_pairs={{0,8},{8,16},{16,24},{24,0},{1,9},{9,17},{17,25},{25,1},{2,10},{10... | collective-permute-start | bytes 3096584 | tf_op jit(solution)/shard_map/ppermute | solution.py:290
  202.0 154.8 %collective-permute-start.13 = (bf16[1,2,1008,256]{3,2,1,0:T(8,128)(2,1)}, bf16[1,2,1008,256]{3,2,1,0:T(8,128)(2,1)}, u32[]{:S(2)}, u32[]{:S(2)}) collective-permute-start(bf16[1,2,1008,256]{3,2,1,0:T(8,128)(2,1)} %bitcast.76), channel_id=1, source_target_pairs={{0,16},{8,24},{16,0},{24,8},{1,17},{9,25},{17,1},{25,9},{2,18},{10... | collective-permute-start | bytes 3096584 | tf_op jit(solution)/shard_map/ppermute | solution.py:290
  203.3 153.5 %collective-permute-start.15 = (bf16[1,2,1008,256]{3,2,1,0:T(8,128)(2,1)}, bf16[1,2,1008,256]{3,2,1,0:T(8,128)(2,1)}, u32[]{:S(2)}, u32[]{:S(2)}) collective-permute-start(bf16[1,2,1008,256]{3,2,1,0:T(8,128)(2,1)} %bitcast.75), channel_id=1, source_target_pairs={{0,24},{8,0},{16,8},{24,16},{1,25},{9,1},{17,9},{25,17},{2,26},{10... | collective-permute-start | bytes 3096584 | tf_op jit(solution)/shard_map/ppermute | solution.py:290
  203.4 62.4 %copy-start = (bf16[1,2,1008,256]{3,2,1,0:T(8,128)(2,1)}, bf16[1,2,1008,256]{3,2,1,0:T(8,128)(2,1)S(1)}, u32[]{:S(2)}) copy-start(bf16[1,2,1008,256]{3,2,1,0:T(8,128)(2,1)S(1)} %collective-permute-done.6.other_ref.rest_6_) | copy-start | bytes 3096580
  203.4 214.5 %collective-permute-start.9 = (bf16[1,2,1008,256]{3,2,1,0:T(8,128)(2,1)}, bf16[1,2,1008,256]{3,2,1,0:T(8,128)(2,1)}, u32[]{:S(2)}, u32[]{:S(2)}) collective-permute-start(bf16[1,2,1008,256]{3,2,1,0:T(8,128)(2,1)} %after.14), channel_id=1, source_target_pairs={{0,24},{8,0},{16,8},{24,16},{1,25},{9,1},{17,9},{25,17},{2,26},{10... | collective-permute-start | bytes 3096584 | tf_op jit(solution)/shard_map/ppermute | solution.py:290
  265.8 1.1 copy-start.3
  265.9 175.7 %collective-permute-start.7 = (bf16[1,2,1008,256]{3,2,1,0:T(8,128)(2,1)}, bf16[1,2,1008,256]{3,2,1,0:T(8,128)(2,1)}, u32[]{:S(2)}, u32[]{:S(2)}) collective-permute-start(bf16[1,2,1008,256]{3,2,1,0:T(8,128)(2,1)} %after.12), channel_id=1, source_target_pairs={{0,16},{8,24},{16,0},{24,8},{1,17},{9,25},{17,1},{25,9},{2,18},{10... | collective-permute-start | bytes 3096584 | tf_op jit(solution)/shard_map/ppermute | solution.py:290
  266.9 82.8 %copy-start.6 = (bf16[1,2,1008,256]{3,2,1,0:T(8,128)(2,1)}, bf16[1,2,1008,256]{3,2,1,0:T(8,128)(2,1)S(1)}, u32[]{:S(2)}) copy-start(bf16[1,2,1008,256]{3,2,1,0:T(8,128)(2,1)S(1)} %collective-permute-done.11.other_ref.rest_5_) | copy-start | bytes 3096580
  266.9 182.3 %collective-permute-start.5 = (bf16[1,2,1008,256]{3,2,1,0:T(8,128)(2,1)}, bf16[1,2,1008,256]{3,2,1,0:T(8,128)(2,1)}, u32[]{:S(2)}, u32[]{:S(2)}) collective-permute-start(bf16[1,2,1008,256]{3,2,1,0:T(8,128)(2,1)} %after.10), channel_id=1, source_target_pairs={{0,8},{8,16},{16,24},{24,0},{1,9},{9,17},{17,25},{25,1},{2,10},{10... | collective-permute-start | bytes 3096584 | tf_op jit(solution)/shard_map/ppermute | solution.py:290
  356.8 110.6 %collective-permute-start.12 = (bf16[1,2,1008,256]{3,2,1,0:T(8,128)(2,1)}, bf16[1,2,1008,256]{3,2,1,0:T(8,128)(2,1)}, u32[]{:S(2)}, u32[]{:S(2)}) collective-permute-start(bf16[1,2,1008,256]{3,2,1,0:T(8,128)(2,1)} %after.15), channel_id=1, source_target_pairs={{0,8},{8,16},{16,24},{24,0},{1,9},{9,17},{17,25},{25,1},{2,10},{10... | collective-permute-start | bytes 3096584 | tf_op jit(solution)/shard_map/ppermute | solution.py:290
  356.8 61.2 %copy-start.7 = (bf16[1,2,1008,256]{3,2,1,0:T(8,128)(2,1)S(1)}, bf16[1,2,1008,256]{3,2,1,0:T(8,128)(2,1)}, u32[]{:S(2)}) copy-start(bf16[1,2,1008,256]{3,2,1,0:T(8,128)(2,1)} %copy-done.6) | copy-start | bytes 3096580
  356.8 61.2 %copy-start.10 = (bf16[4,2,144,256]{3,2,1,0:T(8,128)(2,1)S(1)}, bf16[4,2,144,256]{3,2,1,0:T(8,128)(2,1)}, u32[]{:S(2)}) copy-start(bf16[4,2,144,256]{3,2,1,0:T(8,128)(2,1)} %copy-done.9) | copy-start | bytes 1769476
  356.8 61.2 %copy-start.13 = (bf16[4,2,144,256]{3,2,1,0:T(8,128)(2,1)S(1)}, bf16[4,2,144,256]{3,2,1,0:T(8,128)(2,1)}, u32[]{:S(2)}) copy-start(bf16[4,2,144,256]{3,2,1,0:T(8,128)(2,1)} %copy-done.12) | copy-start | bytes 1769476
  356.8 61.2 %copy-start.16 = (bf16[4,2,144,256]{3,2,1,0:T(8,128)(2,1)S(1)}, bf16[4,2,144,256]{3,2,1,0:T(8,128)(2,1)}, u32[]{:S(2)}) copy-start(bf16[4,2,144,256]{3,2,1,0:T(8,128)(2,1)} %copy-done.15) | copy-start | bytes 1769476
  356.8 132.7 %collective-permute-start.14 = (bf16[1,2,1008,256]{3,2,1,0:T(8,128)(2,1)}, bf16[1,2,1008,256]{3,2,1,0:T(8,128)(2,1)}, u32[]{:S(2)}, u32[]{:S(2)}) collective-permute-start(bf16[1,2,1008,256]{3,2,1,0:T(8,128)(2,1)} %after.16), channel_id=1, source_target_pairs={{0,16},{8,24},{16,0},{24,8},{1,17},{9,25},{17,1},{25,9},{2,18},{10... | collective-permute-start | bytes 3096584 | tf_op jit(solution)/shard_map/ppermute | solution.py:290
  418.0 71.5 %collective-permute-start.16 = (bf16[1,2,1008,256]{3,2,1,0:T(8,128)(2,1)}, bf16[1,2,1008,256]{3,2,1,0:T(8,128)(2,1)S(1)}, u32[]{:S(2)}, u32[]{:S(2)}) collective-permute-start(bf16[1,2,1008,256]{3,2,1,0:T(8,128)(2,1)} %after.17), channel_id=1, source_target_pairs={{0,24},{8,0},{16,8},{24,16},{1,25},{9,1},{17,9},{25,17},{2,26},{10... | collective-permute-start | bytes 3096584 | tf_op jit(solution)/shard_map/ppermute | solution.py:290
  418.0 1.1 copy-start.20
  419.1 1.2 copy-start.32
  420.3 10.6 %copy-start.1 = (bf16[1,2,1008,256]{3,2,1,0:T(8,128)(2,1)S(1)}, bf16[1,2,1008,256]{3,2,1,0:T(8,128)(2,1)}, u32[]{:S(2)}) copy-start(bf16[1,2,1008,256]{3,2,1,0:T(8,128)(2,1)} %copy-done) | copy-start | bytes 3096580
  420.3 10.6 %copy-start.4 = (bf16[1,2,1008,256]{3,2,1,0:T(8,128)(2,1)S(1)}, bf16[1,2,1008,256]{3,2,1,0:T(8,128)(2,1)}, u32[]{:S(2)}) copy-start(bf16[1,2,1008,256]{3,2,1,0:T(8,128)(2,1)} %copy-done.3) | copy-start | bytes 3096580
  420.3 10.6 %copy-start.29 = (bf16[1,2,9,112,256]{4,3,2,1,0:T(8,128)(2,1)S(1)}, bf16[1,2,9,112,256]{4,3,2,1,0:T(8,128)(2,1)}, u32[]{:S(2)}) copy-start(bf16[1,2,9,112,256]{4,3,2,1,0:T(8,128)(2,1)} %copy-done.28) | copy-start | bytes 3096580
  430.9 18.4 %copy-start.17 = (bf16[4,2,144,256]{3,2,1,0:T(8,128)(2,1)S(1)}, bf16[4,2,144,256]{3,2,1,0:T(8,128)(2,1)}, u32[]{:S(2)}) copy-start(bf16[4,2,144,256]{3,2,1,0:T(8,128)(2,1)} %copy-done.15) | copy-start | bytes 1769476
  430.9 18.4 %copy-start.23 = (bf16[1,2,9,112,256]{4,3,2,1,0:T(8,128)(2,1)S(1)}, bf16[1,2,9,112,256]{4,3,2,1,0:T(8,128)(2,1)}, u32[]{:S(2)}) copy-start(bf16[1,2,9,112,256]{4,3,2,1,0:T(8,128)(2,1)} %copy-done.22) | copy-start | bytes 3096580
  441.5 126.1 %collective-permute-start.18 = (bf16[2,512,1024]{2,1,0:T(8,128)(2,1)}, bf16[2,512,1024]{2,1,0:T(8,128)(2,1)}, u32[]{:S(2)}, u32[]{:S(2)}) collective-permute-start(bf16[2,512,1024]{2,1,0:T(8,128)(2,1)} %correlate.13), channel_id=1, source_target_pairs={{0,1},{1,0},{2,3},{3,2},{4,5},{5,4},{6,7},{7,6},{8,9},{9,8},{10,11... | collective-permute-start | bytes 6291464 | tf_op jit(solution)/shard_map/ppermute | solution.py:365
  449.2 113.5 %collective-permute-start.19 = (bf16[2,512,1024]{2,1,0:T(8,128)(2,1)}, bf16[2,512,1024]{2,1,0:T(8,128)(2,1)S(1)}, u32[]{:S(2)}, u32[]{:S(2)}) collective-permute-start(bf16[2,512,1024]{2,1,0:T(8,128)(2,1)} %correlate.15), channel_id=1, source_target_pairs={{0,1},{1,0},{2,3},{3,2},{4,5},{5,4},{6,7},{7,6},{8,9},{9,8},{10,11... | collective-permute-start | bytes 6291464 | tf_op jit(solution)/shard_map/ppermute | solution.py:365
  449.3 41.1 %copy-start.26 = (bf16[1,2,9,112,256]{4,3,2,1,0:T(8,128)(2,1)S(1)}, bf16[1,2,9,112,256]{4,3,2,1,0:T(8,128)(2,1)}, u32[]{:S(2)}) copy-start(bf16[1,2,9,112,256]{4,3,2,1,0:T(8,128)(2,1)} %copy-done.25) | copy-start | bytes 3096580
  467.4 110.9 %collective-permute-start.10 = (bf16[2,512,1024]{2,1,0:T(8,128)(2,1)}, bf16[2,512,1024]{2,1,0:T(8,128)(2,1)}, u32[]{:S(2)}, u32[]{:S(2)}) collective-permute-start(bf16[2,512,1024]{2,1,0:T(8,128)(2,1)} %correlate.9), channel_id=1, source_target_pairs={{0,1},{1,0},{2,3},{3,2},{4,5},{5,4},{6,7},{7,6},{8,9},{9,8},{10,11... | collective-permute-start | bytes 6291464 | tf_op jit(solution)/shard_map/ppermute | solution.py:365
  501.0 71.9 %collective-permute-start.17 = (bf16[2,512,1024]{2,1,0:T(8,128)(2,1)}, bf16[2,512,1024]{2,1,0:T(8,128)(2,1)}, u32[]{:S(2)}, u32[]{:S(2)}) collective-permute-start(bf16[2,512,1024]{2,1,0:T(8,128)(2,1)} %correlate.11), channel_id=1, source_target_pairs={{0,1},{1,0},{2,3},{3,2},{4,5},{5,4},{6,7},{7,6},{8,9},{9,8},{10,11... | collective-permute-start | bytes 6291464 | tf_op jit(solution)/shard_map/ppermute | solution.py:365
  512.6 1.2 copy-start.8
  514.9 1.1 copy-start.14
  516.0 1.1 copy-start.18
  518.1 1.2 copy-start.33
  519.3 10.8 %copy-start.2 = (bf16[1,2,1008,256]{3,2,1,0:T(8,128)(2,1)S(1)}, bf16[1,2,1008,256]{3,2,1,0:T(8,128)(2,1)}, u32[]{:S(2)}) copy-start(bf16[1,2,1008,256]{3,2,1,0:T(8,128)(2,1)} %copy-done) | copy-start | bytes 3096580
  519.3 10.8 %copy-start.5 = (bf16[1,2,1008,256]{3,2,1,0:T(8,128)(2,1)S(1)}, bf16[1,2,1008,256]{3,2,1,0:T(8,128)(2,1)}, u32[]{:S(2)}) copy-start(bf16[1,2,1008,256]{3,2,1,0:T(8,128)(2,1)} %copy-done.3) | copy-start | bytes 3096580
  519.3 10.8 %copy-start.30 = (bf16[1,2,9,112,256]{4,3,2,1,0:T(8,128)(2,1)S(1)}, bf16[1,2,9,112,256]{4,3,2,1,0:T(8,128)(2,1)}, u32[]{:S(2)}) copy-start(bf16[1,2,9,112,256]{4,3,2,1,0:T(8,128)(2,1)} %copy-done.28) | copy-start | bytes 3096580
  530.2 10.8 %copy-start.27 = (bf16[1,2,9,112,256]{4,3,2,1,0:T(8,128)(2,1)S(1)}, bf16[1,2,9,112,256]{4,3,2,1,0:T(8,128)(2,1)}, u32[]{:S(2)}) copy-start(bf16[1,2,9,112,256]{4,3,2,1,0:T(8,128)(2,1)} %copy-done.25) | copy-start | bytes 3096580
  541.0 10.9 %copy-start.24 = (bf16[1,2,9,112,256]{4,3,2,1,0:T(8,128)(2,1)S(1)}, bf16[1,2,9,112,256]{4,3,2,1,0:T(8,128)(2,1)}, u32[]{:S(2)}) copy-start(bf16[1,2,9,112,256]{4,3,2,1,0:T(8,128)(2,1)} %copy-done.22) | copy-start | bytes 3096580
  (10 other events, 9.5 us)

commit v2 on v1

--- a/solution.py
+++ b/solution.py
@@ -13,9 +13,9 @@
 TAPS = 12
 GROUP = 9
 BLOCK = 16
-FIRST = 1
+PARTS = (1, 3)
 SPREAD = BLOCK + 1
-VMEM = 48 * 1024 * 1024
+VMEM = 60 * 1024 * 1024
 
 
 def window_values():
@@ -36,31 +36,42 @@
     return np.stack([real, imag], 1).astype(np.float32)
 
 
-def front_kernel(splits, owners, keep_ref, hist_ref, volts_ref, window_ref, table_ref, *rest):
+def front_kernel(
+    splits, owners, turned, tail, keep_ref, hist_ref, volts_ref, window_ref, table_ref, *rest
+):
     outs, power_ref = rest[: owners * splits], rest[owners * splits]
-    ring, filt, spread = rest[owners * splits + 1 :]
+    tail_ref = rest[owners * splits + 1] if tail else None
+    ring, filt, spread = rest[-3:]
     step = pl.program_id(0)
     now = lax.rem(step, 2)
     before = 1 - now
     inputs = ring.shape[-1]
     tiles = inputs // 128
     span = BLOCK * SUBBAND_COUNT
-
-    def turn(ref, slot):
+    skipped = (BLOCK + 1 - TAPS) * SUBBAND_COUNT
+
+    def turn(ref, slot, begin):
         def columns(c, _):
             at = pl.multiple_of(c * 128, 128)
             for part in range(2):
                 ring[slot, part, pl.ds(at, 128), :] = ref[part, 0, :, pl.ds(at, 128)].T
             return 0
 
-        lax.fori_loop(0, span // 128, columns, 0)
+        lax.fori_loop(begin, span // 128, columns, 0, unroll=6 if begin == 0 else 1)
 
     @pl.when(step == 0)
     def _():
-        turn(hist_ref, 1)
+        if turned:
+            for part in range(2):
+                ring[1, part, pl.ds(skipped, span - skipped), :] = hist_ref[part]
+        else:
+            turn(hist_ref, 1, skipped // 128)
         power_ref[...] = jnp.zeros_like(power_ref)
 
-    turn(volts_ref, now)
+    turn(volts_ref, now, 0)
+    if tail:
+        for part in range(2):
+            tail_ref[part] = ring[now, part, pl.ds(skipped, span - skipped), :]
 
     def filter_rows(j, _):
         base = pl.multiple_of(j * 16, 16)
@@ -91,7 +102,7 @@
             ]
         return 0
 
-    lax.fori_loop(0, BLOCK, transform, 0)
+    lax.fori_loop(0, BLOCK, transform, 0, unroll=4)
 
     groups = SUBBAND_COUNT // owners // GROUP
     power = [jnp.zeros((BLOCK, 128), jnp.float32) for _ in range(tiles)]
@@ -113,12 +124,12 @@
                         power[tile] = power[tile] + value * value
                 return tuple(power)
 
-            power = lax.fori_loop(0, GROUP, channel, tuple(power))
+            power = lax.fori_loop(0, GROUP, channel, tuple(power), unroll=3)
     for tile in range(tiles):
         power_ref[:, tile * 128 : (tile + 1) * 128] += power[tile]
 
 
-def front(volts, hist, hist_block, first, steps, splits, owners, keep, window, table):
+def front(volts, hist, first, steps, splits, owners, keep, window, table, tail):
     inputs = volts.shape[2]
     span = BLOCK * SUBBAND_COUNT
     groups = SUBBAND_COUNT // owners // GROUP
@@ -134,14 +145,23 @@
     ]
     outs.append(jax.ShapeDtypeStruct((BLOCK, inputs), jnp.float32))
     out_specs.append(pl.BlockSpec((BLOCK, inputs), lambda s: (0, 0)))
+    kept = (TAPS - 1) * SUBBAND_COUNT
+    if tail:
+        outs.append(jax.ShapeDtypeStruct((2, kept, inputs), jnp.bfloat16))
+        out_specs.append(pl.BlockSpec((2, kept, inputs), lambda s: (0, 0, 0)))
+    if hist is None:
+        hist, hist_spec = volts, pl.BlockSpec((2, 1, inputs, span), lambda s: (0, 0, 0, first - 1))
+        turned = False
+    else:
+        hist_spec, turned = pl.BlockSpec((2, kept, inputs), lambda s: (0, 0, 0)), True
     macs = 2 * SUBBAND_COUNT * frames * inputs * 2 * SUBBAND_COUNT
     result = pl.pallas_call(
-        functools.partial(front_kernel, splits, owners),
+        functools.partial(front_kernel, splits, owners, turned, tail),
         grid=(steps,),
         out_shape=outs,
         in_specs=[
             pl.BlockSpec(memory_space=pltpu.SMEM),
-            pl.BlockSpec((2, 1, inputs, span), lambda s: (0, 0, 0, hist_block)),
+            hist_spec,
             pl.BlockSpec((2, 1, inputs, span), lambda s: (0, 0, 0, first + s)),
             pl.BlockSpec(window.shape, lambda s: (0, 0, 0)),
             pl.BlockSpec(table.shape, lambda s: (0, 0)),
@@ -158,7 +178,8 @@
         ),
         name="front",
     )(keep, hist, volts, window, table)
-    return result[:-1], result[-1]
+    count = owners * splits
+    return result[:count], result[count], result[count + 1] if tail else None
 
 
 def after_kernel(value_ref, other_ref, out_ref):
@@ -178,64 +199,66 @@
     )(value, other)
 
 
-def correlate_kernel(owners, group, place_ref, *rest):
-    early, late = rest[:owners], rest[owners : 2 * owners]
-    out_ref, held, turned, sems = rest[2 * owners :]
+def correlate_kernel(owners, picks, place_ref, *rest):
+    count = len(picks)
+    pieces = [rest[n * owners : (n + 1) * owners] for n in range(count)]
+    out_ref, held, turned, sems = rest[-4:]
     me, half = place_ref[0], place_ref[1]
     column = pl.program_id(0)
-    per_half = turned.shape[0]
-    lead = early[0].shape[2]
+    per_half = owners // 2
+    inputs, depth = turned.shape[2], held.shape[2]
 
     @pl.when(column == 0)
     def _():
         copies = []
         for d in range(owners):
             source = lax.rem(me - d + owners, owners)
-            copies.append(
-                pltpu.make_async_copy(
-                    early[d].at[group], held.at[source, :, pl.ds(0, lead)], sems.at[0, d]
+            at = 0
+            for n in range(count):
+                size = pieces[n][d].shape[2]
+                copies.append(
+                    pltpu.make_async_copy(
+                        pieces[n][d].at[picks[n]], held.at[source, :, pl.ds(at, size)], sems.at[n, d]
+                    )
                 )
-            )
-            copies.append(
-                pltpu.make_async_copy(
-                    late[d].at[0],
-                    held.at[source, :, pl.ds(lead, late[d].shape[2])],
-                    sems.at[1, d],
-                )
-            )
+                at += size
         for copy in copies:
             copy.start()
         for copy in copies:
             copy.wait()
         for r in range(per_half):
-            for part in range(2):
-                turned[r, part] = held[half * per_half + r, part].T
-
-    real, imag = held[column, 0], held[column, 1]
-    width = real.shape[1]
-    dot = functools.partial(jnp.dot, preferred_element_type=jnp.float32)
-    for r in range(per_half):
-        rows = slice(r * width, (r + 1) * width)
-        out_ref[0, rows, :] = (dot(turned[r, 0], real) + dot(turned[r, 1], imag)).astype(out_ref.dtype)
-        out_ref[1, rows, :] = (dot(turned[r, 1], real) - dot(turned[r, 0], imag)).astype(out_ref.dtype)
-
-
-def correlate(place, early, late, group, dtype):
-    owners = len(early)
-    inputs = late[0].shape[-1]
-    depth = early[0].shape[2] + late[0].shape[2]
+            real = held[half * per_half + r, 0].T
+            imag = held[half * per_half + r, 1].T
+            turned[0, r, :, pl.ds(0, depth)] = real
+            turned[0, r, :, pl.ds(depth, depth)] = imag
+            turned[1, r, :, pl.ds(0, depth)] = imag
+            turned[1, r, :, pl.ds(depth, depth)] = -real
+
+    left = turned[...].reshape(2 * per_half * inputs, 2 * depth)
+    right = held[column].reshape(2 * depth, inputs)
+    both = jnp.dot(left, right, preferred_element_type=jnp.float32)
+    out_ref[...] = both.reshape(2, per_half * inputs, inputs).astype(out_ref.dtype)
+
+
+def correlate(place, pieces, picks, dtype, earlier):
+    owners = len(pieces[0])
+    inputs = pieces[0][0].shape[-1]
+    depth = sum(piece[0].shape[2] for piece in pieces)
     rows = owners // 2 * inputs
+    operands = [value for piece in pieces for value in piece]
+    if earlier is not None:
+        operands.append(earlier)
     anywhere = pl.BlockSpec(memory_space=pl.ANY)
     return pl.pallas_call(
-        functools.partial(correlate_kernel, owners, group),
+        functools.partial(correlate_kernel, owners, picks),
         grid=(owners,),
         out_shape=jax.ShapeDtypeStruct((2, rows, owners * inputs), dtype),
-        in_specs=[pl.BlockSpec(memory_space=pltpu.SMEM)] + [anywhere] * (2 * owners),
+        in_specs=[pl.BlockSpec(memory_space=pltpu.SMEM)] + [anywhere] * len(operands),
         out_specs=pl.BlockSpec((2, rows, inputs), lambda b: (0, 0, b)),
         scratch_shapes=[
             pltpu.VMEM((owners, 2, depth, inputs), jnp.bfloat16),
-            pltpu.VMEM((owners // 2, 2, inputs, depth), jnp.bfloat16),
-            pltpu.SemaphoreType.DMA((2, owners)),
+            pltpu.VMEM((2, owners // 2, inputs, 2 * depth), jnp.bfloat16),
+            pltpu.SemaphoreType.DMA((len(pieces), owners)),
         ],
         compiler_params=pltpu.CompilerParams(vmem_limit_bytes=VMEM),
         cost_estimate=pl.CostEstimate(
@@ -244,7 +267,7 @@
             transcendentals=0,
         ),
         name="correlate",
-    )(place, *early, *late)
+    )(place, *operands)
 
 
 def equalize_kernel(rows_ref, columns_ref, mine_ref, theirs_ref, *rest):
@@ -310,7 +333,6 @@
     fine = SUBBAND_COUNT // owners
     groups = fine // GROUP
     blocks = frames // BLOCK
-    span = BLOCK * SUBBAND_COUNT
 
     keep_all = keep_table(flagged)
     keep_mine = lax.dynamic_index_in_dim(keep_all, lax.axis_index("band"), 0, keepdims=False)
@@ -325,28 +347,33 @@
         jnp.asarray(window_values())[:, :, None], (TAPS, SUBBAND_COUNT, 128)
     )
 
-    halo = passed_on(volts[:, :, :, (blocks - 1) * span :])
-    rest = blocks - FIRST
-    early, power_a = front(volts, volts, rest - 1, rest, FIRST, 1, owners, keep_ahead, window, table)
-    late, power_b = front(volts, halo, 0, 0, rest, groups, owners, keep_ahead, window, table)
-
-    early = [x.reshape(groups, 2, GROUP * FIRST * BLOCK, inputs) for x in early]
-    late = [x.reshape(1, 2, GROUP * rest * BLOCK, inputs) for x in late]
-    late = [[late[d * groups + j] for d in range(owners)] for j in range(groups)]
-
-    sent = [early[0]] + [shift(early[d], d) for d in range(1, owners)]
+    parts, power, halo, end = [], [], None, blocks
+    for size in PARTS:
+        end -= size
+        spectra, part_power, tail = front(
+            volts, None, end, size, 1, owners, keep_ahead, window, table, halo is None
+        )
+        if tail is not None:
+            halo = passed_on(tail)
+        parts.append([x.reshape(groups, 2, GROUP * size * BLOCK, inputs) for x in spectra])
+        power.append(part_power)
+    spectra, part_power, _ = front(
+        volts, halo, 0, end, groups, owners, keep_ahead, window, table, False
+    )
+    power.append(part_power)
+    spectra = [x.reshape(1, 2, GROUP * end * BLOCK, inputs) for x in spectra]
+    for j in range(groups):
+        parts.append([spectra[d * groups + j] for d in range(owners)])
+
     arrived = []
-    for j in range(groups):
-        gate = sent if j == 1 else arrived[j - 2] if j > 1 else None
-        got = [late[j][0]]
+    for n, part in enumerate(parts):
+        got = [part[0]]
         for d in range(1, owners):
-            value = late[j][d]
-            if gate is not None:
-                value = after(value, gate[d])
+            value = part[d] if n < 2 else after(part[d], arrived[n - 2][d])
             got.append(shift(value, d))
         arrived.append(got)
 
-    local = jnp.sum(power_a + power_b, axis=0)
+    local = jnp.sum(sum(power), axis=0)
     total = lax.psum(local, ("band", "tm"))
     scale = lax.rsqrt(total / (frames_all * jnp.sum(keep_all)) + 1e-06)
     scales = lax.all_gather(scale, "station", axis=0, tiled=True)
@@ -360,10 +387,13 @@
     send_place = jnp.stack([me, 1 - half]).astype(jnp.int32)
     mine_place = jnp.stack([me, half]).astype(jnp.int32)
     out = None
+    shared = len(PARTS)
     for j in range(groups):
-        theirs = correlate(send_place, sent, arrived[j], j, jnp.bfloat16)
+        pieces = arrived[:shared] + [arrived[shared + j]]
+        picks = (j,) * shared + (0,)
+        theirs = correlate(send_place, pieces, picks, jnp.bfloat16, out)
         theirs = lax.ppermute(theirs, "tm", other)
-        mine = correlate(mine_place, sent, arrived[j], j, jnp.float32)
+        mine = correlate(mine_place, pieces, picks, jnp.float32, None)
         out = equalize(
             (row_scales / denom[j])[:, None], scales[None, :], mine, theirs, out, j, groups
         )
@@ -437,7 +467,7 @@
         and (SUBBAND_COUNT // owners) % GROUP == 0
         and lax.axis_size("tm") == 2
         and frames % BLOCK == 0
-        and frames // BLOCK > FIRST
+        and frames // BLOCK > sum(PARTS)
     )
     return (pipelined if fits else plain)(volts, flagged)
 

time: 590 us -> 574 us (0.973)
  waiting for transfers between devices: 170 us -> 274 us
  starting transfers between devices: 85.7 us -> 25.8 us
  blocking collectives: 88.9 us -> 59.8 us
  Pallas kernels: 212 us -> 188 us
  local copies, waits for them, and re-layouts: 22.6 us -> 15.8 us
    ppermute x15 -> x18, waiting for transfers between devices: 170 us -> 274 us  [shift(): lax.ppermute(value, 'station', [(s, (s + d) % count) for s in range(count)])]
    psum x1, blocking collectives: 81.8 us -> 11.3 us  [pipelined(): total = lax.psum(local, ('band', 'tm'))]
    ppermute x15 -> x18, starting transfers between devices: 72.9 us -> 20.2 us  [shift(): lax.ppermute(value, 'station', [(s, (s + d) % count) for s in range(count)])]
    all_gather x1, blocking collectives: 7.06 us -> 48.5 us  [pipelined(): scales = lax.all_gather(scale, 'station', axis=0, tiled=True)]
    pallas_call x10 -> x11, Pallas kernels: 191 us -> 166 us  [the longest x3 83.3 us: front(): pl.pallas_call(functools.partial(front_kernel, splits, owners, turned, ta...]
    unnamed x77 -> x33, local copies, waits for them, and re-layouts: 17.5 us -> 6.5 us
    ppermute x4, starting transfers between devices: 11.5 us -> 4.37 us  [pipelined(): theirs = lax.ppermute(theirs, 'tm', other)]
  transfers between devices with their start and end apart: 20 -> 23, of which waited for: 5 -> 10; matrix products, arithmetic and copies ran while one was open for 1% -> 2% of each run, Pallas kernels for 35% -> 22%
where the time goes in v2:
time: 574 us; the launch traced here: 570 us
  waiting for transfers between devices  274 us (48%)
  Pallas kernels  188 us (33%)
  blocking collectives  59.8 us (10%)
  starting transfers between devices  25.8 us (4%)
  local copies, waits for them, and re-layouts  15.8 us (3%)
  other arithmetic  6.11 us (1%)
    ppermute x18, waiting for transfers between devices, shift(): lax.ppermute(value, 'station', [(s, (s + d) % count) for s in range(count)])  274 us
    pallas_call x3, Pallas kernels, front(): pl.pallas_call(functools.partial(front_kernel, splits, owners, turned, ta...  83.3 us
    pallas_call x8, Pallas kernels, correlate(): pl.pallas_call(functools.partial(correlate_kernel, owners, picks), grid=(...  83.1 us
    all_gather x1, blocking collectives, pipelined(): scales = lax.all_gather(scale, 'station', axis=0, tiled=True)  48.5 us
    pallas_call x4, Pallas kernels, equalize(): pl.pallas_call(equalize_kernel, grid=(rows // block,), out_shape=jax.Shap...  21.4 us
    ppermute x18, starting transfers between devices, shift(): lax.ppermute(value, 'station', [(s, (s + d) % count) for s in range(count)])  20.2 us
  transfers between devices with their start and end apart: 23, of which 10 were waited for; matrix products, arithmetic and copies ran while one was open for 2% of the time, Pallas kernels for 22%

profile of v2, /device:TPU:11, one launch (start us, length us, event | category | flops | bytes accessed | tf_op | source)
XLA Modules:
  0.0 570.3 jit_solution(14601943467556327305)
XLA Ops:
  2.2 1.7 constant_dynamic-slice_fusion.table_ref
  3.9 2.0 broadcast_in_dim.14.window_ref
  5.9 14.6 %front.3 = (bf16[4,2,9,16,256]{4,3,2,1,0:T(8,128)(2,1)}, bf16[4,2,9,16,256]{4,3,2,1,0:T(8,128)(2,1)}, bf16[4,2,9,16,256]{4,3,2,1,0:T(8,128)(2,1)}, bf16[4,2,9,16...) custom-call(f32[144]{0:T(256)} %dynamic_slice.17.keep_ref, ...), custom_call_target="tpu_custom_call" | custom-call | flops 2717908992 | bytes 9437184 | tf_op jit(solution)/shard_map/front/pallas_call | solution.py:158
  20.4 1.3 collective-permute-start
  21.7 30.6 %front.4 = (bf16[4,2,9,48,256]{4,3,2,1,0:T(8,128)(2,1)}, bf16[4,2,9,48,256]{4,3,2,1,0:T(8,128)(2,1)}, bf16[4,2,9,48,256]{4,3,2,1,0:T(8,128)(2,1)}, bf16[4,2,9,48,256]{4,3,2,1,0:T(8,128)(2,1)}, f32[16,256]{1,0:T(8,128)}) custom-call(f32[144]{0:T(256)} %dynamic_slice.17.keep_ref, bf16[2,1,256,18432]{3,2,1,0:T(8,128)(2,1)} %volts_ref.5, ...), custom_call_target="tpu_custom_call" | custom-call | flops 8153726976 | bytes 28311552 | tf_op jit(solution)/shard_map/front/pallas_call | solution.py:158
  52.3 1.3 collective-permute-start.4
  53.6 1.3 collective-permute-start.1
  54.9 1.0 collective-permute-start.5
  56.1 47.0 %collective-permute-done.1.rest_1_.other_ref = bf16[4,2,144,256]{3,2,1,0:T(8,128)(2,1)} collective-permute-done((bf16[4,2,144,256]{3,2,1,0:T(8,128)(2,1)}, bf16[4,2,144,256]{3,2,1,0:T(8,128)(2,1)}, u32[]{:S(2)}, u32[]{:S(2)}) %collective-permute-start.1) | collective-permute-done | bytes 589856 | tf_op jit(solution)/shard_map/ppermute | solution.py:313
  103.1 2.3 collective-permute-start.2
  105.6 38.2 %front.5 = (bf16[1,2,9,64,256]{4,3,2,1,0:T(8,128)(2,1)}, bf16[1,2,9,64,256]{4,3,2,1,0:T(8,128)(2,1)}, bf16[1,2,9,64,256]{4,3,2,1,0:T(8,128)(2,1)}, bf16[1,2,9,64...) custom-call(f32[144]{0:T(256)} %dynamic_slice.17.keep_ref, ...), custom_call_target="tpu_custom_call" | custom-call | flops 10871635968 | bytes 37748736 | tf_op jit(solution)/shard_map/front/pallas_call | solution.py:158
  143.8 110.0 %collective-permute-done.2.rest_2_.other_ref = bf16[4,2,144,256]{3,2,1,0:T(8,128)(2,1)} collective-permute-done((bf16[4,2,144,256]{3,2,1,0:T(8,128)(2,1)}, bf16[4,2,144,256]{3,2,1,0:T(8,128)(2,1)}, u32[]{:S(2)}, u32[]{:S(2)}) %collective-permute-start.2) | collective-permute-done | bytes 589856 | tf_op jit(solution)/shard_map/ppermute | solution.py:313
  253.9 4.5 collective-permute-done.3.rest_3_.other_ref
  259.6 8.9 %collective-permute-done.13.other_ref.rest_9_ = bf16[1,2,576,256]{3,2,1,0:T(8,128)(2,1)} collective-permute-done((bf16[1,2,576,256]{3,2,1,0:T(8,128)(2,1)}, bf16[1,2,576,256]{3,2,1,0:T(8,128)(2,1)}, u32[]{:S(2)}, u32[]{:S(2)}) %collective-permute-start.13) | collective-permute-done | bytes 589856 | tf_op jit(solution)/shard_map/ppermute | solution.py:313
  268.5 35.4 %collective-permute-done.15.other_ref.rest_10_ = bf16[1,2,576,256]{3,2,1,0:T(8,128)(2,1)} collective-permute-done((bf16[1,2,576,256]{3,2,1,0:T(8,128)(2,1)}, bf16[1,2,576,256]{3,2,1,0:T(8,128)(2,1)}, u32[]{:S(2)}, u32[]{:S(2)}) %collective-permute-start.15) | collective-permute-done | bytes 589856 | tf_op jit(solution)/shard_map/ppermute | solution.py:313
  303.8 5.2 collective-permute-done.17.other_ref.rest_11_
  309.0 10.3 %correlate.12 = bf16[2,512,1024]{2,1,0:T(8,128)(2,1)} custom-call(s32[2]{0:T(128)} %pad_add_fusion.1.place_ref, bf16[4,2,144,256]{3,2,1,0:T(8,128)(2,1)} %bitcast.48, bf16[4,2,144,256]{3,2,1,0:T(8,128)(2,1)} %collective-permute-done.1.rest_1_.other_ref, bf16[4,2,144,256]{3,2,1,0:T(8,128)(2,1)} %collective-permute-done.2.rest_2_.other_ref, ...), custom_call_target="tpu_custom_call" | custom-call | flops 4831838208 | bytes 8912896 | tf_op jit(solution)/shard_map/correlate/pallas_call | solution.py:252
  320.7 1.2 convert_reduce_fusion
  324.7 11.3 %psum.7 = f32[256]{0:T(256)S(1)} all-reduce(f32[256]{0:T(256)S(1)} %add_reduce_fusion), channel_id=1, replica_groups=mesh['station'=4,'band'=4,'tm'=2] {'band','tm'}, use_global_device_ids=true, to_apply=%region_2.3 | all-reduce | flops 256 | bytes 2048 | tf_op jit(solution)/shard_map/psum | solution.py:377
  336.0 1.4 collective-permute-start.7
  337.4 3.0 collective-permute-start.9
  340.5 48.5 %all-gather = f32[4,1,256]{2,1,0:T(1,128)S(1)} all-gather(f32[1,1,256]{2,1,0:T(1,128)S(1)} %bitcast.83), channel_id=1, replica_groups=mesh['station'=4,'band'=4,'tm'=2] {'station'}, dimensions={0}, use_global_device_ids=true | all-gather | bytes 5120 | tf_op jit(solution)/shard_map/all_gather | solution.py:379
  389.0 2.5 broadcast_divide_fusion
  392.4 10.5 %correlate.11.mine_ref = f32[2,512,1024]{2,1,0:T(8,128)} custom-call(s32[2]{0:T(128)} %pad_add_fusion.place_ref, bf16[4,2,144,256]{3,2,1,0:T(8,128)(2,1)} %bitcast.49, bf16[4,2,144,256]{3,2,1,0:T(8,128)(2,1)} %collective-permute-done.1.rest_1_.other_ref, bf16[4,2,144,256]{3,2,1,0:T(8,128)(2,1)} %collective-permute-done.2.rest_2_.other_ref, ...), custom_call_target="tpu_custom_call" | custom-call | flops 4831838208 | bytes 8912896 | tf_op jit(solution)/shard_map/correlate/pallas_call | solution.py:252
  402.9 5.4 equalize.4.rest_12_.rest_0_
  409.5 10.3 %correlate.13 = bf16[2,512,1024]{2,1,0:T(8,128)(2,1)} custom-call(s32[2]{0:T(128)} %pad_add_fusion.1.place_ref, bf16[4,2,144,256]{3,2,1,0:T(8,128)(2,1)} %bitcast.50, bf16[4,2,144,256]{3,2,1,0:T(8,128)(2,1)} %collective-permute-done.1.rest_1_.other_ref, bf16[4,2,144,256]{3,2,1,0:T(8,128)(2,1)} %collective-permute-done.2.rest_2_.other_ref, ...), custom_call_target="tpu_custom_call" | custom-call | flops 4831838208 | bytes 8912896 | tf_op jit(solution)/shard_map/correlate/pallas_call | solution.py:252
  419.8 2.3 collective-permute-start.20
  422.1 2.0 collective-permute-start.14
  424.1 1.2 collective-permute-start.16
  425.2 1.5 collective-permute-start.18
  427.5 10.5 %correlate.10.mine_ref = f32[2,512,1024]{2,1,0:T(8,128)} custom-call(s32[2]{0:T(128)} %pad_add_fusion.place_ref, bf16[4,2,144,256]{3,2,1,0:T(8,128)(2,1)} %bitcast.51, bf16[4,2,144,256]{3,2,1,0:T(8,128)(2,1)} %collective-permute-done.1.rest_1_.other_ref, bf16[4,2,144,256]{3,2,1,0:T(8,128)(2,1)} %collective-permute-done.2.rest_2_.other_ref, ...), custom_call_target="tpu_custom_call" | custom-call | flops 4831838208 | bytes 8912896 | tf_op jit(solution)/shard_map/correlate/pallas_call | solution.py:252
  438.1 1.3 copy-done.6
  439.4 5.3 equalize.5.rest_12_.rest_0_
  444.8 30.2 %collective-permute-done.16.rest_10_ = bf16[1,2,576,256]{3,2,1,0:T(8,128)(2,1)S(1)} collective-permute-done((bf16[1,2,576,256]{3,2,1,0:T(8,128)(2,1)}, bf16[1,2,576,256]{3,2,1,0:T(8,128)(2,1)S(1)}, u32[]{:S(2)}, u32[]{:S(2)}) %collective-permute-start.16) | collective-permute-done | bytes 589856 | tf_op jit(solution)/shard_map/ppermute | solution.py:313
  475.0 2.4 collective-permute-done.18.rest_11_
  477.3 10.3 %correlate.14 = bf16[2,512,1024]{2,1,0:T(8,128)(2,1)} custom-call(s32[2]{0:T(128)} %pad_add_fusion.1.place_ref, bf16[4,2,144,256]{3,2,1,0:T(8,128)(2,1)} %bitcast.52, bf16[4,2,144,256]{3,2,1,0:T(8,128)(2,1)} %collective-permute-done.1.rest_1_.other_ref, bf16[4,2,144,256]{3,2,1,0:T(8,128)(2,1)} %collective-permute-done.2.rest_2_.other_ref, ...), custom_call_target="tpu_custom_call" | custom-call | flops 4831838208 | bytes 8912896 | tf_op jit(solution)/shard_map/correlate/pallas_call | solution.py:252
  488.2 1.9 collective-permute-start.10
  490.0 2.4 collective-permute-start.8
  493.3 10.5 %correlate.9.mine_ref = f32[2,512,1024]{2,1,0:T(8,128)} custom-call(s32[2]{0:T(128)} %pad_add_fusion.place_ref, bf16[4,2,144,256]{3,2,1,0:T(8,128)(2,1)} %bitcast.53, bf16[4,2,144,256]{3,2,1,0:T(8,128)(2,1)} %collective-permute-done.1.rest_1_.other_ref, bf16[4,2,144,256]{3,2,1,0:T(8,128)(2,1)} %collective-permute-done.2.rest_2_.other_ref, ...), custom_call_target="tpu_custom_call" | custom-call | flops 4831838208 | bytes 8912896 | tf_op jit(solution)/shard_map/correlate/pallas_call | solution.py:252
  503.8 1.3 copy-done.5
  505.1 5.3 equalize.6.rest_12_.rest_0_
  510.5 17.8 %collective-permute-done.10.rest_10_ = bf16[1,2,576,256]{3,2,1,0:T(8,128)(2,1)S(1)} collective-permute-done((bf16[1,2,576,256]{3,2,1,0:T(8,128)(2,1)}, bf16[1,2,576,256]{3,2,1,0:T(8,128)(2,1)S(1)}, u32[]{:S(2)}, u32[]{:S(2)}) %collective-permute-start.10) | collective-permute-done | bytes 589856 | tf_op jit(solution)/shard_map/ppermute | solution.py:313
  528.3 12.6 %collective-permute-done.8.rest_9_ = bf16[1,2,576,256]{3,2,1,0:T(8,128)(2,1)} collective-permute-done((bf16[1,2,576,256]{3,2,1,0:T(8,128)(2,1)}, bf16[1,2,576,256]{3,2,1,0:T(8,128)(2,1)}, u32[]{:S(2)}, u32[]{:S(2)}) %collective-permute-start.8) | collective-permute-done | bytes 589856 | tf_op jit(solution)/shard_map/ppermute | solution.py:313
  540.9 10.3 %correlate.15 = bf16[2,512,1024]{2,1,0:T(8,128)(2,1)} custom-call(s32[2]{0:T(128)} %pad_add_fusion.1.place_ref, bf16[4,2,144,256]{3,2,1,0:T(8,128)(2,1)} %bitcast.54, bf16[4,2,144,256]{3,2,1,0:T(8,128)(2,1)} %collective-permute-done.1.rest_1_.other_ref, bf16[4,2,144,256]{3,2,1,0:T(8,128)(2,1)} %collective-permute-done.2.rest_2_.other_ref, ...), custom_call_target="tpu_custom_call" | custom-call | flops 4831838208 | bytes 8912896 | tf_op jit(solution)/shard_map/correlate/pallas_call | solution.py:252
  551.2 1.0 collective-permute-start.22
  553.1 10.5 %correlate.8.mine_ref = f32[2,512,1024]{2,1,0:T(8,128)} custom-call(s32[2]{0:T(128)} %pad_add_fusion.place_ref, bf16[4,2,144,256]{3,2,1,0:T(8,128)(2,1)} %bitcast.55, bf16[4,2,144,256]{3,2,1,0:T(8,128)(2,1)} %collective-permute-done.1.rest_1_.other_ref, bf16[4,2,144,256]{3,2,1,0:T(8,128)(2,1)} %collective-permute-done.2.rest_2_.other_ref, ...), custom_call_target="tpu_custom_call" | custom-call | flops 4831838208 | bytes 8912896 | tf_op jit(solution)/shard_map/correlate/pallas_call | solution.py:252
  563.6 1.3 copy-done.7
  564.9 5.3 equalize.7
  (82 shorter events, 12.7 us)
Async XLA Ops:
  0.9 0.5 copy-start.15
  1.4 19.0 %copy-start.14 = (f32[4,144]{1,0:T(4,128)}, f32[4,144]{1,0:T(4,128)S(1)}, u32[]{:S(2)}) copy-start(f32[4,144]{1,0:T(4,128)S(1)} %convert_element_type.6) | copy-start | bytes 6916
  20.4 85.0 %collective-permute-start = (bf16[2,1584,256]{2,1,0:T(8,128)(2,1)}, bf16[2,1584,256]{2,1,0:T(8,128)(2,1)}, u32[]{:S(2)}, u32[]{:S(2)}) collective-permute-start(bf16[2,1584,256]{2,1,0:T(8,128)(2,1)} %get-tuple-element.35), channel_id=1, source_target_pairs={{0,1},{2,3},{4,5},{6,7},{8,9},{10,11},{12,13},{14,15},{16,17},{18,... | collective-permute-start | bytes 4866056 | tf_op jit(solution)/shard_map/ppermute | solution.py:318
  52.3 206.1 %collective-permute-start.4 = (bf16[4,2,432,256]{3,2,1,0:T(8,128)(2,1)}, bf16[4,2,432,256]{3,2,1,0:T(8,128)(2,1)S(1)}, u32[]{:S(2)}, u32[]{:S(2)}) collective-permute-start(bf16[4,2,432,256]{3,2,1,0:T(8,128)(2,1)} %bitcast.87), channel_id=1, source_target_pairs={{0,8},{8,16},{16,24},{24,0},{1,9},{9,17},{17,25},{25,1},{2,10},{10... | collective-permute-start | bytes 5308424 | tf_op jit(solution)/shard_map/ppermute | solution.py:313
  53.6 49.5 %collective-permute-start.1 = (bf16[4,2,144,256]{3,2,1,0:T(8,128)(2,1)}, bf16[4,2,144,256]{3,2,1,0:T(8,128)(2,1)}, u32[]{:S(2)}, u32[]{:S(2)}) collective-permute-start(bf16[4,2,144,256]{3,2,1,0:T(8,128)(2,1)} %bitcast.9), channel_id=1, source_target_pairs={{0,8},{8,16},{16,24},{24,0},{1,9},{9,17},{17,25},{25,1},{2,10},{10... | collective-permute-start | bytes 1769480 | tf_op jit(solution)/shard_map/ppermute | solution.py:313
  54.9 204.6 %collective-permute-start.5 = (bf16[4,2,432,256]{3,2,1,0:T(8,128)(2,1)}, bf16[4,2,432,256]{3,2,1,0:T(8,128)(2,1)S(1)}, u32[]{:S(2)}, u32[]{:S(2)}) collective-permute-start(bf16[4,2,432,256]{3,2,1,0:T(8,128)(2,1)} %bitcast.86), channel_id=1, source_target_pairs={{0,16},{8,24},{16,0},{24,8},{1,17},{9,25},{17,1},{25,9},{2,18},{10... | collective-permute-start | bytes 5308424 | tf_op jit(solution)/shard_map/ppermute | solution.py:313
  55.9 203.7 %collective-permute-start.6 = (bf16[4,2,432,256]{3,2,1,0:T(8,128)(2,1)}, bf16[4,2,432,256]{3,2,1,0:T(8,128)(2,1)}, u32[]{:S(2)}, u32[]{:S(2)}) collective-permute-start(bf16[4,2,432,256]{3,2,1,0:T(8,128)(2,1)} %bitcast.85), channel_id=1, source_target_pairs={{0,24},{8,0},{16,8},{24,16},{1,25},{9,1},{17,9},{25,17},{2,26},{10... | collective-permute-start | bytes 5308424 | tf_op jit(solution)/shard_map/ppermute | solution.py:313
  103.1 150.8 %collective-permute-start.2 = (bf16[4,2,144,256]{3,2,1,0:T(8,128)(2,1)}, bf16[4,2,144,256]{3,2,1,0:T(8,128)(2,1)}, u32[]{:S(2)}, u32[]{:S(2)}) collective-permute-start(bf16[4,2,144,256]{3,2,1,0:T(8,128)(2,1)} %bitcast.89), channel_id=1, source_target_pairs={{0,16},{8,24},{16,0},{24,8},{1,17},{9,25},{17,1},{25,9},{2,18},{10... | collective-permute-start | bytes 1769480 | tf_op jit(solution)/shard_map/ppermute | solution.py:313
  105.4 153.0 %collective-permute-start.3 = (bf16[4,2,144,256]{3,2,1,0:T(8,128)(2,1)}, bf16[4,2,144,256]{3,2,1,0:T(8,128)(2,1)}, u32[]{:S(2)}, u32[]{:S(2)}) collective-permute-start(bf16[4,2,144,256]{3,2,1,0:T(8,128)(2,1)} %bitcast.88), channel_id=1, source_target_pairs={{0,24},{8,0},{16,8},{24,16},{1,25},{9,1},{17,9},{25,17},{2,26},{10... | collective-permute-start | bytes 1769480 | tf_op jit(solution)/shard_map/ppermute | solution.py:313
  253.9 14.6 %collective-permute-start.13 = (bf16[1,2,576,256]{3,2,1,0:T(8,128)(2,1)}, bf16[1,2,576,256]{3,2,1,0:T(8,128)(2,1)}, u32[]{:S(2)}, u32[]{:S(2)}) collective-permute-start(bf16[1,2,576,256]{3,2,1,0:T(8,128)(2,1)} %after.18), channel_id=1, source_target_pairs={{0,8},{8,16},{16,24},{24,0},{1,9},{9,17},{17,25},{25,1},{2,10},{10... | collective-permute-start | bytes 1769480 | tf_op jit(solution)/shard_map/ppermute | solution.py:313
  258.4 45.4 %collective-permute-start.15 = (bf16[1,2,576,256]{3,2,1,0:T(8,128)(2,1)}, bf16[1,2,576,256]{3,2,1,0:T(8,128)(2,1)}, u32[]{:S(2)}, u32[]{:S(2)}) collective-permute-start(bf16[1,2,576,256]{3,2,1,0:T(8,128)(2,1)} %after.20), channel_id=1, source_target_pairs={{0,16},{8,24},{16,0},{24,8},{1,17},{9,25},{17,1},{25,9},{2,18},{10... | collective-permute-start | bytes 1769480 | tf_op jit(solution)/shard_map/ppermute | solution.py:313
  258.4 50.6 %copy-start = (bf16[4,2,432,256]{3,2,1,0:T(8,128)(2,1)}, bf16[4,2,432,256]{3,2,1,0:T(8,128)(2,1)S(1)}, u32[]{:S(2)}) copy-start(bf16[4,2,432,256]{3,2,1,0:T(8,128)(2,1)S(1)} %collective-permute-done.4.other_ref.rest_5_) | copy-start | bytes 5308420
  258.4 50.6 %collective-permute-start.17 = (bf16[1,2,576,256]{3,2,1,0:T(8,128)(2,1)}, bf16[1,2,576,256]{3,2,1,0:T(8,128)(2,1)}, u32[]{:S(2)}, u32[]{:S(2)}) collective-permute-start(bf16[1,2,576,256]{3,2,1,0:T(8,128)(2,1)} %after.22), channel_id=1, source_target_pairs={{0,24},{8,0},{16,8},{24,16},{1,25},{9,1},{17,9},{25,17},{2,26},{10... | collective-permute-start | bytes 1769480 | tf_op jit(solution)/shard_map/ppermute | solution.py:313
  259.5 49.5 %copy-start.1 = (bf16[4,2,432,256]{3,2,1,0:T(8,128)(2,1)}, bf16[4,2,432,256]{3,2,1,0:T(8,128)(2,1)S(1)}, u32[]{:S(2)}) copy-start(bf16[4,2,432,256]{3,2,1,0:T(8,128)(2,1)S(1)} %collective-permute-done.5.other_ref.rest_6_) | copy-start | bytes 5308420
  309.0 14.9 %copy-start.13 = (f32[16,256]{1,0:T(8,128)S(1)}, f32[16,256]{1,0:T(8,128)}, u32[]{:S(2)}) copy-start(f32[16,256]{1,0:T(8,128)} %get-tuple-element.33) | copy-start | bytes 49156
  319.3 83.6 %collective-permute-start.19 = (bf16[2,512,1024]{2,1,0:T(8,128)(2,1)}, bf16[2,512,1024]{2,1,0:T(8,128)(2,1)}, u32[]{:S(2)}, u32[]{:S(2)}) collective-permute-start(bf16[2,512,1024]{2,1,0:T(8,128)(2,1)} %correlate.12), channel_id=1, source_target_pairs={{0,1},{1,0},{2,3},{3,2},{4,5},{5,4},{6,7},{7,6},{8,9},{9,8},{10,11... | collective-permute-start | bytes 6291464 | tf_op jit(solution)/shard_map/ppermute | solution.py:395
  335.9 72.3 %collective-permute-start.11 = (bf16[1,2,576,256]{3,2,1,0:T(8,128)(2,1)}, bf16[1,2,576,256]{3,2,1,0:T(8,128)(2,1)S(1)}, u32[]{:S(2)}, u32[]{:S(2)}) collective-permute-start(bf16[1,2,576,256]{3,2,1,0:T(8,128)(2,1)} %after.16), channel_id=1, source_target_pairs={{0,24},{8,0},{16,8},{24,16},{1,25},{9,1},{17,9},{25,17},{2,26},{10... | collective-permute-start | bytes 1769480 | tf_op jit(solution)/shard_map/ppermute | solution.py:313
  336.0 72.3 %collective-permute-start.7 = (bf16[1,2,576,256]{3,2,1,0:T(8,128)(2,1)}, bf16[1,2,576,256]{3,2,1,0:T(8,128)(2,1)S(1)}, u32[]{:S(2)}, u32[]{:S(2)}) collective-permute-start(bf16[1,2,576,256]{3,2,1,0:T(8,128)(2,1)} %after.12), channel_id=1, source_target_pairs={{0,8},{8,16},{16,24},{24,0},{1,9},{9,17},{17,25},{25,1},{2,10},{10... | collective-permute-start | bytes 1769480 | tf_op jit(solution)/shard_map/ppermute | solution.py:313
  337.4 70.8 %collective-permute-start.9 = (bf16[1,2,576,256]{3,2,1,0:T(8,128)(2,1)}, bf16[1,2,576,256]{3,2,1,0:T(8,128)(2,1)S(1)}, u32[]{:S(2)}, u32[]{:S(2)}) collective-permute-start(bf16[1,2,576,256]{3,2,1,0:T(8,128)(2,1)} %after.14), channel_id=1, source_target_pairs={{0,16},{8,24},{16,0},{24,8},{1,17},{9,25},{17,1},{25,9},{2,18},{10... | collective-permute-start | bytes 1769480 | tf_op jit(solution)/shard_map/ppermute | solution.py:313
  389.0 13.9 %copy-start.12 = (f32[4,1,256]{2,1,0:T(1,128)}, f32[4,1,256]{2,1,0:T(1,128)S(1)}, u32[]{:S(2)}) copy-start(f32[4,1,256]{2,1,0:T(1,128)S(1)} %all-gather) | copy-start | bytes 12292
  408.3 0.8 copy-start.3
  408.3 1.0 copy-start.2
  408.3 1.2 copy-start.4
  419.8 18.3 %collective-permute-start.20 = (bf16[2,512,1024]{2,1,0:T(8,128)(2,1)}, bf16[2,512,1024]{2,1,0:T(8,128)(2,1)S(1)}, u32[]{:S(2)}, u32[]{:S(2)}) collective-permute-start(bf16[2,512,1024]{2,1,0:T(8,128)(2,1)} %correlate.13), channel_id=1, source_target_pairs={{0,1},{1,0},{2,3},{3,2},{4,5},{5,4},{6,7},{7,6},{8,9},{9,8},{10,11... | collective-permute-start | bytes 6291464 | tf_op jit(solution)/shard_map/ppermute | solution.py:395
  422.1 22.7 %collective-permute-start.14 = (bf16[1,2,576,256]{3,2,1,0:T(8,128)(2,1)}, bf16[1,2,576,256]{3,2,1,0:T(8,128)(2,1)S(1)}, u32[]{:S(2)}, u32[]{:S(2)}) collective-permute-start(bf16[1,2,576,256]{3,2,1,0:T(8,128)(2,1)} %after.19), channel_id=1, source_target_pairs={{0,8},{8,16},{16,24},{24,0},{1,9},{9,17},{17,25},{25,1},{2,10},{10... | collective-permute-start | bytes 1769480 | tf_op jit(solution)/shard_map/ppermute | solution.py:313
  424.1 50.9 %collective-permute-start.16 = (bf16[1,2,576,256]{3,2,1,0:T(8,128)(2,1)}, bf16[1,2,576,256]{3,2,1,0:T(8,128)(2,1)S(1)}, u32[]{:S(2)}, u32[]{:S(2)}) collective-permute-start(bf16[1,2,576,256]{3,2,1,0:T(8,128)(2,1)} %after.21), channel_id=1, source_target_pairs={{0,16},{8,24},{16,0},{24,8},{1,17},{9,25},{17,1},{25,9},{2,18},{10... | collective-permute-start | bytes 1769480 | tf_op jit(solution)/shard_map/ppermute | solution.py:313
  425.2 52.1 %collective-permute-start.18 = (bf16[1,2,576,256]{3,2,1,0:T(8,128)(2,1)}, bf16[1,2,576,256]{3,2,1,0:T(8,128)(2,1)}, u32[]{:S(2)}, u32[]{:S(2)}) collective-permute-start(bf16[1,2,576,256]{3,2,1,0:T(8,128)(2,1)} %after.23), channel_id=1, source_target_pairs={{0,24},{8,0},{16,8},{24,16},{1,25},{9,1},{17,9},{25,17},{2,26},{10... | collective-permute-start | bytes 1769480 | tf_op jit(solution)/shard_map/ppermute | solution.py:313
  438.1 1.3 copy-start.6
  444.7 32.6 %copy-start.8 = (bf16[1,2,576,256]{3,2,1,0:T(8,128)(2,1)}, bf16[1,2,576,256]{3,2,1,0:T(8,128)(2,1)S(1)}, u32[]{:S(2)}) copy-start(bf16[1,2,576,256]{3,2,1,0:T(8,128)(2,1)S(1)} %collective-permute-done.14.rest_9_) | copy-start | bytes 1769476
  475.0 2.4 copy-start.9
  487.6 16.1 %collective-permute-start.21 = (bf16[2,512,1024]{2,1,0:T(8,128)(2,1)}, bf16[2,512,1024]{2,1,0:T(8,128)(2,1)S(1)}, u32[]{:S(2)}, u32[]{:S(2)}) collective-permute-start(bf16[2,512,1024]{2,1,0:T(8,128)(2,1)} %correlate.14), channel_id=1, source_target_pairs={{0,1},{1,0},{2,3},{3,2},{4,5},{5,4},{6,7},{7,6},{8,9},{9,8},{10,11... | collective-permute-start | bytes 6291464 | tf_op jit(solution)/shard_map/ppermute | solution.py:395
  488.2 22.3 %collective-permute-start.12 = (bf16[1,2,576,256]{3,2,1,0:T(8,128)(2,1)}, bf16[1,2,576,256]{3,2,1,0:T(8,128)(2,1)S(1)}, u32[]{:S(2)}, u32[]{:S(2)}) collective-permute-start(bf16[1,2,576,256]{3,2,1,0:T(8,128)(2,1)} %after.17), channel_id=1, source_target_pairs={{0,24},{8,0},{16,8},{24,16},{1,25},{9,1},{17,9},{25,17},{2,26},{10... | collective-permute-start | bytes 1769480 | tf_op jit(solution)/shard_map/ppermute | solution.py:313
  488.2 40.1 %collective-permute-start.10 = (bf16[1,2,576,256]{3,2,1,0:T(8,128)(2,1)}, bf16[1,2,576,256]{3,2,1,0:T(8,128)(2,1)S(1)}, u32[]{:S(2)}, u32[]{:S(2)}) collective-permute-start(bf16[1,2,576,256]{3,2,1,0:T(8,128)(2,1)} %after.15), channel_id=1, source_target_pairs={{0,16},{8,24},{16,0},{24,8},{1,17},{9,25},{17,1},{25,9},{2,18},{10... | collective-permute-start | bytes 1769480 | tf_op jit(solution)/shard_map/ppermute | solution.py:313
  490.0 50.9 %collective-permute-start.8 = (bf16[1,2,576,256]{3,2,1,0:T(8,128)(2,1)}, bf16[1,2,576,256]{3,2,1,0:T(8,128)(2,1)}, u32[]{:S(2)}, u32[]{:S(2)}) collective-permute-start(bf16[1,2,576,256]{3,2,1,0:T(8,128)(2,1)} %after.13), channel_id=1, source_target_pairs={{0,8},{8,16},{16,24},{24,0},{1,9},{9,17},{17,25},{25,1},{2,10},{10... | collective-permute-start | bytes 1769480 | tf_op jit(solution)/shard_map/ppermute | solution.py:313
  503.8 1.3 copy-start.5
  510.5 30.4 %copy-start.10 = (bf16[1,2,576,256]{3,2,1,0:T(8,128)(2,1)}, bf16[1,2,576,256]{3,2,1,0:T(8,128)(2,1)S(1)}, u32[]{:S(2)}) copy-start(bf16[1,2,576,256]{3,2,1,0:T(8,128)(2,1)S(1)} %collective-permute-done.12.rest_11_) | copy-start | bytes 1769476
  528.3 12.6 %copy-start.11 = (bf16[1,2,576,256]{3,2,1,0:T(8,128)(2,1)}, bf16[1,2,576,256]{3,2,1,0:T(8,128)(2,1)S(1)}, u32[]{:S(2)}) copy-start(bf16[1,2,576,256]{3,2,1,0:T(8,128)(2,1)S(1)} %collective-permute-done.10.rest_10_) | copy-start | bytes 1769476
  551.2 12.4 %collective-permute-start.22 = (bf16[2,512,1024]{2,1,0:T(8,128)(2,1)}, bf16[2,512,1024]{2,1,0:T(8,128)(2,1)S(1)}, u32[]{:S(2)}, u32[]{:S(2)}) collective-permute-start(bf16[2,512,1024]{2,1,0:T(8,128)(2,1)} %correlate.15), channel_id=1, source_target_pairs={{0,1},{1,0},{2,3},{3,2},{4,5},{5,4},{6,7},{7,6},{8,9},{9,8},{10,11... | collective-permute-start | bytes 6291464 | tf_op jit(solution)/shard_map/ppermute | solution.py:395
  563.6 1.3 copy-start.7

commit v3 on v2

--- a/solution.py
+++ b/solution.py
@@ -16,6 +16,8 @@
 PARTS = (1, 3)
 SPREAD = BLOCK + 1
 VMEM = 60 * 1024 * 1024
+COST = pl.CostEstimate(flops=1024, bytes_accessed=1024, transcendentals=0)
+IN_FLIGHT = 3
 
 
 def window_values():
@@ -154,7 +156,6 @@
         turned = False
     else:
         hist_spec, turned = pl.BlockSpec((2, kept, inputs), lambda s: (0, 0, 0)), True
-    macs = 2 * SUBBAND_COUNT * frames * inputs * 2 * SUBBAND_COUNT
     result = pl.pallas_call(
         functools.partial(front_kernel, splits, owners, turned, tail),
         grid=(steps,),
@@ -173,40 +174,38 @@
             pltpu.VMEM((inputs // 128, 2 * SUBBAND_COUNT * SPREAD, 128), jnp.float32),
         ],
         compiler_params=pltpu.CompilerParams(vmem_limit_bytes=VMEM),
-        cost_estimate=pl.CostEstimate(
-            flops=2 * macs * 4, bytes_accessed=2 * frames * SUBBAND_COUNT * inputs * 8, transcendentals=0
-        ),
+        cost_estimate=COST,
         name="front",
     )(keep, hist, volts, window, table)
     count = owners * splits
     return result[:count], result[count], result[count + 1] if tail else None
 
 
-def after_kernel(value_ref, other_ref, out_ref):
+def after_kernel(*refs):
     pass
 
 
-def after(value, other):
+def after(value, *others):
     anywhere = pl.BlockSpec(memory_space=pl.ANY)
     return pl.pallas_call(
         after_kernel,
         out_shape=jax.ShapeDtypeStruct(value.shape, value.dtype),
-        in_specs=[anywhere, anywhere],
+        in_specs=[anywhere] * (1 + len(others)),
         out_specs=anywhere,
         input_output_aliases={0: 0},
-        cost_estimate=pl.CostEstimate(flops=0, bytes_accessed=0, transcendentals=0),
+        cost_estimate=COST,
         name="after",
-    )(value, other)
-
-
-def correlate_kernel(owners, picks, place_ref, *rest):
+    )(value, *others)
+
+
+def correlate_kernel(owners, picks, outs, place_ref, *rest):
     count = len(picks)
     pieces = [rest[n * owners : (n + 1) * owners] for n in range(count)]
-    out_ref, held, turned, sems = rest[-4:]
-    me, half = place_ref[0], place_ref[1]
+    out_refs, (held, turned, sems) = rest[-3 - outs : -3], rest[-3:]
+    me = place_ref[0]
     column = pl.program_id(0)
     per_half = owners // 2
-    inputs, depth = turned.shape[2], held.shape[2]
+    inputs, depth = turned.shape[3], held.shape[2]
 
     @pl.when(column == 0)
     def _():
@@ -226,46 +225,44 @@
             copy.start()
         for copy in copies:
             copy.wait()
-        for r in range(per_half):
-            real = held[half * per_half + r, 0].T
-            imag = held[half * per_half + r, 1].T
-            turned[0, r, :, pl.ds(0, depth)] = real
-            turned[0, r, :, pl.ds(depth, depth)] = imag
-            turned[1, r, :, pl.ds(0, depth)] = imag
-            turned[1, r, :, pl.ds(depth, depth)] = -real
-
-    left = turned[...].reshape(2 * per_half * inputs, 2 * depth)
+        for h in range(outs):
+            for r in range(per_half):
+                source = place_ref[1 + h] * per_half + r
+                real, imag = held[source, 0].T, held[source, 1].T
+                turned[h, 0, r, :, pl.ds(0, depth)] = real
+                turned[h, 0, r, :, pl.ds(depth, depth)] = imag
+                turned[h, 1, r, :, pl.ds(0, depth)] = imag
+                turned[h, 1, r, :, pl.ds(depth, depth)] = -real
+
     right = held[column].reshape(2 * depth, inputs)
-    both = jnp.dot(left, right, preferred_element_type=jnp.float32)
-    out_ref[...] = both.reshape(2, per_half * inputs, inputs).astype(out_ref.dtype)
-
-
-def correlate(place, pieces, picks, dtype, earlier):
+    for h in range(outs):
+        left = turned[h].reshape(2 * per_half * inputs, 2 * depth)
+        both = jnp.dot(left, right, preferred_element_type=jnp.float32)
+        both = both.reshape(2, per_half * inputs, inputs)
+        out_refs[h][...] = both.astype(out_refs[h].dtype)
+
+
+def correlate(place, pieces, picks, dtypes, earlier):
     owners = len(pieces[0])
     inputs = pieces[0][0].shape[-1]
     depth = sum(piece[0].shape[2] for piece in pieces)
     rows = owners // 2 * inputs
-    operands = [value for piece in pieces for value in piece]
-    if earlier is not None:
-        operands.append(earlier)
+    operands = [value for piece in pieces for value in piece] + list(earlier)
     anywhere = pl.BlockSpec(memory_space=pl.ANY)
+    outs = len(dtypes)
     return pl.pallas_call(
-        functools.partial(correlate_kernel, owners, picks),
+        functools.partial(correlate_kernel, owners, picks, outs),
         grid=(owners,),
-        out_shape=jax.ShapeDtypeStruct((2, rows, owners * inputs), dtype),
+        out_shape=[jax.ShapeDtypeStruct((2, rows, owners * inputs), dtype) for dtype in dtypes],
         in_specs=[pl.BlockSpec(memory_space=pltpu.SMEM)] + [anywhere] * len(operands),
-        out_specs=pl.BlockSpec((2, rows, inputs), lambda b: (0, 0, b)),
+        out_specs=[pl.BlockSpec((2, rows, inputs), lambda b: (0, 0, b))] * outs,
         scratch_shapes=[
             pltpu.VMEM((owners, 2, depth, inputs), jnp.bfloat16),
-            pltpu.VMEM((2, owners // 2, inputs, 2 * depth), jnp.bfloat16),
+            pltpu.VMEM((outs, 2, owners // 2, inputs, 2 * depth), jnp.bfloat16),
             pltpu.SemaphoreType.DMA((len(pieces), owners)),
         ],
         compiler_params=pltpu.CompilerParams(vmem_limit_bytes=VMEM),
-        cost_estimate=pl.CostEstimate(
-            flops=8 * rows * owners * inputs * depth,
-            bytes_accessed=owners * 4 * depth * inputs + 8 * rows * owners * inputs,
-            transcendentals=0,
-        ),
+        cost_estimate=COST,
         name="correlate",
     )(place, *operands)
 
@@ -278,7 +275,7 @@
         out_ref[0, part] = total * scale
 
 
-def equalize(row_scales, column_scales, mine, theirs, out, group, groups):
+def equalize(row_scales, column_scales, mine, theirs, out, group, groups, waits):
     rows, columns = mine.shape[1:]
     block = rows // 4
     specs = [
@@ -293,6 +290,8 @@
         specs.append(pl.BlockSpec(memory_space=pl.ANY))
         operands.append(out)
         aliases = {4: 0}
+    specs += [pl.BlockSpec(memory_space=pl.ANY)] * len(waits)
+    operands += waits
     return pl.pallas_call(
         equalize_kernel,
         grid=(rows // block,),
@@ -301,9 +300,7 @@
         out_specs=pl.BlockSpec((1, 2, block, columns), lambda r: (group, 0, r, 0)),
         input_output_aliases=aliases,
         compiler_params=pltpu.CompilerParams(vmem_limit_bytes=VMEM),
-        cost_estimate=pl.CostEstimate(
-            flops=6 * rows * columns, bytes_accessed=20 * rows * columns, transcendentals=0
-        ),
+        cost_estimate=COST,
         name="equalize",
     )(*operands)
 
@@ -354,7 +351,8 @@
             volts, None, end, size, 1, owners, keep_ahead, window, table, halo is None
         )
         if tail is not None:
-            halo = passed_on(tail)
+            with jax.named_scope("halo"):
+                halo = passed_on(tail)
         parts.append([x.reshape(groups, 2, GROUP * size * BLOCK, inputs) for x in spectra])
         power.append(part_power)
     spectra, part_power, _ = front(
@@ -365,14 +363,6 @@
     for j in range(groups):
         parts.append([spectra[d * groups + j] for d in range(owners)])
 
-    arrived = []
-    for n, part in enumerate(parts):
-        got = [part[0]]
-        for d in range(1, owners):
-            value = part[d] if n < 2 else after(part[d], arrived[n - 2][d])
-            got.append(shift(value, d))
-        arrived.append(got)
-
     local = jnp.sum(sum(power), axis=0)
     total = lax.psum(local, ("band", "tm"))
     scale = lax.rsqrt(total / (frames_all * jnp.sum(keep_all)) + 1e-06)
@@ -383,20 +373,53 @@
     per_half = scales.shape[0] // 2
     row_scales = lax.dynamic_slice_in_dim(scales, half * per_half, per_half, 0)
 
-    other = [(0, 1), (1, 0)]
-    send_place = jnp.stack([me, 1 - half]).astype(jnp.int32)
-    mine_place = jnp.stack([me, half]).astype(jnp.int32)
-    out = None
+    column_scales = scales[None, :]
+    row_scales = [(row_scales / denom[j])[:, None] for j in range(groups)]
+
+    place = jnp.stack([me, 1 - half, half]).astype(jnp.int32)
     shared = len(PARTS)
+    arrived, flat, out = [], [], None
+
+    def send(n, waits):
+        got = [parts[n][0]]
+        for d in range(1, owners):
+            gates = list(waits.get(d, ()))
+            if len(flat) >= IN_FLIGHT:
+                gates.append(flat[len(flat) - IN_FLIGHT])
+            value = after(parts[n][d], *gates) if gates else parts[n][d]
+            with jax.named_scope(f"part{n}_shift{d}"):
+                got.append(shift(value, d))
+            flat.append(got[-1])
+        arrived.append(got)
+
+    def to_other(j, theirs):
+        with jax.named_scope(f"rows{j}"):
+            return lax.ppermute(theirs, "tm", [(0, 1), (1, 0)])
+
+    def multiply(j, place, dtypes, earlier):
+        pieces = arrived[:shared] + [arrived[shared + j]]
+        return correlate(place, pieces, (j,) * shared + (0,), dtypes, earlier)
+
+    for n in range(shared):
+        send(n, {})
+    send(shared, {owners - 1: [column_scales]})
+    waiting = None
     for j in range(groups):
-        pieces = arrived[:shared] + [arrived[shared + j]]
-        picks = (j,) * shared + (0,)
-        theirs = correlate(send_place, pieces, picks, jnp.bfloat16, out)
-        theirs = lax.ppermute(theirs, "tm", other)
-        mine = correlate(mine_place, pieces, picks, jnp.float32, None)
-        out = equalize(
-            (row_scales / denom[j])[:, None], scales[None, :], mine, theirs, out, j, groups
-        )
+        final = j + 1 == groups
+        if not final:
+            send(shared + j + 1, {})
+            theirs, mine = multiply(j, place, [jnp.bfloat16, jnp.float32], [])
+        else:
+            (theirs,) = multiply(j, place[:2], [jnp.bfloat16], [])
+        if waiting is not None:
+            out = equalize(*waiting, out, j - 1, groups, [theirs])
+        if final:
+            theirs = to_other(j, theirs)
+            (mine,) = multiply(j, place[::2], [jnp.float32], [])
+        else:
+            theirs = to_other(j, after(theirs, *arrived[shared + j + 1][1:]))
+        waiting = (row_scales[j], column_scales, mine, theirs)
+    out = equalize(*waiting, out, groups - 1, groups, [])
     return out[None]
 
 

time: 574 us -> 482 us (0.84)
  waiting for transfers between devices: 274 us -> 215 us
  blocking collectives: 59.8 us -> 38.5 us
  Pallas kernels: 188 us -> 174 us
    ppermute x18, waiting for transfers between devices: 274 us -> 215 us  [shift(): lax.ppermute(value, 'station', [(s, (s + d) % count) for s in range(count)])]
    all_gather x1, blocking collectives: 48.5 us -> 26 us  [pipelined(): scales = lax.all_gather(scale, 'station', axis=0, tiled=True)]
    pallas_call x8 -> x5, Pallas kernels: 83.1 us -> 69.1 us  [correlate(): pl.pallas_call(functools.partial(correlate_kernel, owners, picks, outs),...]
    unnamed x33 -> x43, local copies, waits for them, and re-layouts: 6.5 us -> 11.7 us
  transfers between devices with their start and end apart: 23 -> 23, of which waited for: 10 -> 11; matrix products, arithmetic and copies ran while one was open for 2% -> 2% of each run, Pallas kernels for 22% -> 32%
where the time goes in v3:
time: 482 us; the launch traced here: 481 us
  waiting for transfers between devices  215 us (45%)
  Pallas kernels  174 us (36%)
  blocking collectives  38.5 us (8%)
  starting transfers between devices  27.3 us (6%)
  local copies, waits for them, and re-layouts  20.9 us (4%)
  other arithmetic  5.61 us (1%)
    ppermute x18, waiting for transfers between devices, shift(): lax.ppermute(value, 'station', [(s, (s + d) % count) for s in range(count)])  215 us
    pallas_call x3, Pallas kernels, front(): pl.pallas_call(functools.partial(front_kernel, splits, owners, turned, ta...  83.1 us
    pallas_call x5, Pallas kernels, correlate(): pl.pallas_call(functools.partial(correlate_kernel, owners, picks, outs),...  69.1 us
    all_gather x1, blocking collectives, pipelined(): scales = lax.all_gather(scale, 'station', axis=0, tiled=True)  26 us
    ppermute x18, starting transfers between devices, shift(): lax.ppermute(value, 'station', [(s, (s + d) % count) for s in range(count)])  24.3 us
    pallas_call x4, Pallas kernels, equalize(): pl.pallas_call(equalize_kernel, grid=(rows // block,), out_shape=jax.Shap...  21.4 us
    psum x1, blocking collectives, pipelined(): total = lax.psum(local, ('band', 'tm'))  12.4 us
    unnamed x43, local copies, waits for them, and re-layouts  11.7 us
  transfers between devices with their start and end apart: 23, of which 11 were waited for; matrix products, arithmetic and copies ran while one was open for 2% of the time, Pallas kernels for 32%

profile of v3, /device:TPU:11, one launch (start us, length us, event | category | flops | bytes accessed | tf_op | source)
XLA Modules:
  0.0 481.3 jit_solution(8590865381707867583)
XLA Ops:
  1.7 1.7 constant_dynamic-slice_fusion.table_ref
  3.3 1.9 broadcast_in_dim.26.window_ref
  5.3 14.4 %front.3 = (bf16[4,2,9,16,256]{4,3,2,1,0:T(8,128)(2,1)}, bf16[4,2,9,16,256]{4,3,2,1,0:T(8,128)(2,1)}, bf16[4,2,9,16,256]{4,3,2,1,0:T(8,128)(2,1)}, bf16[4,2,9,16...) custom-call(f32[144]{0:T(256)} %dynamic_slice.17.keep_ref, ...), custom_call_target="tpu_custom_call" | custom-call | flops 1024 | bytes 1024 | tf_op jit(solution)/shard_map/front/pallas_call | solution.py:159
  19.6 2.3 collective-permute-start.2
  21.9 1.5 collective-permute-start.3
  23.4 1.3 collective-permute-start
  24.7 30.6 %front.4 = (bf16[4,2,9,48,256]{4,3,2,1,0:T(8,128)(2,1)}, bf16[4,2,9,48,256]{4,3,2,1,0:T(8,128)(2,1)}, bf16[4,2,9,48,256]{4,3,2,1,0:T(8,128)(2,1)}, bf16[4,2,9,48,256]{4,3,2,1,0:T(8,128)(2,1)}, f32[16,256]{1,0:T(8,128)}) custom-call(f32[144]{0:T(256)} %dynamic_slice.17.keep_ref, bf16[2,1,256,18432]{3,2,1,0:T(8,128)(2,1)} %volts_ref.5, ...), custom_call_target="tpu_custom_call" | custom-call | flops 1024 | bytes 1024 | tf_op jit(solution)/shard_map/front/pallas_call | solution.py:159
  56.9 54.1 %collective-permute-done.1.refs_1_.rest_1_ = bf16[4,2,144,256]{3,2,1,0:T(8,128)(2,1)S(1)} collective-permute-done((bf16[4,2,144,256]{3,2,1,0:T(8,128)(2,1)}, bf16[4,2,144,256]{3,2,1,0:T(8,128)(2,1)S(1)}, u32[]{:S(2)}, u32[]{:S(2)}) %collective-permute-start.1) | collective-permute-done | bytes 589856 | tf_op jit(solution)/shard_map/part0_shift1/ppermute | solution.py:310
  111.8 2.1 collective-permute-start.4
  113.9 33.9 %collective-permute-done.3.refs_1_.rest_3_ = bf16[4,2,144,256]{3,2,1,0:T(8,128)(2,1)} collective-permute-done((bf16[4,2,144,256]{3,2,1,0:T(8,128)(2,1)}, bf16[4,2,144,256]{3,2,1,0:T(8,128)(2,1)}, u32[]{:S(2)}, u32[]{:S(2)}) %collective-permute-start.3) | collective-permute-done | bytes 589856 | tf_op jit(solution)/shard_map/part0_shift3/ppermute | solution.py:310
  149.1 38.1 %front.5 = (bf16[1,2,9,64,256]{4,3,2,1,0:T(8,128)(2,1)}, bf16[1,2,9,64,256]{4,3,2,1,0:T(8,128)(2,1)}, bf16[1,2,9,64,256]{4,3,2,1,0:T(8,128)(2,1)}, bf16[1,2,9,64...) custom-call(f32[144]{0:T(256)} %dynamic_slice.17.keep_ref, ...), custom_call_target="tpu_custom_call" | custom-call | flops 1024 | bytes 1024 | tf_op jit(solution)/shard_map/front/pallas_call | solution.py:159
  188.0 12.4 %psum.7 = f32[256]{0:T(256)S(1)} all-reduce(f32[256]{0:T(256)S(1)} %add_reduce_fusion), channel_id=1, replica_groups=mesh['station'=4,'band'=4,'tm'=2] {'band','tm'}, use_global_device_ids=true, to_apply=%region_2.3 | all-reduce | flops 256 | bytes 2048 | tf_op jit(solution)/shard_map/psum | solution.py:367
  200.5 26.0 %all-gather = f32[4,1,256]{2,1,0:T(1,128)} all-gather(f32[1,1,256]{2,1,0:T(1,128)S(1)} %bitcast.80), channel_id=1, replica_groups=mesh['station'=4,'band'=4,'tm'=2] {'station'}, dimensions={0}, use_global_device_ids=true | all-gather | bytes 5120 | tf_op jit(solution)/shard_map/all_gather | solution.py:369
  226.5 1.2 copy-done
  227.7 2.9 collective-permute-start.11
  230.6 1.2 copy-done.1
  231.9 2.1 collective-permute-start.7
  233.9 22.0 %collective-permute-done.11.refs_1_.rest_10_ = bf16[1,2,576,256]{3,2,1,0:T(8,128)(2,1)S(1)} collective-permute-done((bf16[1,2,576,256]{3,2,1,0:T(8,128)(2,1)}, bf16[1,2,576,256]{3,2,1,0:T(8,128)(2,1)S(1)}, u32[]{:S(2)}, u32[]{:S(2)}) %collective-permute-start.11) | collective-permute-done | bytes 589856 | tf_op jit(solution)/shard_map/part2_shift2/ppermute | solution.py:310
  256.8 3.3 collective-permute-start.12
  260.1 33.8 %collective-permute-done.7.refs_1_.rest_9_ = bf16[1,2,576,256]{3,2,1,0:T(8,128)(2,1)S(1)} collective-permute-done((bf16[1,2,576,256]{3,2,1,0:T(8,128)(2,1)}, bf16[1,2,576,256]{3,2,1,0:T(8,128)(2,1)S(1)}, u32[]{:S(2)}, u32[]{:S(2)}) %collective-permute-start.7) | collective-permute-done | bytes 589856 | tf_op jit(solution)/shard_map/part2_shift1/ppermute | solution.py:310
  294.8 2.1 collective-permute-start.8
  296.9 11.0 %collective-permute-done.15.refs_1_.rest_11_ = bf16[1,2,576,256]{3,2,1,0:T(8,128)(2,1)S(1)} collective-permute-done((bf16[1,2,576,256]{3,2,1,0:T(8,128)(2,1)}, bf16[1,2,576,256]{3,2,1,0:T(8,128)(2,1)S(1)}, u32[]{:S(2)}, u32[]{:S(2)}) %collective-permute-start.15) | collective-permute-done | bytes 589856 | tf_op jit(solution)/shard_map/part2_shift3/ppermute | solution.py:310
  309.3 16.0 %correlate.9 = (bf16[2,512,1024]{2,1,0:T(8,128)(2,1)}, f32[2,512,1024]{2,1,0:T(8,128)}) custom-call(s32[3]{0:T(128)} %pad_add_fusion.place_ref, bf16[4,2,144,256]{3,2,1,0:T(8,128)(2,1)} %bitcast.45, bf16[4,2,144,256]{3,2,1,0:T(8,128)(2,1)} %copy-done.3, bf16[4,2,144,256]{3,2,1,0:T(8,128)(2,1)} %copy-done.2, ...), custom_call_target="tpu_custom_call" | custom-call | flops 1024 | bytes 1024 | tf_op jit(solution)/shard_map/correlate/pallas_call | solution.py:253
  325.3 6.6 %collective-permute-done.8.refs_1_.rest_9_ = bf16[1,2,576,256]{3,2,1,0:T(8,128)(2,1)S(1)} collective-permute-done((bf16[1,2,576,256]{3,2,1,0:T(8,128)(2,1)}, bf16[1,2,576,256]{3,2,1,0:T(8,128)(2,1)S(1)}, u32[]{:S(2)}, u32[]{:S(2)}) %collective-permute-start.8) | collective-permute-done | bytes 589856 | tf_op jit(solution)/shard_map/part3_shift1/ppermute | solution.py:310
  331.9 1.3 collective-permute-done.16.refs_1_.rest_11_.refs_3_
  333.2 0.8 copy-done.9
  334.5 2.5 collective-permute-start.13
  337.1 1.5 collective-permute-start.17
  339.5 2.6 broadcast_divide_fusion
  342.2 0.9 copy.35.rows_ref
  343.0 16.1 %correlate.8 = (bf16[2,512,1024]{2,1,0:T(8,128)(2,1)}, f32[2,512,1024]{2,1,0:T(8,128)}) custom-call(s32[3]{0:T(128)} %pad_add_fusion.place_ref, bf16[4,2,144,256]{3,2,1,0:T(8,128)(2,1)} %bitcast.46, bf16[4,2,144,256]{3,2,1,0:T(8,128)(2,1)} %copy-done.3, bf16[4,2,144,256]{3,2,1,0:T(8,128)(2,1)} %copy-done.2, ...), custom_call_target="tpu_custom_call" | custom-call | flops 1024 | bytes 1024 | tf_op jit(solution)/shard_map/correlate/pallas_call | solution.py:253
  359.1 5.4 %equalize.4.rest_0_ = f32[4,2,512,1024]{3,2,1,0:T(8,128)} custom-call(f32[512,1]{1,0:T(8,128)} %copy.35.rows_ref, f32[1,1024]{1,0:T(1,128)} %bitcast.71, f32[2,512,1024]{2,1,0:T(8,128)} %get-tuple-element.71.mine_ref, bf16[2,512,1024]{2,1,0:T(8,128)(2,1)} %collective-permute-done.22.theirs_ref, bf16[2,512,1024]{2,1,0:T(8,128)(2,1)} %get-tuple-element.69.refs_0_.rest_0_), custom_call_target="tpu_custom_call" | custom-call | flops 1024 | bytes 1024 | tf_op jit(solution)/shard_map/equalize/pallas_call | solution.py:295
  364.5 23.8 %collective-permute-done.9.refs_1_.rest_9_ = bf16[1,2,576,256]{3,2,1,0:T(8,128)(2,1)S(1)} collective-permute-done((bf16[1,2,576,256]{3,2,1,0:T(8,128)(2,1)}, bf16[1,2,576,256]{3,2,1,0:T(8,128)(2,1)S(1)}, u32[]{:S(2)}, u32[]{:S(2)}) %collective-permute-start.9) | collective-permute-done | bytes 589856 | tf_op jit(solution)/shard_map/part4_shift1/ppermute | solution.py:310
  390.5 2.1 collective-permute-start.10
  392.6 1.2 collective-permute-start.18
  394.4 0.9 copy.36.rows_ref
  395.3 16.1 %correlate.7 = (bf16[2,512,1024]{2,1,0:T(8,128)(2,1)}, f32[2,512,1024]{2,1,0:T(8,128)}) custom-call(s32[3]{0:T(128)} %pad_add_fusion.place_ref, bf16[4,2,144,256]{3,2,1,0:T(8,128)(2,1)} %bitcast.47, bf16[4,2,144,256]{3,2,1,0:T(8,128)(2,1)} %copy-done.3, bf16[4,2,144,256]{3,2,1,0:T(8,128)(2,1)} %copy-done.2, ...), custom_call_target="tpu_custom_call" | custom-call | flops 1024 | bytes 1024 | tf_op jit(solution)/shard_map/correlate/pallas_call | solution.py:253
  411.4 5.4 %equalize.5.rest_0_ = f32[4,2,512,1024]{3,2,1,0:T(8,128)} custom-call(f32[512,1]{1,0:T(8,128)} %copy.36.rows_ref, f32[1,1024]{1,0:T(1,128)} %bitcast.72, f32[2,512,1024]{2,1,0:T(8,128)} %get-tuple-element.68.mine_ref, bf16[2,512,1024]{2,1,0:T(8,128)(2,1)} %collective-permute-done.21.theirs_ref, ...), custom_call_target="tpu_custom_call", output_to_operand_aliasing={{}: (4, {})} | custom-call | flops 1024 | bytes 1024 | tf_op jit(solution)/shard_map/equalize/pallas_call | solution.py:295
  416.8 24.9 %collective-permute-done.10.rest_9_.refs_1_ = bf16[1,2,576,256]{3,2,1,0:T(8,128)(2,1)S(1)} collective-permute-done((bf16[1,2,576,256]{3,2,1,0:T(8,128)(2,1)}, bf16[1,2,576,256]{3,2,1,0:T(8,128)(2,1)S(1)}, u32[]{:S(2)}, u32[]{:S(2)}) %collective-permute-start.10) | collective-permute-done | bytes 589856 | tf_op jit(solution)/shard_map/part5_shift1/ppermute | solution.py:310
  441.7 2.8 collective-permute-done.18.rest_11_.refs_3_
  444.5 0.9 copy-done.12
  445.9 10.4 %correlate.6.rest_1_ = bf16[2,512,1024]{2,1,0:T(8,128)(2,1)} custom-call(s32[2]{0:T(128)} %pad_add_fusion.1.place_ref, bf16[4,2,144,256]{3,2,1,0:T(8,128)(2,1)} %bitcast.48, bf16[4,2,144,256]{3,2,1,0:T(8,128)(2,1)} %copy-done.3, bf16[4,2,144,256]{3,2,1,0:T(8,128)(2,1)} %copy-done.2, bf16[4,2,144,256]{3,2,1,0:T(8,128)(2,1)} %collective-permute-done.3.refs_1_.rest_3_, ...), custom_call_target="tpu_custom_call" | custom-call | flops 1024 | bytes 1024 | tf_op jit(solution)/shard_map/correlate/pallas_call | solution.py:253
  457.1 0.9 copy.37.rows_ref
  457.9 0.9 copy.38.rows_ref
  458.8 10.5 %correlate.5.mine_ref = f32[2,512,1024]{2,1,0:T(8,128)} custom-call(s32[2]{0:T(128)} %slice.18.place_ref, bf16[4,2,144,256]{3,2,1,0:T(8,128)(2,1)} %bitcast.49, bf16[4,2,144,256]{3,2,1,0:T(8,128)(2,1)} %copy-done.3, bf16[4,2,144,256]{3,2,1,0:T(8,128)(2,1)} %copy-done.2, bf16[4,2,144,256]{3,2,1,0:T(8,128)(2,1)} %collective-permute-done.3.refs_1_.rest_3_, ...), custom_call_target="tpu_custom_call" | custom-call | flops 1024 | bytes 1024 | tf_op jit(solution)/shard_map/correlate/pallas_call | solution.py:253
  469.3 1.3 copy-done.16
  470.6 5.3 %equalize.6.rest_0_ = f32[4,2,512,1024]{3,2,1,0:T(8,128)} custom-call(f32[512,1]{1,0:T(8,128)} %copy.37.rows_ref, f32[1,1024]{1,0:T(1,128)} %bitcast.73, f32[2,512,1024]{2,1,0:T(8,128)} %get-tuple-element.65.mine_ref, bf16[2,512,1024]{2,1,0:T(8,128)(2,1)} %copy-done.16, f32[4,2,512,1024]{3,2,1,0:T(8,128)} %equalize.5.rest_0_, ...), custom_call_target="tpu_custom_call", output_to_operand_aliasing={{}: (4, {})} | custom-call | flops 1024 | bytes 1024 | tf_op jit(solution)/shard_map/equalize/pallas_call | solution.py:295
  476.0 5.4 %equalize.7 = f32[4,2,512,1024]{3,2,1,0:T(8,128)} custom-call(f32[512,1]{1,0:T(8,128)} %copy.38.rows_ref, f32[1,1024]{1,0:T(1,128)} %bitcast.74, f32[2,512,1024]{2,1,0:T(8,128)} %correlate.5.mine_ref, bf16[2,512,1024]{2,1,0:T(8,128)(2,1)} %collective-permute-done.19.theirs_ref, f32[4,2,512,1024]{3,2,1,0:T(8,128)} %equalize.6.rest_0_), custom_call_target="tpu_custom_call", output_to_operand_aliasing={{}: (4, {})} | custom-call | flops 1024 | bytes 1024 | tf_op jit(solution)/shard_map/equalize/pallas_call | solution.py:295
  (96 shorter events, 14.2 us)
Async XLA Ops:
  19.6 35.6 %collective-permute-start.2 = (bf16[4,2,144,256]{3,2,1,0:T(8,128)(2,1)}, bf16[4,2,144,256]{3,2,1,0:T(8,128)(2,1)S(1)}, u32[]{:S(2)}, u32[]{:S(2)}) collective-permute-start(bf16[4,2,144,256]{3,2,1,0:T(8,128)(2,1)} %bitcast.84), channel_id=1, source_target_pairs={{0,16},{8,24},{16,0},{24,8},{1,17},{9,25},{17,1},{25,9},{2,18},{10... | collective-permute-start | bytes 1769480 | tf_op jit(solution)/shard_map/part0_shift2/ppermute | solution.py:310
  21.9 89.1 %collective-permute-start.1 = (bf16[4,2,144,256]{3,2,1,0:T(8,128)(2,1)}, bf16[4,2,144,256]{3,2,1,0:T(8,128)(2,1)S(1)}, u32[]{:S(2)}, u32[]{:S(2)}) collective-permute-start(bf16[4,2,144,256]{3,2,1,0:T(8,128)(2,1)} %bitcast.83), channel_id=1, source_target_pairs={{0,8},{8,16},{16,24},{24,0},{1,9},{9,17},{17,25},{25,1},{2,10},{10... | collective-permute-start | bytes 1769480 | tf_op jit(solution)/shard_map/part0_shift1/ppermute | solution.py:310
  21.9 125.9 %collective-permute-start.3 = (bf16[4,2,144,256]{3,2,1,0:T(8,128)(2,1)}, bf16[4,2,144,256]{3,2,1,0:T(8,128)(2,1)}, u32[]{:S(2)}, u32[]{:S(2)}) collective-permute-start(bf16[4,2,144,256]{3,2,1,0:T(8,128)(2,1)} %bitcast.82), channel_id=1, source_target_pairs={{0,24},{8,0},{16,8},{24,16},{1,25},{9,1},{17,9},{25,17},{2,26},{10... | collective-permute-start | bytes 1769480 | tf_op jit(solution)/shard_map/part0_shift3/ppermute | solution.py:310
  23.4 125.7 %collective-permute-start = (bf16[2,1584,256]{2,1,0:T(8,128)(2,1)}, bf16[2,1584,256]{2,1,0:T(8,128)(2,1)}, u32[]{:S(2)}, u32[]{:S(2)}) collective-permute-start(bf16[2,1584,256]{2,1,0:T(8,128)(2,1)} %get-tuple-element.41), channel_id=1, source_target_pairs={{0,1},{2,3},{4,5},{6,7},{8,9},{10,11},{12,13},{14,15},{16,17},{18,... | collective-permute-start | bytes 4866056 | tf_op jit(solution)/shard_map/halo/ppermute | solution.py:315
  55.3 0.8 copy-start.2
  56.1 170.4 %collective-permute-start.5 = (bf16[4,2,432,256]{3,2,1,0:T(8,128)(2,1)}, bf16[4,2,432,256]{3,2,1,0:T(8,128)(2,1)S(1)}, u32[]{:S(2)}, u32[]{:S(2)}) collective-permute-start(bf16[4,2,432,256]{3,2,1,0:T(8,128)(2,1)} %after.19), channel_id=1, source_target_pairs={{0,16},{8,24},{16,0},{24,8},{1,17},{9,25},{17,1},{25,9},{2,18},{10... | collective-permute-start | bytes 5308424 | tf_op jit(solution)/shard_map/part1_shift2/ppermute | solution.py:310
  111.0 0.8 copy-start.3
  111.8 118.8 %collective-permute-start.4 = (bf16[4,2,432,256]{3,2,1,0:T(8,128)(2,1)}, bf16[4,2,432,256]{3,2,1,0:T(8,128)(2,1)S(1)}, u32[]{:S(2)}, u32[]{:S(2)}) collective-permute-start(bf16[4,2,432,256]{3,2,1,0:T(8,128)(2,1)} %after.18), channel_id=1, source_target_pairs={{0,8},{8,16},{16,24},{24,0},{1,9},{9,17},{17,25},{25,1},{2,10},{10... | collective-permute-start | bytes 5308424 | tf_op jit(solution)/shard_map/part1_shift1/ppermute | solution.py:310
  147.9 86.1 %collective-permute-start.6 = (bf16[4,2,432,256]{3,2,1,0:T(8,128)(2,1)}, bf16[4,2,432,256]{3,2,1,0:T(8,128)(2,1)}, u32[]{:S(2)}, u32[]{:S(2)}) collective-permute-start(bf16[4,2,432,256]{3,2,1,0:T(8,128)(2,1)} %after.20), channel_id=1, source_target_pairs={{0,24},{8,0},{16,8},{24,16},{1,25},{9,1},{17,9},{25,17},{2,26},{10... | collective-permute-start | bytes 5308424 | tf_op jit(solution)/shard_map/part1_shift3/ppermute | solution.py:310
  149.1 38.2 %copy-start.18 = (f32[16,256]{1,0:T(8,128)S(1)}, f32[16,256]{1,0:T(8,128)}, u32[]{:S(2)}) copy-start(f32[16,256]{1,0:T(8,128)} %get-tuple-element.39) | copy-start | bytes 49156
  149.1 38.2 %copy-start.19 = (f32[16,256]{1,0:T(8,128)S(1)}, f32[16,256]{1,0:T(8,128)}, u32[]{:S(2)}) copy-start(f32[16,256]{1,0:T(8,128)} %get-tuple-element.40) | copy-start | bytes 49156
  226.5 1.2 copy-start
  227.7 28.2 %collective-permute-start.11 = (bf16[1,2,576,256]{3,2,1,0:T(8,128)(2,1)}, bf16[1,2,576,256]{3,2,1,0:T(8,128)(2,1)S(1)}, u32[]{:S(2)}, u32[]{:S(2)}) collective-permute-start(bf16[1,2,576,256]{3,2,1,0:T(8,128)(2,1)} %after.25), channel_id=1, source_target_pairs={{0,16},{8,24},{16,0},{24,8},{1,17},{9,25},{17,1},{25,9},{2,18},{10... | collective-permute-start | bytes 1769480 | tf_op jit(solution)/shard_map/part2_shift2/ppermute | solution.py:310
  230.6 1.2 copy-start.1
  231.9 62.1 %collective-permute-start.7 = (bf16[1,2,576,256]{3,2,1,0:T(8,128)(2,1)}, bf16[1,2,576,256]{3,2,1,0:T(8,128)(2,1)S(1)}, u32[]{:S(2)}, u32[]{:S(2)}) collective-permute-start(bf16[1,2,576,256]{3,2,1,0:T(8,128)(2,1)} %after.21), channel_id=1, source_target_pairs={{0,8},{8,16},{16,24},{24,0},{1,9},{9,17},{17,25},{25,1},{2,10},{10... | collective-permute-start | bytes 1769480 | tf_op jit(solution)/shard_map/part2_shift1/ppermute | solution.py:310
  233.9 73.9 %collective-permute-start.15 = (bf16[1,2,576,256]{3,2,1,0:T(8,128)(2,1)}, bf16[1,2,576,256]{3,2,1,0:T(8,128)(2,1)S(1)}, u32[]{:S(2)}, u32[]{:S(2)}) collective-permute-start(bf16[1,2,576,256]{3,2,1,0:T(8,128)(2,1)} %after.29), channel_id=1, source_target_pairs={{0,24},{8,0},{16,8},{24,16},{1,25},{9,1},{17,9},{25,17},{2,26},{10... | collective-permute-start | bytes 1769480 | tf_op jit(solution)/shard_map/part2_shift3/ppermute | solution.py:310
  256.0 0.8 copy-start.13
  256.8 68.5 %collective-permute-start.12 = (bf16[1,2,576,256]{3,2,1,0:T(8,128)(2,1)}, bf16[1,2,576,256]{3,2,1,0:T(8,128)(2,1)S(1)}, u32[]{:S(2)}, u32[]{:S(2)}) collective-permute-start(bf16[1,2,576,256]{3,2,1,0:T(8,128)(2,1)} %after.26), channel_id=1, source_target_pairs={{0,16},{8,24},{16,0},{24,8},{1,17},{9,25},{17,1},{25,9},{2,18},{10... | collective-permute-start | bytes 1769480 | tf_op jit(solution)/shard_map/part3_shift2/ppermute | solution.py:310
  293.9 0.8 copy-start.14
  294.8 37.1 %collective-permute-start.8 = (bf16[1,2,576,256]{3,2,1,0:T(8,128)(2,1)}, bf16[1,2,576,256]{3,2,1,0:T(8,128)(2,1)S(1)}, u32[]{:S(2)}, u32[]{:S(2)}) collective-permute-start(bf16[1,2,576,256]{3,2,1,0:T(8,128)(2,1)} %after.22), channel_id=1, source_target_pairs={{0,8},{8,16},{16,24},{24,0},{1,9},{9,17},{17,25},{25,1},{2,10},{10... | collective-permute-start | bytes 1769480 | tf_op jit(solution)/shard_map/part3_shift1/ppermute | solution.py:310
  307.9 0.8 copy-start.15
  308.7 24.5 %collective-permute-start.16 = (bf16[1,2,576,256]{3,2,1,0:T(8,128)(2,1)}, bf16[1,2,576,256]{3,2,1,0:T(8,128)(2,1)S(1)}, u32[]{:S(2)}, u32[]{:S(2)}) collective-permute-start(bf16[1,2,576,256]{3,2,1,0:T(8,128)(2,1)} %after.30), channel_id=1, source_target_pairs={{0,24},{8,0},{16,8},{24,16},{1,25},{9,1},{17,9},{25,17},{2,26},{10... | collective-permute-start | bytes 1769480 | tf_op jit(solution)/shard_map/part3_shift3/ppermute | solution.py:310
  325.3 7.9 %copy-start.4 = (bf16[1,2,576,256]{3,2,1,0:T(8,128)(2,1)}, bf16[1,2,576,256]{3,2,1,0:T(8,128)(2,1)S(1)}, u32[]{:S(2)}) copy-start(bf16[1,2,576,256]{3,2,1,0:T(8,128)(2,1)S(1)} %collective-permute-done.12.refs_1_.rest_10_.refs_2_) | copy-start | bytes 1769476
  331.9 1.3 copy-start.6
  333.2 0.8 copy-start.9
  334.0 25.1 %collective-permute-start.22 = (bf16[2,512,1024]{2,1,0:T(8,128)(2,1)}, bf16[2,512,1024]{2,1,0:T(8,128)(2,1)}, u32[]{:S(2)}, u32[]{:S(2)}) collective-permute-start(bf16[2,512,1024]{2,1,0:T(8,128)(2,1)} %after.35), channel_id=1, source_target_pairs={{0,1},{1,0},{2,3},{3,2},{4,5},{5,4},{6,7},{7,6},{8,9},{9,8},{10,11... | collective-permute-start | bytes 6291464 | tf_op jit(solution)/shard_map/rows0/ppermute | solution.py:397
  334.5 5.0 %copy-start.17 = (f32[4,1,256]{2,1,0:T(1,128)S(1)}, f32[4,1,256]{2,1,0:T(1,128)}, u32[]{:S(2)}) copy-start(f32[4,1,256]{2,1,0:T(1,128)} %all-gather) | copy-start | bytes 12292
  334.5 29.9 %collective-permute-start.13 = (bf16[1,2,576,256]{3,2,1,0:T(8,128)(2,1)}, bf16[1,2,576,256]{3,2,1,0:T(8,128)(2,1)S(1)}, u32[]{:S(2)}, u32[]{:S(2)}) collective-permute-start(bf16[1,2,576,256]{3,2,1,0:T(8,128)(2,1)} %after.27), channel_id=1, source_target_pairs={{0,16},{8,24},{16,0},{24,8},{1,17},{9,25},{17,1},{25,9},{2,18},{10... | collective-permute-start | bytes 1769480 | tf_op jit(solution)/shard_map/part4_shift2/ppermute | solution.py:310
  337.1 51.2 %collective-permute-start.9 = (bf16[1,2,576,256]{3,2,1,0:T(8,128)(2,1)}, bf16[1,2,576,256]{3,2,1,0:T(8,128)(2,1)S(1)}, u32[]{:S(2)}, u32[]{:S(2)}) collective-permute-start(bf16[1,2,576,256]{3,2,1,0:T(8,128)(2,1)} %after.23), channel_id=1, source_target_pairs={{0,8},{8,16},{16,24},{24,0},{1,9},{9,17},{17,25},{25,1},{2,10},{10... | collective-permute-start | bytes 1769480 | tf_op jit(solution)/shard_map/part4_shift1/ppermute | solution.py:310
  337.1 51.5 %collective-permute-start.17 = (bf16[1,2,576,256]{3,2,1,0:T(8,128)(2,1)}, bf16[1,2,576,256]{3,2,1,0:T(8,128)(2,1)S(1)}, u32[]{:S(2)}, u32[]{:S(2)}) collective-permute-start(bf16[1,2,576,256]{3,2,1,0:T(8,128)(2,1)} %after.31), channel_id=1, source_target_pairs={{0,24},{8,0},{16,8},{24,16},{1,25},{9,1},{17,9},{25,17},{2,26},{10... | collective-permute-start | bytes 1769480 | tf_op jit(solution)/shard_map/part4_shift3/ppermute | solution.py:310
  364.5 24.1 %copy-start.5 = (bf16[1,2,576,256]{3,2,1,0:T(8,128)(2,1)}, bf16[1,2,576,256]{3,2,1,0:T(8,128)(2,1)S(1)}, u32[]{:S(2)}) copy-start(bf16[1,2,576,256]{3,2,1,0:T(8,128)(2,1)S(1)} %collective-permute-done.13.refs_1_.rest_10_.refs_2_) | copy-start | bytes 1769476
  388.3 0.8 copy-start.7
  389.1 0.8 copy-start.8
  390.0 21.4 %collective-permute-start.21 = (bf16[2,512,1024]{2,1,0:T(8,128)(2,1)}, bf16[2,512,1024]{2,1,0:T(8,128)(2,1)}, u32[]{:S(2)}, u32[]{:S(2)}) collective-permute-start(bf16[2,512,1024]{2,1,0:T(8,128)(2,1)} %after.34), channel_id=1, source_target_pairs={{0,1},{1,0},{2,3},{3,2},{4,5},{5,4},{6,7},{7,6},{8,9},{9,8},{10,11... | collective-permute-start | bytes 6291464 | tf_op jit(solution)/shard_map/rows1/ppermute | solution.py:397
  390.5 26.3 %collective-permute-start.14 = (bf16[1,2,576,256]{3,2,1,0:T(8,128)(2,1)}, bf16[1,2,576,256]{3,2,1,0:T(8,128)(2,1)S(1)}, u32[]{:S(2)}, u32[]{:S(2)}) collective-permute-start(bf16[1,2,576,256]{3,2,1,0:T(8,128)(2,1)} %after.28), channel_id=1, source_target_pairs={{0,16},{8,24},{16,0},{24,8},{1,17},{9,25},{17,1},{25,9},{2,18},{10... | collective-permute-start | bytes 1769480 | tf_op jit(solution)/shard_map/part5_shift2/ppermute | solution.py:310
  390.5 51.2 %collective-permute-start.10 = (bf16[1,2,576,256]{3,2,1,0:T(8,128)(2,1)}, bf16[1,2,576,256]{3,2,1,0:T(8,128)(2,1)S(1)}, u32[]{:S(2)}, u32[]{:S(2)}) collective-permute-start(bf16[1,2,576,256]{3,2,1,0:T(8,128)(2,1)} %after.24), channel_id=1, source_target_pairs={{0,8},{8,16},{16,24},{24,0},{1,9},{9,17},{17,25},{25,1},{2,10},{10... | collective-permute-start | bytes 1769480 | tf_op jit(solution)/shard_map/part5_shift1/ppermute | solution.py:310
  392.6 51.9 %collective-permute-start.18 = (bf16[1,2,576,256]{3,2,1,0:T(8,128)(2,1)}, bf16[1,2,576,256]{3,2,1,0:T(8,128)(2,1)S(1)}, u32[]{:S(2)}, u32[]{:S(2)}) collective-permute-start(bf16[1,2,576,256]{3,2,1,0:T(8,128)(2,1)} %after.32), channel_id=1, source_target_pairs={{0,24},{8,0},{16,8},{24,16},{1,25},{9,1},{17,9},{25,17},{2,26},{10... | collective-permute-start | bytes 1769480 | tf_op jit(solution)/shard_map/part5_shift3/ppermute | solution.py:310
  416.8 27.7 %copy-start.10 = (bf16[1,2,576,256]{3,2,1,0:T(8,128)(2,1)}, bf16[1,2,576,256]{3,2,1,0:T(8,128)(2,1)S(1)}, u32[]{:S(2)}) copy-start(bf16[1,2,576,256]{3,2,1,0:T(8,128)(2,1)S(1)} %collective-permute-done.14.rest_10_.refs_2_) | copy-start | bytes 1769476
  441.7 2.8 copy-start.11
  444.5 0.9 copy-start.12
  445.3 24.0 %collective-permute-start.20 = (bf16[2,512,1024]{2,1,0:T(8,128)(2,1)}, bf16[2,512,1024]{2,1,0:T(8,128)(2,1)S(1)}, u32[]{:S(2)}, u32[]{:S(2)}) collective-permute-start(bf16[2,512,1024]{2,1,0:T(8,128)(2,1)} %after.33), channel_id=1, source_target_pairs={{0,1},{1,0},{2,3},{3,2},{4,5},{5,4},{6,7},{7,6},{8,9},{9,8},{10,11... | collective-permute-start | bytes 6291464 | tf_op jit(solution)/shard_map/rows2/ppermute | solution.py:397
  445.9 10.5 %copy-start.20 = (s32[3]{0:T(128)S(1)}, s32[3]{0:T(128)}, u32[]{:S(2)}) copy-start(s32[3]{0:T(128)} %pad_add_fusion.place_ref) | copy-start | bytes 40
  456.4 19.6 %collective-permute-start.19 = (bf16[2,512,1024]{2,1,0:T(8,128)(2,1)}, bf16[2,512,1024]{2,1,0:T(8,128)(2,1)}, u32[]{:S(2)}, u32[]{:S(2)}) collective-permute-start(bf16[2,512,1024]{2,1,0:T(8,128)(2,1)} %correlate.6.rest_1_), channel_id=1, source_target_pairs={{0,1},{1,0},{2,3},{3,2},{4,5},{5,4},{6,7},{7,6},{8,9},{9,8},{10,11... | collective-permute-start | bytes 6291464 | tf_op jit(solution)/shard_map/rows3/ppermute | solution.py:397
  469.3 1.3 copy-start.16

commit v4 on v3

--- a/solution.py
+++ b/solution.py
@@ -39,7 +39,7 @@
 
 
 def front_kernel(
-    splits, owners, turned, tail, keep_ref, hist_ref, volts_ref, window_ref, table_ref, *rest
+    splits, owners, turned, tail, me_ref, keep_ref, hist_ref, volts_ref, window_ref, table_ref, *rest
 ):
     outs, power_ref = rest[: owners * splits], rest[owners * splits]
     tail_ref = rest[owners * splits + 1] if tail else None
@@ -59,7 +59,7 @@
                 ring[slot, part, pl.ds(at, 128), :] = ref[part, 0, :, pl.ds(at, 128)].T
             return 0
 
-        lax.fori_loop(begin, span // 128, columns, 0, unroll=6 if begin == 0 else 1)
+        lax.fori_loop(begin, span // 128, columns, 0, unroll=6 if begin == 0 else 5)
 
     @pl.when(step == 0)
     def _():
@@ -67,7 +67,7 @@
             for part in range(2):
                 ring[1, part, pl.ds(skipped, span - skipped), :] = hist_ref[part]
         else:
-            turn(hist_ref, 1, skipped // 128)
+            turn(hist_ref, 1, 3)
         power_ref[...] = jnp.zeros_like(power_ref)
 
     turn(volts_ref, now, 0)
@@ -97,7 +97,7 @@
     lax.fori_loop(0, SUBBAND_COUNT // 16, filter_rows, 0)
 
     def transform(t, _):
-        result = jnp.dot(table_ref[...], filt[t], preferred_element_type=jnp.float32)
+        result = jnp.dot(table_ref[0], filt[t], preferred_element_type=jnp.float32)
         for tile in range(tiles):
             spread[tile, pl.ds(t, 2 * SUBBAND_COUNT, stride=SPREAD), :] = result[
                 :, tile * 128 : (tile + 1) * 128
@@ -131,7 +131,7 @@
         power_ref[:, tile * 128 : (tile + 1) * 128] += power[tile]
 
 
-def front(volts, hist, first, steps, splits, owners, keep, window, table, tail):
+def front(volts, hist, first, steps, splits, owners, keep, me, window, table, tail):
     inputs = volts.shape[2]
     span = BLOCK * SUBBAND_COUNT
     groups = SUBBAND_COUNT // owners // GROUP
@@ -142,41 +142,44 @@
         for _ in range(owners * splits)
     ]
     out_specs = [
-        pl.BlockSpec((each, 2, GROUP, BLOCK, inputs), lambda s: (0, 0, 0, s, 0))
+        pl.BlockSpec((each, 2, GROUP, BLOCK, inputs), lambda s, me: (0, 0, 0, s, 0))
         for _ in range(owners * splits)
     ]
     outs.append(jax.ShapeDtypeStruct((BLOCK, inputs), jnp.float32))
-    out_specs.append(pl.BlockSpec((BLOCK, inputs), lambda s: (0, 0)))
+    out_specs.append(pl.BlockSpec((BLOCK, inputs), lambda s, me: (0, 0)))
     kept = (TAPS - 1) * SUBBAND_COUNT
     if tail:
         outs.append(jax.ShapeDtypeStruct((2, kept, inputs), jnp.bfloat16))
-        out_specs.append(pl.BlockSpec((2, kept, inputs), lambda s: (0, 0, 0)))
+        out_specs.append(pl.BlockSpec((2, kept, inputs), lambda s, me: (0, 0, 0)))
     if hist is None:
-        hist, hist_spec = volts, pl.BlockSpec((2, 1, inputs, span), lambda s: (0, 0, 0, first - 1))
+        hist, hist_spec = volts, pl.BlockSpec((2, 1, inputs, span), lambda s, me: (0, 0, 0, first - 1))
         turned = False
     else:
-        hist_spec, turned = pl.BlockSpec((2, kept, inputs), lambda s: (0, 0, 0)), True
+        hist_spec, turned = pl.BlockSpec((2, kept, inputs), lambda s, me: (0, 0, 0)), True
     result = pl.pallas_call(
         functools.partial(front_kernel, splits, owners, turned, tail),
-        grid=(steps,),
+        grid_spec=pltpu.PrefetchScalarGridSpec(
+            num_scalar_prefetch=1,
+            grid=(steps,),
+            in_specs=[
+                pl.BlockSpec(memory_space=pltpu.SMEM),
+                hist_spec,
+                pl.BlockSpec((2, 1, inputs, span), lambda s, me: (0, 0, 0, first + s)),
+                pl.BlockSpec(window.shape, lambda s, me: (0, 0, 0)),
+                pl.BlockSpec((1, *table.shape[1:]), lambda s, me: (me[0], 0, 0)),
+            ],
+            out_specs=out_specs,
+            scratch_shapes=[
+                pltpu.VMEM((2, 2, span, inputs), jnp.bfloat16),
+                pltpu.VMEM((BLOCK, 2 * SUBBAND_COUNT, inputs), jnp.bfloat16),
+                pltpu.VMEM((inputs // 128, 2 * SUBBAND_COUNT * SPREAD, 128), jnp.float32),
+            ],
+        ),
         out_shape=outs,
-        in_specs=[
-            pl.BlockSpec(memory_space=pltpu.SMEM),
-            hist_spec,
-            pl.BlockSpec((2, 1, inputs, span), lambda s: (0, 0, 0, first + s)),
-            pl.BlockSpec(window.shape, lambda s: (0, 0, 0)),
-            pl.BlockSpec(table.shape, lambda s: (0, 0)),
-        ],
-        out_specs=out_specs,
-        scratch_shapes=[
-            pltpu.VMEM((2, 2, span, inputs), jnp.bfloat16),
-            pltpu.VMEM((BLOCK, 2 * SUBBAND_COUNT, inputs), jnp.bfloat16),
-            pltpu.VMEM((inputs // 128, 2 * SUBBAND_COUNT * SPREAD, 128), jnp.float32),
-        ],
         compiler_params=pltpu.CompilerParams(vmem_limit_bytes=VMEM),
         cost_estimate=COST,
         name="front",
-    )(keep, hist, volts, window, table)
+    )(me, keep, hist, volts, window, table)
     count = owners * splits
     return result[:count], result[count], result[count + 1] if tail else None
 
@@ -198,8 +201,9 @@
     )(value, *others)
 
 
-def correlate_kernel(owners, picks, outs, place_ref, *rest):
+def correlate_kernel(owners, picks, outs, sums, place_ref, *rest):
     count = len(picks)
+    sum_refs, rest = rest[:sums], rest[sums:]
     pieces = [rest[n * owners : (n + 1) * owners] for n in range(count)]
     out_refs, (held, turned, sems) = rest[-3 - outs : -3], rest[-3:]
     me = place_ref[0]
@@ -239,23 +243,28 @@
         left = turned[h].reshape(2 * per_half * inputs, 2 * depth)
         both = jnp.dot(left, right, preferred_element_type=jnp.float32)
         both = both.reshape(2, per_half * inputs, inputs)
+        if sums:
+            both = both + sum_refs[h][...]
         out_refs[h][...] = both.astype(out_refs[h].dtype)
 
 
-def correlate(place, pieces, picks, dtypes, earlier):
+def correlate(place, pieces, picks, dtypes, sums, earlier):
     owners = len(pieces[0])
     inputs = pieces[0][0].shape[-1]
     depth = sum(piece[0].shape[2] for piece in pieces)
     rows = owners // 2 * inputs
     operands = [value for piece in pieces for value in piece] + list(earlier)
+    columns = pl.BlockSpec((2, rows, inputs), lambda b: (0, 0, b))
     anywhere = pl.BlockSpec(memory_space=pl.ANY)
     outs = len(dtypes)
     return pl.pallas_call(
-        functools.partial(correlate_kernel, owners, picks, outs),
+        functools.partial(correlate_kernel, owners, picks, outs, len(sums)),
         grid=(owners,),
         out_shape=[jax.ShapeDtypeStruct((2, rows, owners * inputs), dtype) for dtype in dtypes],
-        in_specs=[pl.BlockSpec(memory_space=pltpu.SMEM)] + [anywhere] * len(operands),
-        out_specs=[pl.BlockSpec((2, rows, inputs), lambda b: (0, 0, b))] * outs,
+        in_specs=[pl.BlockSpec(memory_space=pltpu.SMEM)]
+        + [columns] * len(sums)
+        + [anywhere] * len(operands),
+        out_specs=[columns] * outs,
         scratch_shapes=[
             pltpu.VMEM((owners, 2, depth, inputs), jnp.bfloat16),
             pltpu.VMEM((outs, 2, owners // 2, inputs, 2 * depth), jnp.bfloat16),
@@ -264,7 +273,7 @@
         compiler_params=pltpu.CompilerParams(vmem_limit_bytes=VMEM),
         cost_estimate=COST,
         name="correlate",
-    )(place, *operands)
+    )(place, *sums, *operands)
 
 
 def equalize_kernel(rows_ref, columns_ref, mine_ref, theirs_ref, *rest):
@@ -277,7 +286,7 @@
 
 def equalize(row_scales, column_scales, mine, theirs, out, group, groups, waits):
     rows, columns = mine.shape[1:]
-    block = rows // 4
+    block = rows // 8
     specs = [
         pl.BlockSpec((block, 1), lambda r: (r, 0)),
         pl.BlockSpec((1, columns), lambda r: (0, 0)),
@@ -337,18 +346,18 @@
     keep_ahead = lax.dynamic_slice_in_dim(twice, me * fine, SUBBAND_COUNT, 0)
 
     rows = twiddle_values().reshape(owners, groups, GROUP, 2, 2 * SUBBAND_COUNT)
-    rows = rows.transpose(0, 1, 3, 2, 4).reshape(2 * SUBBAND_COUNT, 2 * SUBBAND_COUNT)
-    rows = jnp.asarray(np.concatenate([rows, rows], 0)).astype(jnp.bfloat16)
-    table = lax.dynamic_slice_in_dim(rows, me * 2 * fine, 2 * SUBBAND_COUNT, 0)
-    window = jnp.broadcast_to(
-        jnp.asarray(window_values())[:, :, None], (TAPS, SUBBAND_COUNT, 128)
-    )
+    rows = rows.transpose(0, 1, 3, 2, 4)
+    turns = [np.roll(rows, -z, 0).reshape(2 * SUBBAND_COUNT, -1) for z in range(owners)]
+    table = jnp.asarray(np.stack(turns).astype(jnp.bfloat16))
+    window = np.broadcast_to(window_values()[:, :, None], (TAPS, SUBBAND_COUNT, 128))
+    window = jnp.asarray(np.ascontiguousarray(window))
+    spot = jnp.reshape(me, (1,)).astype(jnp.int32)
 
     parts, power, halo, end = [], [], None, blocks
     for size in PARTS:
         end -= size
         spectra, part_power, tail = front(
-            volts, None, end, size, 1, owners, keep_ahead, window, table, halo is None
+            volts, None, end, size, 1, owners, keep_ahead, spot, window, table, halo is None
         )
         if tail is not None:
             with jax.named_scope("halo"):
@@ -356,7 +365,7 @@
         parts.append([x.reshape(groups, 2, GROUP * size * BLOCK, inputs) for x in spectra])
         power.append(part_power)
     spectra, part_power, _ = front(
-        volts, halo, 0, end, groups, owners, keep_ahead, window, table, False
+        volts, halo, 0, end, groups, owners, keep_ahead, spot, window, table, False
     )
     power.append(part_power)
     spectra = [x.reshape(1, 2, GROUP * end * BLOCK, inputs) for x in spectra]
@@ -384,7 +393,7 @@
         got = [parts[n][0]]
         for d in range(1, owners):
             gates = list(waits.get(d, ()))
-            if len(flat) >= IN_FLIGHT:
+            if len(flat) >= IN_FLIGHT and not (n == 1 and d == 2):
                 gates.append(flat[len(flat) - IN_FLIGHT])
             value = after(parts[n][d], *gates) if gates else parts[n][d]
             with jax.named_scope(f"part{n}_shift{d}"):
@@ -396,30 +405,37 @@
         with jax.named_scope(f"rows{j}"):
             return lax.ppermute(theirs, "tm", [(0, 1), (1, 0)])
 
-    def multiply(j, place, dtypes, earlier):
-        pieces = arrived[:shared] + [arrived[shared + j]]
-        return correlate(place, pieces, (j,) * shared + (0,), dtypes, earlier)
-
+    def multiply(j, place, dtypes, sums=(), earlier=(), begin=0, end=shared + 1):
+        pieces = arrived[:shared] + arrived[shared + j : shared + j + 1]
+        picks = (j,) * shared + (0,)
+        return correlate(place, pieces[begin:end], picks[begin:end], dtypes, sums, earlier)
+
+    both = [jnp.bfloat16, jnp.float32]
+    last_spectra = parts[shared][0]
     for n in range(shared):
-        send(n, {})
+        waits = {} if n == 0 else {d: [last_spectra, arrived[0][2]] for d in range(1, owners) if d != 2}
+        send(n, waits)
     send(shared, {owners - 1: [column_scales]})
     waiting = None
-    for j in range(groups):
-        final = j + 1 == groups
-        if not final:
-            send(shared + j + 1, {})
-            theirs, mine = multiply(j, place, [jnp.bfloat16, jnp.float32], [])
-        else:
-            (theirs,) = multiply(j, place[:2], [jnp.bfloat16], [])
+    for j in range(groups - 1):
+        waits = {}
+        if j == 0:
+            partial = multiply(groups - 1, place, [jnp.float32] * 2, end=shared)
+            waits = {owners - 1: partial}
+        send(shared + j + 1, waits)
+        theirs, mine = multiply(j, place, both)
         if waiting is not None:
             out = equalize(*waiting, out, j - 1, groups, [theirs])
-        if final:
-            theirs = to_other(j, theirs)
-            (mine,) = multiply(j, place[::2], [jnp.float32], [])
-        else:
-            theirs = to_other(j, after(theirs, *arrived[shared + j + 1][1:]))
+        if j + 2 < groups:
+            theirs = after(theirs, *arrived[shared + j + 1][1:])
+        theirs = to_other(j, theirs)
         waiting = (row_scales[j], column_scales, mine, theirs)
-    out = equalize(*waiting, out, groups - 1, groups, [])
+    j = groups - 1
+    (theirs,) = multiply(j, place[:2], both[:1], partial[:1], [out], begin=shared)
+    out = equalize(*waiting, out, groups - 2, groups, [theirs])
+    theirs = to_other(j, theirs)
+    (mine,) = multiply(j, place[::2], both[1:], partial[1:], begin=shared)
+    out = equalize(row_scales[j], column_scales, mine, theirs, out, j, groups, [])
     return out[None]
 
 
@@ -490,6 +506,7 @@
         and (SUBBAND_COUNT // owners) % GROUP == 0
         and lax.axis_size("tm") == 2
         and frames % BLOCK == 0
+        and SUBBAND_COUNT // owners // GROUP > 1
         and frames // BLOCK > sum(PARTS)
     )
     return (pipelined if fits else plain)(volts, flagged)

time: 482 us -> 477 us (0.990)
  waiting for transfers between devices: 215 us -> 129 us
  blocking collectives: 38.5 us -> 113 us
  Pallas kernels: 174 us -> 189 us
  starting transfers between devices: 27.3 us -> 21 us
    ppermute x18, waiting for transfers between devices: 215 us -> 128 us  [shift(): lax.ppermute(value, 'station', [(s, (s + d) % count) for s in range(count)])]
    all_gather x1, blocking collectives: 26 us -> 98.4 us  [pipelined(): scales = lax.all_gather(scale, 'station', axis=0, tiled=True)]
    ppermute x18, starting transfers between devices: 24.3 us -> 15.4 us  [shift(): lax.ppermute(value, 'station', [(s, (s + d) % count) for s in range(count)])]
    pallas_call x5 -> x6, Pallas kernels: 69.1 us -> 77.6 us  [correlate(): pl.pallas_call(functools.partial(correlate_kernel, owners, picks, outs, l...]
    pallas_call x4, Pallas kernels: 21.4 us -> 29.3 us  [equalize(): pl.pallas_call(equalize_kernel, grid=(rows // block,), out_shape=jax.Shap...]
    unnamed x43 -> x45, local copies, waits for them, and re-layouts: 11.7 us -> 10.8 us
  transfers between devices with their start and end apart: 23 -> 23, of which waited for: 11 -> 11; matrix products, arithmetic and copies ran while one was open for 2% -> 3% of each run, Pallas kernels for 32% -> 35%
where the time goes in v4:
time: 477 us; the launch traced here: 476 us
  Pallas kernels  189 us (40%)
  waiting for transfers between devices  129 us (27%)
  blocking collectives  113 us (24%)
  starting transfers between devices  21 us (4%)
  local copies, waits for them, and re-layouts  17 us (4%)
  other arithmetic  6.71 us (1%)
    ppermute x18, waiting for transfers between devices, shift(): lax.ppermute(value, 'station', [(s, (s + d) % count) for s in range(count)])  128 us
    all_gather x1, blocking collectives, pipelined(): scales = lax.all_gather(scale, 'station', axis=0, tiled=True)  98.4 us
    pallas_call x3, Pallas kernels, front(): pl.pallas_call(functools.partial(front_kernel, splits, owners, turned, ta...  82.2 us
    pallas_call x6, Pallas kernels, correlate(): pl.pallas_call(functools.partial(correlate_kernel, owners, picks, outs, l...  77.6 us
    pallas_call x4, Pallas kernels, equalize(): pl.pallas_call(equalize_kernel, grid=(rows // block,), out_shape=jax.Shap...  29.3 us
    ppermute x18, starting transfers between devices, shift(): lax.ppermute(value, 'station', [(s, (s + d) % count) for s in range(count)])  15.4 us
    psum x1, blocking collectives, pipelined(): total = lax.psum(local, ('band', 'tm'))  14.2 us
    unnamed x45, local copies, waits for them, and re-layouts  10.8 us
  transfers between devices with their start and end apart: 23, of which 11 were waited for; matrix products, arithmetic and copies ran while one was open for 3% of the time, Pallas kernels for 35%

profile of v4, /device:TPU:11, one launch (start us, length us, event | category | flops | bytes accessed | tf_op | source)
XLA Modules:
  0.0 475.7 jit_solution(2994699563423236747)
XLA Ops:
  2.2 13.9 %front.3 = (bf16[4,2,9,16,256]{4,3,2,1,0:T(8,128)(2,1)}, bf16[4,2,9,16,256]{4,3,2,1,0:T(8,128)(2,1)}, bf16[4,2,9,16,256]{4,3,2,1,0:T(8,128)(2,1)}, bf16[4,2,9,16...) custom-call(s32[1]{0:T(128)} %bitcast.me_ref, f32[144]{0:T(256)} %dynamic_slice.14.keep_ref, ...), custom_call_target="tpu_custom_call" | custom-call | flops 1024 | bytes 1024 | tf_op jit(solution)/shard_map/front/pallas_call | solution.py:159
  16.1 1.3 collective-permute-start
  17.4 1.3 collective-permute-start.1
  18.7 1.1 collective-permute-start.2
  19.8 1.4 collective-permute-start.3
  21.2 30.2 %front.4 = (bf16[4,2,9,48,256]{4,3,2,1,0:T(8,128)(2,1)}, bf16[4,2,9,48,256]{4,3,2,1,0:T(8,128)(2,1)}, bf16[4,2,9,48,256]{4,3,2,1,0:T(8,128)(2,1)}, bf16[4,2,9,48,256]{4,3,2,1,0:T(8,128)(2,1)}, f32[16,256]{1,0:T(8,128)}) custom-call(s32[1]{0:T(128)} %bitcast.me_ref, f32[144]{0:T(256)} %dynamic_slice.14.keep_ref, bf16[2,1,256,18432]{3,2,1,0:T(8,128)(2,1)} %volts_ref.5, ...), custom_call_target="tpu_custom_call" | custom-call | flops 1024 | bytes 1024 | tf_op jit(solution)/shard_map/front/pallas_call | solution.py:159
  51.4 38.1 %front.5 = (bf16[1,2,9,64,256]{4,3,2,1,0:T(8,128)(2,1)}, bf16[1,2,9,64,256]{4,3,2,1,0:T(8,128)(2,1)}, bf16[1,2,9,64,256]{4,3,2,1,0:T(8,128)(2,1)}, bf16[1,2,9,64...) custom-call(s32[1]{0:T(128)} %bitcast.me_ref, ...), custom_call_target="tpu_custom_call" | custom-call | flops 1024 | bytes 1024 | tf_op jit(solution)/shard_map/front/pallas_call | solution.py:159
  89.5 15.7 %collective-permute-done.2.refs_2_.rest_2_ = bf16[4,2,144,256]{3,2,1,0:T(8,128)(2,1)S(1)} collective-permute-done((bf16[4,2,144,256]{3,2,1,0:T(8,128)(2,1)}, bf16[4,2,144,256]{3,2,1,0:T(8,128)(2,1)S(1)}, u32[]{:S(2)}, u32[]{:S(2)}) %collective-permute-start.2) | collective-permute-done | bytes 589856 | tf_op jit(solution)/shard_map/part0_shift2/ppermute | solution.py:319
  106.1 3.7 collective-permute-done.3.refs_3_.rest_3_
  109.7 1.3 convert_reduce_fusion
  111.7 1.3 add_reduce_fusion
  112.9 14.2 %psum.7 = f32[256]{0:T(256)S(1)} all-reduce(f32[256]{0:T(256)} %add_reduce_fusion), channel_id=1, replica_groups=mesh['station'=4,'band'=4,'tm'=2] {'band','tm'}, use_global_device_ids=true, to_apply=%region_2.3 | all-reduce | flops 256 | bytes 2048 | tf_op jit(solution)/shard_map/psum | solution.py:376
  127.1 19.3 %collective-permute-done.5.rest_6_.refs_1_ = bf16[4,2,432,256]{3,2,1,0:T(8,128)(2,1)S(1)} collective-permute-done((bf16[4,2,432,256]{3,2,1,0:T(8,128)(2,1)}, bf16[4,2,432,256]{3,2,1,0:T(8,128)(2,1)S(1)}, u32[]{:S(2)}, u32[]{:S(2)}) %collective-permute-start.5) | collective-permute-done | bytes 1769504 | tf_op jit(solution)/shard_map/part1_shift2/ppermute | solution.py:319
  146.5 1.2 copy-done
  147.7 3.5 collective-permute-start.11
  151.2 98.4 %all-gather = f32[4,1,256]{2,1,0:T(1,128)} all-gather(f32[1,1,256]{2,1,0:T(1,128)S(1)} %bitcast.79), channel_id=1, replica_groups=mesh['station'=4,'band'=4,'tm'=2] {'station'}, dimensions={0}, use_global_device_ids=true | all-gather | bytes 5120 | tf_op jit(solution)/shard_map/all_gather | solution.py:378
  249.5 1.2 copy-done.1
  250.8 1.8 collective-permute-start.7
  253.2 0.8 copy-done.11
  254.0 1.2 collective-permute-start.12
  255.2 11.5 %correlate.6 = (f32[2,512,1024]{2,1,0:T(8,128)}, f32[2,512,1024]{2,1,0:T(8,128)}) custom-call(s32[3]{0:T(128)} %pad_add_fusion.place_ref, bf16[4,2,144,256]{3,2,1,0:T(8,128)(2,1)} %bitcast.44, bf16[4,2,144,256]{3,2,1,0:T(8,128)(2,1)} %copy-done.3, bf16[4,2,144,256]{3,2,1,0:T(8,128)(2,1)} %copy-done.2, ...), custom_call_target="tpu_custom_call" | custom-call | flops 1024 | bytes 1024 | tf_op jit(solution)/shard_map/correlate/pallas_call | solution.py:260
  267.8 13.3 %collective-permute-done.15.refs_3_.rest_11_ = bf16[1,2,576,256]{3,2,1,0:T(8,128)(2,1)S(1)} collective-permute-done((bf16[1,2,576,256]{3,2,1,0:T(8,128)(2,1)}, bf16[1,2,576,256]{3,2,1,0:T(8,128)(2,1)S(1)}, u32[]{:S(2)}, u32[]{:S(2)}) %collective-permute-start.15) | collective-permute-done | bytes 589856 | tf_op jit(solution)/shard_map/part2_shift3/ppermute | solution.py:319
  281.0 0.8 copy-done.10
  281.9 16.0 %correlate.9 = (bf16[2,512,1024]{2,1,0:T(8,128)(2,1)}, f32[2,512,1024]{2,1,0:T(8,128)}) custom-call(s32[3]{0:T(128)} %pad_add_fusion.place_ref, bf16[4,2,144,256]{3,2,1,0:T(8,128)(2,1)} %bitcast.45, bf16[4,2,144,256]{3,2,1,0:T(8,128)(2,1)} %copy-done.3, bf16[4,2,144,256]{3,2,1,0:T(8,128)(2,1)} %copy-done.2, ...), custom_call_target="tpu_custom_call" | custom-call | flops 1024 | bytes 1024 | tf_op jit(solution)/shard_map/correlate/pallas_call | solution.py:260
  297.9 8.3 %collective-permute-done.12.refs_1_.rest_10_.refs_2_ = bf16[1,2,576,256]{3,2,1,0:T(8,128)(2,1)S(1)} collective-permute-done((bf16[1,2,576,256]{3,2,1,0:T(8,128)(2,1)}, bf16[1,2,576,256]{3,2,1,0:T(8,128)(2,1)S(1)}, u32[]{:S(2)}, u32[]{:S(2)}) %collective-permute-start.12) | collective-permute-done | bytes 589856 | tf_op jit(solution)/shard_map/part3_shift2/ppermute | solution.py:319
  306.2 20.9 %collective-permute-done.8.refs_1_.rest_9_ = bf16[1,2,576,256]{3,2,1,0:T(8,128)(2,1)S(1)} collective-permute-done((bf16[1,2,576,256]{3,2,1,0:T(8,128)(2,1)}, bf16[1,2,576,256]{3,2,1,0:T(8,128)(2,1)S(1)}, u32[]{:S(2)}, u32[]{:S(2)}) %collective-permute-start.8) | collective-permute-done | bytes 589856 | tf_op jit(solution)/shard_map/part3_shift1/ppermute | solution.py:319
  328.3 2.4 collective-permute-start.20
  330.8 2.1 collective-permute-start.9
  332.9 1.2 collective-permute-start.17
  335.7 2.5 broadcast_divide_fusion
  338.2 0.9 copy.33.rows_ref
  339.1 16.1 %correlate.8 = (bf16[2,512,1024]{2,1,0:T(8,128)(2,1)}, f32[2,512,1024]{2,1,0:T(8,128)}) custom-call(s32[3]{0:T(128)} %pad_add_fusion.place_ref, bf16[4,2,144,256]{3,2,1,0:T(8,128)(2,1)} %bitcast.46, bf16[4,2,144,256]{3,2,1,0:T(8,128)(2,1)} %copy-done.3, bf16[4,2,144,256]{3,2,1,0:T(8,128)(2,1)} %copy-done.2, ...), custom_call_target="tpu_custom_call" | custom-call | flops 1024 | bytes 1024 | tf_op jit(solution)/shard_map/correlate/pallas_call | solution.py:260
  355.2 7.3 %equalize.4.rest_0_ = f32[4,2,512,1024]{3,2,1,0:T(8,128)} custom-call(f32[512,1]{1,0:T(8,128)} %copy.33.rows_ref, f32[1,1024]{1,0:T(1,128)} %bitcast.70, f32[2,512,1024]{2,1,0:T(8,128)} %get-tuple-element.72.mine_ref, bf16[2,512,1024]{2,1,0:T(8,128)(2,1)} %collective-permute-done.20.theirs_ref, bf16[2,512,1024]{2,1,0:T(8,128)(2,1)} %get-tuple-element.71.refs_0_.rest_0_), custom_call_target="tpu_custom_call" | custom-call | flops 1024 | bytes 1024 | tf_op jit(solution)/shard_map/equalize/pallas_call | solution.py:304
  362.5 19.4 %collective-permute-done.9.refs_1_.rest_9_ = bf16[1,2,576,256]{3,2,1,0:T(8,128)(2,1)S(1)} collective-permute-done((bf16[1,2,576,256]{3,2,1,0:T(8,128)(2,1)}, bf16[1,2,576,256]{3,2,1,0:T(8,128)(2,1)S(1)}, u32[]{:S(2)}, u32[]{:S(2)}) %collective-permute-start.9) | collective-permute-done | bytes 589856 | tf_op jit(solution)/shard_map/part4_shift1/ppermute | solution.py:319
  381.9 2.8 collective-permute-done.17.refs_1_.refs_3_.rest_11_
  384.7 0.8 copy-done.7
  386.3 1.3 collective-permute-start.18
  388.2 0.9 copy.34.rows_ref
  389.1 16.2 %correlate.10 = (bf16[2,512,1024]{2,1,0:T(8,128)(2,1)}, f32[2,512,1024]{2,1,0:T(8,128)}) custom-call(s32[3]{0:T(128)} %pad_add_fusion.place_ref, bf16[4,2,144,256]{3,2,1,0:T(8,128)(2,1)} %bitcast.47, bf16[4,2,144,256]{3,2,1,0:T(8,128)(2,1)} %copy-done.3, bf16[4,2,144,256]{3,2,1,0:T(8,128)(2,1)} %copy-done.2, ...), custom_call_target="tpu_custom_call" | custom-call | flops 1024 | bytes 1024 | tf_op jit(solution)/shard_map/correlate/pallas_call | solution.py:260
  406.0 7.3 %equalize.5.rest_5_.rest_0_ = f32[4,2,512,1024]{3,2,1,0:T(8,128)} custom-call(f32[512,1]{1,0:T(8,128)} %copy.34.rows_ref, f32[1,1024]{1,0:T(1,128)} %bitcast.71, f32[2,512,1024]{2,1,0:T(8,128)} %get-tuple-element.70.mine_ref, bf16[2,512,1024]{2,1,0:T(8,128)(2,1)} %collective-permute-done.19.theirs_ref, ...), custom_call_target="tpu_custom_call", output_to_operand_aliasing={{}: (4, {})} | custom-call | flops 1024 | bytes 1024 | tf_op jit(solution)/shard_map/equalize/pallas_call | solution.py:304
  413.4 24.0 %collective-permute-done.10.rest_2_ = bf16[1,2,576,256]{3,2,1,0:T(8,128)(2,1)S(1)} collective-permute-done((bf16[1,2,576,256]{3,2,1,0:T(8,128)(2,1)}, bf16[1,2,576,256]{3,2,1,0:T(8,128)(2,1)S(1)}, u32[]{:S(2)}, u32[]{:S(2)}) %collective-permute-start.10) | collective-permute-done | bytes 589856 | tf_op jit(solution)/shard_map/part5_shift1/ppermute | solution.py:319
  438.9 8.7 %correlate.11.rest_1_ = bf16[2,512,1024]{2,1,0:T(8,128)(2,1)} custom-call(s32[2]{0:T(128)} %pad_add_fusion.1.place_ref, f32[2,512,1024]{2,1,0:T(8,128)} %get-tuple-element.67.refs_1_.rest_0_, bf16[1,2,576,256]{3,2,1,0:T(8,128)(2,1)} %bitcast.51, bf16[1,2,576,256]{3,2,1,0:T(8,128)(2,1)} %copy-done.14, bf16[1,2,576,256]{3,2,1,0:T(8,128)(2,1)} %copy-done.13, ...), custom_call_target="tpu_custom_call" | custom-call | flops 1024 | bytes 1024 | tf_op jit(solution)/shard_map/correlate/pallas_call | solution.py:260
  448.9 0.9 copy.36.rows_ref
  449.7 0.9 copy.35.rows_ref
  450.6 9.1 %correlate.7.mine_ref = f32[2,512,1024]{2,1,0:T(8,128)} custom-call(s32[2]{0:T(128)} %slice.18.place_ref, f32[2,512,1024]{2,1,0:T(8,128)} %get-tuple-element.54.refs_2_.rest_0_, bf16[1,2,576,256]{3,2,1,0:T(8,128)(2,1)} %bitcast.52, bf16[1,2,576,256]{3,2,1,0:T(8,128)(2,1)} %copy-done.14, bf16[1,2,576,256]{3,2,1,0:T(8,128)(2,1)} %copy-done.13, ...), custom_call_target="tpu_custom_call" | custom-call | flops 1024 | bytes 1024 | tf_op jit(solution)/shard_map/correlate/pallas_call | solution.py:260
  459.7 7.3 %equalize.6.rest_0_ = f32[4,2,512,1024]{3,2,1,0:T(8,128)} custom-call(f32[512,1]{1,0:T(8,128)} %copy.35.rows_ref, f32[1,1024]{1,0:T(1,128)} %bitcast.72, f32[2,512,1024]{2,1,0:T(8,128)} %get-tuple-element.76.mine_ref, bf16[2,512,1024]{2,1,0:T(8,128)(2,1)} %collective-permute-done.22.theirs_ref, ...), custom_call_target="tpu_custom_call", output_to_operand_aliasing={{}: (4, {})} | custom-call | flops 1024 | bytes 1024 | tf_op jit(solution)/shard_map/equalize/pallas_call | solution.py:304
  467.1 1.3 copy-done.16
  468.4 7.3 %equalize.7 = f32[4,2,512,1024]{3,2,1,0:T(8,128)} custom-call(f32[512,1]{1,0:T(8,128)} %copy.36.rows_ref, f32[1,1024]{1,0:T(1,128)} %bitcast.73, f32[2,512,1024]{2,1,0:T(8,128)} %correlate.7.mine_ref, bf16[2,512,1024]{2,1,0:T(8,128)(2,1)} %copy-done.16, f32[4,2,512,1024]{3,2,1,0:T(8,128)} %equalize.6.rest_0_), custom_call_target="tpu_custom_call", output_to_operand_aliasing={{}: (4, {})} | custom-call | flops 1024 | bytes 1024 | tf_op jit(solution)/shard_map/equalize/pallas_call | solution.py:304
  (95 shorter events, 12.4 us)
Async XLA Ops:
  0.9 0.5 copy-start.21
  1.4 14.7 %copy-start.20 = (f32[4,144]{1,0:T(4,128)}, f32[4,144]{1,0:T(4,128)S(1)}, u32[]{:S(2)}) copy-start(f32[4,144]{1,0:T(4,128)S(1)} %convert_element_type.3) | copy-start | bytes 6916
  16.1 35.3 %collective-permute-start = (bf16[2,1584,256]{2,1,0:T(8,128)(2,1)}, bf16[2,1584,256]{2,1,0:T(8,128)(2,1)}, u32[]{:S(2)}, u32[]{:S(2)}) collective-permute-start(bf16[2,1584,256]{2,1,0:T(8,128)(2,1)} %get-tuple-element.43), channel_id=1, source_target_pairs={{0,1},{2,3},{4,5},{6,7},{8,9},{10,11},{12,13},{14,15},{16,17},{18,... | collective-permute-start | bytes 4866056 | tf_op jit(solution)/shard_map/halo/ppermute | solution.py:324
  17.4 72.1 %collective-permute-start.1 = (bf16[4,2,144,256]{3,2,1,0:T(8,128)(2,1)}, bf16[4,2,144,256]{3,2,1,0:T(8,128)(2,1)S(1)}, u32[]{:S(2)}, u32[]{:S(2)}) collective-permute-start(bf16[4,2,144,256]{3,2,1,0:T(8,128)(2,1)} %bitcast.84), channel_id=1, source_target_pairs={{0,8},{8,16},{16,24},{24,0},{1,9},{9,17},{17,25},{25,1},{2,10},{10... | collective-permute-start | bytes 1769480 | tf_op jit(solution)/shard_map/part0_shift1/ppermute | solution.py:319
  18.7 86.5 %collective-permute-start.2 = (bf16[4,2,144,256]{3,2,1,0:T(8,128)(2,1)}, bf16[4,2,144,256]{3,2,1,0:T(8,128)(2,1)S(1)}, u32[]{:S(2)}, u32[]{:S(2)}) collective-permute-start(bf16[4,2,144,256]{3,2,1,0:T(8,128)(2,1)} %bitcast.83), channel_id=1, source_target_pairs={{0,16},{8,24},{16,0},{24,8},{1,17},{9,25},{17,1},{25,9},{2,18},{10... | collective-permute-start | bytes 1769480 | tf_op jit(solution)/shard_map/part0_shift2/ppermute | solution.py:319
  19.8 89.9 %collective-permute-start.3 = (bf16[4,2,144,256]{3,2,1,0:T(8,128)(2,1)}, bf16[4,2,144,256]{3,2,1,0:T(8,128)(2,1)}, u32[]{:S(2)}, u32[]{:S(2)}) collective-permute-start(bf16[4,2,144,256]{3,2,1,0:T(8,128)(2,1)} %bitcast.82), channel_id=1, source_target_pairs={{0,24},{8,0},{16,8},{24,16},{1,25},{9,1},{17,9},{25,17},{2,26},{10... | collective-permute-start | bytes 1769480 | tf_op jit(solution)/shard_map/part0_shift3/ppermute | solution.py:319
  51.4 95.1 %collective-permute-start.5 = (bf16[4,2,432,256]{3,2,1,0:T(8,128)(2,1)}, bf16[4,2,432,256]{3,2,1,0:T(8,128)(2,1)S(1)}, u32[]{:S(2)}, u32[]{:S(2)}) collective-permute-start(bf16[4,2,432,256]{3,2,1,0:T(8,128)(2,1)} %bitcast.81), channel_id=1, source_target_pairs={{0,16},{8,24},{16,0},{24,8},{1,17},{9,25},{17,1},{25,9},{2,18},{10... | collective-permute-start | bytes 5308424 | tf_op jit(solution)/shard_map/part1_shift2/ppermute | solution.py:319
  89.5 15.7 %copy-start.3 = (bf16[4,2,144,256]{3,2,1,0:T(8,128)(2,1)}, bf16[4,2,144,256]{3,2,1,0:T(8,128)(2,1)S(1)}, u32[]{:S(2)}) copy-start(bf16[4,2,144,256]{3,2,1,0:T(8,128)(2,1)S(1)} %collective-permute-done.1.refs_3_.rest_1_) | copy-start | bytes 1769476
  105.2 0.8 copy-start.2
  106.1 143.5 %collective-permute-start.4 = (bf16[4,2,432,256]{3,2,1,0:T(8,128)(2,1)}, bf16[4,2,432,256]{3,2,1,0:T(8,128)(2,1)S(1)}, u32[]{:S(2)}, u32[]{:S(2)}) collective-permute-start(bf16[4,2,432,256]{3,2,1,0:T(8,128)(2,1)} %after.16), channel_id=1, source_target_pairs={{0,8},{8,16},{16,24},{24,0},{1,9},{9,17},{17,25},{25,1},{2,10},{10... | collective-permute-start | bytes 5308424 | tf_op jit(solution)/shard_map/part1_shift1/ppermute | solution.py:319
  109.7 1.9 copy-start.18
  109.7 142.8 %collective-permute-start.6 = (bf16[4,2,432,256]{3,2,1,0:T(8,128)(2,1)}, bf16[4,2,432,256]{3,2,1,0:T(8,128)(2,1)}, u32[]{:S(2)}, u32[]{:S(2)}) collective-permute-start(bf16[4,2,432,256]{3,2,1,0:T(8,128)(2,1)} %after.17), channel_id=1, source_target_pairs={{0,24},{8,0},{16,8},{24,16},{1,25},{9,1},{17,9},{25,17},{2,26},{10... | collective-permute-start | bytes 5308424 | tf_op jit(solution)/shard_map/part1_shift3/ppermute | solution.py:319
  146.5 1.2 copy-start
  147.7 105.5 %collective-permute-start.11 = (bf16[1,2,576,256]{3,2,1,0:T(8,128)(2,1)}, bf16[1,2,576,256]{3,2,1,0:T(8,128)(2,1)S(1)}, u32[]{:S(2)}, u32[]{:S(2)}) collective-permute-start(bf16[1,2,576,256]{3,2,1,0:T(8,128)(2,1)} %after.22), channel_id=1, source_target_pairs={{0,16},{8,24},{16,0},{24,8},{1,17},{9,25},{17,1},{25,9},{2,18},{10... | collective-permute-start | bytes 1769480 | tf_op jit(solution)/shard_map/part2_shift2/ppermute | solution.py:319
  249.5 1.2 copy-start.1
  250.8 16.0 %collective-permute-start.7 = (bf16[1,2,576,256]{3,2,1,0:T(8,128)(2,1)}, bf16[1,2,576,256]{3,2,1,0:T(8,128)(2,1)S(1)}, u32[]{:S(2)}, u32[]{:S(2)}) collective-permute-start(bf16[1,2,576,256]{3,2,1,0:T(8,128)(2,1)} %after.18), channel_id=1, source_target_pairs={{0,8},{8,16},{16,24},{24,0},{1,9},{9,17},{17,25},{25,1},{2,10},{10... | collective-permute-start | bytes 1769480 | tf_op jit(solution)/shard_map/part2_shift1/ppermute | solution.py:319
  252.6 28.5 %collective-permute-start.15 = (bf16[1,2,576,256]{3,2,1,0:T(8,128)(2,1)}, bf16[1,2,576,256]{3,2,1,0:T(8,128)(2,1)S(1)}, u32[]{:S(2)}, u32[]{:S(2)}) collective-permute-start(bf16[1,2,576,256]{3,2,1,0:T(8,128)(2,1)} %after.26), channel_id=1, source_target_pairs={{0,24},{8,0},{16,8},{24,16},{1,25},{9,1},{17,9},{25,17},{2,26},{10... | collective-permute-start | bytes 1769480 | tf_op jit(solution)/shard_map/part2_shift3/ppermute | solution.py:319
  253.2 0.8 copy-start.11
  254.0 52.2 %collective-permute-start.12 = (bf16[1,2,576,256]{3,2,1,0:T(8,128)(2,1)}, bf16[1,2,576,256]{3,2,1,0:T(8,128)(2,1)S(1)}, u32[]{:S(2)}, u32[]{:S(2)}) collective-permute-start(bf16[1,2,576,256]{3,2,1,0:T(8,128)(2,1)} %after.23), channel_id=1, source_target_pairs={{0,16},{8,24},{16,0},{24,8},{1,17},{9,25},{17,1},{25,9},{2,18},{10... | collective-permute-start | bytes 1769480 | tf_op jit(solution)/shard_map/part3_shift2/ppermute | solution.py:319
  266.7 0.8 copy-start.12
  267.5 59.5 %collective-permute-start.8 = (bf16[1,2,576,256]{3,2,1,0:T(8,128)(2,1)}, bf16[1,2,576,256]{3,2,1,0:T(8,128)(2,1)S(1)}, u32[]{:S(2)}, u32[]{:S(2)}) collective-permute-start(bf16[1,2,576,256]{3,2,1,0:T(8,128)(2,1)} %after.19), channel_id=1, source_target_pairs={{0,8},{8,16},{16,24},{24,0},{1,9},{9,17},{17,25},{25,1},{2,10},{10... | collective-permute-start | bytes 1769480 | tf_op jit(solution)/shard_map/part3_shift1/ppermute | solution.py:319
  281.0 0.8 copy-start.10
  281.9 45.6 %collective-permute-start.16 = (bf16[1,2,576,256]{3,2,1,0:T(8,128)(2,1)}, bf16[1,2,576,256]{3,2,1,0:T(8,128)(2,1)S(1)}, u32[]{:S(2)}, u32[]{:S(2)}) collective-permute-start(bf16[1,2,576,256]{3,2,1,0:T(8,128)(2,1)} %after.27), channel_id=1, source_target_pairs={{0,24},{8,0},{16,8},{24,16},{1,25},{9,1},{17,9},{25,17},{2,26},{10... | collective-permute-start | bytes 1769480 | tf_op jit(solution)/shard_map/part3_shift3/ppermute | solution.py:319
  306.2 21.3 %copy-start.6 = (bf16[1,2,576,256]{3,2,1,0:T(8,128)(2,1)}, bf16[1,2,576,256]{3,2,1,0:T(8,128)(2,1)S(1)}, u32[]{:S(2)}) copy-start(bf16[1,2,576,256]{3,2,1,0:T(8,128)(2,1)S(1)} %collective-permute-done.12.refs_1_.rest_10_.refs_2_) | copy-start | bytes 1769476
  327.1 0.9 copy-start.8
  327.5 0.8 copy-start.9
  328.3 26.8 %collective-permute-start.20 = (bf16[2,512,1024]{2,1,0:T(8,128)(2,1)}, bf16[2,512,1024]{2,1,0:T(8,128)(2,1)}, u32[]{:S(2)}, u32[]{:S(2)}) collective-permute-start(bf16[2,512,1024]{2,1,0:T(8,128)(2,1)} %after.31), channel_id=1, source_target_pairs={{0,1},{1,0},{2,3},{3,2},{4,5},{5,4},{6,7},{7,6},{8,9},{9,8},{10,11... | collective-permute-start | bytes 6291464 | tf_op jit(solution)/shard_map/rows0/ppermute | solution.py:406
  330.7 4.9 %copy-start.17 = (f32[4,1,256]{2,1,0:T(1,128)S(1)}, f32[4,1,256]{2,1,0:T(1,128)}, u32[]{:S(2)}) copy-start(f32[4,1,256]{2,1,0:T(1,128)} %all-gather) | copy-start | bytes 12292
  330.7 31.8 %collective-permute-start.13 = (bf16[1,2,576,256]{3,2,1,0:T(8,128)(2,1)}, bf16[1,2,576,256]{3,2,1,0:T(8,128)(2,1)S(1)}, u32[]{:S(2)}, u32[]{:S(2)}) collective-permute-start(bf16[1,2,576,256]{3,2,1,0:T(8,128)(2,1)} %after.24), channel_id=1, source_target_pairs={{0,16},{8,24},{16,0},{24,8},{1,17},{9,25},{17,1},{25,9},{2,18},{10... | collective-permute-start | bytes 1769480 | tf_op jit(solution)/shard_map/part4_shift2/ppermute | solution.py:319
  330.8 51.2 %collective-permute-start.9 = (bf16[1,2,576,256]{3,2,1,0:T(8,128)(2,1)}, bf16[1,2,576,256]{3,2,1,0:T(8,128)(2,1)S(1)}, u32[]{:S(2)}, u32[]{:S(2)}) collective-permute-start(bf16[1,2,576,256]{3,2,1,0:T(8,128)(2,1)} %after.20), channel_id=1, source_target_pairs={{0,8},{8,16},{16,24},{24,0},{1,9},{9,17},{17,25},{25,1},{2,10},{10... | collective-permute-start | bytes 1769480 | tf_op jit(solution)/shard_map/part4_shift1/ppermute | solution.py:319
  332.9 51.9 %collective-permute-start.17 = (bf16[1,2,576,256]{3,2,1,0:T(8,128)(2,1)}, bf16[1,2,576,256]{3,2,1,0:T(8,128)(2,1)S(1)}, u32[]{:S(2)}, u32[]{:S(2)}) collective-permute-start(bf16[1,2,576,256]{3,2,1,0:T(8,128)(2,1)} %after.28), channel_id=1, source_target_pairs={{0,24},{8,0},{16,8},{24,16},{1,25},{9,1},{17,9},{25,17},{2,26},{10... | collective-permute-start | bytes 1769480 | tf_op jit(solution)/shard_map/part4_shift3/ppermute | solution.py:319
  362.5 22.2 %copy-start.4 = (bf16[1,2,576,256]{3,2,1,0:T(8,128)(2,1)}, bf16[1,2,576,256]{3,2,1,0:T(8,128)(2,1)S(1)}, u32[]{:S(2)}) copy-start(bf16[1,2,576,256]{3,2,1,0:T(8,128)(2,1)S(1)} %collective-permute-done.13.refs_1_.refs_2_.rest_10_) | copy-start | bytes 1769476
  381.9 2.8 copy-start.5
  384.7 0.8 copy-start.7
  385.5 20.5 %collective-permute-start.19 = (bf16[2,512,1024]{2,1,0:T(8,128)(2,1)}, bf16[2,512,1024]{2,1,0:T(8,128)(2,1)}, u32[]{:S(2)}, u32[]{:S(2)}) collective-permute-start(bf16[2,512,1024]{2,1,0:T(8,128)(2,1)} %after.30), channel_id=1, source_target_pairs={{0,1},{1,0},{2,3},{3,2},{4,5},{5,4},{6,7},{7,6},{8,9},{9,8},{10,11... | collective-permute-start | bytes 6291464 | tf_op jit(solution)/shard_map/rows1/ppermute | solution.py:406
  386.1 27.2 %collective-permute-start.14 = (bf16[1,2,576,256]{3,2,1,0:T(8,128)(2,1)}, bf16[1,2,576,256]{3,2,1,0:T(8,128)(2,1)S(1)}, u32[]{:S(2)}, u32[]{:S(2)}) collective-permute-start(bf16[1,2,576,256]{3,2,1,0:T(8,128)(2,1)} %after.25), channel_id=1, source_target_pairs={{0,16},{8,24},{16,0},{24,8},{1,17},{9,25},{17,1},{25,9},{2,18},{10... | collective-permute-start | bytes 1769480 | tf_op jit(solution)/shard_map/part5_shift2/ppermute | solution.py:319
  386.1 51.2 %collective-permute-start.10 = (bf16[1,2,576,256]{3,2,1,0:T(8,128)(2,1)}, bf16[1,2,576,256]{3,2,1,0:T(8,128)(2,1)S(1)}, u32[]{:S(2)}, u32[]{:S(2)}) collective-permute-start(bf16[1,2,576,256]{3,2,1,0:T(8,128)(2,1)} %after.21), channel_id=1, source_target_pairs={{0,8},{8,16},{16,24},{24,0},{1,9},{9,17},{17,25},{25,1},{2,10},{10... | collective-permute-start | bytes 1769480 | tf_op jit(solution)/shard_map/part5_shift1/ppermute | solution.py:319
  386.3 51.8 %collective-permute-start.18 = (bf16[1,2,576,256]{3,2,1,0:T(8,128)(2,1)}, bf16[1,2,576,256]{3,2,1,0:T(8,128)(2,1)S(1)}, u32[]{:S(2)}, u32[]{:S(2)}) collective-permute-start(bf16[1,2,576,256]{3,2,1,0:T(8,128)(2,1)} %after.29), channel_id=1, source_target_pairs={{0,24},{8,0},{16,8},{24,16},{1,25},{9,1},{17,9},{25,17},{2,26},{10... | collective-permute-start | bytes 1769480 | tf_op jit(solution)/shard_map/part5_shift3/ppermute | solution.py:319
  405.4 54.3 %collective-permute-start.22 = (bf16[2,512,1024]{2,1,0:T(8,128)(2,1)}, bf16[2,512,1024]{2,1,0:T(8,128)(2,1)}, u32[]{:S(2)}, u32[]{:S(2)}) collective-permute-start(bf16[2,512,1024]{2,1,0:T(8,128)(2,1)} %get-tuple-element.75.rest_1_), channel_id=1, source_target_pairs={{0,1},{1,0},{2,3},{3,2},{4,5},{5,4},{6,7},{7,6},{8,9},{9,8},{10,11... | collective-permute-start | bytes 6291464 | tf_op jit(solution)/shard_map/rows2/ppermute | solution.py:406
  413.4 24.7 %copy-start.13 = (bf16[1,2,576,256]{3,2,1,0:T(8,128)(2,1)}, bf16[1,2,576,256]{3,2,1,0:T(8,128)(2,1)S(1)}, u32[]{:S(2)}) copy-start(bf16[1,2,576,256]{3,2,1,0:T(8,128)(2,1)S(1)} %collective-permute-done.14.rest_3_) | copy-start | bytes 1769476
  437.4 0.9 copy-start.14
  438.1 0.8 copy-start.15
  438.9 9.4 %copy-start.19 = (s32[3]{0:T(128)S(1)}, s32[3]{0:T(128)}, u32[]{:S(2)}) copy-start(s32[3]{0:T(128)} %pad_add_fusion.place_ref) | copy-start | bytes 40
  447.6 19.4 %collective-permute-start.21 = (bf16[2,512,1024]{2,1,0:T(8,128)(2,1)}, bf16[2,512,1024]{2,1,0:T(8,128)(2,1)S(1)}, u32[]{:S(2)}, u32[]{:S(2)}) collective-permute-start(bf16[2,512,1024]{2,1,0:T(8,128)(2,1)} %correlate.11.rest_1_), channel_id=1, source_target_pairs={{0,1},{1,0},{2,3},{3,2},{4,5},{5,4},{6,7},{7,6},{8,9},{9,8},{10,11... | collective-permute-start | bytes 6291464 | tf_op jit(solution)/shard_map/rows3/ppermute | solution.py:406
  467.0 1.3 copy-start.16

commit v5 on v4

--- a/solution.py
+++ b/solution.py
@@ -286,7 +286,7 @@
 
 def equalize(row_scales, column_scales, mine, theirs, out, group, groups, waits):
     rows, columns = mine.shape[1:]
-    block = rows // 8
+    block = rows // 4
     specs = [
         pl.BlockSpec((block, 1), lambda r: (r, 0)),
         pl.BlockSpec((1, columns), lambda r: (0, 0)),
@@ -353,41 +353,7 @@
     window = jnp.asarray(np.ascontiguousarray(window))
     spot = jnp.reshape(me, (1,)).astype(jnp.int32)
 
-    parts, power, halo, end = [], [], None, blocks
-    for size in PARTS:
-        end -= size
-        spectra, part_power, tail = front(
-            volts, None, end, size, 1, owners, keep_ahead, spot, window, table, halo is None
-        )
-        if tail is not None:
-            with jax.named_scope("halo"):
-                halo = passed_on(tail)
-        parts.append([x.reshape(groups, 2, GROUP * size * BLOCK, inputs) for x in spectra])
-        power.append(part_power)
-    spectra, part_power, _ = front(
-        volts, halo, 0, end, groups, owners, keep_ahead, spot, window, table, False
-    )
-    power.append(part_power)
-    spectra = [x.reshape(1, 2, GROUP * end * BLOCK, inputs) for x in spectra]
-    for j in range(groups):
-        parts.append([spectra[d * groups + j] for d in range(owners)])
-
-    local = jnp.sum(sum(power), axis=0)
-    total = lax.psum(local, ("band", "tm"))
-    scale = lax.rsqrt(total / (frames_all * jnp.sum(keep_all)) + 1e-06)
-    scales = lax.all_gather(scale, "station", axis=0, tiled=True)
-    kept = lax.dynamic_slice_in_dim(keep_mine, me * fine, fine, 0)
-    counts = kept.reshape(groups, GROUP).sum(-1)
-    denom = frames_all * jnp.maximum(counts, 1.0)
-    per_half = scales.shape[0] // 2
-    row_scales = lax.dynamic_slice_in_dim(scales, half * per_half, per_half, 0)
-
-    column_scales = scales[None, :]
-    row_scales = [(row_scales / denom[j])[:, None] for j in range(groups)]
-
-    place = jnp.stack([me, 1 - half, half]).astype(jnp.int32)
-    shared = len(PARTS)
-    arrived, flat, out = [], [], None
+    parts, arrived, flat, out = [], [], [], None
 
     def send(n, waits):
         got = [parts[n][0]]
@@ -401,6 +367,43 @@
             flat.append(got[-1])
         arrived.append(got)
 
+    power, halo, end = [], None, blocks
+    for size in PARTS:
+        end -= size
+        spectra, part_power, tail = front(
+            volts, None, end, size, 1, owners, keep_ahead, spot, window, table, halo is None
+        )
+        if tail is not None:
+            halo = tail
+        parts.append([x.reshape(groups, 2, GROUP * size * BLOCK, inputs) for x in spectra])
+        power.append(part_power)
+        if len(parts) == 1:
+            send(0, {})
+    with jax.named_scope("halo"):
+        halo = passed_on(halo)
+    spectra, part_power, _ = front(
+        volts, halo, 0, end, groups, owners, keep_ahead, spot, window, table, False
+    )
+    power.append(part_power)
+    spectra = [x.reshape(1, 2, GROUP * end * BLOCK, inputs) for x in spectra]
+    for j in range(groups):
+        parts.append([spectra[d * groups + j] for d in range(owners)])
+
+    local = jnp.sum(sum(power), axis=0)
+    total = lax.psum(local, ("band", "tm"))
+    scale = lax.rsqrt(total / (frames_all * jnp.sum(keep_all)) + 1e-06)
+    scales = lax.all_gather(scale, "station", axis=0, tiled=True)
+    kept = lax.dynamic_slice_in_dim(keep_mine, me * fine, fine, 0)
+    counts = kept.reshape(groups, GROUP).sum(-1)
+    denom = frames_all * jnp.maximum(counts, 1.0)
+    per_half = scales.shape[0] // 2
+    row_scales = lax.dynamic_slice_in_dim(scales, half * per_half, per_half, 0)
+
+    column_scales = scales[None, :]
+    row_scales = [(row_scales / denom[j])[:, None] for j in range(groups)]
+
+    place = jnp.stack([me, 1 - half, half]).astype(jnp.int32)
+    shared = len(PARTS)
     def to_other(j, theirs):
         with jax.named_scope(f"rows{j}"):
             return lax.ppermute(theirs, "tm", [(0, 1), (1, 0)])
@@ -412,9 +415,8 @@
 
     both = [jnp.bfloat16, jnp.float32]
     last_spectra = parts[shared][0]
-    for n in range(shared):
-        waits = {} if n == 0 else {d: [last_spectra, arrived[0][2]] for d in range(1, owners) if d != 2}
-        send(n, waits)
+    for n in range(1, shared):
+        send(n, {d: [last_spectra, arrived[0][2]] for d in range(1, owners) if d != 2})
     send(shared, {owners - 1: [column_scales]})
     waiting = None
     for j in range(groups - 1):
@@ -431,10 +433,9 @@
         theirs = to_other(j, theirs)
         waiting = (row_scales[j], column_scales, mine, theirs)
     j = groups - 1
-    (theirs,) = multiply(j, place[:2], both[:1], partial[:1], [out], begin=shared)
+    theirs, mine = multiply(j, place, both, partial, [out], begin=shared)
     out = equalize(*waiting, out, groups - 2, groups, [theirs])
     theirs = to_other(j, theirs)
-    (mine,) = multiply(j, place[::2], both[1:], partial[1:], begin=shared)
     out = equalize(row_scales[j], column_scales, mine, theirs, out, j, groups, [])
     return out[None]
 

time: 477 us -> 467 us (0.979)
  Pallas kernels: 189 us -> 176 us
    pallas_call x4, Pallas kernels: 29.3 us -> 21.4 us  [equalize(): pl.pallas_call(equalize_kernel, grid=(rows // block,), out_shape=jax.Shap...]
    pallas_call x6 -> x5, Pallas kernels: 77.6 us -> 72.7 us  [correlate(): pl.pallas_call(functools.partial(correlate_kernel, owners, picks, outs, l...]
    unnamed x45 -> x41, local copies, waits for them, and re-layouts: 10.8 us -> 10.2 us
  transfers between devices with their start and end apart: 23 -> 23, of which waited for: 11 -> 12; matrix products, arithmetic and copies ran while one was open for 3% -> 2% of each run, Pallas kernels for 35% -> 34%
where the time goes in v5:
time: 467 us; the launch traced here: 465 us
  Pallas kernels  176 us (38%)
  waiting for transfers between devices  133 us (28%)
  blocking collectives  112 us (24%)
  starting transfers between devices  20.8 us (4%)
  local copies, waits for them, and re-layouts  15.7 us (3%)
  other arithmetic  6.21 us (1%)
    ppermute x18, waiting for transfers between devices, shift(): lax.ppermute(value, 'station', [(s, (s + d) % count) for s in range(count)])  133 us
    all_gather x1, blocking collectives, pipelined(): scales = lax.all_gather(scale, 'station', axis=0, tiled=True)  98.3 us
    pallas_call x3, Pallas kernels, front(): pl.pallas_call(functools.partial(front_kernel, splits, owners, turned, ta...  82.2 us
    pallas_call x5, Pallas kernels, correlate(): pl.pallas_call(functools.partial(correlate_kernel, owners, picks, outs, l...  72.7 us
    pallas_call x4, Pallas kernels, equalize(): pl.pallas_call(equalize_kernel, grid=(rows // block,), out_shape=jax.Shap...  21.4 us
    ppermute x18, starting transfers between devices, shift(): lax.ppermute(value, 'station', [(s, (s + d) % count) for s in range(count)])  15.2 us
    psum x1, blocking collectives, pipelined(): total = lax.psum(local, ('band', 'tm'))  14.2 us
    unnamed x41, local copies, waits for them, and re-layouts  10.2 us
  transfers between devices with their start and end apart: 23, of which 12 were waited for; matrix products, arithmetic and copies ran while one was open for 2% of the time, Pallas kernels for 34%

profile of v5, /device:TPU:11, one launch (start us, length us, event | category | flops | bytes accessed | tf_op | source)
XLA Modules:
  0.0 465.4 jit_solution(16666905904235528332)
XLA Ops:
  2.2 13.9 %front.3 = (bf16[4,2,9,16,256]{4,3,2,1,0:T(8,128)(2,1)}, bf16[4,2,9,16,256]{4,3,2,1,0:T(8,128)(2,1)}, bf16[4,2,9,16,256]{4,3,2,1,0:T(8,128)(2,1)}, bf16[4,2,9,16...) custom-call(s32[1]{0:T(128)} %bitcast.me_ref, f32[144]{0:T(256)} %dynamic_slice.14.keep_ref, ...), custom_call_target="tpu_custom_call" | custom-call | flops 1024 | bytes 1024 | tf_op jit(solution)/shard_map/front/pallas_call | solution.py:159
  16.1 1.3 collective-permute-start
  17.3 1.3 collective-permute-start.1
  18.7 1.1 collective-permute-start.2
  19.8 1.4 collective-permute-start.3
  21.2 30.1 %front.4 = (bf16[4,2,9,48,256]{4,3,2,1,0:T(8,128)(2,1)}, bf16[4,2,9,48,256]{4,3,2,1,0:T(8,128)(2,1)}, bf16[4,2,9,48,256]{4,3,2,1,0:T(8,128)(2,1)}, bf16[4,2,9,48,256]{4,3,2,1,0:T(8,128)(2,1)}, f32[16,256]{1,0:T(8,128)}) custom-call(s32[1]{0:T(128)} %bitcast.me_ref, f32[144]{0:T(256)} %dynamic_slice.14.keep_ref, bf16[2,1,256,18432]{3,2,1,0:T(8,128)(2,1)} %volts_ref.5, ...), custom_call_target="tpu_custom_call" | custom-call | flops 1024 | bytes 1024 | tf_op jit(solution)/shard_map/front/pallas_call | solution.py:159
  51.4 38.1 %front.5 = (bf16[1,2,9,64,256]{4,3,2,1,0:T(8,128)(2,1)}, bf16[1,2,9,64,256]{4,3,2,1,0:T(8,128)(2,1)}, bf16[1,2,9,64,256]{4,3,2,1,0:T(8,128)(2,1)}, bf16[1,2,9,64...) custom-call(s32[1]{0:T(128)} %bitcast.me_ref, ...), custom_call_target="tpu_custom_call" | custom-call | flops 1024 | bytes 1024 | tf_op jit(solution)/shard_map/front/pallas_call | solution.py:159
  89.6 15.6 %collective-permute-done.2.refs_2_.rest_2_ = bf16[4,2,144,256]{3,2,1,0:T(8,128)(2,1)S(1)} collective-permute-done((bf16[4,2,144,256]{3,2,1,0:T(8,128)(2,1)}, bf16[4,2,144,256]{3,2,1,0:T(8,128)(2,1)S(1)}, u32[]{:S(2)}, u32[]{:S(2)}) %collective-permute-start.2) | collective-permute-done | bytes 589856 | tf_op jit(solution)/shard_map/part0_shift2/ppermute | solution.py:319
  106.0 3.6 collective-permute-done.3.refs_3_.rest_3_
  109.7 1.3 convert_reduce_fusion
  111.5 1.3 add_reduce_fusion
  112.9 14.2 %psum.7 = f32[256]{0:T(256)S(1)} all-reduce(f32[256]{0:T(256)} %add_reduce_fusion), channel_id=1, replica_groups=mesh['station'=4,'band'=4,'tm'=2] {'band','tm'}, use_global_device_ids=true, to_apply=%region_2.3 | all-reduce | flops 256 | bytes 2048 | tf_op jit(solution)/shard_map/psum | solution.py:393
  127.1 19.3 %collective-permute-done.5.rest_6_.refs_1_ = bf16[4,2,432,256]{3,2,1,0:T(8,128)(2,1)S(1)} collective-permute-done((bf16[4,2,432,256]{3,2,1,0:T(8,128)(2,1)}, bf16[4,2,432,256]{3,2,1,0:T(8,128)(2,1)S(1)}, u32[]{:S(2)}, u32[]{:S(2)}) %collective-permute-start.5) | collective-permute-done | bytes 1769504 | tf_op jit(solution)/shard_map/part1_shift2/ppermute | solution.py:319
  146.4 1.2 copy-done
  147.6 3.5 collective-permute-start.11
  151.1 98.3 %all-gather = f32[4,1,256]{2,1,0:T(1,128)} all-gather(f32[1,1,256]{2,1,0:T(1,128)S(1)} %bitcast.78), channel_id=1, replica_groups=mesh['station'=4,'band'=4,'tm'=2] {'station'}, dimensions={0}, use_global_device_ids=true | all-gather | bytes 5120 | tf_op jit(solution)/shard_map/all_gather | solution.py:395
  249.3 1.3 copy-done.1
  250.6 1.6 collective-permute-start.7
  252.9 0.8 copy-done.11
  253.8 1.2 collective-permute-start.12
  255.0 11.4 %correlate.5 = (f32[2,512,1024]{2,1,0:T(8,128)}, f32[2,512,1024]{2,1,0:T(8,128)}) custom-call(s32[3]{0:T(128)} %pad_add_fusion.place_ref, bf16[4,2,144,256]{3,2,1,0:T(8,128)(2,1)} %bitcast.44, bf16[4,2,144,256]{3,2,1,0:T(8,128)(2,1)} %copy-done.3, bf16[4,2,144,256]{3,2,1,0:T(8,128)(2,1)} %copy-done.2, ...), custom_call_target="tpu_custom_call" | custom-call | flops 1024 | bytes 1024 | tf_op jit(solution)/shard_map/correlate/pallas_call | solution.py:260
  267.5 13.5 %collective-permute-done.15.refs_3_.rest_11_ = bf16[1,2,576,256]{3,2,1,0:T(8,128)(2,1)S(1)} collective-permute-done((bf16[1,2,576,256]{3,2,1,0:T(8,128)(2,1)}, bf16[1,2,576,256]{3,2,1,0:T(8,128)(2,1)S(1)}, u32[]{:S(2)}, u32[]{:S(2)}) %collective-permute-start.15) | collective-permute-done | bytes 589856 | tf_op jit(solution)/shard_map/part2_shift3/ppermute | solution.py:319
  281.9 16.0 %correlate.7 = (bf16[2,512,1024]{2,1,0:T(8,128)(2,1)}, f32[2,512,1024]{2,1,0:T(8,128)}) custom-call(s32[3]{0:T(128)} %pad_add_fusion.place_ref, bf16[4,2,144,256]{3,2,1,0:T(8,128)(2,1)} %bitcast.45, bf16[4,2,144,256]{3,2,1,0:T(8,128)(2,1)} %copy-done.3, bf16[4,2,144,256]{3,2,1,0:T(8,128)(2,1)} %copy-done.2, ...), custom_call_target="tpu_custom_call" | custom-call | flops 1024 | bytes 1024 | tf_op jit(solution)/shard_map/correlate/pallas_call | solution.py:260
  297.9 7.6 %collective-permute-done.12.refs_1_.rest_10_.refs_2_ = bf16[1,2,576,256]{3,2,1,0:T(8,128)(2,1)S(1)} collective-permute-done((bf16[1,2,576,256]{3,2,1,0:T(8,128)(2,1)}, bf16[1,2,576,256]{3,2,1,0:T(8,128)(2,1)S(1)}, u32[]{:S(2)}, u32[]{:S(2)}) %collective-permute-start.12) | collective-permute-done | bytes 589856 | tf_op jit(solution)/shard_map/part3_shift2/ppermute | solution.py:319
  305.5 21.2 %collective-permute-done.8.refs_1_.rest_9_ = bf16[1,2,576,256]{3,2,1,0:T(8,128)(2,1)S(1)} collective-permute-done((bf16[1,2,576,256]{3,2,1,0:T(8,128)(2,1)}, bf16[1,2,576,256]{3,2,1,0:T(8,128)(2,1)S(1)}, u32[]{:S(2)}, u32[]{:S(2)}) %collective-permute-start.8) | collective-permute-done | bytes 589856 | tf_op jit(solution)/shard_map/part3_shift1/ppermute | solution.py:319
  328.1 2.3 collective-permute-start.20
  330.4 2.1 collective-permute-start.9
  332.5 1.2 collective-permute-start.17
  335.3 2.6 broadcast_divide_fusion
  338.0 0.9 copy.33.rows_ref
  338.8 16.1 %correlate.6 = (bf16[2,512,1024]{2,1,0:T(8,128)(2,1)}, f32[2,512,1024]{2,1,0:T(8,128)}) custom-call(s32[3]{0:T(128)} %pad_add_fusion.place_ref, bf16[4,2,144,256]{3,2,1,0:T(8,128)(2,1)} %bitcast.46, bf16[4,2,144,256]{3,2,1,0:T(8,128)(2,1)} %copy-done.3, bf16[4,2,144,256]{3,2,1,0:T(8,128)(2,1)} %copy-done.2, ...), custom_call_target="tpu_custom_call" | custom-call | flops 1024 | bytes 1024 | tf_op jit(solution)/shard_map/correlate/pallas_call | solution.py:260
  354.9 5.4 %equalize.4.rest_0_ = f32[4,2,512,1024]{3,2,1,0:T(8,128)} custom-call(f32[512,1]{1,0:T(8,128)} %copy.33.rows_ref, f32[1,1024]{1,0:T(1,128)} %bitcast.69, f32[2,512,1024]{2,1,0:T(8,128)} %get-tuple-element.74.mine_ref, bf16[2,512,1024]{2,1,0:T(8,128)(2,1)} %collective-permute-done.20.theirs_ref, bf16[2,512,1024]{2,1,0:T(8,128)(2,1)} %get-tuple-element.73.refs_0_.rest_0_), custom_call_target="tpu_custom_call" | custom-call | flops 1024 | bytes 1024 | tf_op jit(solution)/shard_map/equalize/pallas_call | solution.py:304
  360.3 21.3 %collective-permute-done.9.refs_1_.rest_9_ = bf16[1,2,576,256]{3,2,1,0:T(8,128)(2,1)S(1)} collective-permute-done((bf16[1,2,576,256]{3,2,1,0:T(8,128)(2,1)}, bf16[1,2,576,256]{3,2,1,0:T(8,128)(2,1)S(1)}, u32[]{:S(2)}, u32[]{:S(2)}) %collective-permute-start.9) | collective-permute-done | bytes 589856 | tf_op jit(solution)/shard_map/part4_shift1/ppermute | solution.py:319
  381.6 2.8 collective-permute-done.17.refs_1_.refs_3_.rest_11_
  384.4 0.8 copy-done.7
  386.0 1.3 collective-permute-start.18
  387.3 0.9 copy.34.rows_ref
  388.1 16.1 %correlate.8 = (bf16[2,512,1024]{2,1,0:T(8,128)(2,1)}, f32[2,512,1024]{2,1,0:T(8,128)}) custom-call(s32[3]{0:T(128)} %pad_add_fusion.place_ref, bf16[4,2,144,256]{3,2,1,0:T(8,128)(2,1)} %bitcast.47, bf16[4,2,144,256]{3,2,1,0:T(8,128)(2,1)} %copy-done.3, bf16[4,2,144,256]{3,2,1,0:T(8,128)(2,1)} %copy-done.2, ...), custom_call_target="tpu_custom_call" | custom-call | flops 1024 | bytes 1024 | tf_op jit(solution)/shard_map/correlate/pallas_call | solution.py:260
  404.9 5.3 %equalize.5.rest_6_.rest_0_ = f32[4,2,512,1024]{3,2,1,0:T(8,128)} custom-call(f32[512,1]{1,0:T(8,128)} %copy.34.rows_ref, f32[1,1024]{1,0:T(1,128)} %bitcast.70, f32[2,512,1024]{2,1,0:T(8,128)} %get-tuple-element.72.mine_ref, bf16[2,512,1024]{2,1,0:T(8,128)(2,1)} %collective-permute-done.19.theirs_ref, ...), custom_call_target="tpu_custom_call", output_to_operand_aliasing={{}: (4, {})} | custom-call | flops 1024 | bytes 1024 | tf_op jit(solution)/shard_map/equalize/pallas_call | solution.py:304
  410.3 1.5 collective-permute-done.14.rest_4_
  411.8 25.3 %collective-permute-done.10.rest_3_ = bf16[1,2,576,256]{3,2,1,0:T(8,128)(2,1)S(1)} collective-permute-done((bf16[1,2,576,256]{3,2,1,0:T(8,128)(2,1)}, bf16[1,2,576,256]{3,2,1,0:T(8,128)(2,1)S(1)}, u32[]{:S(2)}, u32[]{:S(2)}) %collective-permute-start.10) | collective-permute-done | bytes 589856 | tf_op jit(solution)/shard_map/part5_shift1/ppermute | solution.py:319
  437.0 0.8 collective-permute-done.18.rest_5_
  437.9 13.0 %correlate.9 = (bf16[2,512,1024]{2,1,0:T(8,128)(2,1)}, f32[2,512,1024]{2,1,0:T(8,128)}) custom-call(s32[3]{0:T(128)} %pad_add_fusion.place_ref, f32[2,512,1024]{2,1,0:T(8,128)} %get-tuple-element.56.refs_1_.rest_0_, f32[2,512,1024]{2,1,0:T(8,128)} %get-tuple-element.57.refs_2_.rest_1_, bf16[1,2,576,256]{3,2,1,0:T(8,128)(2,1)} %bitcast.53, ...), custom_call_target="tpu_custom_call" | custom-call | flops 1024 | bytes 1024 | tf_op jit(solution)/shard_map/correlate/pallas_call | solution.py:260
  451.6 0.9 copy.36.rows_ref
  452.4 0.9 copy.35.rows_ref
  453.3 1.3 copy-done.13
  454.7 5.3 %equalize.6.rest_0_ = f32[4,2,512,1024]{3,2,1,0:T(8,128)} custom-call(f32[512,1]{1,0:T(8,128)} %copy.35.rows_ref, f32[1,1024]{1,0:T(1,128)} %bitcast.71, f32[2,512,1024]{2,1,0:T(8,128)} %get-tuple-element.80.mine_ref, bf16[2,512,1024]{2,1,0:T(8,128)(2,1)} %copy-done.13, f32[4,2,512,1024]{3,2,1,0:T(8,128)} %equalize.5.rest_6_.rest_0_, ...), custom_call_target="tpu_custom_call", output_to_operand_aliasing={{}: (4, {})} | custom-call | flops 1024 | bytes 1024 | tf_op jit(solution)/shard_map/equalize/pallas_call | solution.py:304
  460.0 5.4 %equalize.7 = f32[4,2,512,1024]{3,2,1,0:T(8,128)} custom-call(f32[512,1]{1,0:T(8,128)} %copy.36.rows_ref, f32[1,1024]{1,0:T(1,128)} %bitcast.72, f32[2,512,1024]{2,1,0:T(8,128)} %get-tuple-element.78.mine_ref, bf16[2,512,1024]{2,1,0:T(8,128)(2,1)} %collective-permute-done.21.theirs_ref, ...), custom_call_target="tpu_custom_call", output_to_operand_aliasing={{}: (4, {})} | custom-call | flops 1024 | bytes 1024 | tf_op jit(solution)/shard_map/equalize/pallas_call | solution.py:304
  (88 shorter events, 10.8 us)
Async XLA Ops:
  0.9 0.6 copy-start.19
  1.5 14.6 %copy-start.18 = (f32[4,144]{1,0:T(4,128)}, f32[4,144]{1,0:T(4,128)S(1)}, u32[]{:S(2)}) copy-start(f32[4,144]{1,0:T(4,128)S(1)} %convert_element_type.3) | copy-start | bytes 6916
  16.1 35.3 %collective-permute-start = (bf16[2,1584,256]{2,1,0:T(8,128)(2,1)}, bf16[2,1584,256]{2,1,0:T(8,128)(2,1)}, u32[]{:S(2)}, u32[]{:S(2)}) collective-permute-start(bf16[2,1584,256]{2,1,0:T(8,128)(2,1)} %get-tuple-element.45), channel_id=1, source_target_pairs={{0,1},{2,3},{4,5},{6,7},{8,9},{10,11},{12,13},{14,15},{16,17},{18,... | collective-permute-start | bytes 4866056 | tf_op jit(solution)/shard_map/halo/ppermute | solution.py:324
  17.3 72.2 %collective-permute-start.1 = (bf16[4,2,144,256]{3,2,1,0:T(8,128)(2,1)}, bf16[4,2,144,256]{3,2,1,0:T(8,128)(2,1)S(1)}, u32[]{:S(2)}, u32[]{:S(2)}) collective-permute-start(bf16[4,2,144,256]{3,2,1,0:T(8,128)(2,1)} %bitcast.83), channel_id=1, source_target_pairs={{0,8},{8,16},{16,24},{24,0},{1,9},{9,17},{17,25},{25,1},{2,10},{10... | collective-permute-start | bytes 1769480 | tf_op jit(solution)/shard_map/part0_shift1/ppermute | solution.py:319
  18.7 86.5 %collective-permute-start.2 = (bf16[4,2,144,256]{3,2,1,0:T(8,128)(2,1)}, bf16[4,2,144,256]{3,2,1,0:T(8,128)(2,1)S(1)}, u32[]{:S(2)}, u32[]{:S(2)}) collective-permute-start(bf16[4,2,144,256]{3,2,1,0:T(8,128)(2,1)} %bitcast.82), channel_id=1, source_target_pairs={{0,16},{8,24},{16,0},{24,8},{1,17},{9,25},{17,1},{25,9},{2,18},{10... | collective-permute-start | bytes 1769480 | tf_op jit(solution)/shard_map/part0_shift2/ppermute | solution.py:319
  19.8 89.9 %collective-permute-start.3 = (bf16[4,2,144,256]{3,2,1,0:T(8,128)(2,1)}, bf16[4,2,144,256]{3,2,1,0:T(8,128)(2,1)}, u32[]{:S(2)}, u32[]{:S(2)}) collective-permute-start(bf16[4,2,144,256]{3,2,1,0:T(8,128)(2,1)} %bitcast.81), channel_id=1, source_target_pairs={{0,24},{8,0},{16,8},{24,16},{1,25},{9,1},{17,9},{25,17},{2,26},{10... | collective-permute-start | bytes 1769480 | tf_op jit(solution)/shard_map/part0_shift3/ppermute | solution.py:319
  51.3 95.1 %collective-permute-start.5 = (bf16[4,2,432,256]{3,2,1,0:T(8,128)(2,1)}, bf16[4,2,432,256]{3,2,1,0:T(8,128)(2,1)S(1)}, u32[]{:S(2)}, u32[]{:S(2)}) collective-permute-start(bf16[4,2,432,256]{3,2,1,0:T(8,128)(2,1)} %bitcast.80), channel_id=1, source_target_pairs={{0,16},{8,24},{16,0},{24,8},{1,17},{9,25},{17,1},{25,9},{2,18},{10... | collective-permute-start | bytes 5308424 | tf_op jit(solution)/shard_map/part1_shift2/ppermute | solution.py:319
  89.5 15.7 %copy-start.3 = (bf16[4,2,144,256]{3,2,1,0:T(8,128)(2,1)}, bf16[4,2,144,256]{3,2,1,0:T(8,128)(2,1)S(1)}, u32[]{:S(2)}) copy-start(bf16[4,2,144,256]{3,2,1,0:T(8,128)(2,1)S(1)} %collective-permute-done.1.refs_3_.rest_1_) | copy-start | bytes 1769476
  105.2 0.8 copy-start.2
  106.0 143.3 %collective-permute-start.4 = (bf16[4,2,432,256]{3,2,1,0:T(8,128)(2,1)}, bf16[4,2,432,256]{3,2,1,0:T(8,128)(2,1)S(1)}, u32[]{:S(2)}, u32[]{:S(2)}) collective-permute-start(bf16[4,2,432,256]{3,2,1,0:T(8,128)(2,1)} %after.16), channel_id=1, source_target_pairs={{0,8},{8,16},{16,24},{24,0},{1,9},{9,17},{17,25},{25,1},{2,10},{10... | collective-permute-start | bytes 5308424 | tf_op jit(solution)/shard_map/part1_shift1/ppermute | solution.py:319
  109.7 1.8 copy-start.17
  109.7 142.6 %collective-permute-start.6 = (bf16[4,2,432,256]{3,2,1,0:T(8,128)(2,1)}, bf16[4,2,432,256]{3,2,1,0:T(8,128)(2,1)}, u32[]{:S(2)}, u32[]{:S(2)}) collective-permute-start(bf16[4,2,432,256]{3,2,1,0:T(8,128)(2,1)} %after.17), channel_id=1, source_target_pairs={{0,24},{8,0},{16,8},{24,16},{1,25},{9,1},{17,9},{25,17},{2,26},{10... | collective-permute-start | bytes 5308424 | tf_op jit(solution)/shard_map/part1_shift3/ppermute | solution.py:319
  146.4 1.2 copy-start
  147.6 105.4 %collective-permute-start.11 = (bf16[1,2,576,256]{3,2,1,0:T(8,128)(2,1)}, bf16[1,2,576,256]{3,2,1,0:T(8,128)(2,1)S(1)}, u32[]{:S(2)}, u32[]{:S(2)}) collective-permute-start(bf16[1,2,576,256]{3,2,1,0:T(8,128)(2,1)} %after.22), channel_id=1, source_target_pairs={{0,16},{8,24},{16,0},{24,8},{1,17},{9,25},{17,1},{25,9},{2,18},{10... | collective-permute-start | bytes 1769480 | tf_op jit(solution)/shard_map/part2_shift2/ppermute | solution.py:319
  249.3 1.3 copy-start.1
  250.6 15.8 %collective-permute-start.7 = (bf16[1,2,576,256]{3,2,1,0:T(8,128)(2,1)}, bf16[1,2,576,256]{3,2,1,0:T(8,128)(2,1)S(1)}, u32[]{:S(2)}, u32[]{:S(2)}) collective-permute-start(bf16[1,2,576,256]{3,2,1,0:T(8,128)(2,1)} %after.18), channel_id=1, source_target_pairs={{0,8},{8,16},{16,24},{24,0},{1,9},{9,17},{17,25},{25,1},{2,10},{10... | collective-permute-start | bytes 1769480 | tf_op jit(solution)/shard_map/part2_shift1/ppermute | solution.py:319
  252.3 28.8 %collective-permute-start.15 = (bf16[1,2,576,256]{3,2,1,0:T(8,128)(2,1)}, bf16[1,2,576,256]{3,2,1,0:T(8,128)(2,1)S(1)}, u32[]{:S(2)}, u32[]{:S(2)}) collective-permute-start(bf16[1,2,576,256]{3,2,1,0:T(8,128)(2,1)} %after.26), channel_id=1, source_target_pairs={{0,24},{8,0},{16,8},{24,16},{1,25},{9,1},{17,9},{25,17},{2,26},{10... | collective-permute-start | bytes 1769480 | tf_op jit(solution)/shard_map/part2_shift3/ppermute | solution.py:319
  252.9 0.8 copy-start.11
  253.8 51.7 %collective-permute-start.12 = (bf16[1,2,576,256]{3,2,1,0:T(8,128)(2,1)}, bf16[1,2,576,256]{3,2,1,0:T(8,128)(2,1)S(1)}, u32[]{:S(2)}, u32[]{:S(2)}) collective-permute-start(bf16[1,2,576,256]{3,2,1,0:T(8,128)(2,1)} %after.23), channel_id=1, source_target_pairs={{0,16},{8,24},{16,0},{24,8},{1,17},{9,25},{17,1},{25,9},{2,18},{10... | collective-permute-start | bytes 1769480 | tf_op jit(solution)/shard_map/part3_shift2/ppermute | solution.py:319
  266.5 0.8 copy-start.12
  267.3 59.3 %collective-permute-start.8 = (bf16[1,2,576,256]{3,2,1,0:T(8,128)(2,1)}, bf16[1,2,576,256]{3,2,1,0:T(8,128)(2,1)S(1)}, u32[]{:S(2)}, u32[]{:S(2)}) collective-permute-start(bf16[1,2,576,256]{3,2,1,0:T(8,128)(2,1)} %after.19), channel_id=1, source_target_pairs={{0,8},{8,16},{16,24},{24,0},{1,9},{9,17},{17,25},{25,1},{2,10},{10... | collective-permute-start | bytes 1769480 | tf_op jit(solution)/shard_map/part3_shift1/ppermute | solution.py:319
  281.1 0.8 copy-start.10
  281.9 45.3 %collective-permute-start.16 = (bf16[1,2,576,256]{3,2,1,0:T(8,128)(2,1)}, bf16[1,2,576,256]{3,2,1,0:T(8,128)(2,1)S(1)}, u32[]{:S(2)}, u32[]{:S(2)}) collective-permute-start(bf16[1,2,576,256]{3,2,1,0:T(8,128)(2,1)} %after.27), channel_id=1, source_target_pairs={{0,24},{8,0},{16,8},{24,16},{1,25},{9,1},{17,9},{25,17},{2,26},{10... | collective-permute-start | bytes 1769480 | tf_op jit(solution)/shard_map/part3_shift3/ppermute | solution.py:319
  305.5 21.7 %copy-start.5 = (bf16[1,2,576,256]{3,2,1,0:T(8,128)(2,1)}, bf16[1,2,576,256]{3,2,1,0:T(8,128)(2,1)S(1)}, u32[]{:S(2)}) copy-start(bf16[1,2,576,256]{3,2,1,0:T(8,128)(2,1)S(1)} %collective-permute-done.12.refs_1_.rest_10_.refs_2_) | copy-start | bytes 1769476
  326.6 0.8 copy-start.8
  327.2 0.8 copy-start.9
  328.1 26.9 %collective-permute-start.20 = (bf16[2,512,1024]{2,1,0:T(8,128)(2,1)}, bf16[2,512,1024]{2,1,0:T(8,128)(2,1)}, u32[]{:S(2)}, u32[]{:S(2)}) collective-permute-start(bf16[2,512,1024]{2,1,0:T(8,128)(2,1)} %after.31), channel_id=1, source_target_pairs={{0,1},{1,0},{2,3},{3,2},{4,5},{5,4},{6,7},{7,6},{8,9},{9,8},{10,11... | collective-permute-start | bytes 6291464 | tf_op jit(solution)/shard_map/rows0/ppermute | solution.py:409
  330.4 4.9 %copy-start.16 = (f32[4,1,256]{2,1,0:T(1,128)S(1)}, f32[4,1,256]{2,1,0:T(1,128)}, u32[]{:S(2)}) copy-start(f32[4,1,256]{2,1,0:T(1,128)} %all-gather) | copy-start | bytes 12292
  330.4 29.9 %collective-permute-start.13 = (bf16[1,2,576,256]{3,2,1,0:T(8,128)(2,1)}, bf16[1,2,576,256]{3,2,1,0:T(8,128)(2,1)S(1)}, u32[]{:S(2)}, u32[]{:S(2)}) collective-permute-start(bf16[1,2,576,256]{3,2,1,0:T(8,128)(2,1)} %after.24), channel_id=1, source_target_pairs={{0,16},{8,24},{16,0},{24,8},{1,17},{9,25},{17,1},{25,9},{2,18},{10... | collective-permute-start | bytes 1769480 | tf_op jit(solution)/shard_map/part4_shift2/ppermute | solution.py:319
  330.4 51.2 %collective-permute-start.9 = (bf16[1,2,576,256]{3,2,1,0:T(8,128)(2,1)}, bf16[1,2,576,256]{3,2,1,0:T(8,128)(2,1)S(1)}, u32[]{:S(2)}, u32[]{:S(2)}) collective-permute-start(bf16[1,2,576,256]{3,2,1,0:T(8,128)(2,1)} %after.20), channel_id=1, source_target_pairs={{0,8},{8,16},{16,24},{24,0},{1,9},{9,17},{17,25},{25,1},{2,10},{10... | collective-permute-start | bytes 1769480 | tf_op jit(solution)/shard_map/part4_shift1/ppermute | solution.py:319
  332.5 51.8 %collective-permute-start.17 = (bf16[1,2,576,256]{3,2,1,0:T(8,128)(2,1)}, bf16[1,2,576,256]{3,2,1,0:T(8,128)(2,1)S(1)}, u32[]{:S(2)}, u32[]{:S(2)}) collective-permute-start(bf16[1,2,576,256]{3,2,1,0:T(8,128)(2,1)} %after.28), channel_id=1, source_target_pairs={{0,24},{8,0},{16,8},{24,16},{1,25},{9,1},{17,9},{25,17},{2,26},{10... | collective-permute-start | bytes 1769480 | tf_op jit(solution)/shard_map/part4_shift3/ppermute | solution.py:319
  360.3 24.1 %copy-start.4 = (bf16[1,2,576,256]{3,2,1,0:T(8,128)(2,1)}, bf16[1,2,576,256]{3,2,1,0:T(8,128)(2,1)S(1)}, u32[]{:S(2)}) copy-start(bf16[1,2,576,256]{3,2,1,0:T(8,128)(2,1)S(1)} %collective-permute-done.13.refs_1_.refs_2_.rest_10_) | copy-start | bytes 1769476
  381.6 2.8 copy-start.6
  384.4 0.8 copy-start.7
  385.2 19.7 %collective-permute-start.19 = (bf16[2,512,1024]{2,1,0:T(8,128)(2,1)}, bf16[2,512,1024]{2,1,0:T(8,128)(2,1)}, u32[]{:S(2)}, u32[]{:S(2)}) collective-permute-start(bf16[2,512,1024]{2,1,0:T(8,128)(2,1)} %after.30), channel_id=1, source_target_pairs={{0,1},{1,0},{2,3},{3,2},{4,5},{5,4},{6,7},{7,6},{8,9},{9,8},{10,11... | collective-permute-start | bytes 6291464 | tf_op jit(solution)/shard_map/rows1/ppermute | solution.py:409
  385.8 26.0 %collective-permute-start.14 = (bf16[1,2,576,256]{3,2,1,0:T(8,128)(2,1)}, bf16[1,2,576,256]{3,2,1,0:T(8,128)(2,1)S(1)}, u32[]{:S(2)}, u32[]{:S(2)}) collective-permute-start(bf16[1,2,576,256]{3,2,1,0:T(8,128)(2,1)} %after.25), channel_id=1, source_target_pairs={{0,16},{8,24},{16,0},{24,8},{1,17},{9,25},{17,1},{25,9},{2,18},{10... | collective-permute-start | bytes 1769480 | tf_op jit(solution)/shard_map/part5_shift2/ppermute | solution.py:319
  385.8 51.2 %collective-permute-start.10 = (bf16[1,2,576,256]{3,2,1,0:T(8,128)(2,1)}, bf16[1,2,576,256]{3,2,1,0:T(8,128)(2,1)S(1)}, u32[]{:S(2)}, u32[]{:S(2)}) collective-permute-start(bf16[1,2,576,256]{3,2,1,0:T(8,128)(2,1)} %after.21), channel_id=1, source_target_pairs={{0,8},{8,16},{16,24},{24,0},{1,9},{9,17},{17,25},{25,1},{2,10},{10... | collective-permute-start | bytes 1769480 | tf_op jit(solution)/shard_map/part5_shift1/ppermute | solution.py:319
  386.0 51.9 %collective-permute-start.18 = (bf16[1,2,576,256]{3,2,1,0:T(8,128)(2,1)}, bf16[1,2,576,256]{3,2,1,0:T(8,128)(2,1)}, u32[]{:S(2)}, u32[]{:S(2)}) collective-permute-start(bf16[1,2,576,256]{3,2,1,0:T(8,128)(2,1)} %after.29), channel_id=1, source_target_pairs={{0,24},{8,0},{16,8},{24,16},{1,25},{9,1},{17,9},{25,17},{2,26},{10... | collective-permute-start | bytes 1769480 | tf_op jit(solution)/shard_map/part5_shift3/ppermute | solution.py:319
  404.2 49.1 %collective-permute-start.22 = (bf16[2,512,1024]{2,1,0:T(8,128)(2,1)}, bf16[2,512,1024]{2,1,0:T(8,128)(2,1)S(1)}, u32[]{:S(2)}, u32[]{:S(2)}) collective-permute-start(bf16[2,512,1024]{2,1,0:T(8,128)(2,1)} %get-tuple-element.77.rest_1_), channel_id=1, source_target_pairs={{0,1},{1,0},{2,3},{3,2},{4,5},{5,4},{6,7},{7,6},{8,9},{9,8},{10,11... | collective-permute-start | bytes 6291464 | tf_op jit(solution)/shard_map/rows2/ppermute | solution.py:409
  411.8 26.1 %copy-start.14 = (bf16[1,2,576,256]{3,2,1,0:T(8,128)(2,1)}, bf16[1,2,576,256]{3,2,1,0:T(8,128)(2,1)S(1)}, u32[]{:S(2)}) copy-start(bf16[1,2,576,256]{3,2,1,0:T(8,128)(2,1)S(1)} %collective-permute-done.14.rest_4_) | copy-start | bytes 1769476
  437.0 0.8 copy-start.15
  450.9 9.1 %collective-permute-start.21 = (bf16[2,512,1024]{2,1,0:T(8,128)(2,1)}, bf16[2,512,1024]{2,1,0:T(8,128)(2,1)}, u32[]{:S(2)}, u32[]{:S(2)}) collective-permute-start(bf16[2,512,1024]{2,1,0:T(8,128)(2,1)} %get-tuple-element.79.rest_1_), channel_id=1, source_target_pairs={{0,1},{1,0},{2,3},{3,2},{4,5},{5,4},{6,7},{7,6},{8,9},{9,8},{10,11... | collective-permute-start | bytes 6291464 | tf_op jit(solution)/shard_map/rows3/ppermute | solution.py:409
  453.3 1.3 copy-start.13

commit v6 on v5

--- a/solution.py
+++ b/solution.py
@@ -17,6 +17,7 @@
 SPREAD = BLOCK + 1
 VMEM = 60 * 1024 * 1024
 COST = pl.CostEstimate(flops=1024, bytes_accessed=1024, transcendentals=0)
+DROPPED = 3
 IN_FLIGHT = 3
 
 
@@ -38,12 +39,17 @@
     return np.stack([real, imag], 1).astype(np.float32)
 
 
+def unrolled(count):
+    return max(n for n in range(1, 7) if count % n == 0)
+
+
 def front_kernel(
-    splits, owners, turned, tail, me_ref, keep_ref, hist_ref, volts_ref, window_ref, table_ref, *rest
+    sizes, owners, turned, tail, me_ref, keep_ref, hist_ref, volts_ref, window_ref, table_ref, pick_ref, *rest
 ):
+    splits, slots = len(sizes), sum(sizes)
     outs, power_ref = rest[: owners * splits], rest[owners * splits]
     tail_ref = rest[owners * splits + 1] if tail else None
-    ring, filt, spread = rest[-3:]
+    ring, filt, spread, picked = rest[-4:]
     step = pl.program_id(0)
     now = lax.rem(step, 2)
     before = 1 - now
@@ -69,6 +75,8 @@
         else:
             turn(hist_ref, 1, 3)
         power_ref[...] = jnp.zeros_like(power_ref)
+        chosen = jnp.dot(pick_ref[...], table_ref[0], preferred_element_type=jnp.float32)
+        picked[...] = chosen.astype(jnp.bfloat16)
 
     turn(volts_ref, now, 0)
     if tail:
@@ -97,54 +105,48 @@
     lax.fori_loop(0, SUBBAND_COUNT // 16, filter_rows, 0)
 
     def transform(t, _):
-        result = jnp.dot(table_ref[0], filt[t], preferred_element_type=jnp.float32)
+        result = jnp.dot(picked[...], filt[t], preferred_element_type=jnp.float32)
         for tile in range(tiles):
-            spread[tile, pl.ds(t, 2 * SUBBAND_COUNT, stride=SPREAD), :] = result[
+            spread[tile, pl.ds(t, 2 * owners * slots, stride=SPREAD), :] = result[
                 :, tile * 128 : (tile + 1) * 128
             ]
         return 0
 
     lax.fori_loop(0, BLOCK, transform, 0, unroll=4)
 
-    groups = SUBBAND_COUNT // owners // GROUP
     power = [jnp.zeros((BLOCK, 128), jnp.float32) for _ in range(tiles)]
     for d in range(owners):
-        for j in range(groups):
-            out = outs[d * splits + j] if splits > 1 else outs[d]
-            place = 0 if splits > 1 else j
-
-            def channel(f, power, d=d, j=j, out=out, place=place):
-                keep = keep_ref[(d * groups + j) * GROUP + f]
+        for q in range(splits):
+            out = outs[d * splits + q]
+            begin = d * slots + sum(sizes[:q])
+
+            def channel(f, power, out=out, begin=begin):
+                keep = keep_ref[begin + f]
                 power = list(power)
                 for part in range(2):
-                    row = ((d * groups + j) * 2 + part) * GROUP + f
+                    row = (begin + f) * 2 + part
                     for tile in range(tiles):
                         value = spread[tile, pl.ds(row * SPREAD, BLOCK), :] * keep
                         value = value.astype(jnp.bfloat16)
-                        out[place, part, f, :, tile * 128 : (tile + 1) * 128] = value
+                        out[part, f, :, tile * 128 : (tile + 1) * 128] = value
                         value = value.astype(jnp.float32)
                         power[tile] = power[tile] + value * value
                 return tuple(power)
 
-            power = lax.fori_loop(0, GROUP, channel, tuple(power), unroll=3)
+            power = lax.fori_loop(0, sizes[q], channel, tuple(power), unroll=unrolled(sizes[q]))
     for tile in range(tiles):
         power_ref[:, tile * 128 : (tile + 1) * 128] += power[tile]
 
 
-def front(volts, hist, first, steps, splits, owners, keep, me, window, table, tail):
+def front(volts, hist, first, steps, sizes, owners, keep, me, window, table, pick, tail):
     inputs = volts.shape[2]
     span = BLOCK * SUBBAND_COUNT
-    groups = SUBBAND_COUNT // owners // GROUP
-    each = groups // splits
     frames = steps * BLOCK
-    outs = [
-        jax.ShapeDtypeStruct((each, 2, GROUP, frames, inputs), jnp.bfloat16)
-        for _ in range(owners * splits)
-    ]
-    out_specs = [
-        pl.BlockSpec((each, 2, GROUP, BLOCK, inputs), lambda s, me: (0, 0, 0, s, 0))
-        for _ in range(owners * splits)
-    ]
+    outs, out_specs = [], []
+    for _ in range(owners):
+        for size in sizes:
+            outs.append(jax.ShapeDtypeStruct((2, size, frames, inputs), jnp.bfloat16))
+            out_specs.append(pl.BlockSpec((2, size, BLOCK, inputs), lambda s, me: (0, 0, s, 0)))
     outs.append(jax.ShapeDtypeStruct((BLOCK, inputs), jnp.float32))
     out_specs.append(pl.BlockSpec((BLOCK, inputs), lambda s, me: (0, 0)))
     kept = (TAPS - 1) * SUBBAND_COUNT
@@ -157,7 +159,7 @@
     else:
         hist_spec, turned = pl.BlockSpec((2, kept, inputs), lambda s, me: (0, 0, 0)), True
     result = pl.pallas_call(
-        functools.partial(front_kernel, splits, owners, turned, tail),
+        functools.partial(front_kernel, sizes, owners, turned, tail),
         grid_spec=pltpu.PrefetchScalarGridSpec(
             num_scalar_prefetch=1,
             grid=(steps,),
@@ -167,20 +169,22 @@
                 pl.BlockSpec((2, 1, inputs, span), lambda s, me: (0, 0, 0, first + s)),
                 pl.BlockSpec(window.shape, lambda s, me: (0, 0, 0)),
                 pl.BlockSpec((1, *table.shape[1:]), lambda s, me: (me[0], 0, 0)),
+                pl.BlockSpec(pick.shape, lambda s, me: (0, 0)),
             ],
             out_specs=out_specs,
             scratch_shapes=[
                 pltpu.VMEM((2, 2, span, inputs), jnp.bfloat16),
                 pltpu.VMEM((BLOCK, 2 * SUBBAND_COUNT, inputs), jnp.bfloat16),
-                pltpu.VMEM((inputs // 128, 2 * SUBBAND_COUNT * SPREAD, 128), jnp.float32),
+                pltpu.VMEM((inputs // 128, pick.shape[0] * SPREAD, 128), jnp.float32),
+                pltpu.VMEM((pick.shape[0], 2 * SUBBAND_COUNT), jnp.bfloat16),
             ],
         ),
         out_shape=outs,
         compiler_params=pltpu.CompilerParams(vmem_limit_bytes=VMEM),
         cost_estimate=COST,
         name="front",
-    )(me, keep, hist, volts, window, table)
-    count = owners * splits
+    )(me, keep, hist, volts, window, table, pick)
+    count = owners * len(sizes)
     return result[:count], result[count], result[count + 1] if tail else None
 
 
@@ -201,7 +205,7 @@
     )(value, *others)
 
 
-def correlate_kernel(owners, picks, outs, sums, place_ref, *rest):
+def correlate_kernel(owners, picks, outs, sums, place_ref, mask_ref, *rest):
     count = len(picks)
     sum_refs, rest = rest[:sums], rest[sums:]
     pieces = [rest[n * owners : (n + 1) * owners] for n in range(count)]
@@ -218,10 +222,12 @@
             source = lax.rem(me - d + owners, owners)
             at = 0
             for n in range(count):
-                size = pieces[n][d].shape[2]
+                begin, size = picks[n]
                 copies.append(
                     pltpu.make_async_copy(
-                        pieces[n][d].at[picks[n]], held.at[source, :, pl.ds(at, size)], sems.at[n, d]
+                        pieces[n][d].at[:, pl.ds(begin, size)],
+                        held.at[source, :, pl.ds(at, size)],
+                        sems.at[n, d],
                     )
                 )
                 at += size
@@ -232,7 +238,8 @@
         for h in range(outs):
             for r in range(per_half):
                 source = place_ref[1 + h] * per_half + r
-                real, imag = held[source, 0].T, held[source, 1].T
+                real = held[source, 0].T * mask_ref[...]
+                imag = held[source, 1].T * mask_ref[...]
                 turned[h, 0, r, :, pl.ds(0, depth)] = real
                 turned[h, 0, r, :, pl.ds(depth, depth)] = imag
                 turned[h, 1, r, :, pl.ds(0, depth)] = imag
@@ -248,10 +255,10 @@
         out_refs[h][...] = both.astype(out_refs[h].dtype)
 
 
-def correlate(place, pieces, picks, dtypes, sums, earlier):
+def correlate(place, mask, pieces, picks, dtypes, sums, earlier):
     owners = len(pieces[0])
     inputs = pieces[0][0].shape[-1]
-    depth = sum(piece[0].shape[2] for piece in pieces)
+    depth = sum(size for _, size in picks)
     rows = owners // 2 * inputs
     operands = [value for piece in pieces for value in piece] + list(earlier)
     columns = pl.BlockSpec((2, rows, inputs), lambda b: (0, 0, b))
@@ -261,7 +268,7 @@
         functools.partial(correlate_kernel, owners, picks, outs, len(sums)),
         grid=(owners,),
         out_shape=[jax.ShapeDtypeStruct((2, rows, owners * inputs), dtype) for dtype in dtypes],
-        in_specs=[pl.BlockSpec(memory_space=pltpu.SMEM)]
+        in_specs=[pl.BlockSpec(memory_space=pltpu.SMEM), pl.BlockSpec((1, depth), lambda b: (0, 0))]
         + [columns] * len(sums)
         + [anywhere] * len(operands),
         out_specs=[columns] * outs,
@@ -273,7 +280,7 @@
         compiler_params=pltpu.CompilerParams(vmem_limit_bytes=VMEM),
         cost_estimate=COST,
         name="correlate",
-    )(place, *sums, *operands)
+    )(place, mask, *sums, *operands)
 
 
 def equalize_kernel(rows_ref, columns_ref, mine_ref, theirs_ref, *rest):
@@ -331,6 +338,15 @@
 
 def pipelined(volts, flagged):
     owners = lax.axis_size("station")
+    keep_all = keep_table(flagged)
+    kept = keep_all.reshape(-1, SUBBAND_COUNT // owners).sum(-1)
+    spare = (SUBBAND_COUNT // owners - jnp.max(kept)).astype(jnp.int32)
+    branches = [functools.partial(slotted, dropped) for dropped in range(DROPPED + 1)]
+    return lax.switch(jnp.minimum(spare, DROPPED), branches, volts, keep_all)
+
+
+def slotted(dropped, volts, keep_all):
+    owners = lax.axis_size("station")
     me = lax.axis_index("station")
     half = lax.axis_index("tm")
     inputs = volts.shape[2]
@@ -339,14 +355,29 @@
     fine = SUBBAND_COUNT // owners
     groups = fine // GROUP
     blocks = frames // BLOCK
-
-    keep_all = keep_table(flagged)
+    slots = fine - dropped
+
     keep_mine = lax.dynamic_index_in_dim(keep_all, lax.axis_index("band"), 0, keepdims=False)
     twice = jnp.concatenate([keep_mine, keep_mine])
-    keep_ahead = lax.dynamic_slice_in_dim(twice, me * fine, SUBBAND_COUNT, 0)
-
-    rows = twiddle_values().reshape(owners, groups, GROUP, 2, 2 * SUBBAND_COUNT)
-    rows = rows.transpose(0, 1, 3, 2, 4)
+    keep_ahead = lax.dynamic_slice_in_dim(twice, me * fine, SUBBAND_COUNT, 0).reshape(owners, fine)
+
+    earlier = np.tril(np.ones((fine, fine), np.float32), -1)
+    flags = 1.0 - keep_ahead
+    before = jnp.sum(flags[:, None, :] * earlier, -1)
+    out_of = flags * (before < dropped)
+    gone = jnp.minimum(before, float(dropped))
+    place_of = jnp.where(out_of > 0, -1.0, np.arange(fine, dtype=np.float32) - gone)
+    holds = place_of[:, None, :] == np.arange(slots, dtype=np.float32)[None, :, None]
+    holds = holds.astype(jnp.float32)
+    keep_slots = jnp.sum(holds * keep_ahead[:, None, :], -1).reshape(-1)
+    channel_of = jnp.sum(holds * np.arange(fine, dtype=np.float32), -1)
+    member = jnp.sum(holds[0].reshape(slots, groups, GROUP), -1)
+    row_of = (channel_of + fine * np.arange(owners, dtype=np.float32)[:, None]).reshape(-1)
+    row_of = (2.0 * row_of[:, None] + np.arange(2, dtype=np.float32)).reshape(-1)
+    pick = row_of[:, None] == np.arange(2 * SUBBAND_COUNT, dtype=np.float32)[None, :]
+    pick = pick.astype(jnp.bfloat16)
+
+    rows = twiddle_values().reshape(owners, 2 * fine, 2 * SUBBAND_COUNT)
     turns = [np.roll(rows, -z, 0).reshape(2 * SUBBAND_COUNT, -1) for z in range(owners)]
     table = jnp.asarray(np.stack(turns).astype(jnp.bfloat16))
     window = np.broadcast_to(window_values()[:, :, None], (TAPS, SUBBAND_COUNT, 128))
@@ -371,23 +402,25 @@
     for size in PARTS:
         end -= size
         spectra, part_power, tail = front(
-            volts, None, end, size, 1, owners, keep_ahead, spot, window, table, halo is None
+            volts, None, end, size, (slots,), owners, keep_slots, spot, window, table, pick, halo is None
         )
         if tail is not None:
             halo = tail
-        parts.append([x.reshape(groups, 2, GROUP * size * BLOCK, inputs) for x in spectra])
+        parts.append([x.reshape(2, slots * size * BLOCK, inputs) for x in spectra])
         power.append(part_power)
         if len(parts) == 1:
             send(0, {})
     with jax.named_scope("halo"):
         halo = passed_on(halo)
+    sizes = (GROUP,) * (groups - 1) + (GROUP - dropped,)
     spectra, part_power, _ = front(
-        volts, halo, 0, end, groups, owners, keep_ahead, spot, window, table, False
+        volts, halo, 0, end, sizes, owners, keep_slots, spot, window, table, pick, False
     )
     power.append(part_power)
-    spectra = [x.reshape(1, 2, GROUP * end * BLOCK, inputs) for x in spectra]
     for j in range(groups):
-        parts.append([spectra[d * groups + j] for d in range(owners)])
+        parts.append(
+            [spectra[d * groups + j].reshape(2, -1, inputs) for d in range(owners)]
+        )
 
     local = jnp.sum(sum(power), axis=0)
     total = lax.psum(local, ("band", "tm"))
@@ -408,10 +441,22 @@
         with jax.named_scope(f"rows{j}"):
             return lax.ppermute(theirs, "tm", [(0, 1), (1, 0)])
 
-    def multiply(j, place, dtypes, sums=(), earlier=(), begin=0, end=shared + 1):
-        pieces = arrived[:shared] + arrived[shared + j : shared + j + 1]
-        picks = (j,) * shared + (0,)
-        return correlate(place, pieces[begin:end], picks[begin:end], dtypes, sums, earlier)
+    end_frames = end * BLOCK
+
+    def multiply(j, place, dtypes, sums=(), earlier=(), begin=0, end=None):
+        low, high = max(0, j * GROUP - dropped), min(slots, (j + 1) * GROUP)
+        pieces = [(arrived[n], low, high, 0, PARTS[n] * BLOCK) for n in range(shared)]
+        if end is None:
+            pieces.append((arrived[shared + j], j * GROUP, high, j * GROUP, end_frames))
+        if end is None and low < j * GROUP:
+            pieces.append(
+                (arrived[shared + j - 1], low, j * GROUP, (j - 1) * GROUP, end_frames)
+            )
+        pieces = pieces[begin:end]
+        picks = tuple(((a - first) * size, (b - a) * size) for _, a, b, first, size in pieces)
+        mask = jnp.concatenate([jnp.repeat(member[a:b, j], size) for _, a, b, _, size in pieces])
+        mask = mask.astype(jnp.bfloat16)[None, :]
+        return correlate(place, mask, [x[0] for x in pieces], picks, dtypes, sums, earlier)
 
     both = [jnp.bfloat16, jnp.float32]
     last_spectra = parts[shared][0]

time: 467 us -> 477 us (1.021); the launches traced: 465 us -> 469 us
  blocking collectives: 112 us -> 69.6 us
  loops' own time: 0 us -> 15.3 us
  starting transfers between devices: 20.8 us -> 28.5 us
  Pallas kernels: 176 us -> 183 us
  local copies, waits for them, and re-layouts: 15.7 us -> 22.3 us
  waiting for transfers between devices: 133 us -> 139 us
    all_gather x1, blocking collectives: 98.3 us -> 58.3 us  [slotted(): scales = lax.all_gather(scale, 'station', axis=0, tiled=True)]
    another operation x0 -> x1, loops' own time: none -> 15.3 us  [pipelined(): return lax.switch(jnp.minimum(spare, DROPPED), branches, volts, keep_all)]
    cond x0 -> x44, local copies, waits for them, and re-layouts: none -> 11 us
    ppermute x18, starting transfers between devices: 15.2 us -> 24.8 us  [shift(): lax.ppermute(value, 'station', [(s, (s + d) % count) for s in range(count)])]
    unnamed x41 -> x1, local copies, waits for them, and re-layouts: 10.2 us -> 0.78 us
    pallas_call x5, Pallas kernels: 72.7 us -> 78.5 us  [correlate(): pl.pallas_call(functools.partial(correlate_kernel, owners, picks, outs, l...]
    ppermute x18, waiting for transfers between devices: 133 us -> 139 us  [shift(): lax.ppermute(value, 'station', [(s, (s + d) % count) for s in range(count)])]
  transfers between devices with their start and end apart: 23 -> 23, of which waited for: 12 -> 10; matrix products, arithmetic and copies ran while one was open for 2% -> 3% of each run, Pallas kernels for 34% -> 35%
where the time goes in v6:
time: 477 us; the launch traced here: 469 us
  Pallas kernels  183 us (38%)
  waiting for transfers between devices  139 us (29%)
  blocking collectives  69.6 us (15%)
  starting transfers between devices  28.5 us (6%)
  local copies, waits for them, and re-layouts  22.3 us (5%)
  loops' own time  15.3 us (3%)
  other arithmetic  9.85 us (2%)
    ppermute x18, waiting for transfers between devices, shift(): lax.ppermute(value, 'station', [(s, (s + d) % count) for s in range(count)])  139 us
    pallas_call x3, Pallas kernels, front(): pl.pallas_call(functools.partial(front_kernel, sizes, owners, turned, tai...  82.7 us
    pallas_call x5, Pallas kernels, correlate(): pl.pallas_call(functools.partial(correlate_kernel, owners, picks, outs, l...  78.5 us
    all_gather x1, blocking collectives, slotted(): scales = lax.all_gather(scale, 'station', axis=0, tiled=True)  58.3 us
    ppermute x18, starting transfers between devices, shift(): lax.ppermute(value, 'station', [(s, (s + d) % count) for s in range(count)])  24.8 us
    pallas_call x4, Pallas kernels, equalize(): pl.pallas_call(equalize_kernel, grid=(rows // block,), out_shape=jax.Shap...  21.4 us
    another operation x1, loops' own time, pipelined(): return lax.switch(jnp.minimum(spare, DROPPED), branches, volts, keep_all)  15.3 us
    psum x1, blocking collectives, slotted(): total = lax.psum(local, ('band', 'tm'))  11.3 us
  transfers between devices with their start and end apart: 23, of which 10 were waited for; matrix products, arithmetic and copies ran while one was open for 3% of the time, Pallas kernels for 35%

profile of v6, /device:TPU:11, one launch (start us, length us, event | category | flops | bytes accessed | tf_op | source)
XLA Modules:
  0.0 469.0 jit_solution(8532927797560185353)
XLA Ops:
  2.4 465.2 %conditional.1 = (f32[1,4,2,512,1024]{4,3,2,1,0:T(8,128)}) conditional(s32[]{:T(128)} %clamp.19, (f32[4,144]{1,0:T(4,128)S(1)}, f32[36,36]{1,0:T(8,128)}, f32[36]{0:T(128)S(1)}, (), f32[36]{0:T(128)S(1)}, /*index=5*/f32[4,1]{0,1:T(1,128)}, f32[2]{0:T(128)S(1)}, f32[1,288]{1,0:T(1,128)}, ...), branch_computations={%region_3.12_spmd, %region_12.21_spmd, %region_21.30_spmd, %region... | conditional | flops 257862 | bytes 160150688 | solution.py:345
  10.2 0.8 multiply_reduce_fusion.2
  14.6 14.4 %front.18 = (bf16[2,34,16,256]{3,2,1,0:T(8,128)(2,1)}, bf16[2,34,16,256]{3,2,1,0:T(8,128)(2,1)}, bf16[2,34,16,256]{3,2,1,0:T(8,128)(2,1)}, bf16[2,34,16,256]{3,2...) custom-call(s32[1]{0:T(128)} %bitcast.96.me_ref, f32[136]{0:T(256)} %reshape.1485.keep_ref, ...), custom_call_target="tpu_custom_call" | custom-call | flops 1024 | bytes 1024 | tf_op jit(solution)/shard_map/cond/branch_2_fun/front/pallas_call | solution.py:161
  29.0 1.3 collective-permute-start.46
  30.3 2.4 collective-permute-start.48
  32.9 1.3 collective-permute-start.47
  34.2 30.1 %front.19 = (bf16[2,34,48,256]{3,2,1,0:T(8,128)(2,1)}, bf16[2,34,48,256]{3,2,1,0:T(8,128)(2,1)}, bf16[2,34,48,256]{3,2,1,0:T(8,128)(2,1)}, bf16[2,34,48,256]{3,2,1,0:T(8,128)(2,1)}, f32[16,256]{1,0:T(8,128)}) custom-call(s32[1]{0:T(128)} %bitcast.96.me_ref, f32[136]{0:T(256)} %reshape.1485.keep_ref, ...), custom_call_target="tpu_custom_call" | custom-call | flops 1024 | bytes 1024 | tf_op jit(solution)/shard_map/cond/branch_2_fun/front/pallas_call | solution.py:161
  64.3 1.9 collective-permute-start.51
  66.2 38.1 %front.20 = (bf16[2,9,64,256]{3,2,1,0:T(8,128)(2,1)}, bf16[2,9,64,256]{3,2,1,0:T(8,128)(2,1)}, bf16[2,9,64,256]{3,2,1,0:T(8,128)(2,1)}, bf16[2,7,64,256]{3,2,1,0...) custom-call(s32[1]{0:T(128)} %bitcast.96.me_ref, ...), custom_call_target="tpu_custom_call" | custom-call | flops 1024 | bytes 1024 | tf_op jit(solution)/shard_map/cond/branch_2_fun/front/pallas_call | solution.py:161
  104.3 11.4 %collective-permute-done.49.refs_3_.rest_3_ = bf16[2,544,256]{2,1,0:T(8,128)(2,1)} collective-permute-done((bf16[2,544,256]{2,1,0:T(8,128)(2,1)}, bf16[2,544,256]{2,1,0:T(8,128)(2,1)}, u32[]{:S(2)}, u32[]{:S(2)}) %collective-permute-start.49) | collective-permute-done | bytes 557088 | tf_op jit(solution)/shard_map/cond/branch_2_fun/part0_shift3/ppermute | solution.py:326
  115.7 37.0 %collective-permute-done.47.refs_3_.rest_1_ = bf16[2,544,256]{2,1,0:T(8,128)(2,1)} collective-permute-done((bf16[2,544,256]{2,1,0:T(8,128)(2,1)}, bf16[2,544,256]{2,1,0:T(8,128)(2,1)}, u32[]{:S(2)}, u32[]{:S(2)}) %collective-permute-start.47) | collective-permute-done | bytes 557088 | tf_op jit(solution)/shard_map/cond/branch_2_fun/part0_shift1/ppermute | solution.py:326
  152.7 2.2 collective-permute-start.50
  156.4 11.3 %psum.26 = f32[256]{0:T(256)S(1)} all-reduce(f32[256]{0:T(256)S(1)} %add_reduce_fusion.2), channel_id=1, replica_groups=mesh['station'=4,'band'=4,'tm'=2] {'band','tm'}, use_global_device_ids=true, to_apply=%region_26.26 | all-reduce | flops 256 | bytes 2048 | tf_op jit(solution)/shard_map/cond/branch_2_fun/psum | solution.py:426
  167.7 58.3 %all-gather.2 = f32[4,1,256]{2,1,0:T(1,128)} all-gather(f32[1,1,256]{2,1,0:T(1,128)S(1)} %bitcast.408), channel_id=1, replica_groups=mesh['station'=4,'band'=4,'tm'=2] {'station'}, dimensions={0}, use_global_device_ids=true | all-gather | bytes 5120 | tf_op jit(solution)/shard_map/cond/branch_2_fun/all_gather | solution.py:428
  226.0 1.2 copy-done.12
  227.2 2.8 collective-permute-start.57
  230.0 1.2 copy-done.13
  231.2 1.2 collective-permute-start.61
  232.4 1.2 collective-permute-start.53
  235.3 32.4 %collective-permute-done.57.refs_1_.rest_14_.rest_10_ = bf16[2,576,256]{2,1,0:T(8,128)(2,1)S(1)} collective-permute-done((bf16[2,576,256]{2,1,0:T(8,128)(2,1)}, bf16[2,576,256]{2,1,0:T(8,128)(2,1)S(1)}, u32[]{:S(2)}, u32[]{:S(2)}) %collective-permute-start.57) | collective-permute-done | bytes 589856 | tf_op jit(solution)/shard_map/cond/branch_2_fun/part2_shift2/ppermute | solution.py:326
  268.5 3.0 collective-permute-start.58
  271.5 11.5 %correlate.30 = (f32[2,512,1024]{2,1,0:T(8,128)}, f32[2,512,1024]{2,1,0:T(8,128)}) custom-call(s32[3]{0:T(128)} %pad_add_fusion.2.place_ref, bf16[1,576]{1,0:T(2,128)(2,1)} %pad_maximum_fusion.5.mask_ref, bf16[2,544,256]{2,1,0:T(8,128)(2,1)} %bitcast.277, bf16[2,544,256]{2,1,0:T(8,128)(2,1)} %collective-permute-done.47.refs_3_.rest_1_, ...), custom_call_target="tpu_custom_call" | custom-call | flops 1024 | bytes 1024 | tf_op jit(solution)/shard_map/cond/branch_2_fun/correlate/pallas_call | solution.py:267
  283.0 5.3 %collective-permute-done.61.refs_3_.rest_15_.rest_11_ = bf16[2,576,256]{2,1,0:T(8,128)(2,1)S(1)} collective-permute-done((bf16[2,576,256]{2,1,0:T(8,128)(2,1)}, bf16[2,576,256]{2,1,0:T(8,128)(2,1)S(1)}, u32[]{:S(2)}, u32[]{:S(2)}) %collective-permute-start.61) | collective-permute-done | bytes 589856 | tf_op jit(solution)/shard_map/cond/branch_2_fun/part2_shift3/ppermute | solution.py:326
  289.1 10.2 %collective-permute-done.53.refs_1_.rest_13_.rest_9_ = bf16[2,576,256]{2,1,0:T(8,128)(2,1)S(1)} collective-permute-done((bf16[2,576,256]{2,1,0:T(8,128)(2,1)}, bf16[2,576,256]{2,1,0:T(8,128)(2,1)S(1)}, u32[]{:S(2)}, u32[]{:S(2)}) %collective-permute-start.53) | collective-permute-done | bytes 589856 | tf_op jit(solution)/shard_map/cond/branch_2_fun/part2_shift1/ppermute | solution.py:326
  300.1 2.2 collective-permute-start.54
  303.5 16.1 %correlate.32 = (bf16[2,512,1024]{2,1,0:T(8,128)(2,1)}, f32[2,512,1024]{2,1,0:T(8,128)}) custom-call(s32[3]{0:T(128)} %pad_add_fusion.2.place_ref, bf16[1,1152]{1,0:T(2,128)(2,1)} %concatenate.290.mask_ref, bf16[2,544,256]{2,1,0:T(8,128)(2,1)} %bitcast.278, bf16[2,544,256]{2,1,0:T(8,128)(2,1)} %collective-permute-done.47.refs_3_.rest_1_, ...), custom_call_target="tpu_custom_call" | custom-call | flops 1024 | bytes 1024 | tf_op jit(solution)/shard_map/cond/branch_2_fun/correlate/pallas_call | solution.py:267
  319.6 12.9 %collective-permute-done.62.refs_1_.rest_11_.refs_3_.rest_15_ = bf16[2,576,256]{2,1,0:T(8,128)(2,1)S(1)} collective-permute-done((bf16[2,576,256]{2,1,0:T(8,128)(2,1)}, bf16[2,576,256]{2,1,0:T(8,128)(2,1)S(1)}, u32[]{:S(2)}, u32[]{:S(2)}) %collective-permute-start.62) | collective-permute-done | bytes 589856 | tf_op jit(solution)/shard_map/cond/branch_2_fun/part3_shift3/ppermute | solution.py:326
  332.6 0.9 copy-done.19
  334.7 2.1 collective-permute-start.59
  337.2 1.1 collective-permute-start.55
  340.2 2.7 broadcast_divide_fusion.8
  342.9 0.9 copy.201.rows_ref
  343.8 19.0 %correlate.31 = (bf16[2,512,1024]{2,1,0:T(8,128)(2,1)}, f32[2,512,1024]{2,1,0:T(8,128)}) custom-call(s32[3]{0:T(128)} %pad_add_fusion.2.place_ref, bf16[1,1408]{1,0:T(2,128)(2,1)} %concatenate.286.mask_ref, bf16[2,544,256]{2,1,0:T(8,128)(2,1)} %bitcast.279, bf16[2,544,256]{2,1,0:T(8,128)(2,1)} %collective-permute-done.47.refs_3_.rest_1_, ...), custom_call_target="tpu_custom_call" | custom-call | flops 1024 | bytes 1024 | tf_op jit(solution)/shard_map/cond/branch_2_fun/correlate/pallas_call | solution.py:267
  362.8 5.4 %equalize.24.rest_0_ = f32[4,2,512,1024]{3,2,1,0:T(8,128)} custom-call(f32[512,1]{1,0:T(8,128)} %copy.201.rows_ref, f32[1,1024]{1,0:T(1,128)} %bitcast.363, f32[2,512,1024]{2,1,0:T(8,128)} %get-tuple-element.239.mine_ref, bf16[2,512,1024]{2,1,0:T(8,128)(2,1)} %collective-permute-done.66.theirs_ref, bf16[2,512,1024]{2,1,0:T(8,128)(2,1)} %get-tuple-element.238.refs_0_.rest_0_), custom_call_target="tpu_custom_call" | custom-call | flops 1024 | bytes 1024 | tf_op jit(solution)/shard_map/cond/branch_2_fun/equalize/pallas_call | solution.py:311
  368.1 7.3 %collective-permute-done.59.refs_1_.refs_2_.rest_10_.rest_8_ = bf16[2,576,256]{2,1,0:T(8,128)(2,1)S(1)} collective-permute-done((bf16[2,576,256]{2,1,0:T(8,128)(2,1)}, bf16[2,576,256]{2,1,0:T(8,128)(2,1)S(1)}, u32[]{:S(2)}, u32[]{:S(2)}) %collective-permute-start.59) | collective-permute-done | bytes 589856 | tf_op jit(solution)/shard_map/cond/branch_2_fun/part4_shift2/ppermute | solution.py:326
  375.4 12.4 %collective-permute-done.63.refs_1_.refs_3_.rest_11_.rest_9_ = bf16[2,576,256]{2,1,0:T(8,128)(2,1)S(1)} collective-permute-done((bf16[2,576,256]{2,1,0:T(8,128)(2,1)}, bf16[2,576,256]{2,1,0:T(8,128)(2,1)S(1)}, u32[]{:S(2)}, u32[]{:S(2)}) %collective-permute-start.63) | collective-permute-done | bytes 589856 | tf_op jit(solution)/shard_map/cond/branch_2_fun/part4_shift3/ppermute | solution.py:326
  390.1 2.6 collective-permute-start.64
  395.3 0.9 copy.202.rows_ref
  396.2 18.9 %correlate.33 = (bf16[2,512,1024]{2,1,0:T(8,128)(2,1)}, f32[2,512,1024]{2,1,0:T(8,128)}) custom-call(s32[3]{0:T(128)} %pad_add_fusion.2.place_ref, bf16[1,1408]{1,0:T(2,128)(2,1)} %concatenate.295.mask_ref, bf16[2,544,256]{2,1,0:T(8,128)(2,1)} %bitcast.280, bf16[2,544,256]{2,1,0:T(8,128)(2,1)} %collective-permute-done.47.refs_3_.rest_1_, ...), custom_call_target="tpu_custom_call" | custom-call | flops 1024 | bytes 1024 | tf_op jit(solution)/shard_map/cond/branch_2_fun/correlate/pallas_call | solution.py:267
  415.8 1.3 copy-done.52
  417.1 5.3 %equalize.25.rest_10_.rest_0_ = f32[4,2,512,1024]{3,2,1,0:T(8,128)} custom-call(f32[512,1]{1,0:T(8,128)} %copy.202.rows_ref, f32[1,1024]{1,0:T(1,128)} %bitcast.364, f32[2,512,1024]{2,1,0:T(8,128)} %get-tuple-element.237.mine_ref, bf16[2,512,1024]{2,1,0:T(8,128)(2,1)} %copy-done.52, ...), custom_call_target="tpu_custom_call", output_to_operand_aliasing={{}: (4, {})} | custom-call | flops 1024 | bytes 1024 | tf_op jit(solution)/shard_map/cond/branch_2_fun/equalize/pallas_call | solution.py:311
  422.4 9.8 %collective-permute-done.64.rest_5_ = bf16[2,448,256]{2,1,0:T(8,128)(2,1)S(1)} collective-permute-done((bf16[2,448,256]{2,1,0:T(8,128)(2,1)}, bf16[2,448,256]{2,1,0:T(8,128)(2,1)S(1)}, u32[]{:S(2)}, u32[]{:S(2)}) %collective-permute-start.64) | collective-permute-done | bytes 458784 | tf_op jit(solution)/shard_map/cond/branch_2_fun/part5_shift3/ppermute | solution.py:326
  433.1 13.0 %correlate.34 = (bf16[2,512,1024]{2,1,0:T(8,128)(2,1)}, f32[2,512,1024]{2,1,0:T(8,128)}) custom-call(s32[3]{0:T(128)} %pad_add_fusion.2.place_ref, bf16[1,576]{1,0:T(2,128)(2,1)} %pad_maximum_fusion.4.mask_ref, f32[2,512,1024]{2,1,0:T(8,128)} %get-tuple-element.220.refs_1_.rest_0_, f32[2,512,1024]{2,1,0:T(8,128)} %get-tuple-element.221.refs_2_.rest_1_, ...), custom_call_target="tpu_custom_call" | custom-call | flops 1024 | bytes 1024 | tf_op jit(solution)/shard_map/cond/branch_2_fun/correlate/pallas_call | solution.py:267
  446.8 0.8 copy.203.rows_ref
  447.7 0.8 copy.204.rows_ref
  448.5 5.3 %equalize.26.rest_0_ = f32[4,2,512,1024]{3,2,1,0:T(8,128)} custom-call(f32[512,1]{1,0:T(8,128)} %copy.203.rows_ref, f32[1,1024]{1,0:T(1,128)} %bitcast.365, f32[2,512,1024]{2,1,0:T(8,128)} %get-tuple-element.244.mine_ref, bf16[2,512,1024]{2,1,0:T(8,128)(2,1)} %collective-permute-done.68.theirs_ref, ...), custom_call_target="tpu_custom_call", output_to_operand_aliasing={{}: (4, {})} | custom-call | flops 1024 | bytes 1024 | tf_op jit(solution)/shard_map/cond/branch_2_fun/equalize/pallas_call | solution.py:311
  453.9 1.3 copy-done.58
  455.2 5.3 %equalize.27 = f32[4,2,512,1024]{3,2,1,0:T(8,128)} custom-call(f32[512,1]{1,0:T(8,128)} %copy.204.rows_ref, f32[1,1024]{1,0:T(1,128)} %bitcast.366, f32[2,512,1024]{2,1,0:T(8,128)} %get-tuple-element.242.mine_ref, bf16[2,512,1024]{2,1,0:T(8,128)(2,1)} %copy-done.58, f32[4,2,512,1024]{3,2,1,0:T(8,128)} %equalize.26.rest_0_), custom_call_target="tpu_custom_call", output_to_operand_aliasing={{}: (4, {})} | custom-call | flops 1024 | bytes 1024 | tf_op jit(solution)/shard_map/cond/branch_2_fun/equalize/pallas_call | solution.py:311
  (156 shorter events, 22.5 us)
Async XLA Ops:
  14.6 19.6 %copy-start.2 = (bf16[4,288,288]{2,1,0:T(8,128)(2,1)S(1)}, bf16[4,288,288]{2,1,0:T(8,128)(2,1)}, u32[]{:S(2)}) copy-start(bf16[4,288,288]{2,1,0:T(8,128)(2,1)} %get-tuple-element.202.table_ref) | copy-start | bytes 1990660 | tf_op jit(solution)/shard_map/cond
  14.6 19.6 %copy-start.6 = (f32[12,144,128]{2,1,0:T(8,128)S(1)}, f32[12,144,128]{2,1,0:T(8,128)}, u32[]{:S(2)}) copy-start(f32[12,144,128]{2,1,0:T(8,128)} %get-tuple-element.201.window_ref) | copy-start | bytes 2654212 | tf_op jit(solution)/shard_map/cond
  29.0 37.2 %collective-permute-start.46 = (bf16[2,1584,256]{2,1,0:T(8,128)(2,1)}, bf16[2,1584,256]{2,1,0:T(8,128)(2,1)}, u32[]{:S(2)}, u32[]{:S(2)}) collective-permute-start(bf16[2,1584,256]{2,1,0:T(8,128)(2,1)} %get-tuple-element.209), channel_id=1, source_target_pairs={{0,1},{2,3},{4,5},{6,7},{8,9},{10,11},{12,13},{14,15},{16,17},{18,... | collective-permute-start | bytes 4866056 | tf_op jit(solution)/shard_map/cond/branch_2_fun/halo/ppermute | solution.py:331
  30.3 74.0 %collective-permute-start.48 = (bf16[2,544,256]{2,1,0:T(8,128)(2,1)}, bf16[2,544,256]{2,1,0:T(8,128)(2,1)}, u32[]{:S(2)}, u32[]{:S(2)}) collective-permute-start(bf16[2,544,256]{2,1,0:T(8,128)(2,1)} %bitcast.426), channel_id=1, source_target_pairs={{0,16},{8,24},{16,0},{24,8},{1,17},{9,25},{17,1},{25,9},{2,18},{10... | collective-permute-start | bytes 1671176 | tf_op jit(solution)/shard_map/cond/branch_2_fun/part0_shift2/ppermute | solution.py:326
  32.7 83.0 %collective-permute-start.49 = (bf16[2,544,256]{2,1,0:T(8,128)(2,1)}, bf16[2,544,256]{2,1,0:T(8,128)(2,1)}, u32[]{:S(2)}, u32[]{:S(2)}) collective-permute-start(bf16[2,544,256]{2,1,0:T(8,128)(2,1)} %bitcast.425), channel_id=1, source_target_pairs={{0,24},{8,0},{16,8},{24,16},{1,25},{9,1},{17,9},{25,17},{2,26},{10... | collective-permute-start | bytes 1671176 | tf_op jit(solution)/shard_map/cond/branch_2_fun/part0_shift3/ppermute | solution.py:326
  32.9 119.9 %collective-permute-start.47 = (bf16[2,544,256]{2,1,0:T(8,128)(2,1)}, bf16[2,544,256]{2,1,0:T(8,128)(2,1)}, u32[]{:S(2)}, u32[]{:S(2)}) collective-permute-start(bf16[2,544,256]{2,1,0:T(8,128)(2,1)} %bitcast.424), channel_id=1, source_target_pairs={{0,8},{8,16},{16,24},{24,0},{1,9},{9,17},{17,25},{25,1},{2,10},{10... | collective-permute-start | bytes 1671176 | tf_op jit(solution)/shard_map/cond/branch_2_fun/part0_shift1/ppermute | solution.py:326
  64.3 161.7 %collective-permute-start.51 = (bf16[2,1632,256]{2,1,0:T(8,128)(2,1)}, bf16[2,1632,256]{2,1,0:T(8,128)(2,1)S(1)}, u32[]{:S(2)}, u32[]{:S(2)}) collective-permute-start(bf16[2,1632,256]{2,1,0:T(8,128)(2,1)} %bitcast.416), channel_id=1, source_target_pairs={{0,16},{8,24},{16,0},{24,8},{1,17},{9,25},{17,1},{25,9},{2,18},{10... | collective-permute-start | bytes 5013512 | tf_op jit(solution)/shard_map/cond/branch_2_fun/part1_shift2/ppermute | solution.py:326
  115.7 114.3 %collective-permute-start.52 = (bf16[2,1632,256]{2,1,0:T(8,128)(2,1)}, bf16[2,1632,256]{2,1,0:T(8,128)(2,1)S(1)}, u32[]{:S(2)}, u32[]{:S(2)}) collective-permute-start(bf16[2,1632,256]{2,1,0:T(8,128)(2,1)} %after.97), channel_id=1, source_target_pairs={{0,24},{8,0},{16,8},{24,16},{1,25},{9,1},{17,9},{25,17},{2,26},{10... | collective-permute-start | bytes 5013512 | tf_op jit(solution)/shard_map/cond/branch_2_fun/part1_shift3/ppermute | solution.py:326
  152.7 3.6 copy-start.76
  152.7 3.6 copy-start.79
  152.7 3.6 copy-start.82
  152.7 79.7 %collective-permute-start.50 = (bf16[2,1632,256]{2,1,0:T(8,128)(2,1)}, bf16[2,1632,256]{2,1,0:T(8,128)(2,1)}, u32[]{:S(2)}, u32[]{:S(2)}) collective-permute-start(bf16[2,1632,256]{2,1,0:T(8,128)(2,1)} %after.96), channel_id=1, source_target_pairs={{0,8},{8,16},{16,24},{24,0},{1,9},{9,17},{17,25},{25,1},{2,10},{10... | collective-permute-start | bytes 5013512 | tf_op jit(solution)/shard_map/cond/branch_2_fun/part1_shift1/ppermute | solution.py:326
  226.0 1.2 copy-start.12
  227.2 40.5 %collective-permute-start.57 = (bf16[2,576,256]{2,1,0:T(8,128)(2,1)}, bf16[2,576,256]{2,1,0:T(8,128)(2,1)S(1)}, u32[]{:S(2)}, u32[]{:S(2)}) collective-permute-start(bf16[2,576,256]{2,1,0:T(8,128)(2,1)} %after.102), channel_id=1, source_target_pairs={{0,16},{8,24},{16,0},{24,8},{1,17},{9,25},{17,1},{25,9},{2,18},{10... | collective-permute-start | bytes 1769480 | tf_op jit(solution)/shard_map/cond/branch_2_fun/part2_shift2/ppermute | solution.py:326
  230.0 1.2 copy-start.13
  231.2 57.1 %collective-permute-start.61 = (bf16[2,576,256]{2,1,0:T(8,128)(2,1)}, bf16[2,576,256]{2,1,0:T(8,128)(2,1)S(1)}, u32[]{:S(2)}, u32[]{:S(2)}) collective-permute-start(bf16[2,576,256]{2,1,0:T(8,128)(2,1)} %after.106), channel_id=1, source_target_pairs={{0,24},{8,0},{16,8},{24,16},{1,25},{9,1},{17,9},{25,17},{2,26},{10... | collective-permute-start | bytes 1769480 | tf_op jit(solution)/shard_map/cond/branch_2_fun/part2_shift3/ppermute | solution.py:326
  232.4 66.9 %collective-permute-start.53 = (bf16[2,576,256]{2,1,0:T(8,128)(2,1)}, bf16[2,576,256]{2,1,0:T(8,128)(2,1)S(1)}, u32[]{:S(2)}, u32[]{:S(2)}) collective-permute-start(bf16[2,576,256]{2,1,0:T(8,128)(2,1)} %after.98), channel_id=1, source_target_pairs={{0,8},{8,16},{16,24},{24,0},{1,9},{9,17},{17,25},{25,1},{2,10},{10... | collective-permute-start | bytes 1769480 | tf_op jit(solution)/shard_map/cond/branch_2_fun/part2_shift1/ppermute | solution.py:326
  267.7 0.8 copy-start.46
  268.5 51.1 %collective-permute-start.58 = (bf16[2,576,256]{2,1,0:T(8,128)(2,1)}, bf16[2,576,256]{2,1,0:T(8,128)(2,1)S(1)}, u32[]{:S(2)}, u32[]{:S(2)}) collective-permute-start(bf16[2,576,256]{2,1,0:T(8,128)(2,1)} %after.103), channel_id=1, source_target_pairs={{0,16},{8,24},{16,0},{24,8},{1,17},{9,25},{17,1},{25,9},{2,18},{10... | collective-permute-start | bytes 1769480 | tf_op jit(solution)/shard_map/cond/branch_2_fun/part3_shift2/ppermute | solution.py:326
  288.3 0.8 copy-start.43
  289.1 43.5 %collective-permute-start.62 = (bf16[2,576,256]{2,1,0:T(8,128)(2,1)}, bf16[2,576,256]{2,1,0:T(8,128)(2,1)S(1)}, u32[]{:S(2)}, u32[]{:S(2)}) collective-permute-start(bf16[2,576,256]{2,1,0:T(8,128)(2,1)} %after.107), channel_id=1, source_target_pairs={{0,24},{8,0},{16,8},{24,16},{1,25},{9,1},{17,9},{25,17},{2,26},{10... | collective-permute-start | bytes 1769480 | tf_op jit(solution)/shard_map/cond/branch_2_fun/part3_shift3/ppermute | solution.py:326
  299.3 0.8 copy-start.47
  300.1 32.4 %collective-permute-start.54 = (bf16[2,576,256]{2,1,0:T(8,128)(2,1)}, bf16[2,576,256]{2,1,0:T(8,128)(2,1)S(1)}, u32[]{:S(2)}, u32[]{:S(2)}) collective-permute-start(bf16[2,576,256]{2,1,0:T(8,128)(2,1)} %after.99), channel_id=1, source_target_pairs={{0,8},{8,16},{16,24},{24,0},{1,9},{9,17},{17,25},{25,1},{2,10},{10... | collective-permute-start | bytes 1769480 | tf_op jit(solution)/shard_map/cond/branch_2_fun/part3_shift1/ppermute | solution.py:326
  319.6 12.9 %copy-start.16 = (bf16[2,576,256]{2,1,0:T(8,128)(2,1)}, bf16[2,576,256]{2,1,0:T(8,128)(2,1)S(1)}, u32[]{:S(2)}) copy-start(bf16[2,576,256]{2,1,0:T(8,128)(2,1)S(1)} %collective-permute-done.58.refs_1_.rest_10_.refs_2_.rest_14_) | copy-start | bytes 1769476 | tf_op jit(solution)/shard_map/cond
  332.5 0.9 copy-start.19
  332.5 1.1 copy-start.22
  333.6 29.1 %collective-permute-start.66 = (bf16[2,512,1024]{2,1,0:T(8,128)(2,1)}, bf16[2,512,1024]{2,1,0:T(8,128)(2,1)}, u32[]{:S(2)}, u32[]{:S(2)}) collective-permute-start(bf16[2,512,1024]{2,1,0:T(8,128)(2,1)} %after.111), channel_id=1, source_target_pairs={{0,1},{1,0},{2,3},{3,2},{4,5},{5,4},{6,7},{7,6},{8,9},{9,8},{10,11... | collective-permute-start | bytes 6291464 | tf_op jit(solution)/shard_map/cond/branch_2_fun/rows0/ppermute | solution.py:442
  334.7 5.5 %copy-start.70 = (f32[4,1,256]{2,1,0:T(1,128)S(1)}, f32[4,1,256]{2,1,0:T(1,128)}, u32[]{:S(2)}) copy-start(f32[4,1,256]{2,1,0:T(1,128)} %all-gather.2) | copy-start | bytes 12292 | tf_op jit(solution)/shard_map/cond
  334.7 40.7 %collective-permute-start.59 = (bf16[2,576,256]{2,1,0:T(8,128)(2,1)}, bf16[2,576,256]{2,1,0:T(8,128)(2,1)S(1)}, u32[]{:S(2)}, u32[]{:S(2)}) collective-permute-start(bf16[2,576,256]{2,1,0:T(8,128)(2,1)} %after.104), channel_id=1, source_target_pairs={{0,16},{8,24},{16,0},{24,8},{1,17},{9,25},{17,1},{25,9},{2,18},{10... | collective-permute-start | bytes 1769480 | tf_op jit(solution)/shard_map/cond/branch_2_fun/part4_shift2/ppermute | solution.py:326
  336.8 51.1 %collective-permute-start.63 = (bf16[2,576,256]{2,1,0:T(8,128)(2,1)}, bf16[2,576,256]{2,1,0:T(8,128)(2,1)S(1)}, u32[]{:S(2)}, u32[]{:S(2)}) collective-permute-start(bf16[2,576,256]{2,1,0:T(8,128)(2,1)} %after.108), channel_id=1, source_target_pairs={{0,24},{8,0},{16,8},{24,16},{1,25},{9,1},{17,9},{25,17},{2,26},{10... | collective-permute-start | bytes 1769480 | tf_op jit(solution)/shard_map/cond/branch_2_fun/part4_shift3/ppermute | solution.py:326
  337.2 50.9 %collective-permute-start.55 = (bf16[2,576,256]{2,1,0:T(8,128)(2,1)}, bf16[2,576,256]{2,1,0:T(8,128)(2,1)S(1)}, u32[]{:S(2)}, u32[]{:S(2)}) collective-permute-start(bf16[2,576,256]{2,1,0:T(8,128)(2,1)} %after.100), channel_id=1, source_target_pairs={{0,8},{8,16},{16,24},{24,0},{1,9},{9,17},{17,25},{25,1},{2,10},{10... | collective-permute-start | bytes 1769480 | tf_op jit(solution)/shard_map/cond/branch_2_fun/part4_shift1/ppermute | solution.py:326
  375.4 12.6 %copy-start.28 = (bf16[2,576,256]{2,1,0:T(8,128)(2,1)}, bf16[2,576,256]{2,1,0:T(8,128)(2,1)S(1)}, u32[]{:S(2)}) copy-start(bf16[2,576,256]{2,1,0:T(8,128)(2,1)S(1)} %collective-permute-done.59.refs_1_.refs_2_.rest_10_.rest_8_) | copy-start | bytes 1769476 | tf_op jit(solution)/shard_map/cond
  387.9 0.8 copy-start.30
  388.7 0.8 copy-start.32
  389.5 26.3 %collective-permute-start.65 = (bf16[2,512,1024]{2,1,0:T(8,128)(2,1)}, bf16[2,512,1024]{2,1,0:T(8,128)(2,1)S(1)}, u32[]{:S(2)}, u32[]{:S(2)}) collective-permute-start(bf16[2,512,1024]{2,1,0:T(8,128)(2,1)} %after.110), channel_id=1, source_target_pairs={{0,1},{1,0},{2,3},{3,2},{4,5},{5,4},{6,7},{7,6},{8,9},{9,8},{10,11... | collective-permute-start | bytes 6291464 | tf_op jit(solution)/shard_map/cond/branch_2_fun/rows1/ppermute | solution.py:442
  390.1 32.3 %collective-permute-start.60 = (bf16[2,448,256]{2,1,0:T(8,128)(2,1)}, bf16[2,448,256]{2,1,0:T(8,128)(2,1)S(1)}, u32[]{:S(2)}, u32[]{:S(2)}) collective-permute-start(bf16[2,448,256]{2,1,0:T(8,128)(2,1)} %after.105), channel_id=1, source_target_pairs={{0,16},{8,24},{16,0},{24,8},{1,17},{9,25},{17,1},{25,9},{2,18},{10... | collective-permute-start | bytes 1376264 | tf_op jit(solution)/shard_map/cond/branch_2_fun/part5_shift2/ppermute | solution.py:326
  390.1 42.1 %collective-permute-start.64 = (bf16[2,448,256]{2,1,0:T(8,128)(2,1)}, bf16[2,448,256]{2,1,0:T(8,128)(2,1)S(1)}, u32[]{:S(2)}, u32[]{:S(2)}) collective-permute-start(bf16[2,448,256]{2,1,0:T(8,128)(2,1)} %after.109), channel_id=1, source_target_pairs={{0,24},{8,0},{16,8},{24,16},{1,25},{9,1},{17,9},{25,17},{2,26},{10... | collective-permute-start | bytes 1376264 | tf_op jit(solution)/shard_map/cond/branch_2_fun/part5_shift3/ppermute | solution.py:326
  392.7 39.5 %collective-permute-start.56 = (bf16[2,448,256]{2,1,0:T(8,128)(2,1)}, bf16[2,448,256]{2,1,0:T(8,128)(2,1)S(1)}, u32[]{:S(2)}, u32[]{:S(2)}) collective-permute-start(bf16[2,448,256]{2,1,0:T(8,128)(2,1)} %after.101), channel_id=1, source_target_pairs={{0,8},{8,16},{16,24},{24,0},{1,9},{9,17},{17,25},{25,1},{2,10},{10... | collective-permute-start | bytes 1376264 | tf_op jit(solution)/shard_map/cond/branch_2_fun/part5_shift1/ppermute | solution.py:326
  415.1 33.4 %collective-permute-start.68 = (bf16[2,512,1024]{2,1,0:T(8,128)(2,1)}, bf16[2,512,1024]{2,1,0:T(8,128)(2,1)}, u32[]{:S(2)}, u32[]{:S(2)}) collective-permute-start(bf16[2,512,1024]{2,1,0:T(8,128)(2,1)} %get-tuple-element.241.rest_1_), channel_id=1, source_target_pairs={{0,1},{1,0},{2,3},{3,2},{4,5},{5,4},{6,7},{7,6},{8,9},{9,8},{10,11... | collective-permute-start | bytes 6291464 | tf_op jit(solution)/shard_map/cond/branch_2_fun/rows2/ppermute | solution.py:442
  415.8 1.3 copy-start.52
  422.4 9.8 %copy-start.64 = (bf16[2,448,256]{2,1,0:T(8,128)(2,1)}, bf16[2,448,256]{2,1,0:T(8,128)(2,1)S(1)}, u32[]{:S(2)}) copy-start(bf16[2,448,256]{2,1,0:T(8,128)(2,1)S(1)} %collective-permute-done.60.rest_4_) | copy-start | bytes 1376260 | tf_op jit(solution)/shard_map/cond
  432.2 0.8 copy-start.65
  432.2 0.9 copy-start.66
  446.2 7.7 %collective-permute-start.67 = (bf16[2,512,1024]{2,1,0:T(8,128)(2,1)}, bf16[2,512,1024]{2,1,0:T(8,128)(2,1)S(1)}, u32[]{:S(2)}, u32[]{:S(2)}) collective-permute-start(bf16[2,512,1024]{2,1,0:T(8,128)(2,1)} %get-tuple-element.243.rest_1_), channel_id=1, source_target_pairs={{0,1},{1,0},{2,3},{3,2},{4,5},{5,4},{6,7},{7,6},{8,9},{9,8},{10,11... | collective-permute-start | bytes 6291464 | tf_op jit(solution)/shard_map/cond/branch_2_fun/rows3/ppermute | solution.py:442
  453.9 1.3 copy-start.58

commit v7 on v5

--- a/solution.py
+++ b/solution.py
@@ -13,7 +13,8 @@
 TAPS = 12
 GROUP = 9
 BLOCK = 16
-PARTS = (1, 3)
+PARTS = (1, 4)
+RUNS = (1, 1, 1, 1)
 SPREAD = BLOCK + 1
 VMEM = 60 * 1024 * 1024
 COST = pl.CostEstimate(flops=1024, bytes_accessed=1024, transcendentals=0)
@@ -39,10 +40,12 @@
 
 
 def front_kernel(
-    splits, owners, turned, tail, me_ref, keep_ref, hist_ref, volts_ref, window_ref, table_ref, *rest
+    runs, owners, turned, tail, me_ref, keep_ref, hist_ref, volts_ref, window_ref, table_ref, *rest
 ):
+    splits = len(runs)
     outs, power_ref = rest[: owners * splits], rest[owners * splits]
     tail_ref = rest[owners * splits + 1] if tail else None
+    homes = [(q, place) for q, run in enumerate(runs) for place in range(run)]
     ring, filt, spread = rest[-3:]
     step = pl.program_id(0)
     now = lax.rem(step, 2)
@@ -110,8 +113,8 @@
     power = [jnp.zeros((BLOCK, 128), jnp.float32) for _ in range(tiles)]
     for d in range(owners):
         for j in range(groups):
-            out = outs[d * splits + j] if splits > 1 else outs[d]
-            place = 0 if splits > 1 else j
+            q, place = homes[j]
+            out = outs[d * splits + q]
 
             def channel(f, power, d=d, j=j, out=out, place=place):
                 keep = keep_ref[(d * groups + j) * GROUP + f]
@@ -131,20 +134,17 @@
         power_ref[:, tile * 128 : (tile + 1) * 128] += power[tile]
 
 
-def front(volts, hist, first, steps, splits, owners, keep, me, window, table, tail):
+def front(volts, hist, first, steps, runs, owners, keep, me, window, table, tail):
     inputs = volts.shape[2]
     span = BLOCK * SUBBAND_COUNT
-    groups = SUBBAND_COUNT // owners // GROUP
-    each = groups // splits
     frames = steps * BLOCK
-    outs = [
-        jax.ShapeDtypeStruct((each, 2, GROUP, frames, inputs), jnp.bfloat16)
-        for _ in range(owners * splits)
-    ]
-    out_specs = [
-        pl.BlockSpec((each, 2, GROUP, BLOCK, inputs), lambda s, me: (0, 0, 0, s, 0))
-        for _ in range(owners * splits)
-    ]
+    outs, out_specs = [], []
+    for _ in range(owners):
+        for run in runs:
+            outs.append(jax.ShapeDtypeStruct((run, 2, GROUP, frames, inputs), jnp.bfloat16))
+            out_specs.append(
+                pl.BlockSpec((run, 2, GROUP, BLOCK, inputs), lambda s, me: (0, 0, 0, s, 0))
+            )
     outs.append(jax.ShapeDtypeStruct((BLOCK, inputs), jnp.float32))
     out_specs.append(pl.BlockSpec((BLOCK, inputs), lambda s, me: (0, 0)))
     kept = (TAPS - 1) * SUBBAND_COUNT
@@ -157,7 +157,7 @@
     else:
         hist_spec, turned = pl.BlockSpec((2, kept, inputs), lambda s, me: (0, 0, 0)), True
     result = pl.pallas_call(
-        functools.partial(front_kernel, splits, owners, turned, tail),
+        functools.partial(front_kernel, runs, owners, turned, tail),
         grid_spec=pltpu.PrefetchScalarGridSpec(
             num_scalar_prefetch=1,
             grid=(steps,),
@@ -180,7 +180,7 @@
         cost_estimate=COST,
         name="front",
     )(me, keep, hist, volts, window, table)
-    count = owners * splits
+    count = owners * len(runs)
     return result[:count], result[count], result[count + 1] if tail else None
 
 
@@ -278,17 +278,21 @@
 
 def equalize_kernel(rows_ref, columns_ref, mine_ref, theirs_ref, *rest):
     out_ref = rest[-1]
-    scale = rows_ref[...] * columns_ref[...]
-    for part in range(2):
-        total = mine_ref[part] + theirs_ref[part].astype(jnp.float32)
-        out_ref[0, part] = total * scale
+    rows = rows_ref.shape[1]
+    by_row = jnp.broadcast_to(rows_ref[...], (rows, rows)).T
+    for at in range(0, columns_ref.shape[1], rows):
+        columns = slice(at, at + rows)
+        scale = by_row * columns_ref[:, columns]
+        for part in range(2):
+            total = mine_ref[part, :, columns] + theirs_ref[part, :, columns].astype(jnp.float32)
+            out_ref[0, part, :, columns] = total * scale
 
 
 def equalize(row_scales, column_scales, mine, theirs, out, group, groups, waits):
     rows, columns = mine.shape[1:]
-    block = rows // 4
+    block = 128
     specs = [
-        pl.BlockSpec((block, 1), lambda r: (r, 0)),
+        pl.BlockSpec((1, block), lambda r: (0, r)),
         pl.BlockSpec((1, columns), lambda r: (0, 0)),
         pl.BlockSpec((2, block, columns), lambda r: (0, r, 0)),
         pl.BlockSpec((2, block, columns), lambda r: (0, r, 0)),
@@ -353,6 +357,10 @@
     window = jnp.asarray(np.ascontiguousarray(window))
     spot = jnp.reshape(me, (1,)).astype(jnp.int32)
 
+    if groups != sum(RUNS):
+        runs = (1,) * groups
+    else:
+        runs = RUNS
     parts, arrived, flat, out = [], [], [], None
 
     def send(n, waits):
@@ -371,7 +379,7 @@
     for size in PARTS:
         end -= size
         spectra, part_power, tail = front(
-            volts, None, end, size, 1, owners, keep_ahead, spot, window, table, halo is None
+            volts, None, end, size, (groups,), owners, keep_ahead, spot, window, table, halo is None
         )
         if tail is not None:
             halo = tail
@@ -382,12 +390,16 @@
     with jax.named_scope("halo"):
         halo = passed_on(halo)
     spectra, part_power, _ = front(
-        volts, halo, 0, end, groups, owners, keep_ahead, spot, window, table, False
+        volts, halo, 0, end, runs, owners, keep_ahead, spot, window, table, False
     )
     power.append(part_power)
-    spectra = [x.reshape(1, 2, GROUP * end * BLOCK, inputs) for x in spectra]
-    for j in range(groups):
-        parts.append([spectra[d * groups + j] for d in range(owners)])
+    for q, run in enumerate(runs):
+        parts.append(
+            [
+                spectra[d * len(runs) + q].reshape(run, 2, GROUP * end * BLOCK, inputs)
+                for d in range(owners)
+            ]
+        )
 
     local = jnp.sum(sum(power), axis=0)
     total = lax.psum(local, ("band", "tm"))
@@ -400,7 +412,7 @@
     row_scales = lax.dynamic_slice_in_dim(scales, half * per_half, per_half, 0)
 
     column_scales = scales[None, :]
-    row_scales = [(row_scales / denom[j])[:, None] for j in range(groups)]
+    row_scales = [(row_scales / denom[j])[None, :] for j in range(groups)]
 
     place = jnp.stack([me, 1 - half, half]).astype(jnp.int32)
     shared = len(PARTS)
@@ -408,9 +420,12 @@
         with jax.named_scope(f"rows{j}"):
             return lax.ppermute(theirs, "tm", [(0, 1), (1, 0)])
 
+    homes = [(q, at) for q, run in enumerate(runs) for at in range(run)]
+
     def multiply(j, place, dtypes, sums=(), earlier=(), begin=0, end=shared + 1):
-        pieces = arrived[:shared] + arrived[shared + j : shared + j + 1]
-        picks = (j,) * shared + (0,)
+        q, at = homes[j]
+        pieces = arrived[:shared] + arrived[shared + q : shared + q + 1]
+        picks = (j,) * shared + (at,)
         return correlate(place, pieces[begin:end], picks[begin:end], dtypes, sums, earlier)
 
     both = [jnp.bfloat16, jnp.float32]
@@ -418,25 +433,31 @@
     for n in range(1, shared):
         send(n, {d: [last_spectra, arrived[0][2]] for d in range(1, owners) if d != 2})
     send(shared, {owners - 1: [column_scales]})
-    waiting = None
-    for j in range(groups - 1):
-        waits = {}
-        if j == 0:
-            partial = multiply(groups - 1, place, [jnp.float32] * 2, end=shared)
-            waits = {owners - 1: partial}
-        send(shared + j + 1, waits)
-        theirs, mine = multiply(j, place, both)
-        if waiting is not None:
-            out = equalize(*waiting, out, j - 1, groups, [theirs])
-        if j + 2 < groups:
-            theirs = after(theirs, *arrived[shared + j + 1][1:])
-        theirs = to_other(j, theirs)
-        waiting = (row_scales[j], column_scales, mine, theirs)
+    partial = multiply(groups - 1, place, [jnp.float32] * 2, end=shared)
+    waiting = []
+
+    def settle(out, earlier):
+        for j, mine, theirs in waiting:
+            out = equalize(row_scales[j], column_scales, mine, theirs, out, j, groups, earlier)
+        waiting.clear()
+        return out
+
+    done = 0
+    for q, run in enumerate(runs[:-1]):
+        send(shared + q + 1, {owners - 1: partial} if q == 0 else {})
+        results = [multiply(j, place, both) for j in range(done, done + run)]
+        if waiting:
+            out = settle(out, [x[0] for x in results])
+        for j, (theirs, mine) in enumerate(results, done):
+            if q + 2 < len(runs):
+                theirs = after(theirs, *arrived[shared + q + 1][1:])
+            waiting.append((j, mine, to_other(j, theirs)))
+        done += run
     j = groups - 1
-    theirs, mine = multiply(j, place, both, partial, [out], begin=shared)
-    out = equalize(*waiting, out, groups - 2, groups, [theirs])
-    theirs = to_other(j, theirs)
-    out = equalize(row_scales[j], column_scales, mine, theirs, out, j, groups, [])
+    theirs, mine = multiply(j, place, both, partial, [] if out is None else [out], begin=shared)
+    out = settle(out, [theirs])
+    waiting.append((j, mine, to_other(j, theirs)))
+    out = settle(out, [])
     return out[None]
 
 
@@ -508,6 +529,7 @@
         and lax.axis_size("tm") == 2
         and frames % BLOCK == 0
         and SUBBAND_COUNT // owners // GROUP > 1
+        and owners * volts.shape[2] // 2 % 128 == 0
         and frames // BLOCK > sum(PARTS)
     )
     return (pipelined if fits else plain)(volts, flagged)

time: 467 us -> 462 us (0.989)
  blocking collectives: 112 us -> 131 us
  waiting for transfers between devices: 133 us -> 114 us
    ppermute x18, waiting for transfers between devices: 133 us -> 114 us  [shift(): lax.ppermute(value, 'station', [(s, (s + d) % count) for s in range(count)])]
    all_gather x1, blocking collectives: 98.3 us -> 117 us  [pipelined(): scales = lax.all_gather(scale, 'station', axis=0, tiled=True)]
    unnamed x41 -> x45, local copies, waits for them, and re-layouts: 10.2 us -> 12 us
  transfers between devices with their start and end apart: 23 -> 23, of which waited for: 12 -> 10; matrix products, arithmetic and copies ran while one was open for 2% -> 1% of each run, Pallas kernels for 34% -> 34%
where the time goes in v7:
time: 462 us; the launch traced here: 461 us
  Pallas kernels  176 us (38%)
  blocking collectives  131 us (28%)
  waiting for transfers between devices  114 us (25%)
  starting transfers between devices  21.5 us (5%)
  local copies, waits for them, and re-layouts  13.4 us (3%)
  other arithmetic  4.71 us (1%)
    all_gather x1, blocking collectives, pipelined(): scales = lax.all_gather(scale, 'station', axis=0, tiled=True)  117 us
    ppermute x18, waiting for transfers between devices, shift(): lax.ppermute(value, 'station', [(s, (s + d) % count) for s in range(count)])  114 us
    pallas_call x3, Pallas kernels, front(): pl.pallas_call(functools.partial(front_kernel, runs, owners, turned, tail...  82.1 us
    pallas_call x5, Pallas kernels, correlate(): pl.pallas_call(functools.partial(correlate_kernel, owners, picks, outs, l...  72.7 us
    pallas_call x4, Pallas kernels, equalize(): pl.pallas_call(equalize_kernel, grid=(rows // block,), out_shape=jax.Shap...  21.1 us
    ppermute x18, starting transfers between devices, shift(): lax.ppermute(value, 'station', [(s, (s + d) % count) for s in range(count)])  15.4 us
    psum x1, blocking collectives, pipelined(): total = lax.psum(local, ('band', 'tm'))  14.2 us
    unnamed x45, local copies, waits for them, and re-layouts  12 us
  transfers between devices with their start and end apart: 23, of which 10 were waited for; matrix products, arithmetic and copies ran while one was open for 1% of the time, Pallas kernels for 34%

profile of v7, /device:TPU:11, one launch (start us, length us, event | category | flops | bytes accessed | tf_op | source)
XLA Modules:
  0.0 461.1 jit_solution(18061450277247131794)
XLA Ops:
  0.0 0.8 copy.24
  1.6 13.9 %front.3 = (bf16[4,2,9,16,256]{4,3,2,1,0:T(8,128)(2,1)}, bf16[4,2,9,16,256]{4,3,2,1,0:T(8,128)(2,1)}, bf16[4,2,9,16,256]{4,3,2,1,0:T(8,128)(2,1)}, bf16[4,2,9,16...) custom-call(s32[1]{0:T(128)} %bitcast.me_ref, f32[144]{0:T(256)} %dynamic_slice.14.keep_ref, ...), custom_call_target="tpu_custom_call" | custom-call | flops 1024 | bytes 1024 | tf_op jit(solution)/shard_map/front/pallas_call | solution.py:159
  15.5 1.3 collective-permute-start
  16.8 1.3 collective-permute-start.1
  18.2 1.1 collective-permute-start.2
  19.3 1.4 collective-permute-start.3
  20.7 38.6 %front.4 = (bf16[4,2,9,64,256]{4,3,2,1,0:T(8,128)(2,1)}, bf16[4,2,9,64,256]{4,3,2,1,0:T(8,128)(2,1)}, bf16[4,2,9,64,256]{4,3,2,1,0:T(8,128)(2,1)}, bf16[4,2,9,64,256]{4,3,2,1,0:T(8,128)(2,1)}, f32[16,256]{1,0:T(8,128)}) custom-call(s32[1]{0:T(128)} %bitcast.me_ref, f32[144]{0:T(256)} %dynamic_slice.14.keep_ref, bf16[2,1,256,18432]{3,2,1,0:T(8,128)(2,1)} %volts_ref.5, ...), custom_call_target="tpu_custom_call" | custom-call | flops 1024 | bytes 1024 | tf_op jit(solution)/shard_map/front/pallas_call | solution.py:159
  59.3 29.6 %front.5 = (bf16[1,2,9,48,256]{4,3,2,1,0:T(8,128)(2,1)}, bf16[1,2,9,48,256]{4,3,2,1,0:T(8,128)(2,1)}, bf16[1,2,9,48,256]{4,3,2,1,0:T(8,128)(2,1)}, bf16[1,2,9,48...) custom-call(s32[1]{0:T(128)} %bitcast.me_ref, ...), custom_call_target="tpu_custom_call" | custom-call | flops 1024 | bytes 1024 | tf_op jit(solution)/shard_map/front/pallas_call | solution.py:159
  89.0 28.3 %collective-permute-done.2.refs_2_.rest_2_ = bf16[4,2,144,256]{3,2,1,0:T(8,128)(2,1)S(1)} collective-permute-done((bf16[4,2,144,256]{3,2,1,0:T(8,128)(2,1)}, bf16[4,2,144,256]{3,2,1,0:T(8,128)(2,1)S(1)}, u32[]{:S(2)}, u32[]{:S(2)}) %collective-permute-start.2) | collective-permute-done | bytes 589856 | tf_op jit(solution)/shard_map/part0_shift2/ppermute | solution.py:323
  117.3 0.8 copy-done.1
  118.1 3.7 collective-permute-done.3.refs_3_.rest_3_
  123.2 14.2 %psum.7 = f32[256]{0:T(256)S(1)} all-reduce(f32[256]{0:T(256)S(1)} %add_reduce_fusion), channel_id=1, replica_groups=mesh['station'=4,'band'=4,'tm'=2] {'band','tm'}, use_global_device_ids=true, to_apply=%region_2.3 | all-reduce | flops 256 | bytes 2048 | tf_op jit(solution)/shard_map/psum | solution.py:405
  137.4 33.8 %collective-permute-done.5.rest_6_.refs_1_ = bf16[4,2,576,256]{3,2,1,0:T(8,128)(2,1)S(1)} collective-permute-done((bf16[4,2,576,256]{3,2,1,0:T(8,128)(2,1)}, bf16[4,2,576,256]{3,2,1,0:T(8,128)(2,1)S(1)}, u32[]{:S(2)}, u32[]{:S(2)}) %collective-permute-start.5) | collective-permute-done | bytes 2359328 | tf_op jit(solution)/shard_map/part1_shift2/ppermute | solution.py:323
  171.2 1.5 copy-done
  172.7 3.5 collective-permute-start.11
  176.2 116.9 %all-gather = f32[4,1,256]{2,1,0:T(1,128)} all-gather(f32[1,1,256]{2,1,0:T(1,128)S(1)} %bitcast.78), channel_id=1, replica_groups=mesh['station'=4,'band'=4,'tm'=2] {'station'}, dimensions={0}, use_global_device_ids=true | all-gather | bytes 5120 | tf_op jit(solution)/shard_map/all_gather | solution.py:407
  293.1 1.6 collective-permute-start.7
  295.4 0.8 copy-done.12
  296.1 1.3 collective-permute-start.12
  297.4 12.8 %correlate.5 = (f32[2,512,1024]{2,1,0:T(8,128)}, f32[2,512,1024]{2,1,0:T(8,128)}) custom-call(s32[3]{0:T(128)} %pad_add_fusion.place_ref, bf16[4,2,144,256]{3,2,1,0:T(8,128)(2,1)} %bitcast.44, bf16[4,2,144,256]{3,2,1,0:T(8,128)(2,1)} %copy-done.2, bf16[4,2,144,256]{3,2,1,0:T(8,128)(2,1)} %copy-done.1, ...), custom_call_target="tpu_custom_call" | custom-call | flops 1024 | bytes 1024 | tf_op jit(solution)/shard_map/correlate/pallas_call | solution.py:260
  310.3 0.8 copy-done.13
  311.2 4.4 collective-permute-done.15.refs_3_.rest_11_
  315.6 0.8 copy-done.14
  316.4 16.0 %correlate.7 = (bf16[2,512,1024]{2,1,0:T(8,128)(2,1)}, f32[2,512,1024]{2,1,0:T(8,128)}) custom-call(s32[3]{0:T(128)} %pad_add_fusion.place_ref, bf16[4,2,144,256]{3,2,1,0:T(8,128)(2,1)} %bitcast.45, bf16[4,2,144,256]{3,2,1,0:T(8,128)(2,1)} %copy-done.2, bf16[4,2,144,256]{3,2,1,0:T(8,128)(2,1)} %copy-done.1, ...), custom_call_target="tpu_custom_call" | custom-call | flops 1024 | bytes 1024 | tf_op jit(solution)/shard_map/correlate/pallas_call | solution.py:260
  332.4 2.6 collective-permute-done.12.refs_1_.rest_10_.refs_2_
  335.0 14.9 %collective-permute-done.8.refs_1_.rest_9_ = bf16[1,2,432,256]{3,2,1,0:T(8,128)(2,1)S(1)} collective-permute-done((bf16[1,2,432,256]{3,2,1,0:T(8,128)(2,1)}, bf16[1,2,432,256]{3,2,1,0:T(8,128)(2,1)S(1)}, u32[]{:S(2)}, u32[]{:S(2)}) %collective-permute-start.8) | collective-permute-done | bytes 442400 | tf_op jit(solution)/shard_map/part3_shift1/ppermute | solution.py:323
  350.0 0.8 copy-done.4
  350.9 2.9 collective-permute-start.20
  354.2 2.1 collective-permute-start.9
  356.3 1.1 collective-permute-start.17
  358.0 3.1 broadcast_divide_fusion
  361.1 16.1 %correlate.6 = (bf16[2,512,1024]{2,1,0:T(8,128)(2,1)}, f32[2,512,1024]{2,1,0:T(8,128)}) custom-call(s32[3]{0:T(128)} %pad_add_fusion.place_ref, bf16[4,2,144,256]{3,2,1,0:T(8,128)(2,1)} %bitcast.46, bf16[4,2,144,256]{3,2,1,0:T(8,128)(2,1)} %copy-done.2, bf16[4,2,144,256]{3,2,1,0:T(8,128)(2,1)} %copy-done.1, ...), custom_call_target="tpu_custom_call" | custom-call | flops 1024 | bytes 1024 | tf_op jit(solution)/shard_map/correlate/pallas_call | solution.py:260
  377.2 1.3 copy-done.10
  378.5 5.3 %equalize.4.rest_0_ = f32[4,2,512,1024]{3,2,1,0:T(8,128)} custom-call(f32[1,512]{1,0:T(1,128)} %bitcast.76, f32[1,1024]{1,0:T(1,128)} %bitcast.69, f32[2,512,1024]{2,1,0:T(8,128)} %get-tuple-element.74.mine_ref, bf16[2,512,1024]{2,1,0:T(8,128)(2,1)} %copy-done.10, bf16[2,512,1024]{2,1,0:T(8,128)(2,1)} %get-tuple-element.73.refs_0_.rest_0_), custom_call_target="tpu_custom_call" | custom-call | flops 1024 | bytes 1024 | tf_op jit(solution)/shard_map/equalize/pallas_call | solution.py:308
  383.8 8.9 %collective-permute-done.9.refs_1_.rest_9_ = bf16[1,2,432,256]{3,2,1,0:T(8,128)(2,1)S(1)} collective-permute-done((bf16[1,2,432,256]{3,2,1,0:T(8,128)(2,1)}, bf16[1,2,432,256]{3,2,1,0:T(8,128)(2,1)S(1)}, u32[]{:S(2)}, u32[]{:S(2)}) %collective-permute-start.9) | collective-permute-done | bytes 442400 | tf_op jit(solution)/shard_map/part4_shift1/ppermute | solution.py:323
  392.7 2.8 collective-permute-done.17.refs_1_.refs_3_.rest_11_
  395.5 0.8 copy-done.8
  396.9 1.4 collective-permute-start.18
  398.3 16.2 %correlate.8 = (bf16[2,512,1024]{2,1,0:T(8,128)(2,1)}, f32[2,512,1024]{2,1,0:T(8,128)}) custom-call(s32[3]{0:T(128)} %pad_add_fusion.place_ref, bf16[4,2,144,256]{3,2,1,0:T(8,128)(2,1)} %bitcast.47, bf16[4,2,144,256]{3,2,1,0:T(8,128)(2,1)} %copy-done.2, bf16[4,2,144,256]{3,2,1,0:T(8,128)(2,1)} %copy-done.1, ...), custom_call_target="tpu_custom_call" | custom-call | flops 1024 | bytes 1024 | tf_op jit(solution)/shard_map/correlate/pallas_call | solution.py:260
  414.5 0.7 collective-permute-start.22
  415.2 1.3 copy-done.9
  416.5 5.3 %equalize.5.rest_6_.rest_0_ = f32[4,2,512,1024]{3,2,1,0:T(8,128)} custom-call(f32[1,512]{1,0:T(1,128)} %bitcast.75, f32[1,1024]{1,0:T(1,128)} %bitcast.70, f32[2,512,1024]{2,1,0:T(8,128)} %get-tuple-element.72.mine_ref, bf16[2,512,1024]{2,1,0:T(8,128)(2,1)} %copy-done.9, f32[4,2,512,1024]{3,2,1,0:T(8,128)} %equalize.4.rest_0_, ...), custom_call_target="tpu_custom_call", output_to_operand_aliasing={{}: (4, {})} | custom-call | flops 1024 | bytes 1024 | tf_op jit(solution)/shard_map/equalize/pallas_call | solution.py:308
  421.8 13.7 %collective-permute-done.10.rest_3_ = bf16[1,2,432,256]{3,2,1,0:T(8,128)(2,1)S(1)} collective-permute-done((bf16[1,2,432,256]{3,2,1,0:T(8,128)(2,1)}, bf16[1,2,432,256]{3,2,1,0:T(8,128)(2,1)S(1)}, u32[]{:S(2)}, u32[]{:S(2)}) %collective-permute-start.10) | collective-permute-done | bytes 442400 | tf_op jit(solution)/shard_map/part5_shift1/ppermute | solution.py:323
  436.2 0.7 copy-done.17
  436.9 11.6 %correlate.9 = (bf16[2,512,1024]{2,1,0:T(8,128)(2,1)}, f32[2,512,1024]{2,1,0:T(8,128)}) custom-call(s32[3]{0:T(128)} %pad_add_fusion.place_ref, f32[2,512,1024]{2,1,0:T(8,128)} %get-tuple-element.56.refs_1_.rest_0_, f32[2,512,1024]{2,1,0:T(8,128)} %get-tuple-element.57.refs_2_.rest_1_, bf16[1,2,432,256]{3,2,1,0:T(8,128)(2,1)} %bitcast.64, ...), custom_call_target="tpu_custom_call" | custom-call | flops 1024 | bytes 1024 | tf_op jit(solution)/shard_map/correlate/pallas_call | solution.py:260
  449.2 5.3 %equalize.6.rest_0_ = f32[4,2,512,1024]{3,2,1,0:T(8,128)} custom-call(f32[1,512]{1,0:T(1,128)} %bitcast.74, f32[1,1024]{1,0:T(1,128)} %bitcast.71, f32[2,512,1024]{2,1,0:T(8,128)} %get-tuple-element.80.mine_ref, bf16[2,512,1024]{2,1,0:T(8,128)(2,1)} %collective-permute-done.22.theirs_ref, ...), custom_call_target="tpu_custom_call", output_to_operand_aliasing={{}: (4, {})} | custom-call | flops 1024 | bytes 1024 | tf_op jit(solution)/shard_map/equalize/pallas_call | solution.py:308
  454.5 1.4 copy-done.11
  455.9 5.3 %equalize.7 = f32[4,2,512,1024]{3,2,1,0:T(8,128)} custom-call(f32[1,512]{1,0:T(1,128)} %bitcast.77, f32[1,1024]{1,0:T(1,128)} %bitcast.72, f32[2,512,1024]{2,1,0:T(8,128)} %get-tuple-element.78.mine_ref, bf16[2,512,1024]{2,1,0:T(8,128)(2,1)} %copy-done.11, f32[4,2,512,1024]{3,2,1,0:T(8,128)} %equalize.6.rest_0_), custom_call_target="tpu_custom_call", output_to_operand_aliasing={{}: (4, {})} | custom-call | flops 1024 | bytes 1024 | tf_op jit(solution)/shard_map/equalize/pallas_call | solution.py:308
  (88 shorter events, 5.8 us)
Async XLA Ops:
  15.5 43.8 %collective-permute-start = (bf16[2,1584,256]{2,1,0:T(8,128)(2,1)}, bf16[2,1584,256]{2,1,0:T(8,128)(2,1)}, u32[]{:S(2)}, u32[]{:S(2)}) collective-permute-start(bf16[2,1584,256]{2,1,0:T(8,128)(2,1)} %get-tuple-element.45), channel_id=1, source_target_pairs={{0,1},{2,3},{4,5},{6,7},{8,9},{10,11},{12,13},{14,15},{16,17},{18,... | collective-permute-start | bytes 4866056 | tf_op jit(solution)/shard_map/halo/ppermute | solution.py:328
  16.8 72.2 %collective-permute-start.1 = (bf16[4,2,144,256]{3,2,1,0:T(8,128)(2,1)}, bf16[4,2,144,256]{3,2,1,0:T(8,128)(2,1)S(1)}, u32[]{:S(2)}, u32[]{:S(2)}) collective-permute-start(bf16[4,2,144,256]{3,2,1,0:T(8,128)(2,1)} %bitcast.83), channel_id=1, source_target_pairs={{0,8},{8,16},{16,24},{24,0},{1,9},{9,17},{17,25},{25,1},{2,10},{10... | collective-permute-start | bytes 1769480 | tf_op jit(solution)/shard_map/part0_shift1/ppermute | solution.py:323
  18.2 99.1 %collective-permute-start.2 = (bf16[4,2,144,256]{3,2,1,0:T(8,128)(2,1)}, bf16[4,2,144,256]{3,2,1,0:T(8,128)(2,1)S(1)}, u32[]{:S(2)}, u32[]{:S(2)}) collective-permute-start(bf16[4,2,144,256]{3,2,1,0:T(8,128)(2,1)} %bitcast.82), channel_id=1, source_target_pairs={{0,16},{8,24},{16,0},{24,8},{1,17},{9,25},{17,1},{25,9},{2,18},{10... | collective-permute-start | bytes 1769480 | tf_op jit(solution)/shard_map/part0_shift2/ppermute | solution.py:323
  19.3 102.5 %collective-permute-start.3 = (bf16[4,2,144,256]{3,2,1,0:T(8,128)(2,1)}, bf16[4,2,144,256]{3,2,1,0:T(8,128)(2,1)}, u32[]{:S(2)}, u32[]{:S(2)}) collective-permute-start(bf16[4,2,144,256]{3,2,1,0:T(8,128)(2,1)} %bitcast.81), channel_id=1, source_target_pairs={{0,24},{8,0},{16,8},{24,16},{1,25},{9,1},{17,9},{25,17},{2,26},{10... | collective-permute-start | bytes 1769480 | tf_op jit(solution)/shard_map/part0_shift3/ppermute | solution.py:323
  59.2 112.0 %collective-permute-start.5 = (bf16[4,2,576,256]{3,2,1,0:T(8,128)(2,1)}, bf16[4,2,576,256]{3,2,1,0:T(8,128)(2,1)S(1)}, u32[]{:S(2)}, u32[]{:S(2)}) collective-permute-start(bf16[4,2,576,256]{3,2,1,0:T(8,128)(2,1)} %bitcast.80), channel_id=1, source_target_pairs={{0,16},{8,24},{16,0},{24,8},{1,17},{9,25},{17,1},{25,9},{2,18},{10... | collective-permute-start | bytes 7077896 | tf_op jit(solution)/shard_map/part1_shift2/ppermute | solution.py:323
  89.0 28.3 %copy-start.2 = (bf16[4,2,144,256]{3,2,1,0:T(8,128)(2,1)}, bf16[4,2,144,256]{3,2,1,0:T(8,128)(2,1)S(1)}, u32[]{:S(2)}) copy-start(bf16[4,2,144,256]{3,2,1,0:T(8,128)(2,1)S(1)} %collective-permute-done.1.refs_3_.rest_1_) | copy-start | bytes 1769476
  117.3 0.8 copy-start.1
  118.1 174.9 %collective-permute-start.4 = (bf16[4,2,576,256]{3,2,1,0:T(8,128)(2,1)}, bf16[4,2,576,256]{3,2,1,0:T(8,128)(2,1)}, u32[]{:S(2)}, u32[]{:S(2)}) collective-permute-start(bf16[4,2,576,256]{3,2,1,0:T(8,128)(2,1)} %after.16), channel_id=1, source_target_pairs={{0,8},{8,16},{16,24},{24,0},{1,9},{9,17},{17,25},{25,1},{2,10},{10... | collective-permute-start | bytes 7077896 | tf_op jit(solution)/shard_map/part1_shift1/ppermute | solution.py:323
  121.8 1.3 copy-start.19
  121.8 1.3 copy-start.20
  121.8 1.3 copy-start.21
  121.8 172.9 %collective-permute-start.6 = (bf16[4,2,576,256]{3,2,1,0:T(8,128)(2,1)}, bf16[4,2,576,256]{3,2,1,0:T(8,128)(2,1)}, u32[]{:S(2)}, u32[]{:S(2)}) collective-permute-start(bf16[4,2,576,256]{3,2,1,0:T(8,128)(2,1)} %after.17), channel_id=1, source_target_pairs={{0,24},{8,0},{16,8},{24,16},{1,25},{9,1},{17,9},{25,17},{2,26},{10... | collective-permute-start | bytes 7077896 | tf_op jit(solution)/shard_map/part1_shift3/ppermute | solution.py:323
  171.2 1.5 copy-start
  172.7 122.7 %collective-permute-start.11 = (bf16[1,2,432,256]{3,2,1,0:T(8,128)(2,1)}, bf16[1,2,432,256]{3,2,1,0:T(8,128)(2,1)S(1)}, u32[]{:S(2)}, u32[]{:S(2)}) collective-permute-start(bf16[1,2,432,256]{3,2,1,0:T(8,128)(2,1)} %after.22), channel_id=1, source_target_pairs={{0,16},{8,24},{16,0},{24,8},{1,17},{9,25},{17,1},{25,9},{2,18},{10... | collective-permute-start | bytes 1327112 | tf_op jit(solution)/shard_map/part2_shift2/ppermute | solution.py:323
  293.1 17.2 %collective-permute-start.7 = (bf16[1,2,432,256]{3,2,1,0:T(8,128)(2,1)}, bf16[1,2,432,256]{3,2,1,0:T(8,128)(2,1)S(1)}, u32[]{:S(2)}, u32[]{:S(2)}) collective-permute-start(bf16[1,2,432,256]{3,2,1,0:T(8,128)(2,1)} %after.18), channel_id=1, source_target_pairs={{0,8},{8,16},{16,24},{24,0},{1,9},{9,17},{17,25},{25,1},{2,10},{10... | collective-permute-start | bytes 1327112 | tf_op jit(solution)/shard_map/part2_shift1/ppermute | solution.py:323
  294.7 20.9 %collective-permute-start.15 = (bf16[1,2,432,256]{3,2,1,0:T(8,128)(2,1)}, bf16[1,2,432,256]{3,2,1,0:T(8,128)(2,1)S(1)}, u32[]{:S(2)}, u32[]{:S(2)}) collective-permute-start(bf16[1,2,432,256]{3,2,1,0:T(8,128)(2,1)} %after.26), channel_id=1, source_target_pairs={{0,24},{8,0},{16,8},{24,16},{1,25},{9,1},{17,9},{25,17},{2,26},{10... | collective-permute-start | bytes 1327112 | tf_op jit(solution)/shard_map/part2_shift3/ppermute | solution.py:323
  295.4 0.8 copy-start.12
  296.1 38.9 %collective-permute-start.12 = (bf16[1,2,432,256]{3,2,1,0:T(8,128)(2,1)}, bf16[1,2,432,256]{3,2,1,0:T(8,128)(2,1)S(1)}, u32[]{:S(2)}, u32[]{:S(2)}) collective-permute-start(bf16[1,2,432,256]{3,2,1,0:T(8,128)(2,1)} %after.23), channel_id=1, source_target_pairs={{0,16},{8,24},{16,0},{24,8},{1,17},{9,25},{17,1},{25,9},{2,18},{10... | collective-permute-start | bytes 1327112 | tf_op jit(solution)/shard_map/part3_shift2/ppermute | solution.py:323
  310.3 0.8 copy-start.13
  311.0 38.9 %collective-permute-start.8 = (bf16[1,2,432,256]{3,2,1,0:T(8,128)(2,1)}, bf16[1,2,432,256]{3,2,1,0:T(8,128)(2,1)S(1)}, u32[]{:S(2)}, u32[]{:S(2)}) collective-permute-start(bf16[1,2,432,256]{3,2,1,0:T(8,128)(2,1)} %after.19), channel_id=1, source_target_pairs={{0,8},{8,16},{16,24},{24,0},{1,9},{9,17},{17,25},{25,1},{2,10},{10... | collective-permute-start | bytes 1327112 | tf_op jit(solution)/shard_map/part3_shift1/ppermute | solution.py:323
  315.6 0.8 copy-start.14
  316.4 33.5 %collective-permute-start.16 = (bf16[1,2,432,256]{3,2,1,0:T(8,128)(2,1)}, bf16[1,2,432,256]{3,2,1,0:T(8,128)(2,1)S(1)}, u32[]{:S(2)}, u32[]{:S(2)}) collective-permute-start(bf16[1,2,432,256]{3,2,1,0:T(8,128)(2,1)} %after.27), channel_id=1, source_target_pairs={{0,24},{8,0},{16,8},{24,16},{1,25},{9,1},{17,9},{25,17},{2,26},{10... | collective-permute-start | bytes 1327112 | tf_op jit(solution)/shard_map/part3_shift3/ppermute | solution.py:323
  335.0 15.0 %copy-start.3 = (bf16[1,2,432,256]{3,2,1,0:T(8,128)(2,1)}, bf16[1,2,432,256]{3,2,1,0:T(8,128)(2,1)S(1)}, u32[]{:S(2)}) copy-start(bf16[1,2,432,256]{3,2,1,0:T(8,128)(2,1)S(1)} %collective-permute-done.12.refs_1_.rest_10_.refs_2_) | copy-start | bytes 1327108
  350.0 0.8 copy-start.4
  350.0 0.9 copy-start.5
  350.9 7.2 %copy-start.18 = (f32[4,1,256]{2,1,0:T(1,128)S(1)}, f32[4,1,256]{2,1,0:T(1,128)}, u32[]{:S(2)}) copy-start(f32[4,1,256]{2,1,0:T(1,128)} %all-gather) | copy-start | bytes 12292
  350.9 26.3 %collective-permute-start.20 = (bf16[2,512,1024]{2,1,0:T(8,128)(2,1)}, bf16[2,512,1024]{2,1,0:T(8,128)(2,1)S(1)}, u32[]{:S(2)}, u32[]{:S(2)}) collective-permute-start(bf16[2,512,1024]{2,1,0:T(8,128)(2,1)} %after.31), channel_id=1, source_target_pairs={{0,1},{1,0},{2,3},{3,2},{4,5},{5,4},{6,7},{7,6},{8,9},{9,8},{10,11... | collective-permute-start | bytes 6291464 | tf_op jit(solution)/shard_map/rows0/ppermute | solution.py:421
  354.1 29.7 %collective-permute-start.13 = (bf16[1,2,432,256]{3,2,1,0:T(8,128)(2,1)}, bf16[1,2,432,256]{3,2,1,0:T(8,128)(2,1)S(1)}, u32[]{:S(2)}, u32[]{:S(2)}) collective-permute-start(bf16[1,2,432,256]{3,2,1,0:T(8,128)(2,1)} %after.24), channel_id=1, source_target_pairs={{0,16},{8,24},{16,0},{24,8},{1,17},{9,25},{17,1},{25,9},{2,18},{10... | collective-permute-start | bytes 1327112 | tf_op jit(solution)/shard_map/part4_shift2/ppermute | solution.py:323
  354.2 38.5 %collective-permute-start.9 = (bf16[1,2,432,256]{3,2,1,0:T(8,128)(2,1)}, bf16[1,2,432,256]{3,2,1,0:T(8,128)(2,1)S(1)}, u32[]{:S(2)}, u32[]{:S(2)}) collective-permute-start(bf16[1,2,432,256]{3,2,1,0:T(8,128)(2,1)} %after.20), channel_id=1, source_target_pairs={{0,8},{8,16},{16,24},{24,0},{1,9},{9,17},{17,25},{25,1},{2,10},{10... | collective-permute-start | bytes 1327112 | tf_op jit(solution)/shard_map/part4_shift1/ppermute | solution.py:323
  356.3 39.2 %collective-permute-start.17 = (bf16[1,2,432,256]{3,2,1,0:T(8,128)(2,1)}, bf16[1,2,432,256]{3,2,1,0:T(8,128)(2,1)S(1)}, u32[]{:S(2)}, u32[]{:S(2)}) collective-permute-start(bf16[1,2,432,256]{3,2,1,0:T(8,128)(2,1)} %after.28), channel_id=1, source_target_pairs={{0,24},{8,0},{16,8},{24,16},{1,25},{9,1},{17,9},{25,17},{2,26},{10... | collective-permute-start | bytes 1327112 | tf_op jit(solution)/shard_map/part4_shift3/ppermute | solution.py:323
  377.2 1.3 copy-start.10
  383.8 11.7 %copy-start.6 = (bf16[1,2,432,256]{3,2,1,0:T(8,128)(2,1)}, bf16[1,2,432,256]{3,2,1,0:T(8,128)(2,1)S(1)}, u32[]{:S(2)}) copy-start(bf16[1,2,432,256]{3,2,1,0:T(8,128)(2,1)S(1)} %collective-permute-done.13.refs_1_.refs_2_.rest_10_) | copy-start | bytes 1327108
  392.7 2.8 copy-start.7
  395.5 0.8 copy-start.8
  396.3 18.9 %collective-permute-start.19 = (bf16[2,512,1024]{2,1,0:T(8,128)(2,1)}, bf16[2,512,1024]{2,1,0:T(8,128)(2,1)S(1)}, u32[]{:S(2)}, u32[]{:S(2)}) collective-permute-start(bf16[2,512,1024]{2,1,0:T(8,128)(2,1)} %after.30), channel_id=1, source_target_pairs={{0,1},{1,0},{2,3},{3,2},{4,5},{5,4},{6,7},{7,6},{8,9},{9,8},{10,11... | collective-permute-start | bytes 6291464 | tf_op jit(solution)/shard_map/rows1/ppermute | solution.py:421
  396.8 25.0 %collective-permute-start.14 = (bf16[1,2,432,256]{3,2,1,0:T(8,128)(2,1)}, bf16[1,2,432,256]{3,2,1,0:T(8,128)(2,1)S(1)}, u32[]{:S(2)}, u32[]{:S(2)}) collective-permute-start(bf16[1,2,432,256]{3,2,1,0:T(8,128)(2,1)} %after.25), channel_id=1, source_target_pairs={{0,16},{8,24},{16,0},{24,8},{1,17},{9,25},{17,1},{25,9},{2,18},{10... | collective-permute-start | bytes 1327112 | tf_op jit(solution)/shard_map/part5_shift2/ppermute | solution.py:323
  396.8 38.6 %collective-permute-start.10 = (bf16[1,2,432,256]{3,2,1,0:T(8,128)(2,1)}, bf16[1,2,432,256]{3,2,1,0:T(8,128)(2,1)S(1)}, u32[]{:S(2)}, u32[]{:S(2)}) collective-permute-start(bf16[1,2,432,256]{3,2,1,0:T(8,128)(2,1)} %after.21), channel_id=1, source_target_pairs={{0,8},{8,16},{16,24},{24,0},{1,9},{9,17},{17,25},{25,1},{2,10},{10... | collective-permute-start | bytes 1327112 | tf_op jit(solution)/shard_map/part5_shift1/ppermute | solution.py:323
  396.9 39.2 %collective-permute-start.18 = (bf16[1,2,432,256]{3,2,1,0:T(8,128)(2,1)}, bf16[1,2,432,256]{3,2,1,0:T(8,128)(2,1)S(1)}, u32[]{:S(2)}, u32[]{:S(2)}) collective-permute-start(bf16[1,2,432,256]{3,2,1,0:T(8,128)(2,1)} %after.29), channel_id=1, source_target_pairs={{0,24},{8,0},{16,8},{24,16},{1,25},{9,1},{17,9},{25,17},{2,26},{10... | collective-permute-start | bytes 1327112 | tf_op jit(solution)/shard_map/part5_shift3/ppermute | solution.py:323
  414.5 34.7 %collective-permute-start.22 = (bf16[2,512,1024]{2,1,0:T(8,128)(2,1)}, bf16[2,512,1024]{2,1,0:T(8,128)(2,1)}, u32[]{:S(2)}, u32[]{:S(2)}) collective-permute-start(bf16[2,512,1024]{2,1,0:T(8,128)(2,1)} %get-tuple-element.77.rest_1_), channel_id=1, source_target_pairs={{0,1},{1,0},{2,3},{3,2},{4,5},{5,4},{6,7},{7,6},{8,9},{9,8},{10,11... | collective-permute-start | bytes 6291464 | tf_op jit(solution)/shard_map/rows2/ppermute | solution.py:421
  415.2 1.3 copy-start.9
  421.8 14.3 %copy-start.15 = (bf16[1,2,432,256]{3,2,1,0:T(8,128)(2,1)}, bf16[1,2,432,256]{3,2,1,0:T(8,128)(2,1)S(1)}, u32[]{:S(2)}) copy-start(bf16[1,2,432,256]{3,2,1,0:T(8,128)(2,1)S(1)} %collective-permute-done.14.rest_4_) | copy-start | bytes 1327108
  435.4 0.8 copy-start.16
  436.1 0.8 copy-start.17
  448.6 5.9 %collective-permute-start.21 = (bf16[2,512,1024]{2,1,0:T(8,128)(2,1)}, bf16[2,512,1024]{2,1,0:T(8,128)(2,1)S(1)}, u32[]{:S(2)}, u32[]{:S(2)}) collective-permute-start(bf16[2,512,1024]{2,1,0:T(8,128)(2,1)} %get-tuple-element.79.rest_1_), channel_id=1, source_target_pairs={{0,1},{1,0},{2,3},{3,2},{4,5},{5,4},{6,7},{7,6},{8,9},{9,8},{10,11... | collective-permute-start | bytes 6291464 | tf_op jit(solution)/shard_map/rows3/ppermute | solution.py:421
  454.5 1.4 copy-start.11

commit v8 on v7

--- a/solution.py
+++ b/solution.py
@@ -16,7 +16,7 @@
 PARTS = (1, 4)
 RUNS = (1, 1, 1, 1)
 SPREAD = BLOCK + 1
-VMEM = 60 * 1024 * 1024
+VMEM = 62 * 1024 * 1024
 COST = pl.CostEstimate(flops=1024, bytes_accessed=1024, transcendentals=0)
 IN_FLIGHT = 3
 
@@ -432,7 +432,7 @@
     last_spectra = parts[shared][0]
     for n in range(1, shared):
         send(n, {d: [last_spectra, arrived[0][2]] for d in range(1, owners) if d != 2})
-    send(shared, {owners - 1: [column_scales]})
+    send(shared, {min(2, owners - 1): [column_scales]})
     partial = multiply(groups - 1, place, [jnp.float32] * 2, end=shared)
     waiting = []
 

time: 462 us -> 464 us (level)
  blocking collectives: 131 us -> 153 us
  waiting for transfers between devices: 114 us -> 99.8 us
    all_gather x1, blocking collectives: 117 us -> 139 us  [pipelined(): scales = lax.all_gather(scale, 'station', axis=0, tiled=True)]
    ppermute x18, waiting for transfers between devices: 114 us -> 99.8 us  [shift(): lax.ppermute(value, 'station', [(s, (s + d) % count) for s in range(count)])]
    unnamed x45 -> x39, local copies, waits for them, and re-layouts: 12 us -> 7.84 us
  transfers between devices with their start and end apart: 23 -> 23, of which waited for: 10 -> 11; matrix products, arithmetic and copies ran while one was open for 1% -> 1% of each run, Pallas kernels for 34% -> 34%
where the time goes in v8:
time: 464 us; the launch traced here: 463 us
  Pallas kernels  176 us (38%)
  blocking collectives  153 us (33%)
  waiting for transfers between devices  99.8 us (22%)
  starting transfers between devices  19.5 us (4%)
  local copies, waits for them, and re-layouts  9.32 us (2%)
  other arithmetic  4.72 us (1%)
    all_gather x1, blocking collectives, pipelined(): scales = lax.all_gather(scale, 'station', axis=0, tiled=True)  139 us
    ppermute x18, waiting for transfers between devices, shift(): lax.ppermute(value, 'station', [(s, (s + d) % count) for s in range(count)])  99.8 us
    pallas_call x3, Pallas kernels, front(): pl.pallas_call(functools.partial(front_kernel, runs, owners, turned, tail...  82.2 us
    pallas_call x5, Pallas kernels, correlate(): pl.pallas_call(functools.partial(correlate_kernel, owners, picks, outs, l...  72.7 us
    pallas_call x4, Pallas kernels, equalize(): pl.pallas_call(equalize_kernel, grid=(rows // block,), out_shape=jax.Shap...  21.1 us
    ppermute x18, starting transfers between devices, shift(): lax.ppermute(value, 'station', [(s, (s + d) % count) for s in range(count)])  15.8 us
    psum x1, blocking collectives, pipelined(): total = lax.psum(local, ('band', 'tm'))  14.2 us
  transfers between devices with their start and end apart: 23, of which 11 were waited for; matrix products, arithmetic and copies ran while one was open for 1% of the time, Pallas kernels for 34%

profile of v8, /device:TPU:11, one launch (start us, length us, event | category | flops | bytes accessed | tf_op | source)
XLA Modules:
  0.0 463.1 jit_solution(1954297412483841184)
XLA Ops:
  0.0 0.8 copy.24
  1.0 0.6 dynamic_slice.14.keep_ref
  1.6 14.0 %front.3 = (bf16[4,2,9,16,256]{4,3,2,1,0:T(8,128)(2,1)}, bf16[4,2,9,16,256]{4,3,2,1,0:T(8,128)(2,1)}, bf16[4,2,9,16,256]{4,3,2,1,0:T(8,128)(2,1)}, bf16[4,2,9,16...) custom-call(s32[1]{0:T(128)} %bitcast.me_ref, f32[144]{0:T(256)} %dynamic_slice.14.keep_ref, ...), custom_call_target="tpu_custom_call" | custom-call | flops 1024 | bytes 1024 | tf_op jit(solution)/shard_map/front/pallas_call | solution.py:159
  15.6 1.3 collective-permute-start
  16.9 1.4 collective-permute-start.1
  18.2 1.1 collective-permute-start.2
  19.3 1.4 collective-permute-start.3
  20.7 38.6 %front.4 = (bf16[4,2,9,64,256]{4,3,2,1,0:T(8,128)(2,1)}, bf16[4,2,9,64,256]{4,3,2,1,0:T(8,128)(2,1)}, bf16[4,2,9,64,256]{4,3,2,1,0:T(8,128)(2,1)}, bf16[4,2,9,64,256]{4,3,2,1,0:T(8,128)(2,1)}, f32[16,256]{1,0:T(8,128)}) custom-call(s32[1]{0:T(128)} %bitcast.me_ref, f32[144]{0:T(256)} %dynamic_slice.14.keep_ref, bf16[2,1,256,18432]{3,2,1,0:T(8,128)(2,1)} %volts_ref.5, ...), custom_call_target="tpu_custom_call" | custom-call | flops 1024 | bytes 1024 | tf_op jit(solution)/shard_map/front/pallas_call | solution.py:159
  59.4 29.7 %front.5 = (bf16[1,2,9,48,256]{4,3,2,1,0:T(8,128)(2,1)}, bf16[1,2,9,48,256]{4,3,2,1,0:T(8,128)(2,1)}, bf16[1,2,9,48,256]{4,3,2,1,0:T(8,128)(2,1)}, bf16[1,2,9,48...) custom-call(s32[1]{0:T(128)} %bitcast.me_ref, ...), custom_call_target="tpu_custom_call" | custom-call | flops 1024 | bytes 1024 | tf_op jit(solution)/shard_map/front/pallas_call | solution.py:159
  89.1 28.3 %collective-permute-done.2.refs_2_.rest_2_ = bf16[4,2,144,256]{3,2,1,0:T(8,128)(2,1)S(1)} collective-permute-done((bf16[4,2,144,256]{3,2,1,0:T(8,128)(2,1)}, bf16[4,2,144,256]{3,2,1,0:T(8,128)(2,1)S(1)}, u32[]{:S(2)}, u32[]{:S(2)}) %collective-permute-start.2) | collective-permute-done | bytes 589856 | tf_op jit(solution)/shard_map/part0_shift2/ppermute | solution.py:323
  117.3 0.8 copy-done.1
  118.2 3.7 collective-permute-done.3.refs_3_.rest_3_
  121.9 0.6 convert_reduce_fusion
  123.2 14.2 %psum.7 = f32[256]{0:T(256)S(1)} all-reduce(f32[256]{0:T(256)S(1)} %add_reduce_fusion), channel_id=1, replica_groups=mesh['station'=4,'band'=4,'tm'=2] {'band','tm'}, use_global_device_ids=true, to_apply=%region_2.3 | all-reduce | flops 256 | bytes 2048 | tf_op jit(solution)/shard_map/psum | solution.py:405
  137.3 138.7 %all-gather = f32[4,1,256]{2,1,0:T(1,128)} all-gather(f32[1,1,256]{2,1,0:T(1,128)S(1)} %bitcast.78), channel_id=1, replica_groups=mesh['station'=4,'band'=4,'tm'=2] {'station'}, dimensions={0}, use_global_device_ids=true | all-gather | bytes 5120 | tf_op jit(solution)/shard_map/all_gather | solution.py:407
  276.1 1.5 copy-done
  277.5 2.4 collective-permute-start.7
  279.9 0.6 pad_add_fusion.place_ref
  280.5 14.2 %collective-permute-done.11.refs_1_.rest_10_ = bf16[1,2,432,256]{3,2,1,0:T(8,128)(2,1)S(1)} collective-permute-done((bf16[1,2,432,256]{3,2,1,0:T(8,128)(2,1)}, bf16[1,2,432,256]{3,2,1,0:T(8,128)(2,1)S(1)}, u32[]{:S(2)}, u32[]{:S(2)}) %collective-permute-start.11) | collective-permute-done | bytes 442400 | tf_op jit(solution)/shard_map/part2_shift2/ppermute | solution.py:323
  294.8 0.8 copy-done.9
  295.6 3.1 collective-permute-start.12
  298.7 12.9 %correlate.5 = (f32[2,512,1024]{2,1,0:T(8,128)}, f32[2,512,1024]{2,1,0:T(8,128)}) custom-call(s32[3]{0:T(128)} %pad_add_fusion.place_ref, bf16[4,2,144,256]{3,2,1,0:T(8,128)(2,1)} %bitcast.44, bf16[4,2,144,256]{3,2,1,0:T(8,128)(2,1)} %copy-done.2, bf16[4,2,144,256]{3,2,1,0:T(8,128)(2,1)} %copy-done.1, ...), custom_call_target="tpu_custom_call" | custom-call | flops 1024 | bytes 1024 | tf_op jit(solution)/shard_map/correlate/pallas_call | solution.py:260
  311.6 11.7 %collective-permute-done.7.refs_1_.rest_9_ = bf16[1,2,432,256]{3,2,1,0:T(8,128)(2,1)S(1)} collective-permute-done((bf16[1,2,432,256]{3,2,1,0:T(8,128)(2,1)}, bf16[1,2,432,256]{3,2,1,0:T(8,128)(2,1)S(1)}, u32[]{:S(2)}, u32[]{:S(2)}) %collective-permute-start.7) | collective-permute-done | bytes 442400 | tf_op jit(solution)/shard_map/part2_shift1/ppermute | solution.py:323
  323.2 0.8 copy-done.10
  324.0 2.6 collective-permute-start.8
  326.6 0.6 collective-permute-done.15.refs_3_.rest_11_
  327.2 0.8 copy-done.11
  328.0 16.0 %correlate.7 = (bf16[2,512,1024]{2,1,0:T(8,128)(2,1)}, f32[2,512,1024]{2,1,0:T(8,128)}) custom-call(s32[3]{0:T(128)} %pad_add_fusion.place_ref, bf16[4,2,144,256]{3,2,1,0:T(8,128)(2,1)} %bitcast.45, bf16[4,2,144,256]{3,2,1,0:T(8,128)(2,1)} %copy-done.2, bf16[4,2,144,256]{3,2,1,0:T(8,128)(2,1)} %copy-done.1, ...), custom_call_target="tpu_custom_call" | custom-call | flops 1024 | bytes 1024 | tf_op jit(solution)/shard_map/correlate/pallas_call | solution.py:260
  344.0 7.7 %collective-permute-done.8.refs_1_.rest_9_ = bf16[1,2,432,256]{3,2,1,0:T(8,128)(2,1)S(1)} collective-permute-done((bf16[1,2,432,256]{3,2,1,0:T(8,128)(2,1)}, bf16[1,2,432,256]{3,2,1,0:T(8,128)(2,1)S(1)}, u32[]{:S(2)}, u32[]{:S(2)}) %collective-permute-start.8) | collective-permute-done | bytes 442400 | tf_op jit(solution)/shard_map/part3_shift1/ppermute | solution.py:323
  351.7 4.0 collective-permute-done.16.refs_1_.rest_11_.refs_3_
  355.7 0.8 copy-done.5
  357.4 2.2 collective-permute-start.9
  359.7 0.7 fusion.1
  360.4 3.1 broadcast_divide_fusion
  363.5 16.1 %correlate.6 = (bf16[2,512,1024]{2,1,0:T(8,128)(2,1)}, f32[2,512,1024]{2,1,0:T(8,128)}) custom-call(s32[3]{0:T(128)} %pad_add_fusion.place_ref, bf16[4,2,144,256]{3,2,1,0:T(8,128)(2,1)} %bitcast.46, bf16[4,2,144,256]{3,2,1,0:T(8,128)(2,1)} %copy-done.2, bf16[4,2,144,256]{3,2,1,0:T(8,128)(2,1)} %copy-done.1, ...), custom_call_target="tpu_custom_call" | custom-call | flops 1024 | bytes 1024 | tf_op jit(solution)/shard_map/correlate/pallas_call | solution.py:260
  379.6 5.3 %equalize.4.rest_0_ = f32[4,2,512,1024]{3,2,1,0:T(8,128)} custom-call(f32[1,512]{1,0:T(1,128)} %bitcast.76, f32[1,1024]{1,0:T(1,128)} %bitcast.69, f32[2,512,1024]{2,1,0:T(8,128)} %get-tuple-element.74.mine_ref, bf16[2,512,1024]{2,1,0:T(8,128)(2,1)} %collective-permute-done.20.theirs_ref, bf16[2,512,1024]{2,1,0:T(8,128)(2,1)} %get-tuple-element.73.refs_0_.rest_0_), custom_call_target="tpu_custom_call" | custom-call | flops 1024 | bytes 1024 | tf_op jit(solution)/shard_map/equalize/pallas_call | solution.py:308
  384.9 10.9 %collective-permute-done.9.refs_1_.rest_9_ = bf16[1,2,432,256]{3,2,1,0:T(8,128)(2,1)S(1)} collective-permute-done((bf16[1,2,432,256]{3,2,1,0:T(8,128)(2,1)}, bf16[1,2,432,256]{3,2,1,0:T(8,128)(2,1)S(1)}, u32[]{:S(2)}, u32[]{:S(2)}) %collective-permute-start.9) | collective-permute-done | bytes 442400 | tf_op jit(solution)/shard_map/part4_shift1/ppermute | solution.py:323
  395.8 3.1 collective-permute-done.17.refs_1_.refs_3_.rest_11_
  399.0 0.8 copy-done.8
  400.3 1.5 collective-permute-start.18
  401.8 16.1 %correlate.8 = (bf16[2,512,1024]{2,1,0:T(8,128)(2,1)}, f32[2,512,1024]{2,1,0:T(8,128)}) custom-call(s32[3]{0:T(128)} %pad_add_fusion.place_ref, bf16[4,2,144,256]{3,2,1,0:T(8,128)(2,1)} %bitcast.47, bf16[4,2,144,256]{3,2,1,0:T(8,128)(2,1)} %copy-done.2, bf16[4,2,144,256]{3,2,1,0:T(8,128)(2,1)} %copy-done.1, ...), custom_call_target="tpu_custom_call" | custom-call | flops 1024 | bytes 1024 | tf_op jit(solution)/shard_map/correlate/pallas_call | solution.py:260
  417.9 0.7 collective-permute-start.22
  418.5 5.3 %equalize.5.rest_6_.rest_0_ = f32[4,2,512,1024]{3,2,1,0:T(8,128)} custom-call(f32[1,512]{1,0:T(1,128)} %bitcast.75, f32[1,1024]{1,0:T(1,128)} %bitcast.70, f32[2,512,1024]{2,1,0:T(8,128)} %get-tuple-element.72.mine_ref, bf16[2,512,1024]{2,1,0:T(8,128)(2,1)} %collective-permute-done.19.theirs_ref, ...), custom_call_target="tpu_custom_call", output_to_operand_aliasing={{}: (4, {})} | custom-call | flops 1024 | bytes 1024 | tf_op jit(solution)/shard_map/equalize/pallas_call | solution.py:308
  423.8 15.1 %collective-permute-done.10.rest_3_ = bf16[1,2,432,256]{3,2,1,0:T(8,128)(2,1)S(1)} collective-permute-done((bf16[1,2,432,256]{3,2,1,0:T(8,128)(2,1)}, bf16[1,2,432,256]{3,2,1,0:T(8,128)(2,1)S(1)}, u32[]{:S(2)}, u32[]{:S(2)}) %collective-permute-start.10) | collective-permute-done | bytes 442400 | tf_op jit(solution)/shard_map/part5_shift1/ppermute | solution.py:323
  440.3 11.6 %correlate.9 = (bf16[2,512,1024]{2,1,0:T(8,128)(2,1)}, f32[2,512,1024]{2,1,0:T(8,128)}) custom-call(s32[3]{0:T(128)} %pad_add_fusion.place_ref, f32[2,512,1024]{2,1,0:T(8,128)} %get-tuple-element.56.refs_1_.rest_0_, f32[2,512,1024]{2,1,0:T(8,128)} %get-tuple-element.57.refs_2_.rest_1_, bf16[1,2,432,256]{3,2,1,0:T(8,128)(2,1)} %bitcast.64, ...), custom_call_target="tpu_custom_call" | custom-call | flops 1024 | bytes 1024 | tf_op jit(solution)/shard_map/correlate/pallas_call | solution.py:260
  451.9 0.6 collective-permute-start.21
  452.6 5.3 %equalize.6.rest_0_ = f32[4,2,512,1024]{3,2,1,0:T(8,128)} custom-call(f32[1,512]{1,0:T(1,128)} %bitcast.74, f32[1,1024]{1,0:T(1,128)} %bitcast.71, f32[2,512,1024]{2,1,0:T(8,128)} %get-tuple-element.80.mine_ref, bf16[2,512,1024]{2,1,0:T(8,128)(2,1)} %collective-permute-done.22.theirs_ref, ...), custom_call_target="tpu_custom_call", output_to_operand_aliasing={{}: (4, {})} | custom-call | flops 1024 | bytes 1024 | tf_op jit(solution)/shard_map/equalize/pallas_call | solution.py:308
  457.8 5.3 %equalize.7 = f32[4,2,512,1024]{3,2,1,0:T(8,128)} custom-call(f32[1,512]{1,0:T(1,128)} %bitcast.77, f32[1,1024]{1,0:T(1,128)} %bitcast.72, f32[2,512,1024]{2,1,0:T(8,128)} %get-tuple-element.78.mine_ref, bf16[2,512,1024]{2,1,0:T(8,128)(2,1)} %collective-permute-done.21.theirs_ref, f32[4,2,512,1024]{3,2,1,0:T(8,128)} %equalize.6.rest_0_), custom_call_target="tpu_custom_call", output_to_operand_aliasing={{}: (4, {})} | custom-call | flops 1024 | bytes 1024 | tf_op jit(solution)/shard_map/equalize/pallas_call | solution.py:308
  (82 shorter events, 3.3 us)
Async XLA Ops:
  15.6 43.8 %collective-permute-start = (bf16[2,1584,256]{2,1,0:T(8,128)(2,1)}, bf16[2,1584,256]{2,1,0:T(8,128)(2,1)}, u32[]{:S(2)}, u32[]{:S(2)}) collective-permute-start(bf16[2,1584,256]{2,1,0:T(8,128)(2,1)} %get-tuple-element.45), channel_id=1, source_target_pairs={{0,1},{2,3},{4,5},{6,7},{8,9},{10,11},{12,13},{14,15},{16,17},{18,... | collective-permute-start | bytes 4866056 | tf_op jit(solution)/shard_map/halo/ppermute | solution.py:328
  16.9 72.2 %collective-permute-start.1 = (bf16[4,2,144,256]{3,2,1,0:T(8,128)(2,1)}, bf16[4,2,144,256]{3,2,1,0:T(8,128)(2,1)S(1)}, u32[]{:S(2)}, u32[]{:S(2)}) collective-permute-start(bf16[4,2,144,256]{3,2,1,0:T(8,128)(2,1)} %bitcast.83), channel_id=1, source_target_pairs={{0,8},{8,16},{16,24},{24,0},{1,9},{9,17},{17,25},{25,1},{2,10},{10... | collective-permute-start | bytes 1769480 | tf_op jit(solution)/shard_map/part0_shift1/ppermute | solution.py:323
  18.2 99.1 %collective-permute-start.2 = (bf16[4,2,144,256]{3,2,1,0:T(8,128)(2,1)}, bf16[4,2,144,256]{3,2,1,0:T(8,128)(2,1)S(1)}, u32[]{:S(2)}, u32[]{:S(2)}) collective-permute-start(bf16[4,2,144,256]{3,2,1,0:T(8,128)(2,1)} %bitcast.82), channel_id=1, source_target_pairs={{0,16},{8,24},{16,0},{24,8},{1,17},{9,25},{17,1},{25,9},{2,18},{10... | collective-permute-start | bytes 1769480 | tf_op jit(solution)/shard_map/part0_shift2/ppermute | solution.py:323
  19.3 102.5 %collective-permute-start.3 = (bf16[4,2,144,256]{3,2,1,0:T(8,128)(2,1)}, bf16[4,2,144,256]{3,2,1,0:T(8,128)(2,1)}, u32[]{:S(2)}, u32[]{:S(2)}) collective-permute-start(bf16[4,2,144,256]{3,2,1,0:T(8,128)(2,1)} %bitcast.81), channel_id=1, source_target_pairs={{0,24},{8,0},{16,8},{24,16},{1,25},{9,1},{17,9},{25,17},{2,26},{10... | collective-permute-start | bytes 1769480 | tf_op jit(solution)/shard_map/part0_shift3/ppermute | solution.py:323
  59.3 216.7 %collective-permute-start.5 = (bf16[4,2,576,256]{3,2,1,0:T(8,128)(2,1)}, bf16[4,2,576,256]{3,2,1,0:T(8,128)(2,1)}, u32[]{:S(2)}, u32[]{:S(2)}) collective-permute-start(bf16[4,2,576,256]{3,2,1,0:T(8,128)(2,1)} %bitcast.80), channel_id=1, source_target_pairs={{0,16},{8,24},{16,0},{24,8},{1,17},{9,25},{17,1},{25,9},{2,18},{10... | collective-permute-start | bytes 7077896 | tf_op jit(solution)/shard_map/part1_shift2/ppermute | solution.py:323
  89.1 28.3 %copy-start.2 = (bf16[4,2,144,256]{3,2,1,0:T(8,128)(2,1)}, bf16[4,2,144,256]{3,2,1,0:T(8,128)(2,1)S(1)}, u32[]{:S(2)}) copy-start(bf16[4,2,144,256]{3,2,1,0:T(8,128)(2,1)S(1)} %collective-permute-done.1.refs_3_.rest_1_) | copy-start | bytes 1769476
  117.3 0.8 copy-start.1
  118.2 157.9 %collective-permute-start.4 = (bf16[4,2,576,256]{3,2,1,0:T(8,128)(2,1)}, bf16[4,2,576,256]{3,2,1,0:T(8,128)(2,1)S(1)}, u32[]{:S(2)}, u32[]{:S(2)}) collective-permute-start(bf16[4,2,576,256]{3,2,1,0:T(8,128)(2,1)} %after.16), channel_id=1, source_target_pairs={{0,8},{8,16},{16,24},{24,0},{1,9},{9,17},{17,25},{25,1},{2,10},{10... | collective-permute-start | bytes 7077896 | tf_op jit(solution)/shard_map/part1_shift1/ppermute | solution.py:323
  121.9 1.3 copy-start.16
  121.9 1.3 copy-start.17
  121.9 1.3 copy-start.18
  121.9 158.1 %collective-permute-start.6 = (bf16[4,2,576,256]{3,2,1,0:T(8,128)(2,1)}, bf16[4,2,576,256]{3,2,1,0:T(8,128)(2,1)}, u32[]{:S(2)}, u32[]{:S(2)}) collective-permute-start(bf16[4,2,576,256]{3,2,1,0:T(8,128)(2,1)} %after.17), channel_id=1, source_target_pairs={{0,24},{8,0},{16,8},{24,16},{1,25},{9,1},{17,9},{25,17},{2,26},{10... | collective-permute-start | bytes 7077896 | tf_op jit(solution)/shard_map/part1_shift3/ppermute | solution.py:323
  276.0 18.7 %collective-permute-start.11 = (bf16[1,2,432,256]{3,2,1,0:T(8,128)(2,1)}, bf16[1,2,432,256]{3,2,1,0:T(8,128)(2,1)S(1)}, u32[]{:S(2)}, u32[]{:S(2)}) collective-permute-start(bf16[1,2,432,256]{3,2,1,0:T(8,128)(2,1)} %after.22), channel_id=1, source_target_pairs={{0,16},{8,24},{16,0},{24,8},{1,17},{9,25},{17,1},{25,9},{2,18},{10... | collective-permute-start | bytes 1327112 | tf_op jit(solution)/shard_map/part2_shift2/ppermute | solution.py:323
  276.0 1.5 copy-start
  277.5 45.7 %collective-permute-start.7 = (bf16[1,2,432,256]{3,2,1,0:T(8,128)(2,1)}, bf16[1,2,432,256]{3,2,1,0:T(8,128)(2,1)S(1)}, u32[]{:S(2)}, u32[]{:S(2)}) collective-permute-start(bf16[1,2,432,256]{3,2,1,0:T(8,128)(2,1)} %after.18), channel_id=1, source_target_pairs={{0,8},{8,16},{16,24},{24,0},{1,9},{9,17},{17,25},{25,1},{2,10},{10... | collective-permute-start | bytes 1327112 | tf_op jit(solution)/shard_map/part2_shift1/ppermute | solution.py:323
  279.9 47.3 %collective-permute-start.15 = (bf16[1,2,432,256]{3,2,1,0:T(8,128)(2,1)}, bf16[1,2,432,256]{3,2,1,0:T(8,128)(2,1)S(1)}, u32[]{:S(2)}, u32[]{:S(2)}) collective-permute-start(bf16[1,2,432,256]{3,2,1,0:T(8,128)(2,1)} %after.26), channel_id=1, source_target_pairs={{0,24},{8,0},{16,8},{24,16},{1,25},{9,1},{17,9},{25,17},{2,26},{10... | collective-permute-start | bytes 1327112 | tf_op jit(solution)/shard_map/part2_shift3/ppermute | solution.py:323
  294.8 0.8 copy-start.9
  295.6 48.4 %collective-permute-start.12 = (bf16[1,2,432,256]{3,2,1,0:T(8,128)(2,1)}, bf16[1,2,432,256]{3,2,1,0:T(8,128)(2,1)S(1)}, u32[]{:S(2)}, u32[]{:S(2)}) collective-permute-start(bf16[1,2,432,256]{3,2,1,0:T(8,128)(2,1)} %after.23), channel_id=1, source_target_pairs={{0,16},{8,24},{16,0},{24,8},{1,17},{9,25},{17,1},{25,9},{2,18},{10... | collective-permute-start | bytes 1327112 | tf_op jit(solution)/shard_map/part3_shift2/ppermute | solution.py:323
  323.2 0.8 copy-start.10
  324.0 27.7 %collective-permute-start.8 = (bf16[1,2,432,256]{3,2,1,0:T(8,128)(2,1)}, bf16[1,2,432,256]{3,2,1,0:T(8,128)(2,1)S(1)}, u32[]{:S(2)}, u32[]{:S(2)}) collective-permute-start(bf16[1,2,432,256]{3,2,1,0:T(8,128)(2,1)} %after.19), channel_id=1, source_target_pairs={{0,8},{8,16},{16,24},{24,0},{1,9},{9,17},{17,25},{25,1},{2,10},{10... | collective-permute-start | bytes 1327112 | tf_op jit(solution)/shard_map/part3_shift1/ppermute | solution.py:323
  327.2 0.8 copy-start.11
  328.0 27.7 %collective-permute-start.16 = (bf16[1,2,432,256]{3,2,1,0:T(8,128)(2,1)}, bf16[1,2,432,256]{3,2,1,0:T(8,128)(2,1)S(1)}, u32[]{:S(2)}, u32[]{:S(2)}) collective-permute-start(bf16[1,2,432,256]{3,2,1,0:T(8,128)(2,1)} %after.27), channel_id=1, source_target_pairs={{0,24},{8,0},{16,8},{24,16},{1,25},{9,1},{17,9},{25,17},{2,26},{10... | collective-permute-start | bytes 1327112 | tf_op jit(solution)/shard_map/part3_shift3/ppermute | solution.py:323
  344.0 11.7 %copy-start.3 = (bf16[1,2,432,256]{3,2,1,0:T(8,128)(2,1)}, bf16[1,2,432,256]{3,2,1,0:T(8,128)(2,1)S(1)}, u32[]{:S(2)}) copy-start(bf16[1,2,432,256]{3,2,1,0:T(8,128)(2,1)S(1)} %collective-permute-done.12.refs_1_.rest_10_.refs_2_) | copy-start | bytes 1327108
  351.7 4.0 copy-start.4
  355.7 0.8 copy-start.5
  356.5 3.9 copy-start.15
  356.5 23.1 %collective-permute-start.20 = (bf16[2,512,1024]{2,1,0:T(8,128)(2,1)}, bf16[2,512,1024]{2,1,0:T(8,128)(2,1)}, u32[]{:S(2)}, u32[]{:S(2)}) collective-permute-start(bf16[2,512,1024]{2,1,0:T(8,128)(2,1)} %after.31), channel_id=1, source_target_pairs={{0,1},{1,0},{2,3},{3,2},{4,5},{5,4},{6,7},{7,6},{8,9},{9,8},{10,11... | collective-permute-start | bytes 6291464 | tf_op jit(solution)/shard_map/rows0/ppermute | solution.py:421
  357.3 27.7 %collective-permute-start.13 = (bf16[1,2,432,256]{3,2,1,0:T(8,128)(2,1)}, bf16[1,2,432,256]{3,2,1,0:T(8,128)(2,1)S(1)}, u32[]{:S(2)}, u32[]{:S(2)}) collective-permute-start(bf16[1,2,432,256]{3,2,1,0:T(8,128)(2,1)} %after.24), channel_id=1, source_target_pairs={{0,16},{8,24},{16,0},{24,8},{1,17},{9,25},{17,1},{25,9},{2,18},{10... | collective-permute-start | bytes 1327112 | tf_op jit(solution)/shard_map/part4_shift2/ppermute | solution.py:323
  357.4 38.4 %collective-permute-start.9 = (bf16[1,2,432,256]{3,2,1,0:T(8,128)(2,1)}, bf16[1,2,432,256]{3,2,1,0:T(8,128)(2,1)S(1)}, u32[]{:S(2)}, u32[]{:S(2)}) collective-permute-start(bf16[1,2,432,256]{3,2,1,0:T(8,128)(2,1)} %after.20), channel_id=1, source_target_pairs={{0,8},{8,16},{16,24},{24,0},{1,9},{9,17},{17,25},{25,1},{2,10},{10... | collective-permute-start | bytes 1327112 | tf_op jit(solution)/shard_map/part4_shift1/ppermute | solution.py:323
  359.7 39.3 %collective-permute-start.17 = (bf16[1,2,432,256]{3,2,1,0:T(8,128)(2,1)}, bf16[1,2,432,256]{3,2,1,0:T(8,128)(2,1)S(1)}, u32[]{:S(2)}, u32[]{:S(2)}) collective-permute-start(bf16[1,2,432,256]{3,2,1,0:T(8,128)(2,1)} %after.28), channel_id=1, source_target_pairs={{0,24},{8,0},{16,8},{24,16},{1,25},{9,1},{17,9},{25,17},{2,26},{10... | collective-permute-start | bytes 1327112 | tf_op jit(solution)/shard_map/part4_shift3/ppermute | solution.py:323
  384.9 14.0 %copy-start.6 = (bf16[1,2,432,256]{3,2,1,0:T(8,128)(2,1)}, bf16[1,2,432,256]{3,2,1,0:T(8,128)(2,1)S(1)}, u32[]{:S(2)}) copy-start(bf16[1,2,432,256]{3,2,1,0:T(8,128)(2,1)S(1)} %collective-permute-done.13.refs_1_.refs_2_.rest_10_) | copy-start | bytes 1327108
  395.8 3.1 copy-start.7
  398.9 0.8 copy-start.8
  399.8 18.8 %collective-permute-start.19 = (bf16[2,512,1024]{2,1,0:T(8,128)(2,1)}, bf16[2,512,1024]{2,1,0:T(8,128)(2,1)}, u32[]{:S(2)}, u32[]{:S(2)}) collective-permute-start(bf16[2,512,1024]{2,1,0:T(8,128)(2,1)} %after.30), channel_id=1, source_target_pairs={{0,1},{1,0},{2,3},{3,2},{4,5},{5,4},{6,7},{7,6},{8,9},{9,8},{10,11... | collective-permute-start | bytes 6291464 | tf_op jit(solution)/shard_map/rows1/ppermute | solution.py:421
  400.3 23.5 %collective-permute-start.14 = (bf16[1,2,432,256]{3,2,1,0:T(8,128)(2,1)}, bf16[1,2,432,256]{3,2,1,0:T(8,128)(2,1)S(1)}, u32[]{:S(2)}, u32[]{:S(2)}) collective-permute-start(bf16[1,2,432,256]{3,2,1,0:T(8,128)(2,1)} %after.25), channel_id=1, source_target_pairs={{0,16},{8,24},{16,0},{24,8},{1,17},{9,25},{17,1},{25,9},{2,18},{10... | collective-permute-start | bytes 1327112 | tf_op jit(solution)/shard_map/part5_shift2/ppermute | solution.py:323
  400.3 38.6 %collective-permute-start.10 = (bf16[1,2,432,256]{3,2,1,0:T(8,128)(2,1)}, bf16[1,2,432,256]{3,2,1,0:T(8,128)(2,1)S(1)}, u32[]{:S(2)}, u32[]{:S(2)}) collective-permute-start(bf16[1,2,432,256]{3,2,1,0:T(8,128)(2,1)} %after.21), channel_id=1, source_target_pairs={{0,8},{8,16},{16,24},{24,0},{1,9},{9,17},{17,25},{25,1},{2,10},{10... | collective-permute-start | bytes 1327112 | tf_op jit(solution)/shard_map/part5_shift1/ppermute | solution.py:323
  400.3 39.2 %collective-permute-start.18 = (bf16[1,2,432,256]{3,2,1,0:T(8,128)(2,1)}, bf16[1,2,432,256]{3,2,1,0:T(8,128)(2,1)S(1)}, u32[]{:S(2)}, u32[]{:S(2)}) collective-permute-start(bf16[1,2,432,256]{3,2,1,0:T(8,128)(2,1)} %after.29), channel_id=1, source_target_pairs={{0,24},{8,0},{16,8},{24,16},{1,25},{9,1},{17,9},{25,17},{2,26},{10... | collective-permute-start | bytes 1327112 | tf_op jit(solution)/shard_map/part5_shift3/ppermute | solution.py:323
  417.9 34.7 %collective-permute-start.22 = (bf16[2,512,1024]{2,1,0:T(8,128)(2,1)}, bf16[2,512,1024]{2,1,0:T(8,128)(2,1)}, u32[]{:S(2)}, u32[]{:S(2)}) collective-permute-start(bf16[2,512,1024]{2,1,0:T(8,128)(2,1)} %get-tuple-element.77.rest_1_), channel_id=1, source_target_pairs={{0,1},{1,0},{2,3},{3,2},{4,5},{5,4},{6,7},{7,6},{8,9},{9,8},{10,11... | collective-permute-start | bytes 6291464 | tf_op jit(solution)/shard_map/rows2/ppermute | solution.py:421
  423.8 15.6 %copy-start.12 = (bf16[1,2,432,256]{3,2,1,0:T(8,128)(2,1)}, bf16[1,2,432,256]{3,2,1,0:T(8,128)(2,1)S(1)}, u32[]{:S(2)}) copy-start(bf16[1,2,432,256]{3,2,1,0:T(8,128)(2,1)S(1)} %collective-permute-done.14.rest_4_) | copy-start | bytes 1327108
  438.9 0.8 copy-start.13
  439.5 0.8 copy-start.14
  451.9 5.9 %collective-permute-start.21 = (bf16[2,512,1024]{2,1,0:T(8,128)(2,1)}, bf16[2,512,1024]{2,1,0:T(8,128)(2,1)}, u32[]{:S(2)}, u32[]{:S(2)}) collective-permute-start(bf16[2,512,1024]{2,1,0:T(8,128)(2,1)} %get-tuple-element.79.rest_1_), channel_id=1, source_target_pairs={{0,1},{1,0},{2,3},{3,2},{4,5},{5,4},{6,7},{7,6},{8,9},{9,8},{10,11... | collective-permute-start | bytes 6291464 | tf_op jit(solution)/shard_map/rows3/ppermute | solution.py:421

commit v9 on v7

--- a/solution.py
+++ b/solution.py
@@ -201,6 +201,42 @@
     )(value, *others)
 
 
+def with_scales_kernel(value_ref, scale_ref, out_ref, rows, sems):
+    size = value_ref.shape[2]
+    left = scale_ref[...]
+    pieces = []
+    for _ in range(3):
+        piece = left.astype(jnp.bfloat16).astype(jnp.float32)
+        pieces.append(jnp.broadcast_to(piece, rows.shape))
+        left = left - piece
+    place = lax.broadcasted_iota(jnp.int32, rows.shape, 0)
+    chosen = jnp.where(place == 0, pieces[0], jnp.where(place == 1, pieces[1], pieces[2]))
+    rows[...] = chosen.astype(jnp.bfloat16)
+    copies = [
+        pltpu.make_async_copy(value_ref.at[0, 0], out_ref.at[pl.ds(0, size)], sems.at[0]),
+        pltpu.make_async_copy(value_ref.at[0, 1], out_ref.at[pl.ds(size, size)], sems.at[1]),
+        pltpu.make_async_copy(rows, out_ref.at[pl.ds(2 * size, 16)], sems.at[2]),
+    ]
+    for copy in copies:
+        copy.start()
+    for copy in copies:
+        copy.wait()
+
+
+def with_scales(value, scale):
+    size, inputs = value.shape[2:]
+    anywhere = pl.BlockSpec(memory_space=pl.ANY)
+    return pl.pallas_call(
+        with_scales_kernel,
+        out_shape=jax.ShapeDtypeStruct((2 * size + 16, inputs), value.dtype),
+        in_specs=[anywhere, pl.BlockSpec(memory_space=pltpu.VMEM)],
+        out_specs=anywhere,
+        scratch_shapes=[pltpu.VMEM((16, inputs), value.dtype), pltpu.SemaphoreType.DMA((3,))],
+        cost_estimate=COST,
+        name="with_scales",
+    )(value, scale)
+
+
 def correlate_kernel(owners, picks, outs, sums, place_ref, *rest):
     count = len(picks)
     sum_refs, rest = rest[:sums], rest[sums:]
@@ -357,19 +393,20 @@
     window = jnp.asarray(np.ascontiguousarray(window))
     spot = jnp.reshape(me, (1,)).astype(jnp.int32)
 
-    if groups != sum(RUNS):
+    if groups != sum(RUNS) or RUNS[0] != 1:
         runs = (1,) * groups
     else:
         runs = RUNS
     parts, arrived, flat, out = [], [], [], None
 
-    def send(n, waits):
+    def send(n, waits, scale=None):
         got = [parts[n][0]]
         for d in range(1, owners):
             gates = list(waits.get(d, ()))
             if len(flat) >= IN_FLIGHT and not (n == 1 and d == 2):
                 gates.append(flat[len(flat) - IN_FLIGHT])
-            value = after(parts[n][d], *gates) if gates else parts[n][d]
+            value = parts[n][d] if scale is None else with_scales(parts[n][d], scale)
+            value = after(value, *gates) if gates else value
             with jax.named_scope(f"part{n}_shift{d}"):
                 got.append(shift(value, d))
             flat.append(got[-1])
@@ -404,16 +441,9 @@
     local = jnp.sum(sum(power), axis=0)
     total = lax.psum(local, ("band", "tm"))
     scale = lax.rsqrt(total / (frames_all * jnp.sum(keep_all)) + 1e-06)
-    scales = lax.all_gather(scale, "station", axis=0, tiled=True)
     kept = lax.dynamic_slice_in_dim(keep_mine, me * fine, fine, 0)
     counts = kept.reshape(groups, GROUP).sum(-1)
     denom = frames_all * jnp.maximum(counts, 1.0)
-    per_half = scales.shape[0] // 2
-    row_scales = lax.dynamic_slice_in_dim(scales, half * per_half, per_half, 0)
-
-    column_scales = scales[None, :]
-    row_scales = [(row_scales / denom[j])[None, :] for j in range(groups)]
-
     place = jnp.stack([me, 1 - half, half]).astype(jnp.int32)
     shared = len(PARTS)
     def to_other(j, theirs):
@@ -432,7 +462,22 @@
     last_spectra = parts[shared][0]
     for n in range(1, shared):
         send(n, {d: [last_spectra, arrived[0][2]] for d in range(1, owners) if d != 2})
-    send(shared, {owners - 1: [column_scales]})
+    send(shared, {}, scale[None, :])
+    got = arrived[shared]
+    size = 2 * got[0].shape[2]
+    by_shift = [scale]
+    for d in range(1, owners):
+        by_shift.append(got[d][size : size + 3].astype(jnp.float32).sum(0))
+        got[d] = got[d][:size].reshape(got[0].shape)
+    source = (me - jnp.arange(owners)) % owners
+    chosen = (jnp.arange(owners)[:, None] == source[None, :]).astype(jnp.float32)
+    scales = jnp.sum(chosen[:, :, None] * jnp.stack(by_shift)[None], axis=1).reshape(-1)
+    per_half = scales.shape[0] // 2
+    row_scales = lax.dynamic_slice_in_dim(scales, half * per_half, per_half, 0)
+
+    column_scales = scales[None, :]
+    row_scales = [(row_scales / denom[j])[None, :] for j in range(groups)]
+
     partial = multiply(groups - 1, place, [jnp.float32] * 2, end=shared)
     waiting = []
 

time: 462 us -> 465 us (level)
  blocking collectives: 131 us -> 12.5 us
  waiting for transfers between devices: 114 us -> 176 us
  Pallas kernels: 176 us -> 221 us
  starting transfers between devices: 21.5 us -> 27 us
  local copies, waits for them, and re-layouts: 13.4 us -> 18.4 us
    all_gather x1 -> x0, blocking collectives: 117 us -> none  [pipelined(): scales = lax.all_gather(scale, 'station', axis=0, tiled=True)]
    ppermute x18, waiting for transfers between devices: 114 us -> 176 us  [shift(): lax.ppermute(value, 'station', [(s, (s + d) % count) for s in range(count)])]
    pallas_call x0 -> x3, Pallas kernels: none -> 45.6 us  [with_scales(): pl.pallas_call(with_scales_kernel, out_shape=jax.ShapeDtypeStruct((2 * si...]
    unnamed x45 -> x51, local copies, waits for them, and re-layouts: 12 us -> 13.5 us
  transfers between devices with their start and end apart: 23 -> 23, of which waited for: 10 -> 9; matrix products, arithmetic and copies ran while one was open for 1% -> 3% of each run, Pallas kernels for 34% -> 44%
where the time goes in v9:
time: 465 us; the launch traced here: 464 us
  Pallas kernels  221 us (48%)
  waiting for transfers between devices  176 us (38%)
  starting transfers between devices  27 us (6%)
  local copies, waits for them, and re-layouts  18.4 us (4%)
  blocking collectives  12.5 us (3%)
  other arithmetic  7.43 us (2%)
    ppermute x18, waiting for transfers between devices, shift(): lax.ppermute(value, 'station', [(s, (s + d) % count) for s in range(count)])  176 us
    pallas_call x3, Pallas kernels, front(): pl.pallas_call(functools.partial(front_kernel, runs, owners, turned, tail...  82.1 us
    pallas_call x5, Pallas kernels, correlate(): pl.pallas_call(functools.partial(correlate_kernel, owners, picks, outs, l...  72.7 us
    pallas_call x3, Pallas kernels, with_scales(): pl.pallas_call(with_scales_kernel, out_shape=jax.ShapeDtypeStruct((2 * si...  45.6 us
    pallas_call x4, Pallas kernels, equalize(): pl.pallas_call(equalize_kernel, grid=(rows // block,), out_shape=jax.Shap...  21.1 us
    ppermute x18, starting transfers between devices, shift(): lax.ppermute(value, 'station', [(s, (s + d) % count) for s in range(count)])  18.6 us
    unnamed x51, local copies, waits for them, and re-layouts  13.5 us
    psum x1, blocking collectives, pipelined(): total = lax.psum(local, ('band', 'tm'))  12.5 us
  transfers between devices with their start and end apart: 23, of which 9 were waited for; matrix products, arithmetic and copies ran while one was open for 3% of the time, Pallas kernels for 44%

profile of v9, /device:TPU:11, one launch (start us, length us, event | category | flops | bytes accessed | tf_op | source)
XLA Modules:
  0.0 464.3 jit_solution(6107455461270155316)
XLA Ops:
  1.7 13.9 %front.3 = (bf16[4,2,9,16,256]{4,3,2,1,0:T(8,128)(2,1)}, bf16[4,2,9,16,256]{4,3,2,1,0:T(8,128)(2,1)}, bf16[4,2,9,16,256]{4,3,2,1,0:T(8,128)(2,1)}, bf16[4,2,9,16...) custom-call(s32[1]{0:T(128)} %bitcast.me_ref, f32[144]{0:T(256)} %dynamic_slice.14.keep_ref, ...), custom_call_target="tpu_custom_call" | custom-call | flops 1024 | bytes 1024 | tf_op jit(solution)/shard_map/front/pallas_call | solution.py:159
  15.6 1.3 collective-permute-start
  16.9 2.4 collective-permute-start.1
  19.2 1.5 collective-permute-start.7
  20.7 38.6 %front.4 = (bf16[4,2,9,64,256]{4,3,2,1,0:T(8,128)(2,1)}, bf16[4,2,9,64,256]{4,3,2,1,0:T(8,128)(2,1)}, bf16[4,2,9,64,256]{4,3,2,1,0:T(8,128)(2,1)}, bf16[4,2,9,64,256]{4,3,2,1,0:T(8,128)(2,1)}, f32[16,256]{1,0:T(8,128)}) custom-call(s32[1]{0:T(128)} %bitcast.me_ref, f32[144]{0:T(256)} %dynamic_slice.14.keep_ref, bf16[2,1,256,18432]{3,2,1,0:T(8,128)(2,1)} %volts_ref.5, ...), custom_call_target="tpu_custom_call" | custom-call | flops 1024 | bytes 1024 | tf_op jit(solution)/shard_map/front/pallas_call | solution.py:159
  59.3 0.9 collective-permute-start.5
  60.2 29.6 %front.5 = (bf16[1,2,9,48,256]{4,3,2,1,0:T(8,128)(2,1)}, bf16[1,2,9,48,256]{4,3,2,1,0:T(8,128)(2,1)}, bf16[1,2,9,48,256]{4,3,2,1,0:T(8,128)(2,1)}, bf16[1,2,9,48...) custom-call(s32[1]{0:T(128)} %bitcast.me_ref, ...), custom_call_target="tpu_custom_call" | custom-call | flops 1024 | bytes 1024 | tf_op jit(solution)/shard_map/front/pallas_call | solution.py:159
  89.8 31.2 %collective-permute-done.2.refs_3_.rest_1_ = bf16[4,2,144,256]{3,2,1,0:T(8,128)(2,1)S(1)} collective-permute-done((bf16[4,2,144,256]{3,2,1,0:T(8,128)(2,1)}, bf16[4,2,144,256]{3,2,1,0:T(8,128)(2,1)S(1)}, u32[]{:S(2)}, u32[]{:S(2)}) %collective-permute-start.2) | collective-permute-done | bytes 589856 | tf_op jit(solution)/shard_map/part0_shift1/ppermute | solution.py:359
  121.0 0.8 copy-done.2
  121.8 2.1 collective-permute-start.3
  123.9 46.5 %collective-permute-done.7.refs_3_.rest_3_ = bf16[4,2,144,256]{3,2,1,0:T(8,128)(2,1)} collective-permute-done((bf16[4,2,144,256]{3,2,1,0:T(8,128)(2,1)}, bf16[4,2,144,256]{3,2,1,0:T(8,128)(2,1)}, u32[]{:S(2)}, u32[]{:S(2)}) %collective-permute-start.7) | collective-permute-done | bytes 589856 | tf_op jit(solution)/shard_map/part0_shift3/ppermute | solution.py:359
  171.9 12.5 %psum.7 = f32[256]{0:T(256)S(1)} all-reduce(f32[256]{0:T(256)S(1)} %add_reduce_fusion), channel_id=1, replica_groups=mesh['station'=4,'band'=4,'tm'=2] {'band','tm'}, use_global_device_ids=true, to_apply=%region_2.3 | all-reduce | flops 256 | bytes 2048 | tf_op jit(solution)/shard_map/psum | solution.py:442
  185.0 15.2 %with_scales.4.refs_0_ = bf16[880,256]{1,0:T(8,128)(2,1)} custom-call(bf16[1,2,432,256]{3,2,1,0:T(8,128)(2,1)} %bitcast.67, f32[1,256]{1,0:T(1,128)} %bitcast.86), custom_call_target="tpu_custom_call" | custom-call | flops 1024 | bytes 1024 | tf_op jit(solution)/shard_map/with_scales/pallas_call | solution.py:229
  200.2 1.5 copy-done
  201.7 1.5 collective-permute-start.6
  203.2 15.2 %with_scales.3.refs_0_ = bf16[880,256]{1,0:T(8,128)(2,1)} custom-call(bf16[1,2,432,256]{3,2,1,0:T(8,128)(2,1)} %bitcast.66, f32[1,256]{1,0:T(1,128)} %bitcast.87), custom_call_target="tpu_custom_call" | custom-call | flops 1024 | bytes 1024 | tf_op jit(solution)/shard_map/with_scales/pallas_call | solution.py:229
  218.4 63.9 %collective-permute-done.3.refs_1_.rest_5_ = bf16[4,2,576,256]{3,2,1,0:T(8,128)(2,1)} collective-permute-done((bf16[4,2,576,256]{3,2,1,0:T(8,128)(2,1)}, bf16[4,2,576,256]{3,2,1,0:T(8,128)(2,1)}, u32[]{:S(2)}, u32[]{:S(2)}) %collective-permute-start.3) | collective-permute-done | bytes 2359328 | tf_op jit(solution)/shard_map/part1_shift1/ppermute | solution.py:359
  282.4 2.2 collective-permute-start.4
  284.6 15.2 %with_scales.5.refs_0_ = bf16[880,256]{1,0:T(8,128)(2,1)} custom-call(bf16[1,2,432,256]{3,2,1,0:T(8,128)(2,1)} %bitcast.65, f32[1,256]{1,0:T(1,128)} %bitcast.88), custom_call_target="tpu_custom_call" | custom-call | flops 1024 | bytes 1024 | tf_op jit(solution)/shard_map/with_scales/pallas_call | solution.py:229
  301.2 1.2 collective-permute-start.13
  302.4 12.9 %correlate.5 = (f32[2,512,1024]{2,1,0:T(8,128)}, f32[2,512,1024]{2,1,0:T(8,128)}) custom-call(s32[3]{0:T(128)} %pad_add_fusion.place_ref, bf16[4,2,144,256]{3,2,1,0:T(8,128)(2,1)} %bitcast.53, bf16[4,2,144,256]{3,2,1,0:T(8,128)(2,1)} %copy-done.2, bf16[4,2,144,256]{3,2,1,0:T(8,128)(2,1)} %copy-done.1, ...), custom_call_target="tpu_custom_call" | custom-call | flops 1024 | bytes 1024 | tf_op jit(solution)/shard_map/correlate/pallas_call | solution.py:296
  315.3 5.6 %collective-permute-done.4.refs_1_ = bf16[880,256]{1,0:T(8,128)(2,1)S(1)} collective-permute-done((bf16[880,256]{1,0:T(8,128)(2,1)}, bf16[880,256]{1,0:T(8,128)(2,1)S(1)}, u32[]{:S(2)}, u32[]{:S(2)}) %collective-permute-start.4) | collective-permute-done | bytes 450592 | tf_op jit(solution)/shard_map/part2_shift1/ppermute | solution.py:359
  320.9 0.8 copy-done.12
  321.7 2.1 collective-permute-start.10
  324.6 1.0 copy-done.15
  326.4 0.8 slice.43
  327.2 1.8 slice.45
  329.0 16.0 %correlate.7 = (bf16[2,512,1024]{2,1,0:T(8,128)(2,1)}, f32[2,512,1024]{2,1,0:T(8,128)}) custom-call(s32[3]{0:T(128)} %pad_add_fusion.place_ref, bf16[4,2,144,256]{3,2,1,0:T(8,128)(2,1)} %bitcast.54, bf16[4,2,144,256]{3,2,1,0:T(8,128)(2,1)} %copy-done.2, bf16[4,2,144,256]{3,2,1,0:T(8,128)(2,1)} %copy-done.1, ...), custom_call_target="tpu_custom_call" | custom-call | flops 1024 | bytes 1024 | tf_op jit(solution)/shard_map/correlate/pallas_call | solution.py:296
  345.0 4.3 collective-permute-done.10.refs_1_.rest_9_
  350.3 5.3 %collective-permute-start.20 = (bf16[2,512,1024]{2,1,0:T(8,128)(2,1)}, bf16[2,512,1024]{2,1,0:T(8,128)(2,1)S(1)}, u32[]{:S(2)}, u32[]{:S(2)}) collective-permute-start(bf16[2,512,1024]{2,1,0:T(8,128)(2,1)} %after.31), channel_id=1, source_target_pairs={{0,1},{1,0},{2,3},{3,2},{4,5},{5,4},{6,7},{7,6},{8,9},{9,8},{10,11... | collective-permute-start | bytes 6291464 | tf_op jit(solution)/shard_map/rows0/ppermute | solution.py:451
  358.8 1.2 collective-permute-start.17
  361.4 3.0 broadcast_divide_fusion
  364.5 16.1 %correlate.6 = (bf16[2,512,1024]{2,1,0:T(8,128)(2,1)}, f32[2,512,1024]{2,1,0:T(8,128)}) custom-call(s32[3]{0:T(128)} %pad_add_fusion.place_ref, bf16[4,2,144,256]{3,2,1,0:T(8,128)(2,1)} %bitcast.55, bf16[4,2,144,256]{3,2,1,0:T(8,128)(2,1)} %copy-done.2, bf16[4,2,144,256]{3,2,1,0:T(8,128)(2,1)} %copy-done.1, ...), custom_call_target="tpu_custom_call" | custom-call | flops 1024 | bytes 1024 | tf_op jit(solution)/shard_map/correlate/pallas_call | solution.py:296
  380.6 1.3 copy-done.10
  381.8 5.3 %equalize.4.rest_0_ = f32[4,2,512,1024]{3,2,1,0:T(8,128)} custom-call(f32[1,512]{1,0:T(1,128)} %bitcast.93, f32[1,1024]{1,0:T(1,128)} %bitcast.80, f32[2,512,1024]{2,1,0:T(8,128)} %get-tuple-element.74.mine_ref, bf16[2,512,1024]{2,1,0:T(8,128)(2,1)} %copy-done.10, bf16[2,512,1024]{2,1,0:T(8,128)(2,1)} %get-tuple-element.73.refs_0_.rest_0_), custom_call_target="tpu_custom_call" | custom-call | flops 1024 | bytes 1024 | tf_op jit(solution)/shard_map/equalize/pallas_call | solution.py:344
  387.1 8.8 %collective-permute-done.11.refs_1_.rest_9_ = bf16[1,2,432,256]{3,2,1,0:T(8,128)(2,1)S(1)} collective-permute-done((bf16[1,2,432,256]{3,2,1,0:T(8,128)(2,1)}, bf16[1,2,432,256]{3,2,1,0:T(8,128)(2,1)S(1)}, u32[]{:S(2)}, u32[]{:S(2)}) %collective-permute-start.11) | collective-permute-done | bytes 442400 | tf_op jit(solution)/shard_map/part4_shift1/ppermute | solution.py:359
  395.9 1.4 collective-permute-done.17.refs_1_.refs_3_.rest_11_
  398.6 1.5 collective-permute-start.12
  400.1 1.2 collective-permute-start.18
  401.3 16.1 %correlate.8 = (bf16[2,512,1024]{2,1,0:T(8,128)(2,1)}, f32[2,512,1024]{2,1,0:T(8,128)}) custom-call(s32[3]{0:T(128)} %pad_add_fusion.place_ref, bf16[4,2,144,256]{3,2,1,0:T(8,128)(2,1)} %bitcast.56, bf16[4,2,144,256]{3,2,1,0:T(8,128)(2,1)} %copy-done.2, bf16[4,2,144,256]{3,2,1,0:T(8,128)(2,1)} %copy-done.1, ...), custom_call_target="tpu_custom_call" | custom-call | flops 1024 | bytes 1024 | tf_op jit(solution)/shard_map/correlate/pallas_call | solution.py:296
  418.1 1.3 copy-done.9
  419.4 5.3 %equalize.5.rest_6_.rest_0_ = f32[4,2,512,1024]{3,2,1,0:T(8,128)} custom-call(f32[1,512]{1,0:T(1,128)} %bitcast.92, f32[1,1024]{1,0:T(1,128)} %bitcast.81, f32[2,512,1024]{2,1,0:T(8,128)} %get-tuple-element.72.mine_ref, bf16[2,512,1024]{2,1,0:T(8,128)(2,1)} %copy-done.9, f32[4,2,512,1024]{3,2,1,0:T(8,128)} %equalize.4.rest_0_, ...), custom_call_target="tpu_custom_call", output_to_operand_aliasing={{}: (4, {})} | custom-call | flops 1024 | bytes 1024 | tf_op jit(solution)/shard_map/equalize/pallas_call | solution.py:344
  424.6 12.5 %collective-permute-done.12.rest_3_ = bf16[1,2,432,256]{3,2,1,0:T(8,128)(2,1)S(1)} collective-permute-done((bf16[1,2,432,256]{3,2,1,0:T(8,128)(2,1)}, bf16[1,2,432,256]{3,2,1,0:T(8,128)(2,1)S(1)}, u32[]{:S(2)}, u32[]{:S(2)}) %collective-permute-start.12) | collective-permute-done | bytes 442400 | tf_op jit(solution)/shard_map/part5_shift1/ppermute | solution.py:359
  437.2 2.2 collective-permute-done.18.rest_5_
  440.1 11.6 %correlate.9 = (bf16[2,512,1024]{2,1,0:T(8,128)(2,1)}, f32[2,512,1024]{2,1,0:T(8,128)}) custom-call(s32[3]{0:T(128)} %pad_add_fusion.place_ref, f32[2,512,1024]{2,1,0:T(8,128)} %get-tuple-element.59.refs_1_.rest_0_, f32[2,512,1024]{2,1,0:T(8,128)} %get-tuple-element.60.refs_2_.rest_1_, bf16[1,2,432,256]{3,2,1,0:T(8,128)(2,1)} %bitcast.76, ...), custom_call_target="tpu_custom_call" | custom-call | flops 1024 | bytes 1024 | tf_op jit(solution)/shard_map/correlate/pallas_call | solution.py:296
  452.4 5.3 %equalize.6.rest_0_ = f32[4,2,512,1024]{3,2,1,0:T(8,128)} custom-call(f32[1,512]{1,0:T(1,128)} %bitcast.91, f32[1,1024]{1,0:T(1,128)} %bitcast.82, f32[2,512,1024]{2,1,0:T(8,128)} %get-tuple-element.80.mine_ref, bf16[2,512,1024]{2,1,0:T(8,128)(2,1)} %collective-permute-done.22.theirs_ref, ...), custom_call_target="tpu_custom_call", output_to_operand_aliasing={{}: (4, {})} | custom-call | flops 1024 | bytes 1024 | tf_op jit(solution)/shard_map/equalize/pallas_call | solution.py:344
  457.7 1.3 copy-done.11
  459.0 5.3 %equalize.7 = f32[4,2,512,1024]{3,2,1,0:T(8,128)} custom-call(f32[1,512]{1,0:T(1,128)} %bitcast.94, f32[1,1024]{1,0:T(1,128)} %bitcast.83, f32[2,512,1024]{2,1,0:T(8,128)} %get-tuple-element.78.mine_ref, bf16[2,512,1024]{2,1,0:T(8,128)(2,1)} %copy-done.11, f32[4,2,512,1024]{3,2,1,0:T(8,128)} %equalize.6.rest_0_), custom_call_target="tpu_custom_call", output_to_operand_aliasing={{}: (4, {})} | custom-call | flops 1024 | bytes 1024 | tf_op jit(solution)/shard_map/equalize/pallas_call | solution.py:344
  (106 shorter events, 15.0 us)
Async XLA Ops:
  15.6 44.6 %collective-permute-start = (bf16[2,1584,256]{2,1,0:T(8,128)(2,1)}, bf16[2,1584,256]{2,1,0:T(8,128)(2,1)}, u32[]{:S(2)}, u32[]{:S(2)}) collective-permute-start(bf16[2,1584,256]{2,1,0:T(8,128)(2,1)} %get-tuple-element.45), channel_id=1, source_target_pairs={{0,1},{2,3},{4,5},{6,7},{8,9},{10,11},{12,13},{14,15},{16,17},{18,... | collective-permute-start | bytes 4866056 | tf_op jit(solution)/shard_map/halo/ppermute | solution.py:364
  16.9 72.9 %collective-permute-start.1 = (bf16[4,2,144,256]{3,2,1,0:T(8,128)(2,1)}, bf16[4,2,144,256]{3,2,1,0:T(8,128)(2,1)S(1)}, u32[]{:S(2)}, u32[]{:S(2)}) collective-permute-start(bf16[4,2,144,256]{3,2,1,0:T(8,128)(2,1)} %bitcast.102), channel_id=1, source_target_pairs={{0,16},{8,24},{16,0},{24,8},{1,17},{9,25},{17,1},{25,9},{2,18},{10... | collective-permute-start | bytes 1769480 | tf_op jit(solution)/shard_map/part0_shift2/ppermute | solution.py:359
  19.2 101.7 %collective-permute-start.2 = (bf16[4,2,144,256]{3,2,1,0:T(8,128)(2,1)}, bf16[4,2,144,256]{3,2,1,0:T(8,128)(2,1)S(1)}, u32[]{:S(2)}, u32[]{:S(2)}) collective-permute-start(bf16[4,2,144,256]{3,2,1,0:T(8,128)(2,1)} %bitcast.101), channel_id=1, source_target_pairs={{0,8},{8,16},{16,24},{24,0},{1,9},{9,17},{17,25},{25,1},{2,10},{10... | collective-permute-start | bytes 1769480 | tf_op jit(solution)/shard_map/part0_shift1/ppermute | solution.py:359
  19.2 151.2 %collective-permute-start.7 = (bf16[4,2,144,256]{3,2,1,0:T(8,128)(2,1)}, bf16[4,2,144,256]{3,2,1,0:T(8,128)(2,1)}, u32[]{:S(2)}, u32[]{:S(2)}) collective-permute-start(bf16[4,2,144,256]{3,2,1,0:T(8,128)(2,1)} %bitcast.100), channel_id=1, source_target_pairs={{0,24},{8,0},{16,8},{24,16},{1,25},{9,1},{17,9},{25,17},{2,26},{10... | collective-permute-start | bytes 1769480 | tf_op jit(solution)/shard_map/part0_shift3/ppermute | solution.py:359
  59.3 140.9 %collective-permute-start.5 = (bf16[4,2,576,256]{3,2,1,0:T(8,128)(2,1)}, bf16[4,2,576,256]{3,2,1,0:T(8,128)(2,1)S(1)}, u32[]{:S(2)}, u32[]{:S(2)}) collective-permute-start(bf16[4,2,576,256]{3,2,1,0:T(8,128)(2,1)} %bitcast.99), channel_id=1, source_target_pairs={{0,16},{8,24},{16,0},{24,8},{1,17},{9,25},{17,1},{25,9},{2,18},{10... | collective-permute-start | bytes 7077896 | tf_op jit(solution)/shard_map/part1_shift2/ppermute | solution.py:359
  89.8 31.2 %copy-start.1 = (bf16[4,2,144,256]{3,2,1,0:T(8,128)(2,1)}, bf16[4,2,144,256]{3,2,1,0:T(8,128)(2,1)S(1)}, u32[]{:S(2)}) copy-start(bf16[4,2,144,256]{3,2,1,0:T(8,128)(2,1)S(1)} %collective-permute-done.1.refs_2_.rest_2_) | copy-start | bytes 1769476
  121.0 0.9 copy-start.2
  121.8 160.5 %collective-permute-start.3 = (bf16[4,2,576,256]{3,2,1,0:T(8,128)(2,1)}, bf16[4,2,576,256]{3,2,1,0:T(8,128)(2,1)}, u32[]{:S(2)}, u32[]{:S(2)}) collective-permute-start(bf16[4,2,576,256]{3,2,1,0:T(8,128)(2,1)} %after.16), channel_id=1, source_target_pairs={{0,8},{8,16},{16,24},{24,0},{1,9},{9,17},{17,25},{25,1},{2,10},{10... | collective-permute-start | bytes 7077896 | tf_op jit(solution)/shard_map/part1_shift1/ppermute | solution.py:359
  170.4 1.4 copy-start.21
  170.4 1.5 copy-start.22
  170.4 1.5 copy-start.23
  170.4 129.4 %collective-permute-start.8 = (bf16[4,2,576,256]{3,2,1,0:T(8,128)(2,1)}, bf16[4,2,576,256]{3,2,1,0:T(8,128)(2,1)}, u32[]{:S(2)}, u32[]{:S(2)}) collective-permute-start(bf16[4,2,576,256]{3,2,1,0:T(8,128)(2,1)} %after.19), channel_id=1, source_target_pairs={{0,24},{8,0},{16,8},{24,16},{1,25},{9,1},{17,9},{25,17},{2,26},{10... | collective-permute-start | bytes 7077896 | tf_op jit(solution)/shard_map/part1_shift3/ppermute | solution.py:359
  200.2 1.5 copy-start
  201.7 98.7 %collective-permute-start.6 = (bf16[880,256]{1,0:T(8,128)(2,1)}, bf16[880,256]{1,0:T(8,128)(2,1)S(1)}, u32[]{:S(2)}, u32[]{:S(2)}) collective-permute-start(bf16[880,256]{1,0:T(8,128)(2,1)} %after.18), channel_id=1, source_target_pairs={{0,16},{8,24},{16,0},{24,8},{1,17},{9,25},{17,1},{25,9},{2,18},{10... | collective-permute-start | bytes 1351688 | tf_op jit(solution)/shard_map/part2_shift2/ppermute | solution.py:359
  282.4 38.5 %collective-permute-start.4 = (bf16[880,256]{1,0:T(8,128)(2,1)}, bf16[880,256]{1,0:T(8,128)(2,1)S(1)}, u32[]{:S(2)}, u32[]{:S(2)}) collective-permute-start(bf16[880,256]{1,0:T(8,128)(2,1)} %after.17), channel_id=1, source_target_pairs={{0,8},{8,16},{16,24},{24,0},{1,9},{9,17},{17,25},{25,1},{2,10},{10... | collective-permute-start | bytes 1351688 | tf_op jit(solution)/shard_map/part2_shift1/ppermute | solution.py:359
  299.8 24.0 %collective-permute-start.9 = (bf16[880,256]{1,0:T(8,128)(2,1)}, bf16[880,256]{1,0:T(8,128)(2,1)S(1)}, u32[]{:S(2)}, u32[]{:S(2)}) collective-permute-start(bf16[880,256]{1,0:T(8,128)(2,1)} %after.20), channel_id=1, source_target_pairs={{0,24},{8,0},{16,8},{24,16},{1,25},{9,1},{17,9},{25,17},{2,26},{10... | collective-permute-start | bytes 1351688 | tf_op jit(solution)/shard_map/part2_shift3/ppermute | solution.py:359
  300.5 0.8 copy-start.14
  301.2 43.8 %collective-permute-start.13 = (bf16[1,2,432,256]{3,2,1,0:T(8,128)(2,1)}, bf16[1,2,432,256]{3,2,1,0:T(8,128)(2,1)S(1)}, u32[]{:S(2)}, u32[]{:S(2)}) collective-permute-start(bf16[1,2,432,256]{3,2,1,0:T(8,128)(2,1)} %after.24), channel_id=1, source_target_pairs={{0,16},{8,24},{16,0},{24,8},{1,17},{9,25},{17,1},{25,9},{2,18},{10... | collective-permute-start | bytes 1327112 | tf_op jit(solution)/shard_map/part3_shift2/ppermute | solution.py:359
  320.9 0.8 copy-start.12
  321.7 27.7 %collective-permute-start.10 = (bf16[1,2,432,256]{3,2,1,0:T(8,128)(2,1)}, bf16[1,2,432,256]{3,2,1,0:T(8,128)(2,1)S(1)}, u32[]{:S(2)}, u32[]{:S(2)}) collective-permute-start(bf16[1,2,432,256]{3,2,1,0:T(8,128)(2,1)} %after.21), channel_id=1, source_target_pairs={{0,8},{8,16},{16,24},{24,0},{1,9},{9,17},{17,25},{25,1},{2,10},{10... | collective-permute-start | bytes 1327112 | tf_op jit(solution)/shard_map/part3_shift1/ppermute | solution.py:359
  323.8 0.8 copy-start.16
  324.6 1.0 copy-start.15
  324.6 1.8 copy-start.13
  324.6 24.8 %collective-permute-start.16 = (bf16[1,2,432,256]{3,2,1,0:T(8,128)(2,1)}, bf16[1,2,432,256]{3,2,1,0:T(8,128)(2,1)S(1)}, u32[]{:S(2)}, u32[]{:S(2)}) collective-permute-start(bf16[1,2,432,256]{3,2,1,0:T(8,128)(2,1)} %after.27), channel_id=1, source_target_pairs={{0,24},{8,0},{16,8},{24,16},{1,25},{9,1},{17,9},{25,17},{2,26},{10... | collective-permute-start | bytes 1327112 | tf_op jit(solution)/shard_map/part3_shift3/ppermute | solution.py:359
  345.0 4.3 copy-start.3
  349.3 0.8 copy-start.4
  349.3 0.9 copy-start.5
  350.3 10.5 %copy-start.20 = (f32[256]{0:T(256)S(1)}, f32[256]{0:T(256)}, u32[]{:S(2)}) copy-start(f32[256]{0:T(256)} %add_rsqrt_fusion) | copy-start | bytes 3076
  350.3 30.3 %collective-permute-start.20 = (bf16[2,512,1024]{2,1,0:T(8,128)(2,1)}, bf16[2,512,1024]{2,1,0:T(8,128)(2,1)S(1)}, u32[]{:S(2)}, u32[]{:S(2)}) collective-permute-start(bf16[2,512,1024]{2,1,0:T(8,128)(2,1)} %after.31), channel_id=1, source_target_pairs={{0,1},{1,0},{2,3},{3,2},{4,5},{5,4},{6,7},{7,6},{8,9},{9,8},{10,11... | collective-permute-start | bytes 6291464 | tf_op jit(solution)/shard_map/rows0/ppermute | solution.py:451
  357.2 29.9 %collective-permute-start.14 = (bf16[1,2,432,256]{3,2,1,0:T(8,128)(2,1)}, bf16[1,2,432,256]{3,2,1,0:T(8,128)(2,1)S(1)}, u32[]{:S(2)}, u32[]{:S(2)}) collective-permute-start(bf16[1,2,432,256]{3,2,1,0:T(8,128)(2,1)} %after.25), channel_id=1, source_target_pairs={{0,16},{8,24},{16,0},{24,8},{1,17},{9,25},{17,1},{25,9},{2,18},{10... | collective-permute-start | bytes 1327112 | tf_op jit(solution)/shard_map/part4_shift2/ppermute | solution.py:359
  358.0 37.9 %collective-permute-start.11 = (bf16[1,2,432,256]{3,2,1,0:T(8,128)(2,1)}, bf16[1,2,432,256]{3,2,1,0:T(8,128)(2,1)S(1)}, u32[]{:S(2)}, u32[]{:S(2)}) collective-permute-start(bf16[1,2,432,256]{3,2,1,0:T(8,128)(2,1)} %after.22), channel_id=1, source_target_pairs={{0,8},{8,16},{16,24},{24,0},{1,9},{9,17},{17,25},{25,1},{2,10},{10... | collective-permute-start | bytes 1327112 | tf_op jit(solution)/shard_map/part4_shift1/ppermute | solution.py:359
  358.8 38.5 %collective-permute-start.17 = (bf16[1,2,432,256]{3,2,1,0:T(8,128)(2,1)}, bf16[1,2,432,256]{3,2,1,0:T(8,128)(2,1)S(1)}, u32[]{:S(2)}, u32[]{:S(2)}) collective-permute-start(bf16[1,2,432,256]{3,2,1,0:T(8,128)(2,1)} %after.28), channel_id=1, source_target_pairs={{0,24},{8,0},{16,8},{24,16},{1,25},{9,1},{17,9},{25,17},{2,26},{10... | collective-permute-start | bytes 1327112 | tf_op jit(solution)/shard_map/part4_shift3/ppermute | solution.py:359
  380.5 1.3 copy-start.10
  387.1 10.1 %copy-start.6 = (bf16[1,2,432,256]{3,2,1,0:T(8,128)(2,1)}, bf16[1,2,432,256]{3,2,1,0:T(8,128)(2,1)S(1)}, u32[]{:S(2)}) copy-start(bf16[1,2,432,256]{3,2,1,0:T(8,128)(2,1)S(1)} %collective-permute-done.14.refs_1_.refs_2_.rest_10_) | copy-start | bytes 1327108
  395.9 1.4 copy-start.7
  397.3 0.8 copy-start.8
  398.0 20.0 %collective-permute-start.19 = (bf16[2,512,1024]{2,1,0:T(8,128)(2,1)}, bf16[2,512,1024]{2,1,0:T(8,128)(2,1)S(1)}, u32[]{:S(2)}, u32[]{:S(2)}) collective-permute-start(bf16[2,512,1024]{2,1,0:T(8,128)(2,1)} %after.30), channel_id=1, source_target_pairs={{0,1},{1,0},{2,3},{3,2},{4,5},{5,4},{6,7},{7,6},{8,9},{9,8},{10,11... | collective-permute-start | bytes 6291464 | tf_op jit(solution)/shard_map/rows1/ppermute | solution.py:451
  398.6 26.0 %collective-permute-start.15 = (bf16[1,2,432,256]{3,2,1,0:T(8,128)(2,1)}, bf16[1,2,432,256]{3,2,1,0:T(8,128)(2,1)S(1)}, u32[]{:S(2)}, u32[]{:S(2)}) collective-permute-start(bf16[1,2,432,256]{3,2,1,0:T(8,128)(2,1)} %after.26), channel_id=1, source_target_pairs={{0,16},{8,24},{16,0},{24,8},{1,17},{9,25},{17,1},{25,9},{2,18},{10... | collective-permute-start | bytes 1327112 | tf_op jit(solution)/shard_map/part5_shift2/ppermute | solution.py:359
  398.6 38.6 %collective-permute-start.12 = (bf16[1,2,432,256]{3,2,1,0:T(8,128)(2,1)}, bf16[1,2,432,256]{3,2,1,0:T(8,128)(2,1)S(1)}, u32[]{:S(2)}, u32[]{:S(2)}) collective-permute-start(bf16[1,2,432,256]{3,2,1,0:T(8,128)(2,1)} %after.23), channel_id=1, source_target_pairs={{0,8},{8,16},{16,24},{24,0},{1,9},{9,17},{17,25},{25,1},{2,10},{10... | collective-permute-start | bytes 1327112 | tf_op jit(solution)/shard_map/part5_shift1/ppermute | solution.py:359
  400.1 39.2 %collective-permute-start.18 = (bf16[1,2,432,256]{3,2,1,0:T(8,128)(2,1)}, bf16[1,2,432,256]{3,2,1,0:T(8,128)(2,1)S(1)}, u32[]{:S(2)}, u32[]{:S(2)}) collective-permute-start(bf16[1,2,432,256]{3,2,1,0:T(8,128)(2,1)} %after.29), channel_id=1, source_target_pairs={{0,24},{8,0},{16,8},{24,16},{1,25},{9,1},{17,9},{25,17},{2,26},{10... | collective-permute-start | bytes 1327112 | tf_op jit(solution)/shard_map/part5_shift3/ppermute | solution.py:359
  417.4 35.0 %collective-permute-start.22 = (bf16[2,512,1024]{2,1,0:T(8,128)(2,1)}, bf16[2,512,1024]{2,1,0:T(8,128)(2,1)}, u32[]{:S(2)}, u32[]{:S(2)}) collective-permute-start(bf16[2,512,1024]{2,1,0:T(8,128)(2,1)} %get-tuple-element.77.rest_1_), channel_id=1, source_target_pairs={{0,1},{1,0},{2,3},{3,2},{4,5},{5,4},{6,7},{7,6},{8,9},{9,8},{10,11... | collective-permute-start | bytes 6291464 | tf_op jit(solution)/shard_map/rows2/ppermute | solution.py:451
  418.1 1.3 copy-start.9
  424.6 14.7 %copy-start.17 = (bf16[1,2,432,256]{3,2,1,0:T(8,128)(2,1)}, bf16[1,2,432,256]{3,2,1,0:T(8,128)(2,1)S(1)}, u32[]{:S(2)}) copy-start(bf16[1,2,432,256]{3,2,1,0:T(8,128)(2,1)S(1)} %collective-permute-done.15.rest_4_) | copy-start | bytes 1327108
  437.2 2.2 copy-start.18
  439.4 0.8 copy-start.19
  451.8 5.9 %collective-permute-start.21 = (bf16[2,512,1024]{2,1,0:T(8,128)(2,1)}, bf16[2,512,1024]{2,1,0:T(8,128)(2,1)S(1)}, u32[]{:S(2)}, u32[]{:S(2)}) collective-permute-start(bf16[2,512,1024]{2,1,0:T(8,128)(2,1)} %get-tuple-element.79.rest_1_), channel_id=1, source_target_pairs={{0,1},{1,0},{2,3},{3,2},{4,5},{5,4},{6,7},{7,6},{8,9},{9,8},{10,11... | collective-permute-start | bytes 6291464 | tf_op jit(solution)/shard_map/rows3/ppermute | solution.py:451
  457.7 1.3 copy-start.11

commit v10 on v9

--- a/solution.py
+++ b/solution.py
@@ -201,37 +201,30 @@
     )(value, *others)
 
 
-def with_scales_kernel(value_ref, scale_ref, out_ref, rows, sems):
+def with_scales_kernel(value_ref, scale_ref, out_ref):
     size = value_ref.shape[2]
     left = scale_ref[...]
     pieces = []
     for _ in range(3):
         piece = left.astype(jnp.bfloat16).astype(jnp.float32)
-        pieces.append(jnp.broadcast_to(piece, rows.shape))
+        pieces.append(jnp.broadcast_to(piece, (16, piece.shape[1])))
         left = left - piece
-    place = lax.broadcasted_iota(jnp.int32, rows.shape, 0)
+    place = lax.broadcasted_iota(jnp.int32, pieces[0].shape, 0)
     chosen = jnp.where(place == 0, pieces[0], jnp.where(place == 1, pieces[1], pieces[2]))
-    rows[...] = chosen.astype(jnp.bfloat16)
-    copies = [
-        pltpu.make_async_copy(value_ref.at[0, 0], out_ref.at[pl.ds(0, size)], sems.at[0]),
-        pltpu.make_async_copy(value_ref.at[0, 1], out_ref.at[pl.ds(size, size)], sems.at[1]),
-        pltpu.make_async_copy(rows, out_ref.at[pl.ds(2 * size, 16)], sems.at[2]),
-    ]
-    for copy in copies:
-        copy.start()
-    for copy in copies:
-        copy.wait()
+    out_ref[pl.ds(0, size), :] = value_ref[0, 0]
+    out_ref[pl.ds(size, size), :] = value_ref[0, 1]
+    out_ref[pl.ds(2 * size, 16), :] = chosen.astype(jnp.bfloat16)
 
 
 def with_scales(value, scale):
     size, inputs = value.shape[2:]
-    anywhere = pl.BlockSpec(memory_space=pl.ANY)
+    whole = pl.BlockSpec(memory_space=pltpu.VMEM)
     return pl.pallas_call(
         with_scales_kernel,
         out_shape=jax.ShapeDtypeStruct((2 * size + 16, inputs), value.dtype),
-        in_specs=[anywhere, pl.BlockSpec(memory_space=pltpu.VMEM)],
-        out_specs=anywhere,
-        scratch_shapes=[pltpu.VMEM((16, inputs), value.dtype), pltpu.SemaphoreType.DMA((3,))],
+        in_specs=[whole, whole],
+        out_specs=whole,
+        compiler_params=pltpu.CompilerParams(vmem_limit_bytes=VMEM),
         cost_estimate=COST,
         name="with_scales",
     )(value, scale)

time: 465 us -> 463 us (level)
  Pallas kernels: 221 us -> 181 us
  waiting for transfers between devices: 176 us -> 215 us
    pallas_call x3, Pallas kernels: 45.6 us -> 5.51 us  [with_scales(): pl.pallas_call(with_scales_kernel, out_shape=jax.ShapeDtypeStruct((2 * si...]
    ppermute x18, waiting for transfers between devices: 176 us -> 215 us  [shift(): lax.ppermute(value, 'station', [(s, (s + d) % count) for s in range(count)])]
  transfers between devices with their start and end apart: 23 -> 23, of which waited for: 9 -> 11; matrix products, arithmetic and copies ran while one was open for 3% -> 3% of each run, Pallas kernels for 44% -> 35%
where the time goes in v10:
time: 463 us; the launch traced here: 462 us
  waiting for transfers between devices  215 us (46%)
  Pallas kernels  181 us (39%)
  starting transfers between devices  26.4 us (6%)
  local copies, waits for them, and re-layouts  18.4 us (4%)
  blocking collectives  12.5 us (3%)
  other arithmetic  7.42 us (2%)
    ppermute x18, waiting for transfers between devices, shift(): lax.ppermute(value, 'station', [(s, (s + d) % count) for s in range(count)])  215 us
    pallas_call x3, Pallas kernels, front(): pl.pallas_call(functools.partial(front_kernel, runs, owners, turned, tail...  82.1 us
    pallas_call x5, Pallas kernels, correlate(): pl.pallas_call(functools.partial(correlate_kernel, owners, picks, outs, l...  72.7 us
    pallas_call x4, Pallas kernels, equalize(): pl.pallas_call(equalize_kernel, grid=(rows // block,), out_shape=jax.Shap...  21.1 us
    ppermute x18, starting transfers between devices, shift(): lax.ppermute(value, 'station', [(s, (s + d) % count) for s in range(count)])  21.1 us
    unnamed x51, local copies, waits for them, and re-layouts  13.5 us
    psum x1, blocking collectives, pipelined(): total = lax.psum(local, ('band', 'tm'))  12.5 us
  transfers between devices with their start and end apart: 23, of which 11 were waited for; matrix products, arithmetic and copies ran while one was open for 3% of the time, Pallas kernels for 35%

profile of v10, /device:TPU:11, one launch (start us, length us, event | category | flops | bytes accessed | tf_op | source)
XLA Modules:
  0.0 462.5 jit_solution(1214126756386520020)
XLA Ops:
  1.7 13.9 %front.3 = (bf16[4,2,9,16,256]{4,3,2,1,0:T(8,128)(2,1)}, bf16[4,2,9,16,256]{4,3,2,1,0:T(8,128)(2,1)}, bf16[4,2,9,16,256]{4,3,2,1,0:T(8,128)(2,1)}, bf16[4,2,9,16...) custom-call(s32[1]{0:T(128)} %bitcast.me_ref, f32[144]{0:T(256)} %dynamic_slice.14.keep_ref, ...), custom_call_target="tpu_custom_call" | custom-call | flops 1024 | bytes 1024 | tf_op jit(solution)/shard_map/front/pallas_call | solution.py:159
  15.6 1.3 collective-permute-start
  16.9 2.4 collective-permute-start.1
  19.2 1.5 collective-permute-start.7
  20.7 38.6 %front.4 = (bf16[4,2,9,64,256]{4,3,2,1,0:T(8,128)(2,1)}, bf16[4,2,9,64,256]{4,3,2,1,0:T(8,128)(2,1)}, bf16[4,2,9,64,256]{4,3,2,1,0:T(8,128)(2,1)}, bf16[4,2,9,64,256]{4,3,2,1,0:T(8,128)(2,1)}, f32[16,256]{1,0:T(8,128)}) custom-call(s32[1]{0:T(128)} %bitcast.me_ref, f32[144]{0:T(256)} %dynamic_slice.14.keep_ref, bf16[2,1,256,18432]{3,2,1,0:T(8,128)(2,1)} %volts_ref.5, ...), custom_call_target="tpu_custom_call" | custom-call | flops 1024 | bytes 1024 | tf_op jit(solution)/shard_map/front/pallas_call | solution.py:159
  59.3 0.9 collective-permute-start.5
  60.2 29.6 %front.5 = (bf16[1,2,9,48,256]{4,3,2,1,0:T(8,128)(2,1)}, bf16[1,2,9,48,256]{4,3,2,1,0:T(8,128)(2,1)}, bf16[1,2,9,48,256]{4,3,2,1,0:T(8,128)(2,1)}, bf16[1,2,9,48...) custom-call(s32[1]{0:T(128)} %bitcast.me_ref, ...), custom_call_target="tpu_custom_call" | custom-call | flops 1024 | bytes 1024 | tf_op jit(solution)/shard_map/front/pallas_call | solution.py:159
  89.8 31.2 %collective-permute-done.2.refs_3_.rest_1_ = bf16[4,2,144,256]{3,2,1,0:T(8,128)(2,1)S(1)} collective-permute-done((bf16[4,2,144,256]{3,2,1,0:T(8,128)(2,1)}, bf16[4,2,144,256]{3,2,1,0:T(8,128)(2,1)S(1)}, u32[]{:S(2)}, u32[]{:S(2)}) %collective-permute-start.2) | collective-permute-done | bytes 589856 | tf_op jit(solution)/shard_map/part0_shift1/ppermute | solution.py:352
  121.0 0.8 copy-done.2
  121.8 2.1 collective-permute-start.3
  123.9 46.5 %collective-permute-done.7.refs_3_.rest_3_ = bf16[4,2,144,256]{3,2,1,0:T(8,128)(2,1)} collective-permute-done((bf16[4,2,144,256]{3,2,1,0:T(8,128)(2,1)}, bf16[4,2,144,256]{3,2,1,0:T(8,128)(2,1)}, u32[]{:S(2)}, u32[]{:S(2)}) %collective-permute-start.7) | collective-permute-done | bytes 589856 | tf_op jit(solution)/shard_map/part0_shift3/ppermute | solution.py:352
  171.9 12.5 %psum.7 = f32[256]{0:T(256)S(1)} all-reduce(f32[256]{0:T(256)S(1)} %add_reduce_fusion), channel_id=1, replica_groups=mesh['station'=4,'band'=4,'tm'=2] {'band','tm'}, use_global_device_ids=true, to_apply=%region_2.3 | all-reduce | flops 256 | bytes 2048 | tf_op jit(solution)/shard_map/psum | solution.py:435
  185.0 1.8 with_scales.4.refs_0_
  186.9 1.5 copy-done
  188.3 1.5 collective-permute-start.6
  189.8 1.8 with_scales.3.refs_0_
  191.7 90.7 %collective-permute-done.3.refs_1_.rest_5_ = bf16[4,2,576,256]{3,2,1,0:T(8,128)(2,1)} collective-permute-done((bf16[4,2,576,256]{3,2,1,0:T(8,128)(2,1)}, bf16[4,2,576,256]{3,2,1,0:T(8,128)(2,1)}, u32[]{:S(2)}, u32[]{:S(2)}) %collective-permute-start.3) | collective-permute-done | bytes 2359328 | tf_op jit(solution)/shard_map/part1_shift1/ppermute | solution.py:352
  282.4 2.2 collective-permute-start.4
  284.6 1.8 with_scales.5.refs_0_
  286.4 4.5 collective-permute-done.8.refs_1_.rest_7_
  292.8 3.0 collective-permute-start.13
  295.8 12.9 %correlate.5 = (f32[2,512,1024]{2,1,0:T(8,128)}, f32[2,512,1024]{2,1,0:T(8,128)}) custom-call(s32[3]{0:T(128)} %pad_add_fusion.place_ref, bf16[4,2,144,256]{3,2,1,0:T(8,128)(2,1)} %bitcast.53, bf16[4,2,144,256]{3,2,1,0:T(8,128)(2,1)} %copy-done.2, bf16[4,2,144,256]{3,2,1,0:T(8,128)(2,1)} %copy-done.1, ...), custom_call_target="tpu_custom_call" | custom-call | flops 1024 | bytes 1024 | tf_op jit(solution)/shard_map/correlate/pallas_call | solution.py:289
  308.7 12.0 %collective-permute-done.4.refs_1_ = bf16[880,256]{1,0:T(8,128)(2,1)S(1)} collective-permute-done((bf16[880,256]{1,0:T(8,128)(2,1)}, bf16[880,256]{1,0:T(8,128)(2,1)S(1)}, u32[]{:S(2)}, u32[]{:S(2)}) %collective-permute-start.4) | collective-permute-done | bytes 450592 | tf_op jit(solution)/shard_map/part2_shift1/ppermute | solution.py:352
  321.5 2.2 collective-permute-start.10
  324.6 1.0 copy-done.15
  327.2 1.8 slice.45
  329.0 16.0 %correlate.7 = (bf16[2,512,1024]{2,1,0:T(8,128)(2,1)}, f32[2,512,1024]{2,1,0:T(8,128)}) custom-call(s32[3]{0:T(128)} %pad_add_fusion.place_ref, bf16[4,2,144,256]{3,2,1,0:T(8,128)(2,1)} %bitcast.54, bf16[4,2,144,256]{3,2,1,0:T(8,128)(2,1)} %copy-done.2, bf16[4,2,144,256]{3,2,1,0:T(8,128)(2,1)} %copy-done.1, ...), custom_call_target="tpu_custom_call" | custom-call | flops 1024 | bytes 1024 | tf_op jit(solution)/shard_map/correlate/pallas_call | solution.py:289
  345.0 4.3 collective-permute-done.10.refs_1_.rest_9_
  350.3 2.2 collective-permute-start.20
  354.1 1.3 collective-permute-start.14
  356.2 1.0 collective-permute-start.11
  359.1 3.0 broadcast_divide_fusion
  362.1 16.1 %correlate.6 = (bf16[2,512,1024]{2,1,0:T(8,128)(2,1)}, f32[2,512,1024]{2,1,0:T(8,128)}) custom-call(s32[3]{0:T(128)} %pad_add_fusion.place_ref, bf16[4,2,144,256]{3,2,1,0:T(8,128)(2,1)} %bitcast.55, bf16[4,2,144,256]{3,2,1,0:T(8,128)(2,1)} %copy-done.2, bf16[4,2,144,256]{3,2,1,0:T(8,128)(2,1)} %copy-done.1, ...), custom_call_target="tpu_custom_call" | custom-call | flops 1024 | bytes 1024 | tf_op jit(solution)/shard_map/correlate/pallas_call | solution.py:289
  378.2 1.3 copy-done.10
  379.5 5.3 %equalize.4.rest_0_ = f32[4,2,512,1024]{3,2,1,0:T(8,128)} custom-call(f32[1,512]{1,0:T(1,128)} %bitcast.93, f32[1,1024]{1,0:T(1,128)} %bitcast.80, f32[2,512,1024]{2,1,0:T(8,128)} %get-tuple-element.74.mine_ref, bf16[2,512,1024]{2,1,0:T(8,128)(2,1)} %copy-done.10, bf16[2,512,1024]{2,1,0:T(8,128)(2,1)} %get-tuple-element.73.refs_0_.rest_0_), custom_call_target="tpu_custom_call" | custom-call | flops 1024 | bytes 1024 | tf_op jit(solution)/shard_map/equalize/pallas_call | solution.py:337
  384.8 9.1 %collective-permute-done.11.refs_1_.rest_9_ = bf16[1,2,432,256]{3,2,1,0:T(8,128)(2,1)S(1)} collective-permute-done((bf16[1,2,432,256]{3,2,1,0:T(8,128)(2,1)}, bf16[1,2,432,256]{3,2,1,0:T(8,128)(2,1)S(1)}, u32[]{:S(2)}, u32[]{:S(2)}) %collective-permute-start.11) | collective-permute-done | bytes 442400 | tf_op jit(solution)/shard_map/part4_shift1/ppermute | solution.py:352
  393.9 1.8 collective-permute-done.17.refs_1_.refs_3_.rest_11_
  397.0 1.3 collective-permute-start.12
  398.3 1.2 collective-permute-start.18
  399.5 16.1 %correlate.8 = (bf16[2,512,1024]{2,1,0:T(8,128)(2,1)}, f32[2,512,1024]{2,1,0:T(8,128)}) custom-call(s32[3]{0:T(128)} %pad_add_fusion.place_ref, bf16[4,2,144,256]{3,2,1,0:T(8,128)(2,1)} %bitcast.56, bf16[4,2,144,256]{3,2,1,0:T(8,128)(2,1)} %copy-done.2, bf16[4,2,144,256]{3,2,1,0:T(8,128)(2,1)} %copy-done.1, ...), custom_call_target="tpu_custom_call" | custom-call | flops 1024 | bytes 1024 | tf_op jit(solution)/shard_map/correlate/pallas_call | solution.py:289
  416.2 1.3 copy-done.9
  417.5 5.3 %equalize.5.rest_6_.rest_0_ = f32[4,2,512,1024]{3,2,1,0:T(8,128)} custom-call(f32[1,512]{1,0:T(1,128)} %bitcast.92, f32[1,1024]{1,0:T(1,128)} %bitcast.81, f32[2,512,1024]{2,1,0:T(8,128)} %get-tuple-element.72.mine_ref, bf16[2,512,1024]{2,1,0:T(8,128)(2,1)} %copy-done.9, f32[4,2,512,1024]{3,2,1,0:T(8,128)} %equalize.4.rest_0_, ...), custom_call_target="tpu_custom_call", output_to_operand_aliasing={{}: (4, {})} | custom-call | flops 1024 | bytes 1024 | tf_op jit(solution)/shard_map/equalize/pallas_call | solution.py:337
  422.8 12.8 %collective-permute-done.12.rest_3_ = bf16[1,2,432,256]{3,2,1,0:T(8,128)(2,1)S(1)} collective-permute-done((bf16[1,2,432,256]{3,2,1,0:T(8,128)(2,1)}, bf16[1,2,432,256]{3,2,1,0:T(8,128)(2,1)S(1)}, u32[]{:S(2)}, u32[]{:S(2)}) %collective-permute-start.12) | collective-permute-done | bytes 442400 | tf_op jit(solution)/shard_map/part5_shift1/ppermute | solution.py:352
  435.6 1.9 collective-permute-done.18.rest_5_
  438.3 11.6 %correlate.9 = (bf16[2,512,1024]{2,1,0:T(8,128)(2,1)}, f32[2,512,1024]{2,1,0:T(8,128)}) custom-call(s32[3]{0:T(128)} %pad_add_fusion.place_ref, f32[2,512,1024]{2,1,0:T(8,128)} %get-tuple-element.59.refs_1_.rest_0_, f32[2,512,1024]{2,1,0:T(8,128)} %get-tuple-element.60.refs_2_.rest_1_, bf16[1,2,432,256]{3,2,1,0:T(8,128)(2,1)} %bitcast.76, ...), custom_call_target="tpu_custom_call" | custom-call | flops 1024 | bytes 1024 | tf_op jit(solution)/shard_map/correlate/pallas_call | solution.py:289
  450.6 5.3 %equalize.6.rest_0_ = f32[4,2,512,1024]{3,2,1,0:T(8,128)} custom-call(f32[1,512]{1,0:T(1,128)} %bitcast.91, f32[1,1024]{1,0:T(1,128)} %bitcast.82, f32[2,512,1024]{2,1,0:T(8,128)} %get-tuple-element.80.mine_ref, bf16[2,512,1024]{2,1,0:T(8,128)(2,1)} %collective-permute-done.22.theirs_ref, ...), custom_call_target="tpu_custom_call", output_to_operand_aliasing={{}: (4, {})} | custom-call | flops 1024 | bytes 1024 | tf_op jit(solution)/shard_map/equalize/pallas_call | solution.py:337
  455.9 1.3 copy-done.11
  457.2 5.3 %equalize.7 = f32[4,2,512,1024]{3,2,1,0:T(8,128)} custom-call(f32[1,512]{1,0:T(1,128)} %bitcast.94, f32[1,1024]{1,0:T(1,128)} %bitcast.83, f32[2,512,1024]{2,1,0:T(8,128)} %get-tuple-element.78.mine_ref, bf16[2,512,1024]{2,1,0:T(8,128)(2,1)} %copy-done.11, f32[4,2,512,1024]{3,2,1,0:T(8,128)} %equalize.6.rest_0_), custom_call_target="tpu_custom_call", output_to_operand_aliasing={{}: (4, {})} | custom-call | flops 1024 | bytes 1024 | tf_op jit(solution)/shard_map/equalize/pallas_call | solution.py:337
  (106 shorter events, 16.8 us)
Async XLA Ops:
  15.6 44.6 %collective-permute-start = (bf16[2,1584,256]{2,1,0:T(8,128)(2,1)}, bf16[2,1584,256]{2,1,0:T(8,128)(2,1)}, u32[]{:S(2)}, u32[]{:S(2)}) collective-permute-start(bf16[2,1584,256]{2,1,0:T(8,128)(2,1)} %get-tuple-element.45), channel_id=1, source_target_pairs={{0,1},{2,3},{4,5},{6,7},{8,9},{10,11},{12,13},{14,15},{16,17},{18,... | collective-permute-start | bytes 4866056 | tf_op jit(solution)/shard_map/halo/ppermute | solution.py:357
  16.9 72.9 %collective-permute-start.1 = (bf16[4,2,144,256]{3,2,1,0:T(8,128)(2,1)}, bf16[4,2,144,256]{3,2,1,0:T(8,128)(2,1)S(1)}, u32[]{:S(2)}, u32[]{:S(2)}) collective-permute-start(bf16[4,2,144,256]{3,2,1,0:T(8,128)(2,1)} %bitcast.102), channel_id=1, source_target_pairs={{0,16},{8,24},{16,0},{24,8},{1,17},{9,25},{17,1},{25,9},{2,18},{10... | collective-permute-start | bytes 1769480 | tf_op jit(solution)/shard_map/part0_shift2/ppermute | solution.py:352
  19.2 101.7 %collective-permute-start.2 = (bf16[4,2,144,256]{3,2,1,0:T(8,128)(2,1)}, bf16[4,2,144,256]{3,2,1,0:T(8,128)(2,1)S(1)}, u32[]{:S(2)}, u32[]{:S(2)}) collective-permute-start(bf16[4,2,144,256]{3,2,1,0:T(8,128)(2,1)} %bitcast.101), channel_id=1, source_target_pairs={{0,8},{8,16},{16,24},{24,0},{1,9},{9,17},{17,25},{25,1},{2,10},{10... | collective-permute-start | bytes 1769480 | tf_op jit(solution)/shard_map/part0_shift1/ppermute | solution.py:352
  19.2 151.2 %collective-permute-start.7 = (bf16[4,2,144,256]{3,2,1,0:T(8,128)(2,1)}, bf16[4,2,144,256]{3,2,1,0:T(8,128)(2,1)}, u32[]{:S(2)}, u32[]{:S(2)}) collective-permute-start(bf16[4,2,144,256]{3,2,1,0:T(8,128)(2,1)} %bitcast.100), channel_id=1, source_target_pairs={{0,24},{8,0},{16,8},{24,16},{1,25},{9,1},{17,9},{25,17},{2,26},{10... | collective-permute-start | bytes 1769480 | tf_op jit(solution)/shard_map/part0_shift3/ppermute | solution.py:352
  59.3 127.6 %collective-permute-start.5 = (bf16[4,2,576,256]{3,2,1,0:T(8,128)(2,1)}, bf16[4,2,576,256]{3,2,1,0:T(8,128)(2,1)S(1)}, u32[]{:S(2)}, u32[]{:S(2)}) collective-permute-start(bf16[4,2,576,256]{3,2,1,0:T(8,128)(2,1)} %bitcast.99), channel_id=1, source_target_pairs={{0,16},{8,24},{16,0},{24,8},{1,17},{9,25},{17,1},{25,9},{2,18},{10... | collective-permute-start | bytes 7077896 | tf_op jit(solution)/shard_map/part1_shift2/ppermute | solution.py:352
  89.8 31.2 %copy-start.1 = (bf16[4,2,144,256]{3,2,1,0:T(8,128)(2,1)}, bf16[4,2,144,256]{3,2,1,0:T(8,128)(2,1)S(1)}, u32[]{:S(2)}) copy-start(bf16[4,2,144,256]{3,2,1,0:T(8,128)(2,1)S(1)} %collective-permute-done.1.refs_2_.rest_2_) | copy-start | bytes 1769476
  121.0 0.9 copy-start.2
  121.8 160.5 %collective-permute-start.3 = (bf16[4,2,576,256]{3,2,1,0:T(8,128)(2,1)}, bf16[4,2,576,256]{3,2,1,0:T(8,128)(2,1)}, u32[]{:S(2)}, u32[]{:S(2)}) collective-permute-start(bf16[4,2,576,256]{3,2,1,0:T(8,128)(2,1)} %after.16), channel_id=1, source_target_pairs={{0,8},{8,16},{16,24},{24,0},{1,9},{9,17},{17,25},{25,1},{2,10},{10... | collective-permute-start | bytes 7077896 | tf_op jit(solution)/shard_map/part1_shift1/ppermute | solution.py:352
  170.4 1.4 copy-start.21
  170.4 1.5 copy-start.22
  170.4 1.5 copy-start.23
  170.4 120.5 %collective-permute-start.8 = (bf16[4,2,576,256]{3,2,1,0:T(8,128)(2,1)}, bf16[4,2,576,256]{3,2,1,0:T(8,128)(2,1)}, u32[]{:S(2)}, u32[]{:S(2)}) collective-permute-start(bf16[4,2,576,256]{3,2,1,0:T(8,128)(2,1)} %after.19), channel_id=1, source_target_pairs={{0,24},{8,0},{16,8},{24,16},{1,25},{9,1},{17,9},{25,17},{2,26},{10... | collective-permute-start | bytes 7077896 | tf_op jit(solution)/shard_map/part1_shift3/ppermute | solution.py:352
  186.9 1.5 copy-start
  188.3 103.7 %collective-permute-start.6 = (bf16[880,256]{1,0:T(8,128)(2,1)}, bf16[880,256]{1,0:T(8,128)(2,1)S(1)}, u32[]{:S(2)}, u32[]{:S(2)}) collective-permute-start(bf16[880,256]{1,0:T(8,128)(2,1)} %after.18), channel_id=1, source_target_pairs={{0,16},{8,24},{16,0},{24,8},{1,17},{9,25},{17,1},{25,9},{2,18},{10... | collective-permute-start | bytes 1351688 | tf_op jit(solution)/shard_map/part2_shift2/ppermute | solution.py:352
  282.4 38.3 %collective-permute-start.4 = (bf16[880,256]{1,0:T(8,128)(2,1)}, bf16[880,256]{1,0:T(8,128)(2,1)S(1)}, u32[]{:S(2)}, u32[]{:S(2)}) collective-permute-start(bf16[880,256]{1,0:T(8,128)(2,1)} %after.17), channel_id=1, source_target_pairs={{0,8},{8,16},{16,24},{24,0},{1,9},{9,17},{17,25},{25,1},{2,10},{10... | collective-permute-start | bytes 1351688 | tf_op jit(solution)/shard_map/part2_shift1/ppermute | solution.py:352
  290.9 32.9 %collective-permute-start.9 = (bf16[880,256]{1,0:T(8,128)(2,1)}, bf16[880,256]{1,0:T(8,128)(2,1)S(1)}, u32[]{:S(2)}, u32[]{:S(2)}) collective-permute-start(bf16[880,256]{1,0:T(8,128)(2,1)} %after.20), channel_id=1, source_target_pairs={{0,24},{8,0},{16,8},{24,16},{1,25},{9,1},{17,9},{25,17},{2,26},{10... | collective-permute-start | bytes 1351688 | tf_op jit(solution)/shard_map/part2_shift3/ppermute | solution.py:352
  292.1 0.8 copy-start.14
  292.8 52.2 %collective-permute-start.13 = (bf16[1,2,432,256]{3,2,1,0:T(8,128)(2,1)}, bf16[1,2,432,256]{3,2,1,0:T(8,128)(2,1)S(1)}, u32[]{:S(2)}, u32[]{:S(2)}) collective-permute-start(bf16[1,2,432,256]{3,2,1,0:T(8,128)(2,1)} %after.24), channel_id=1, source_target_pairs={{0,16},{8,24},{16,0},{24,8},{1,17},{9,25},{17,1},{25,9},{2,18},{10... | collective-permute-start | bytes 1327112 | tf_op jit(solution)/shard_map/part3_shift2/ppermute | solution.py:352
  320.7 0.8 copy-start.12
  321.5 27.8 %collective-permute-start.10 = (bf16[1,2,432,256]{3,2,1,0:T(8,128)(2,1)}, bf16[1,2,432,256]{3,2,1,0:T(8,128)(2,1)S(1)}, u32[]{:S(2)}, u32[]{:S(2)}) collective-permute-start(bf16[1,2,432,256]{3,2,1,0:T(8,128)(2,1)} %after.21), channel_id=1, source_target_pairs={{0,8},{8,16},{16,24},{24,0},{1,9},{9,17},{17,25},{25,1},{2,10},{10... | collective-permute-start | bytes 1327112 | tf_op jit(solution)/shard_map/part3_shift1/ppermute | solution.py:352
  323.8 0.8 copy-start.16
  324.6 1.0 copy-start.15
  324.6 1.8 copy-start.13
  324.6 24.8 %collective-permute-start.16 = (bf16[1,2,432,256]{3,2,1,0:T(8,128)(2,1)}, bf16[1,2,432,256]{3,2,1,0:T(8,128)(2,1)S(1)}, u32[]{:S(2)}, u32[]{:S(2)}) collective-permute-start(bf16[1,2,432,256]{3,2,1,0:T(8,128)(2,1)} %after.27), channel_id=1, source_target_pairs={{0,24},{8,0},{16,8},{24,16},{1,25},{9,1},{17,9},{25,17},{2,26},{10... | collective-permute-start | bytes 1327112 | tf_op jit(solution)/shard_map/part3_shift3/ppermute | solution.py:352
  345.0 4.3 copy-start.3
  349.3 0.8 copy-start.4
  349.3 0.9 copy-start.5
  350.3 8.1 %copy-start.20 = (f32[256]{0:T(256)S(1)}, f32[256]{0:T(256)}, u32[]{:S(2)}) copy-start(f32[256]{0:T(256)} %add_rsqrt_fusion) | copy-start | bytes 3076
  350.3 27.9 %collective-permute-start.20 = (bf16[2,512,1024]{2,1,0:T(8,128)(2,1)}, bf16[2,512,1024]{2,1,0:T(8,128)(2,1)S(1)}, u32[]{:S(2)}, u32[]{:S(2)}) collective-permute-start(bf16[2,512,1024]{2,1,0:T(8,128)(2,1)} %after.31), channel_id=1, source_target_pairs={{0,1},{1,0},{2,3},{3,2},{4,5},{5,4},{6,7},{7,6},{8,9},{9,8},{10,11... | collective-permute-start | bytes 6291464 | tf_op jit(solution)/shard_map/rows0/ppermute | solution.py:444
  354.1 30.6 %collective-permute-start.14 = (bf16[1,2,432,256]{3,2,1,0:T(8,128)(2,1)}, bf16[1,2,432,256]{3,2,1,0:T(8,128)(2,1)S(1)}, u32[]{:S(2)}, u32[]{:S(2)}) collective-permute-start(bf16[1,2,432,256]{3,2,1,0:T(8,128)(2,1)} %after.25), channel_id=1, source_target_pairs={{0,16},{8,24},{16,0},{24,8},{1,17},{9,25},{17,1},{25,9},{2,18},{10... | collective-permute-start | bytes 1327112 | tf_op jit(solution)/shard_map/part4_shift2/ppermute | solution.py:352
  356.2 37.7 %collective-permute-start.11 = (bf16[1,2,432,256]{3,2,1,0:T(8,128)(2,1)}, bf16[1,2,432,256]{3,2,1,0:T(8,128)(2,1)S(1)}, u32[]{:S(2)}, u32[]{:S(2)}) collective-permute-start(bf16[1,2,432,256]{3,2,1,0:T(8,128)(2,1)} %after.22), channel_id=1, source_target_pairs={{0,8},{8,16},{16,24},{24,0},{1,9},{9,17},{17,25},{25,1},{2,10},{10... | collective-permute-start | bytes 1327112 | tf_op jit(solution)/shard_map/part4_shift1/ppermute | solution.py:352
  357.2 38.5 %collective-permute-start.17 = (bf16[1,2,432,256]{3,2,1,0:T(8,128)(2,1)}, bf16[1,2,432,256]{3,2,1,0:T(8,128)(2,1)S(1)}, u32[]{:S(2)}, u32[]{:S(2)}) collective-permute-start(bf16[1,2,432,256]{3,2,1,0:T(8,128)(2,1)} %after.28), channel_id=1, source_target_pairs={{0,24},{8,0},{16,8},{24,16},{1,25},{9,1},{17,9},{25,17},{2,26},{10... | collective-permute-start | bytes 1327112 | tf_op jit(solution)/shard_map/part4_shift3/ppermute | solution.py:352
  378.2 1.3 copy-start.10
  384.8 10.9 %copy-start.6 = (bf16[1,2,432,256]{3,2,1,0:T(8,128)(2,1)}, bf16[1,2,432,256]{3,2,1,0:T(8,128)(2,1)S(1)}, u32[]{:S(2)}) copy-start(bf16[1,2,432,256]{3,2,1,0:T(8,128)(2,1)S(1)} %collective-permute-done.14.refs_1_.refs_2_.rest_10_) | copy-start | bytes 1327108
  393.9 1.8 copy-start.7
  395.6 0.8 copy-start.8
  396.4 19.8 %collective-permute-start.19 = (bf16[2,512,1024]{2,1,0:T(8,128)(2,1)}, bf16[2,512,1024]{2,1,0:T(8,128)(2,1)S(1)}, u32[]{:S(2)}, u32[]{:S(2)}) collective-permute-start(bf16[2,512,1024]{2,1,0:T(8,128)(2,1)} %after.30), channel_id=1, source_target_pairs={{0,1},{1,0},{2,3},{3,2},{4,5},{5,4},{6,7},{7,6},{8,9},{9,8},{10,11... | collective-permute-start | bytes 6291464 | tf_op jit(solution)/shard_map/rows1/ppermute | solution.py:444
  397.0 25.8 %collective-permute-start.15 = (bf16[1,2,432,256]{3,2,1,0:T(8,128)(2,1)}, bf16[1,2,432,256]{3,2,1,0:T(8,128)(2,1)S(1)}, u32[]{:S(2)}, u32[]{:S(2)}) collective-permute-start(bf16[1,2,432,256]{3,2,1,0:T(8,128)(2,1)} %after.26), channel_id=1, source_target_pairs={{0,16},{8,24},{16,0},{24,8},{1,17},{9,25},{17,1},{25,9},{2,18},{10... | collective-permute-start | bytes 1327112 | tf_op jit(solution)/shard_map/part5_shift2/ppermute | solution.py:352
  397.0 38.6 %collective-permute-start.12 = (bf16[1,2,432,256]{3,2,1,0:T(8,128)(2,1)}, bf16[1,2,432,256]{3,2,1,0:T(8,128)(2,1)S(1)}, u32[]{:S(2)}, u32[]{:S(2)}) collective-permute-start(bf16[1,2,432,256]{3,2,1,0:T(8,128)(2,1)} %after.23), channel_id=1, source_target_pairs={{0,8},{8,16},{16,24},{24,0},{1,9},{9,17},{17,25},{25,1},{2,10},{10... | collective-permute-start | bytes 1327112 | tf_op jit(solution)/shard_map/part5_shift1/ppermute | solution.py:352
  398.3 39.2 %collective-permute-start.18 = (bf16[1,2,432,256]{3,2,1,0:T(8,128)(2,1)}, bf16[1,2,432,256]{3,2,1,0:T(8,128)(2,1)S(1)}, u32[]{:S(2)}, u32[]{:S(2)}) collective-permute-start(bf16[1,2,432,256]{3,2,1,0:T(8,128)(2,1)} %after.29), channel_id=1, source_target_pairs={{0,24},{8,0},{16,8},{24,16},{1,25},{9,1},{17,9},{25,17},{2,26},{10... | collective-permute-start | bytes 1327112 | tf_op jit(solution)/shard_map/part5_shift3/ppermute | solution.py:352
  415.6 35.0 %collective-permute-start.22 = (bf16[2,512,1024]{2,1,0:T(8,128)(2,1)}, bf16[2,512,1024]{2,1,0:T(8,128)(2,1)}, u32[]{:S(2)}, u32[]{:S(2)}) collective-permute-start(bf16[2,512,1024]{2,1,0:T(8,128)(2,1)} %get-tuple-element.77.rest_1_), channel_id=1, source_target_pairs={{0,1},{1,0},{2,3},{3,2},{4,5},{5,4},{6,7},{7,6},{8,9},{9,8},{10,11... | collective-permute-start | bytes 6291464 | tf_op jit(solution)/shard_map/rows2/ppermute | solution.py:444
  416.2 1.3 copy-start.9
  422.8 14.7 %copy-start.17 = (bf16[1,2,432,256]{3,2,1,0:T(8,128)(2,1)}, bf16[1,2,432,256]{3,2,1,0:T(8,128)(2,1)S(1)}, u32[]{:S(2)}) copy-start(bf16[1,2,432,256]{3,2,1,0:T(8,128)(2,1)S(1)} %collective-permute-done.15.rest_4_) | copy-start | bytes 1327108
  435.6 2.0 copy-start.18
  437.5 0.8 copy-start.19
  449.9 5.9 %collective-permute-start.21 = (bf16[2,512,1024]{2,1,0:T(8,128)(2,1)}, bf16[2,512,1024]{2,1,0:T(8,128)(2,1)S(1)}, u32[]{:S(2)}, u32[]{:S(2)}) collective-permute-start(bf16[2,512,1024]{2,1,0:T(8,128)(2,1)} %get-tuple-element.79.rest_1_), channel_id=1, source_target_pairs={{0,1},{1,0},{2,3},{3,2},{4,5},{5,4},{6,7},{7,6},{8,9},{9,8},{10,11... | collective-permute-start | bytes 6291464 | tf_op jit(solution)/shard_map/rows3/ppermute | solution.py:444
  455.9 1.3 copy-start.11

commit v11 on v10

--- a/solution.py
+++ b/solution.py
@@ -471,7 +471,6 @@
     column_scales = scales[None, :]
     row_scales = [(row_scales / denom[j])[None, :] for j in range(groups)]
 
-    partial = multiply(groups - 1, place, [jnp.float32] * 2, end=shared)
     waiting = []
 
     def settle(out, earlier):
@@ -482,7 +481,7 @@
 
     done = 0
     for q, run in enumerate(runs[:-1]):
-        send(shared + q + 1, {owners - 1: partial} if q == 0 else {})
+        send(shared + q + 1, {})
         results = [multiply(j, place, both) for j in range(done, done + run)]
         if waiting:
             out = settle(out, [x[0] for x in results])
@@ -492,6 +491,8 @@
             waiting.append((j, mine, to_other(j, theirs)))
         done += run
     j = groups - 1
+    gates = [] if out is None else [out]
+    partial = multiply(j, place, [jnp.float32] * 2, earlier=gates, end=shared)
     theirs, mine = multiply(j, place, both, partial, [] if out is None else [out], begin=shared)
     out = settle(out, [theirs])
     waiting.append((j, mine, to_other(j, theirs)))

time: 463 us -> 464 us (level)
  transfers between devices with their start and end apart: 23 -> 23, of which waited for: 11 -> 10; matrix products, arithmetic and copies ran while one was open for 3% -> 3% of each run, Pallas kernels for 35% -> 35%
where the time goes in v11:
time: 464 us; the launch traced here: 462 us
  waiting for transfers between devices  218 us (47%)
  Pallas kernels  181 us (39%)
  starting transfers between devices  25.5 us (5%)
  local copies, waits for them, and re-layouts  17.3 us (4%)
  blocking collectives  11.3 us (2%)
  other arithmetic  7.64 us (2%)
    ppermute x18, waiting for transfers between devices, shift(): lax.ppermute(value, 'station', [(s, (s + d) % count) for s in range(count)])  218 us
    pallas_call x3, Pallas kernels, front(): pl.pallas_call(functools.partial(front_kernel, runs, owners, turned, tail...  82 us
    pallas_call x5, Pallas kernels, correlate(): pl.pallas_call(functools.partial(correlate_kernel, owners, picks, outs, l...  72.7 us
    ppermute x18, starting transfers between devices, shift(): lax.ppermute(value, 'station', [(s, (s + d) % count) for s in range(count)])  21.3 us
    pallas_call x4, Pallas kernels, equalize(): pl.pallas_call(equalize_kernel, grid=(rows // block,), out_shape=jax.Shap...  21.3 us
    unnamed x51, local copies, waits for them, and re-layouts  12.3 us
    psum x1, blocking collectives, pipelined(): total = lax.psum(local, ('band', 'tm'))  11.3 us
  transfers between devices with their start and end apart: 23, of which 10 were waited for; matrix products, arithmetic and copies ran while one was open for 3% of the time, Pallas kernels for 35%

profile of v11, /device:TPU:11, one launch (start us, length us, event | category | flops | bytes accessed | tf_op | source)
XLA Modules:
  0.0 462.1 jit_solution(3650539474234530438)
XLA Ops:
  1.7 13.9 %front.3 = (bf16[4,2,9,16,256]{4,3,2,1,0:T(8,128)(2,1)}, bf16[4,2,9,16,256]{4,3,2,1,0:T(8,128)(2,1)}, bf16[4,2,9,16,256]{4,3,2,1,0:T(8,128)(2,1)}, bf16[4,2,9,16...) custom-call(s32[1]{0:T(128)} %bitcast.me_ref, f32[144]{0:T(256)} %dynamic_slice.14.keep_ref, ...), custom_call_target="tpu_custom_call" | custom-call | flops 1024 | bytes 1024 | tf_op jit(solution)/shard_map/front/pallas_call | solution.py:159
  15.5 1.3 collective-permute-start
  16.8 2.4 collective-permute-start.1
  19.4 1.3 collective-permute-start.2
  20.7 38.6 %front.4 = (bf16[4,2,9,64,256]{4,3,2,1,0:T(8,128)(2,1)}, bf16[4,2,9,64,256]{4,3,2,1,0:T(8,128)(2,1)}, bf16[4,2,9,64,256]{4,3,2,1,0:T(8,128)(2,1)}, bf16[4,2,9,64,256]{4,3,2,1,0:T(8,128)(2,1)}, f32[16,256]{1,0:T(8,128)}) custom-call(s32[1]{0:T(128)} %bitcast.me_ref, f32[144]{0:T(256)} %dynamic_slice.14.keep_ref, bf16[2,1,256,18432]{3,2,1,0:T(8,128)(2,1)} %volts_ref.5, ...), custom_call_target="tpu_custom_call" | custom-call | flops 1024 | bytes 1024 | tf_op jit(solution)/shard_map/front/pallas_call | solution.py:159
  59.2 1.9 collective-permute-start.5
  61.1 29.6 %front.5 = (bf16[1,2,9,48,256]{4,3,2,1,0:T(8,128)(2,1)}, bf16[1,2,9,48,256]{4,3,2,1,0:T(8,128)(2,1)}, bf16[1,2,9,48,256]{4,3,2,1,0:T(8,128)(2,1)}, bf16[1,2,9,48...) custom-call(s32[1]{0:T(128)} %bitcast.me_ref, ...), custom_call_target="tpu_custom_call" | custom-call | flops 1024 | bytes 1024 | tf_op jit(solution)/shard_map/front/pallas_call | solution.py:159
  90.7 29.0 %collective-permute-done.7.refs_3_.rest_3_ = bf16[4,2,144,256]{3,2,1,0:T(8,128)(2,1)S(1)} collective-permute-done((bf16[4,2,144,256]{3,2,1,0:T(8,128)(2,1)}, bf16[4,2,144,256]{3,2,1,0:T(8,128)(2,1)S(1)}, u32[]{:S(2)}, u32[]{:S(2)}) %collective-permute-start.7) | collective-permute-done | bytes 589856 | tf_op jit(solution)/shard_map/part0_shift3/ppermute | solution.py:352
  119.7 0.8 copy-done.2
  120.5 51.0 %collective-permute-done.2.refs_3_.rest_1_ = bf16[4,2,144,256]{3,2,1,0:T(8,128)(2,1)} collective-permute-done((bf16[4,2,144,256]{3,2,1,0:T(8,128)(2,1)}, bf16[4,2,144,256]{3,2,1,0:T(8,128)(2,1)}, u32[]{:S(2)}, u32[]{:S(2)}) %collective-permute-start.2) | collective-permute-done | bytes 589856 | tf_op jit(solution)/shard_map/part0_shift1/ppermute | solution.py:352
  171.5 2.2 collective-permute-start.3
  175.2 11.3 %psum.7 = f32[256]{0:T(256)S(1)} all-reduce(f32[256]{0:T(256)S(1)} %add_reduce_fusion), channel_id=1, replica_groups=mesh['station'=4,'band'=4,'tm'=2] {'band','tm'}, use_global_device_ids=true, to_apply=%region_2.3 | all-reduce | flops 256 | bytes 2048 | tf_op jit(solution)/shard_map/psum | solution.py:435
  187.1 1.8 with_scales.4.refs_0_
  188.9 33.2 %collective-permute-done.5.refs_1_.rest_6_ = bf16[4,2,576,256]{3,2,1,0:T(8,128)(2,1)S(1)} collective-permute-done((bf16[4,2,576,256]{3,2,1,0:T(8,128)(2,1)}, bf16[4,2,576,256]{3,2,1,0:T(8,128)(2,1)S(1)}, u32[]{:S(2)}, u32[]{:S(2)}) %collective-permute-start.5) | collective-permute-done | bytes 2359328 | tf_op jit(solution)/shard_map/part1_shift2/ppermute | solution.py:352
  222.1 1.5 copy-done
  223.6 3.0 collective-permute-start.6
  226.6 1.8 with_scales.5.refs_0_
  228.4 52.7 %collective-permute-done.8.refs_1_.rest_7_ = bf16[4,2,576,256]{3,2,1,0:T(8,128)(2,1)} collective-permute-done((bf16[4,2,576,256]{3,2,1,0:T(8,128)(2,1)}, bf16[4,2,576,256]{3,2,1,0:T(8,128)(2,1)}, u32[]{:S(2)}, u32[]{:S(2)}) %collective-permute-start.8) | collective-permute-done | bytes 2359328 | tf_op jit(solution)/shard_map/part1_shift3/ppermute | solution.py:352
  281.2 1.8 with_scales.3.refs_0_
  283.0 9.0 %collective-permute-done.3.refs_1_.rest_5_ = bf16[4,2,576,256]{3,2,1,0:T(8,128)(2,1)} collective-permute-done((bf16[4,2,576,256]{3,2,1,0:T(8,128)(2,1)}, bf16[4,2,576,256]{3,2,1,0:T(8,128)(2,1)}, u32[]{:S(2)}, u32[]{:S(2)}) %collective-permute-start.3) | collective-permute-done | bytes 2359328 | tf_op jit(solution)/shard_map/part1_shift1/ppermute | solution.py:352
  292.0 2.2 collective-permute-start.4
  294.2 7.5 %collective-permute-done.6.refs_1_ = bf16[880,256]{1,0:T(8,128)(2,1)S(1)} collective-permute-done((bf16[880,256]{1,0:T(8,128)(2,1)}, bf16[880,256]{1,0:T(8,128)(2,1)S(1)}, u32[]{:S(2)}, u32[]{:S(2)}) %collective-permute-start.6) | collective-permute-done | bytes 450592 | tf_op jit(solution)/shard_map/part2_shift2/ppermute | solution.py:352
  301.7 0.8 copy-done.14
  302.5 3.0 collective-permute-start.11
  305.5 14.1 %collective-permute-done.9.refs_1_ = bf16[880,256]{1,0:T(8,128)(2,1)S(1)} collective-permute-done((bf16[880,256]{1,0:T(8,128)(2,1)}, bf16[880,256]{1,0:T(8,128)(2,1)S(1)}, u32[]{:S(2)}, u32[]{:S(2)}) %collective-permute-start.9) | collective-permute-done | bytes 450592 | tf_op jit(solution)/shard_map/part2_shift3/ppermute | solution.py:352
  320.3 10.0 %collective-permute-done.4.refs_1_ = bf16[880,256]{1,0:T(8,128)(2,1)S(1)} collective-permute-done((bf16[880,256]{1,0:T(8,128)(2,1)}, bf16[880,256]{1,0:T(8,128)(2,1)S(1)}, u32[]{:S(2)}, u32[]{:S(2)}) %collective-permute-start.4) | collective-permute-done | bytes 450592 | tf_op jit(solution)/shard_map/part2_shift1/ppermute | solution.py:352
  331.1 2.1 collective-permute-start.10
  333.8 0.8 slice.44
  334.6 1.8 slice.43
  336.4 0.8 slice.45
  337.2 16.0 %correlate.6 = (bf16[2,512,1024]{2,1,0:T(8,128)(2,1)}, f32[2,512,1024]{2,1,0:T(8,128)}) custom-call(s32[3]{0:T(128)} %pad_add_fusion.place_ref, bf16[4,2,144,256]{3,2,1,0:T(8,128)(2,1)} %bitcast.53, bf16[4,2,144,256]{3,2,1,0:T(8,128)(2,1)} %collective-permute-done.2.refs_3_.rest_1_, bf16[4,2,144,256]{3,2,1,0:T(8,128)(2,1)} %copy-done.1, ...), custom_call_target="tpu_custom_call" | custom-call | flops 1024 | bytes 1024 | tf_op jit(solution)/shard_map/correlate/pallas_call | solution.py:289
  354.4 0.9 collective-permute-start.17
  357.7 0.9 collective-permute-start.15
  360.6 3.1 broadcast_divide_fusion
  363.8 16.1 %correlate.5 = (bf16[2,512,1024]{2,1,0:T(8,128)(2,1)}, f32[2,512,1024]{2,1,0:T(8,128)}) custom-call(s32[3]{0:T(128)} %pad_add_fusion.place_ref, bf16[4,2,144,256]{3,2,1,0:T(8,128)(2,1)} %bitcast.54, bf16[4,2,144,256]{3,2,1,0:T(8,128)(2,1)} %collective-permute-done.2.refs_3_.rest_1_, bf16[4,2,144,256]{3,2,1,0:T(8,128)(2,1)} %copy-done.1, ...), custom_call_target="tpu_custom_call" | custom-call | flops 1024 | bytes 1024 | tf_op jit(solution)/shard_map/correlate/pallas_call | solution.py:289
  379.9 1.3 copy-done.11
  381.3 5.3 %equalize.4.rest_0_ = f32[4,2,512,1024]{3,2,1,0:T(8,128)} custom-call(f32[1,512]{1,0:T(1,128)} %bitcast.93, f32[1,1024]{1,0:T(1,128)} %bitcast.80, f32[2,512,1024]{2,1,0:T(8,128)} %get-tuple-element.68.mine_ref, bf16[2,512,1024]{2,1,0:T(8,128)(2,1)} %copy-done.11, bf16[2,512,1024]{2,1,0:T(8,128)(2,1)} %get-tuple-element.64.refs_0_.rest_0_), custom_call_target="tpu_custom_call" | custom-call | flops 1024 | bytes 1024 | tf_op jit(solution)/shard_map/equalize/pallas_call | solution.py:337
  386.5 10.0 %collective-permute-done.15.refs_3_.rest_11_.refs_1_ = bf16[1,2,432,256]{3,2,1,0:T(8,128)(2,1)S(1)} collective-permute-done((bf16[1,2,432,256]{3,2,1,0:T(8,128)(2,1)}, bf16[1,2,432,256]{3,2,1,0:T(8,128)(2,1)S(1)}, u32[]{:S(2)}, u32[]{:S(2)}) %collective-permute-start.15) | collective-permute-done | bytes 442400 | tf_op jit(solution)/shard_map/part4_shift3/ppermute | solution.py:352
  398.1 0.8 collective-permute-start.16
  398.9 1.4 collective-permute-start.20
  400.3 16.1 %correlate.7 = (bf16[2,512,1024]{2,1,0:T(8,128)(2,1)}, f32[2,512,1024]{2,1,0:T(8,128)}) custom-call(s32[3]{0:T(128)} %pad_add_fusion.place_ref, bf16[4,2,144,256]{3,2,1,0:T(8,128)(2,1)} %bitcast.55, bf16[4,2,144,256]{3,2,1,0:T(8,128)(2,1)} %collective-permute-done.2.refs_3_.rest_1_, bf16[4,2,144,256]{3,2,1,0:T(8,128)(2,1)} %copy-done.1, ...), custom_call_target="tpu_custom_call" | custom-call | flops 1024 | bytes 1024 | tf_op jit(solution)/shard_map/correlate/pallas_call | solution.py:289
  416.4 1.4 copy-done.10
  417.8 5.4 %equalize.5.rest_8_.rest_6_.rest_0_ = f32[4,2,512,1024]{3,2,1,0:T(8,128)} custom-call(f32[1,512]{1,0:T(1,128)} %bitcast.92, f32[1,1024]{1,0:T(1,128)} %bitcast.81, f32[2,512,1024]{2,1,0:T(8,128)} %get-tuple-element.63.mine_ref, bf16[2,512,1024]{2,1,0:T(8,128)(2,1)} %copy-done.10, ...), custom_call_target="tpu_custom_call", output_to_operand_aliasing={{}: (4, {})} | custom-call | flops 1024 | bytes 1024 | tf_op jit(solution)/shard_map/equalize/pallas_call | solution.py:337
  423.9 12.8 %correlate.8 = (f32[2,512,1024]{2,1,0:T(8,128)}, f32[2,512,1024]{2,1,0:T(8,128)}) custom-call(s32[3]{0:T(128)} %pad_add_fusion.place_ref, bf16[4,2,144,256]{3,2,1,0:T(8,128)(2,1)} %bitcast.56, bf16[4,2,144,256]{3,2,1,0:T(8,128)(2,1)} %collective-permute-done.2.refs_3_.rest_1_, bf16[4,2,144,256]{3,2,1,0:T(8,128)(2,1)} %copy-done.1, ...), custom_call_target="tpu_custom_call" | custom-call | flops 1024 | bytes 1024 | tf_op jit(solution)/shard_map/correlate/pallas_call | solution.py:289
  436.7 1.5 collective-permute-done.20.rest_5_
  439.2 11.6 %correlate.9 = (bf16[2,512,1024]{2,1,0:T(8,128)(2,1)}, f32[2,512,1024]{2,1,0:T(8,128)}) custom-call(s32[3]{0:T(128)} %pad_add_fusion.place_ref, f32[2,512,1024]{2,1,0:T(8,128)} %get-tuple-element.72.rest_0_, f32[2,512,1024]{2,1,0:T(8,128)} %get-tuple-element.73.rest_1_, bf16[1,2,432,256]{3,2,1,0:T(8,128)(2,1)} %bitcast.77, ...), custom_call_target="tpu_custom_call" | custom-call | flops 1024 | bytes 1024 | tf_op jit(solution)/shard_map/correlate/pallas_call | solution.py:289
  451.5 5.3 %equalize.6.rest_0_ = f32[4,2,512,1024]{3,2,1,0:T(8,128)} custom-call(f32[1,512]{1,0:T(1,128)} %bitcast.91, f32[1,1024]{1,0:T(1,128)} %bitcast.82, f32[2,512,1024]{2,1,0:T(8,128)} %get-tuple-element.80.mine_ref, bf16[2,512,1024]{2,1,0:T(8,128)(2,1)} %collective-permute-done.22.theirs_ref, ...), custom_call_target="tpu_custom_call", output_to_operand_aliasing={{}: (4, {})} | custom-call | flops 1024 | bytes 1024 | tf_op jit(solution)/shard_map/equalize/pallas_call | solution.py:337
  456.8 5.3 %equalize.7 = f32[4,2,512,1024]{3,2,1,0:T(8,128)} custom-call(f32[1,512]{1,0:T(1,128)} %bitcast.94, f32[1,1024]{1,0:T(1,128)} %bitcast.83, f32[2,512,1024]{2,1,0:T(8,128)} %get-tuple-element.78.mine_ref, bf16[2,512,1024]{2,1,0:T(8,128)(2,1)} %collective-permute-done.21.theirs_ref, f32[4,2,512,1024]{3,2,1,0:T(8,128)} %equalize.6.rest_0_), custom_call_target="tpu_custom_call", output_to_operand_aliasing={{}: (4, {})} | custom-call | flops 1024 | bytes 1024 | tf_op jit(solution)/shard_map/equalize/pallas_call | solution.py:337
  (106 shorter events, 14.8 us)
Async XLA Ops:
  15.5 45.6 %collective-permute-start = (bf16[2,1584,256]{2,1,0:T(8,128)(2,1)}, bf16[2,1584,256]{2,1,0:T(8,128)(2,1)}, u32[]{:S(2)}, u32[]{:S(2)}) collective-permute-start(bf16[2,1584,256]{2,1,0:T(8,128)(2,1)} %get-tuple-element.45), channel_id=1, source_target_pairs={{0,1},{2,3},{4,5},{6,7},{8,9},{10,11},{12,13},{14,15},{16,17},{18,... | collective-permute-start | bytes 4866056 | tf_op jit(solution)/shard_map/halo/ppermute | solution.py:357
  16.8 73.9 %collective-permute-start.1 = (bf16[4,2,144,256]{3,2,1,0:T(8,128)(2,1)}, bf16[4,2,144,256]{3,2,1,0:T(8,128)(2,1)S(1)}, u32[]{:S(2)}, u32[]{:S(2)}) collective-permute-start(bf16[4,2,144,256]{3,2,1,0:T(8,128)(2,1)} %bitcast.102), channel_id=1, source_target_pairs={{0,16},{8,24},{16,0},{24,8},{1,17},{9,25},{17,1},{25,9},{2,18},{10... | collective-permute-start | bytes 1769480 | tf_op jit(solution)/shard_map/part0_shift2/ppermute | solution.py:352
  19.2 100.5 %collective-permute-start.7 = (bf16[4,2,144,256]{3,2,1,0:T(8,128)(2,1)}, bf16[4,2,144,256]{3,2,1,0:T(8,128)(2,1)S(1)}, u32[]{:S(2)}, u32[]{:S(2)}) collective-permute-start(bf16[4,2,144,256]{3,2,1,0:T(8,128)(2,1)} %bitcast.101), channel_id=1, source_target_pairs={{0,24},{8,0},{16,8},{24,16},{1,25},{9,1},{17,9},{25,17},{2,26},{10... | collective-permute-start | bytes 1769480 | tf_op jit(solution)/shard_map/part0_shift3/ppermute | solution.py:352
  19.4 152.2 %collective-permute-start.2 = (bf16[4,2,144,256]{3,2,1,0:T(8,128)(2,1)}, bf16[4,2,144,256]{3,2,1,0:T(8,128)(2,1)}, u32[]{:S(2)}, u32[]{:S(2)}) collective-permute-start(bf16[4,2,144,256]{3,2,1,0:T(8,128)(2,1)} %bitcast.100), channel_id=1, source_target_pairs={{0,8},{8,16},{16,24},{24,0},{1,9},{9,17},{17,25},{25,1},{2,10},{10... | collective-permute-start | bytes 1769480 | tf_op jit(solution)/shard_map/part0_shift1/ppermute | solution.py:352
  59.2 162.9 %collective-permute-start.5 = (bf16[4,2,576,256]{3,2,1,0:T(8,128)(2,1)}, bf16[4,2,576,256]{3,2,1,0:T(8,128)(2,1)S(1)}, u32[]{:S(2)}, u32[]{:S(2)}) collective-permute-start(bf16[4,2,576,256]{3,2,1,0:T(8,128)(2,1)} %bitcast.99), channel_id=1, source_target_pairs={{0,16},{8,24},{16,0},{24,8},{1,17},{9,25},{17,1},{25,9},{2,18},{10... | collective-permute-start | bytes 7077896 | tf_op jit(solution)/shard_map/part1_shift2/ppermute | solution.py:352
  90.7 29.0 %copy-start.1 = (bf16[4,2,144,256]{3,2,1,0:T(8,128)(2,1)}, bf16[4,2,144,256]{3,2,1,0:T(8,128)(2,1)S(1)}, u32[]{:S(2)}) copy-start(bf16[4,2,144,256]{3,2,1,0:T(8,128)(2,1)S(1)} %collective-permute-done.1.refs_2_.rest_2_) | copy-start | bytes 1769476
  119.7 0.8 copy-start.2
  120.5 160.7 %collective-permute-start.8 = (bf16[4,2,576,256]{3,2,1,0:T(8,128)(2,1)}, bf16[4,2,576,256]{3,2,1,0:T(8,128)(2,1)}, u32[]{:S(2)}, u32[]{:S(2)}) collective-permute-start(bf16[4,2,576,256]{3,2,1,0:T(8,128)(2,1)} %after.19), channel_id=1, source_target_pairs={{0,24},{8,0},{16,8},{24,16},{1,25},{9,1},{17,9},{25,17},{2,26},{10... | collective-permute-start | bytes 7077896 | tf_op jit(solution)/shard_map/part1_shift3/ppermute | solution.py:352
  171.5 3.6 copy-start.21
  171.5 3.6 copy-start.22
  171.5 3.7 copy-start.23
  171.5 120.5 %collective-permute-start.3 = (bf16[4,2,576,256]{3,2,1,0:T(8,128)(2,1)}, bf16[4,2,576,256]{3,2,1,0:T(8,128)(2,1)}, u32[]{:S(2)}, u32[]{:S(2)}) collective-permute-start(bf16[4,2,576,256]{3,2,1,0:T(8,128)(2,1)} %after.16), channel_id=1, source_target_pairs={{0,8},{8,16},{16,24},{24,0},{1,9},{9,17},{17,25},{25,1},{2,10},{10... | collective-permute-start | bytes 7077896 | tf_op jit(solution)/shard_map/part1_shift1/ppermute | solution.py:352
  222.1 1.5 copy-start
  223.6 78.1 %collective-permute-start.6 = (bf16[880,256]{1,0:T(8,128)(2,1)}, bf16[880,256]{1,0:T(8,128)(2,1)S(1)}, u32[]{:S(2)}, u32[]{:S(2)}) collective-permute-start(bf16[880,256]{1,0:T(8,128)(2,1)} %after.18), channel_id=1, source_target_pairs={{0,16},{8,24},{16,0},{24,8},{1,17},{9,25},{17,1},{25,9},{2,18},{10... | collective-permute-start | bytes 1351688 | tf_op jit(solution)/shard_map/part2_shift2/ppermute | solution.py:352
  281.2 38.4 %collective-permute-start.9 = (bf16[880,256]{1,0:T(8,128)(2,1)}, bf16[880,256]{1,0:T(8,128)(2,1)S(1)}, u32[]{:S(2)}, u32[]{:S(2)}) collective-permute-start(bf16[880,256]{1,0:T(8,128)(2,1)} %after.20), channel_id=1, source_target_pairs={{0,24},{8,0},{16,8},{24,16},{1,25},{9,1},{17,9},{25,17},{2,26},{10... | collective-permute-start | bytes 1351688 | tf_op jit(solution)/shard_map/part2_shift3/ppermute | solution.py:352
  292.0 38.3 %collective-permute-start.4 = (bf16[880,256]{1,0:T(8,128)(2,1)}, bf16[880,256]{1,0:T(8,128)(2,1)S(1)}, u32[]{:S(2)}, u32[]{:S(2)}) collective-permute-start(bf16[880,256]{1,0:T(8,128)(2,1)} %after.17), channel_id=1, source_target_pairs={{0,8},{8,16},{16,24},{24,0},{1,9},{9,17},{17,25},{25,1},{2,10},{10... | collective-permute-start | bytes 1351688 | tf_op jit(solution)/shard_map/part2_shift1/ppermute | solution.py:352
  301.7 0.8 copy-start.14
  302.5 31.3 %copy-start.15 = (bf16[880,256]{1,0:T(8,128)(2,1)S(1)}, bf16[880,256]{1,0:T(8,128)(2,1)}, u32[]{:S(2)}) copy-start(bf16[880,256]{1,0:T(8,128)(2,1)} %copy-done.14) | copy-start | bytes 1351684
  302.5 50.8 %collective-permute-start.11 = (bf16[1,2,432,256]{3,2,1,0:T(8,128)(2,1)}, bf16[1,2,432,256]{3,2,1,0:T(8,128)(2,1)S(1)}, u32[]{:S(2)}, u32[]{:S(2)}) collective-permute-start(bf16[1,2,432,256]{3,2,1,0:T(8,128)(2,1)} %after.22), channel_id=1, source_target_pairs={{0,16},{8,24},{16,0},{24,8},{1,17},{9,25},{17,1},{25,9},{2,18},{10... | collective-permute-start | bytes 1327112 | tf_op jit(solution)/shard_map/part3_shift2/ppermute | solution.py:352
  319.6 0.8 copy-start.12
  320.3 16.1 %copy-start.13 = (bf16[880,256]{1,0:T(8,128)(2,1)S(1)}, bf16[880,256]{1,0:T(8,128)(2,1)}, u32[]{:S(2)}) copy-start(bf16[880,256]{1,0:T(8,128)(2,1)} %copy-done.12) | copy-start | bytes 1351684
  320.3 32.9 %collective-permute-start.12 = (bf16[1,2,432,256]{3,2,1,0:T(8,128)(2,1)}, bf16[1,2,432,256]{3,2,1,0:T(8,128)(2,1)S(1)}, u32[]{:S(2)}, u32[]{:S(2)}) collective-permute-start(bf16[1,2,432,256]{3,2,1,0:T(8,128)(2,1)} %after.23), channel_id=1, source_target_pairs={{0,24},{8,0},{16,8},{24,16},{1,25},{9,1},{17,9},{25,17},{2,26},{10... | collective-permute-start | bytes 1327112 | tf_op jit(solution)/shard_map/part3_shift3/ppermute | solution.py:352
  330.3 0.8 copy-start.16
  331.1 22.2 %collective-permute-start.10 = (bf16[1,2,432,256]{3,2,1,0:T(8,128)(2,1)}, bf16[1,2,432,256]{3,2,1,0:T(8,128)(2,1)S(1)}, u32[]{:S(2)}, u32[]{:S(2)}) collective-permute-start(bf16[1,2,432,256]{3,2,1,0:T(8,128)(2,1)} %after.21), channel_id=1, source_target_pairs={{0,8},{8,16},{16,24},{24,0},{1,9},{9,17},{17,25},{25,1},{2,10},{10... | collective-permute-start | bytes 1327112 | tf_op jit(solution)/shard_map/part3_shift1/ppermute | solution.py:352
  353.3 0.8 copy-start.3
  353.3 0.9 copy-start.4
  353.3 1.1 copy-start.5
  354.3 5.6 %copy-start.20 = (f32[256]{0:T(256)S(1)}, f32[256]{0:T(256)}, u32[]{:S(2)}) copy-start(f32[256]{0:T(256)} %add_rsqrt_fusion) | copy-start | bytes 3076
  354.4 25.6 %collective-permute-start.17 = (bf16[2,512,1024]{2,1,0:T(8,128)(2,1)}, bf16[2,512,1024]{2,1,0:T(8,128)(2,1)S(1)}, u32[]{:S(2)}, u32[]{:S(2)}) collective-permute-start(bf16[2,512,1024]{2,1,0:T(8,128)(2,1)} %after.28), channel_id=1, source_target_pairs={{0,1},{1,0},{2,3},{3,2},{4,5},{5,4},{6,7},{7,6},{8,9},{9,8},{10,11... | collective-permute-start | bytes 6291464 | tf_op jit(solution)/shard_map/rows0/ppermute | solution.py:444
  356.9 29.6 %collective-permute-start.14 = (bf16[1,2,432,256]{3,2,1,0:T(8,128)(2,1)}, bf16[1,2,432,256]{3,2,1,0:T(8,128)(2,1)S(1)}, u32[]{:S(2)}, u32[]{:S(2)}) collective-permute-start(bf16[1,2,432,256]{3,2,1,0:T(8,128)(2,1)} %after.25), channel_id=1, source_target_pairs={{0,16},{8,24},{16,0},{24,8},{1,17},{9,25},{17,1},{25,9},{2,18},{10... | collective-permute-start | bytes 1327112 | tf_op jit(solution)/shard_map/part4_shift2/ppermute | solution.py:352
  357.7 38.8 %collective-permute-start.15 = (bf16[1,2,432,256]{3,2,1,0:T(8,128)(2,1)}, bf16[1,2,432,256]{3,2,1,0:T(8,128)(2,1)S(1)}, u32[]{:S(2)}, u32[]{:S(2)}) collective-permute-start(bf16[1,2,432,256]{3,2,1,0:T(8,128)(2,1)} %after.26), channel_id=1, source_target_pairs={{0,24},{8,0},{16,8},{24,16},{1,25},{9,1},{17,9},{25,17},{2,26},{10... | collective-permute-start | bytes 1327112 | tf_op jit(solution)/shard_map/part4_shift3/ppermute | solution.py:352
  358.6 37.9 %collective-permute-start.13 = (bf16[1,2,432,256]{3,2,1,0:T(8,128)(2,1)}, bf16[1,2,432,256]{3,2,1,0:T(8,128)(2,1)S(1)}, u32[]{:S(2)}, u32[]{:S(2)}) collective-permute-start(bf16[1,2,432,256]{3,2,1,0:T(8,128)(2,1)} %after.24), channel_id=1, source_target_pairs={{0,8},{8,16},{16,24},{24,0},{1,9},{9,17},{17,25},{25,1},{2,10},{10... | collective-permute-start | bytes 1327112 | tf_op jit(solution)/shard_map/part4_shift1/ppermute | solution.py:352
  379.9 1.3 copy-start.11
  386.5 10.0 %copy-start.6 = (bf16[1,2,432,256]{3,2,1,0:T(8,128)(2,1)}, bf16[1,2,432,256]{3,2,1,0:T(8,128)(2,1)S(1)}, u32[]{:S(2)}) copy-start(bf16[1,2,432,256]{3,2,1,0:T(8,128)(2,1)S(1)} %collective-permute-done.14.refs_2_.rest_10_.refs_1_) | copy-start | bytes 1327108
  396.5 0.8 copy-start.7
  397.3 0.8 copy-start.8
  398.1 18.3 %collective-permute-start.16 = (bf16[2,512,1024]{2,1,0:T(8,128)(2,1)}, bf16[2,512,1024]{2,1,0:T(8,128)(2,1)S(1)}, u32[]{:S(2)}, u32[]{:S(2)}) collective-permute-start(bf16[2,512,1024]{2,1,0:T(8,128)(2,1)} %after.27), channel_id=1, source_target_pairs={{0,1},{1,0},{2,3},{3,2},{4,5},{5,4},{6,7},{7,6},{8,9},{9,8},{10,11... | collective-permute-start | bytes 6291464 | tf_op jit(solution)/shard_map/rows1/ppermute | solution.py:444
  398.9 37.9 %collective-permute-start.19 = (bf16[1,2,432,256]{3,2,1,0:T(8,128)(2,1)}, bf16[1,2,432,256]{3,2,1,0:T(8,128)(2,1)S(1)}, u32[]{:S(2)}, u32[]{:S(2)}) collective-permute-start(bf16[1,2,432,256]{3,2,1,0:T(8,128)(2,1)} %after.30), channel_id=1, source_target_pairs={{0,16},{8,24},{16,0},{24,8},{1,17},{9,25},{17,1},{25,9},{2,18},{10... | collective-permute-start | bytes 1327112 | tf_op jit(solution)/shard_map/part5_shift2/ppermute | solution.py:352
  398.9 39.4 %collective-permute-start.20 = (bf16[1,2,432,256]{3,2,1,0:T(8,128)(2,1)}, bf16[1,2,432,256]{3,2,1,0:T(8,128)(2,1)S(1)}, u32[]{:S(2)}, u32[]{:S(2)}) collective-permute-start(bf16[1,2,432,256]{3,2,1,0:T(8,128)(2,1)} %after.31), channel_id=1, source_target_pairs={{0,24},{8,0},{16,8},{24,16},{1,25},{9,1},{17,9},{25,17},{2,26},{10... | collective-permute-start | bytes 1327112 | tf_op jit(solution)/shard_map/part5_shift3/ppermute | solution.py:352
  400.2 38.0 %collective-permute-start.18 = (bf16[1,2,432,256]{3,2,1,0:T(8,128)(2,1)}, bf16[1,2,432,256]{3,2,1,0:T(8,128)(2,1)S(1)}, u32[]{:S(2)}, u32[]{:S(2)}) collective-permute-start(bf16[1,2,432,256]{3,2,1,0:T(8,128)(2,1)} %after.29), channel_id=1, source_target_pairs={{0,8},{8,16},{16,24},{24,0},{1,9},{9,17},{17,25},{25,1},{2,10},{10... | collective-permute-start | bytes 1327112 | tf_op jit(solution)/shard_map/part5_shift1/ppermute | solution.py:352
  416.4 1.4 copy-start.10
  417.8 5.4 %copy-start.9 = (bf16[2,512,1024]{2,1,0:T(8,128)(2,1)S(1)}, bf16[2,512,1024]{2,1,0:T(8,128)(2,1)}, u32[]{:S(2)}) copy-start(bf16[2,512,1024]{2,1,0:T(8,128)(2,1)} %get-tuple-element.71.rest_1_) | copy-start | bytes 6291460
  423.2 28.3 %collective-permute-start.22 = (bf16[2,512,1024]{2,1,0:T(8,128)(2,1)S(1)}, bf16[2,512,1024]{2,1,0:T(8,128)(2,1)}, u32[]{:S(2)}, u32[]{:S(2)}) collective-permute-start(bf16[2,512,1024]{2,1,0:T(8,128)(2,1)S(1)} %copy-done.9), channel_id=1, source_target_pairs={{0,1},{1,0},{2,3},{3,2},{4,5},{5,4},{6,7},{7,6},{8,9},{9,8},{10,11... | collective-permute-start | bytes 6291464 | tf_op jit(solution)/shard_map/rows2/ppermute | solution.py:444
  436.7 1.5 copy-start.17
  438.3 0.8 copy-start.18
  438.3 1.0 copy-start.19
  450.9 5.9 %collective-permute-start.21 = (bf16[2,512,1024]{2,1,0:T(8,128)(2,1)}, bf16[2,512,1024]{2,1,0:T(8,128)(2,1)}, u32[]{:S(2)}, u32[]{:S(2)}) collective-permute-start(bf16[2,512,1024]{2,1,0:T(8,128)(2,1)} %get-tuple-element.79.rest_1_), channel_id=1, source_target_pairs={{0,1},{1,0},{2,3},{3,2},{4,5},{5,4},{6,7},{7,6},{8,9},{9,8},{10,11... | collective-permute-start | bytes 6291464 | tf_op jit(solution)/shard_map/rows3/ppermute | solution.py:444

commit v12 on v11

--- a/solution.py
+++ b/solution.py
@@ -13,7 +13,7 @@
 TAPS = 12
 GROUP = 9
 BLOCK = 16
-PARTS = (1, 4)
+PARTS = (1, 3)
 RUNS = (1, 1, 1, 1)
 SPREAD = BLOCK + 1
 VMEM = 60 * 1024 * 1024

time: 464 us -> 463 us (level)
    unnamed x51 -> x47, local copies, waits for them, and re-layouts: 12.3 us -> 11.3 us
  transfers between devices with their start and end apart: 23 -> 23, of which waited for: 10 -> 15; matrix products, arithmetic and copies ran while one was open for 3% -> 3% of each run, Pallas kernels for 35% -> 35%
where the time goes in v12:
time: 463 us; the launch traced here: 462 us
  waiting for transfers between devices  214 us (46%)
  Pallas kernels  182 us (39%)
  starting transfers between devices  29.1 us (6%)
  local copies, waits for them, and re-layouts  17 us (4%)
  blocking collectives  11.4 us (2%)
  other arithmetic  8.02 us (2%)
    ppermute x18, waiting for transfers between devices, shift(): lax.ppermute(value, 'station', [(s, (s + d) % count) for s in range(count)])  214 us
    pallas_call x3, Pallas kernels, front(): pl.pallas_call(functools.partial(front_kernel, runs, owners, turned, tail...  82.2 us
    pallas_call x5, Pallas kernels, correlate(): pl.pallas_call(functools.partial(correlate_kernel, owners, picks, outs, l...  72.6 us
    ppermute x18, starting transfers between devices, shift(): lax.ppermute(value, 'station', [(s, (s + d) % count) for s in range(count)])  25.3 us
    pallas_call x4, Pallas kernels, equalize(): pl.pallas_call(equalize_kernel, grid=(rows // block,), out_shape=jax.Shap...  21.3 us
    psum x1, blocking collectives, pipelined(): total = lax.psum(local, ('band', 'tm'))  11.4 us
    unnamed x47, local copies, waits for them, and re-layouts  11.3 us
  transfers between devices with their start and end apart: 23, of which 15 were waited for; matrix products, arithmetic and copies ran while one was open for 3% of the time, Pallas kernels for 35%

profile of v12, /device:TPU:11, one launch (start us, length us, event | category | flops | bytes accessed | tf_op | source)
XLA Modules:
  0.0 462.3 jit_solution(1682126851943492096)
XLA Ops:
  2.2 14.0 %front.3 = (bf16[4,2,9,16,256]{4,3,2,1,0:T(8,128)(2,1)}, bf16[4,2,9,16,256]{4,3,2,1,0:T(8,128)(2,1)}, bf16[4,2,9,16,256]{4,3,2,1,0:T(8,128)(2,1)}, bf16[4,2,9,16...) custom-call(s32[1]{0:T(128)} %bitcast.me_ref, f32[144]{0:T(256)} %dynamic_slice.14.keep_ref, ...), custom_call_target="tpu_custom_call" | custom-call | flops 1024 | bytes 1024 | tf_op jit(solution)/shard_map/front/pallas_call | solution.py:159
  16.2 1.3 collective-permute-start
  17.5 2.4 collective-permute-start.1
  20.0 1.3 collective-permute-start.2
  21.3 30.1 %front.4 = (bf16[4,2,9,48,256]{4,3,2,1,0:T(8,128)(2,1)}, bf16[4,2,9,48,256]{4,3,2,1,0:T(8,128)(2,1)}, bf16[4,2,9,48,256]{4,3,2,1,0:T(8,128)(2,1)}, bf16[4,2,9,48,256]{4,3,2,1,0:T(8,128)(2,1)}, f32[16,256]{1,0:T(8,128)}) custom-call(s32[1]{0:T(128)} %bitcast.me_ref, f32[144]{0:T(256)} %dynamic_slice.14.keep_ref, bf16[2,1,256,18432]{3,2,1,0:T(8,128)(2,1)} %volts_ref.5, ...), custom_call_target="tpu_custom_call" | custom-call | flops 1024 | bytes 1024 | tf_op jit(solution)/shard_map/front/pallas_call | solution.py:159
  51.4 1.9 collective-permute-start.5
  53.3 38.1 %front.5 = (bf16[1,2,9,64,256]{4,3,2,1,0:T(8,128)(2,1)}, bf16[1,2,9,64,256]{4,3,2,1,0:T(8,128)(2,1)}, bf16[1,2,9,64,256]{4,3,2,1,0:T(8,128)(2,1)}, bf16[1,2,9,64...) custom-call(s32[1]{0:T(128)} %bitcast.me_ref, ...), custom_call_target="tpu_custom_call" | custom-call | flops 1024 | bytes 1024 | tf_op jit(solution)/shard_map/front/pallas_call | solution.py:159
  91.5 16.2 %collective-permute-done.7.refs_3_.rest_3_ = bf16[4,2,144,256]{3,2,1,0:T(8,128)(2,1)S(1)} collective-permute-done((bf16[4,2,144,256]{3,2,1,0:T(8,128)(2,1)}, bf16[4,2,144,256]{3,2,1,0:T(8,128)(2,1)S(1)}, u32[]{:S(2)}, u32[]{:S(2)}) %collective-permute-start.7) | collective-permute-done | bytes 589856 | tf_op jit(solution)/shard_map/part0_shift3/ppermute | solution.py:352
  108.6 38.3 %collective-permute-done.2.refs_3_.rest_1_ = bf16[4,2,144,256]{3,2,1,0:T(8,128)(2,1)} collective-permute-done((bf16[4,2,144,256]{3,2,1,0:T(8,128)(2,1)}, bf16[4,2,144,256]{3,2,1,0:T(8,128)(2,1)}, u32[]{:S(2)}, u32[]{:S(2)}) %collective-permute-start.2) | collective-permute-done | bytes 589856 | tf_op jit(solution)/shard_map/part0_shift1/ppermute | solution.py:352
  146.9 2.2 collective-permute-start.3
  149.1 1.3 convert_reduce_fusion.3
  151.0 1.3 add_reduce_fusion
  152.3 11.4 %psum.7 = f32[256]{0:T(256)S(1)} all-reduce(f32[256]{0:T(256)} %add_reduce_fusion), channel_id=1, replica_groups=mesh['station'=4,'band'=4,'tm'=2] {'band','tm'}, use_global_device_ids=true, to_apply=%region_2.3 | all-reduce | flops 256 | bytes 2048 | tf_op jit(solution)/shard_map/psum | solution.py:435
  164.2 1.9 with_scales.4.refs_0_
  166.1 18.7 %collective-permute-done.5.refs_1_.rest_6_ = bf16[4,2,432,256]{3,2,1,0:T(8,128)(2,1)S(1)} collective-permute-done((bf16[4,2,432,256]{3,2,1,0:T(8,128)(2,1)}, bf16[4,2,432,256]{3,2,1,0:T(8,128)(2,1)S(1)}, u32[]{:S(2)}, u32[]{:S(2)}) %collective-permute-start.5) | collective-permute-done | bytes 1769504 | tf_op jit(solution)/shard_map/part1_shift2/ppermute | solution.py:352
  184.9 1.2 copy-done
  186.1 3.0 collective-permute-start.6
  189.0 1.9 with_scales.5.refs_0_
  191.0 43.3 %collective-permute-done.8.refs_1_.rest_7_ = bf16[4,2,432,256]{3,2,1,0:T(8,128)(2,1)S(1)} collective-permute-done((bf16[4,2,432,256]{3,2,1,0:T(8,128)(2,1)}, bf16[4,2,432,256]{3,2,1,0:T(8,128)(2,1)S(1)}, u32[]{:S(2)}, u32[]{:S(2)}) %collective-permute-start.8) | collective-permute-done | bytes 1769504 | tf_op jit(solution)/shard_map/part1_shift3/ppermute | solution.py:352
  234.3 1.3 copy-done.1
  235.6 1.9 with_scales.3.refs_0_
  237.5 10.9 %collective-permute-done.3.refs_1_.rest_5_ = bf16[4,2,432,256]{3,2,1,0:T(8,128)(2,1)} collective-permute-done((bf16[4,2,432,256]{3,2,1,0:T(8,128)(2,1)}, bf16[4,2,432,256]{3,2,1,0:T(8,128)(2,1)}, u32[]{:S(2)}, u32[]{:S(2)}) %collective-permute-start.3) | collective-permute-done | bytes 1769504 | tf_op jit(solution)/shard_map/part1_shift1/ppermute | solution.py:352
  248.4 2.2 collective-permute-start.4
  250.6 10.7 %collective-permute-done.6.refs_1_ = bf16[1168,256]{1,0:T(8,128)(2,1)S(1)} collective-permute-done((bf16[1168,256]{1,0:T(8,128)(2,1)}, bf16[1168,256]{1,0:T(8,128)(2,1)S(1)}, u32[]{:S(2)}, u32[]{:S(2)}) %collective-permute-start.6) | collective-permute-done | bytes 598048 | tf_op jit(solution)/shard_map/part2_shift2/ppermute | solution.py:352
  262.1 3.0 collective-permute-start.11
  265.1 20.3 %collective-permute-done.9.refs_1_ = bf16[1168,256]{1,0:T(8,128)(2,1)S(1)} collective-permute-done((bf16[1168,256]{1,0:T(8,128)(2,1)}, bf16[1168,256]{1,0:T(8,128)(2,1)S(1)}, u32[]{:S(2)}, u32[]{:S(2)}) %collective-permute-start.9) | collective-permute-done | bytes 598048 | tf_op jit(solution)/shard_map/part2_shift3/ppermute | solution.py:352
  286.2 13.1 %collective-permute-done.4.refs_1_ = bf16[1168,256]{1,0:T(8,128)(2,1)} collective-permute-done((bf16[1168,256]{1,0:T(8,128)(2,1)}, bf16[1168,256]{1,0:T(8,128)(2,1)}, u32[]{:S(2)}, u32[]{:S(2)}) %collective-permute-start.4) | collective-permute-done | bytes 598048 | tf_op jit(solution)/shard_map/part2_shift1/ppermute | solution.py:352
  299.4 2.2 collective-permute-start.10
  303.1 1.9 slice.43
  305.9 16.0 %correlate.6 = (bf16[2,512,1024]{2,1,0:T(8,128)(2,1)}, f32[2,512,1024]{2,1,0:T(8,128)}) custom-call(s32[3]{0:T(128)} %pad_add_fusion.place_ref, bf16[4,2,144,256]{3,2,1,0:T(8,128)(2,1)} %bitcast.53, bf16[4,2,144,256]{3,2,1,0:T(8,128)(2,1)} %collective-permute-done.2.refs_3_.rest_1_, bf16[4,2,144,256]{3,2,1,0:T(8,128)(2,1)} %copy-done.2, ...), custom_call_target="tpu_custom_call" | custom-call | flops 1024 | bytes 1024 | tf_op jit(solution)/shard_map/correlate/pallas_call | solution.py:289
  321.9 1.6 collective-permute-done.12.rest_11_.refs_1_.refs_3_
  323.5 1.2 collective-permute-done.10.rest_9_.refs_1_
  327.6 3.0 collective-permute-start.14
  333.6 3.1 broadcast_divide_fusion
  336.7 16.1 %correlate.5 = (bf16[2,512,1024]{2,1,0:T(8,128)(2,1)}, f32[2,512,1024]{2,1,0:T(8,128)}) custom-call(s32[3]{0:T(128)} %pad_add_fusion.place_ref, bf16[4,2,144,256]{3,2,1,0:T(8,128)(2,1)} %bitcast.54, bf16[4,2,144,256]{3,2,1,0:T(8,128)(2,1)} %collective-permute-done.2.refs_3_.rest_1_, bf16[4,2,144,256]{3,2,1,0:T(8,128)(2,1)} %copy-done.2, ...), custom_call_target="tpu_custom_call" | custom-call | flops 1024 | bytes 1024 | tf_op jit(solution)/shard_map/correlate/pallas_call | solution.py:289
  352.8 5.3 %equalize.4.rest_0_ = f32[4,2,512,1024]{3,2,1,0:T(8,128)} custom-call(f32[1,512]{1,0:T(1,128)} %bitcast.93, f32[1,1024]{1,0:T(1,128)} %bitcast.80, f32[2,512,1024]{2,1,0:T(8,128)} %get-tuple-element.68.mine_ref, bf16[2,512,1024]{2,1,0:T(8,128)(2,1)} %collective-permute-done.17.theirs_ref, bf16[2,512,1024]{2,1,0:T(8,128)(2,1)} %get-tuple-element.64.refs_0_.rest_0_), custom_call_target="tpu_custom_call" | custom-call | flops 1024 | bytes 1024 | tf_op jit(solution)/shard_map/equalize/pallas_call | solution.py:337
  358.1 11.2 %collective-permute-done.14.refs_2_.rest_10_.refs_1_ = bf16[1,2,576,256]{3,2,1,0:T(8,128)(2,1)S(1)} collective-permute-done((bf16[1,2,576,256]{3,2,1,0:T(8,128)(2,1)}, bf16[1,2,576,256]{3,2,1,0:T(8,128)(2,1)S(1)}, u32[]{:S(2)}, u32[]{:S(2)}) %collective-permute-start.14) | collective-permute-done | bytes 589856 | tf_op jit(solution)/shard_map/part4_shift2/ppermute | solution.py:352
  369.3 12.4 %collective-permute-done.15.refs_3_.rest_11_.refs_1_ = bf16[1,2,576,256]{3,2,1,0:T(8,128)(2,1)S(1)} collective-permute-done((bf16[1,2,576,256]{3,2,1,0:T(8,128)(2,1)}, bf16[1,2,576,256]{3,2,1,0:T(8,128)(2,1)S(1)}, u32[]{:S(2)}, u32[]{:S(2)}) %collective-permute-start.15) | collective-permute-done | bytes 589856 | tf_op jit(solution)/shard_map/part4_shift3/ppermute | solution.py:352
  384.1 2.5 collective-permute-start.20
  386.6 16.1 %correlate.7 = (bf16[2,512,1024]{2,1,0:T(8,128)(2,1)}, f32[2,512,1024]{2,1,0:T(8,128)}) custom-call(s32[3]{0:T(128)} %pad_add_fusion.place_ref, bf16[4,2,144,256]{3,2,1,0:T(8,128)(2,1)} %bitcast.55, bf16[4,2,144,256]{3,2,1,0:T(8,128)(2,1)} %collective-permute-done.2.refs_3_.rest_1_, bf16[4,2,144,256]{3,2,1,0:T(8,128)(2,1)} %copy-done.2, ...), custom_call_target="tpu_custom_call" | custom-call | flops 1024 | bytes 1024 | tf_op jit(solution)/shard_map/correlate/pallas_call | solution.py:289
  402.7 1.3 copy-done.15
  404.0 5.4 %equalize.5.rest_8_.rest_6_.rest_0_ = f32[4,2,512,1024]{3,2,1,0:T(8,128)} custom-call(f32[1,512]{1,0:T(1,128)} %bitcast.92, f32[1,1024]{1,0:T(1,128)} %bitcast.81, f32[2,512,1024]{2,1,0:T(8,128)} %get-tuple-element.63.mine_ref, bf16[2,512,1024]{2,1,0:T(8,128)(2,1)} %copy-done.15, ...), custom_call_target="tpu_custom_call", output_to_operand_aliasing={{}: (4, {})} | custom-call | flops 1024 | bytes 1024 | tf_op jit(solution)/shard_map/equalize/pallas_call | solution.py:337
  410.0 11.4 %correlate.8 = (f32[2,512,1024]{2,1,0:T(8,128)}, f32[2,512,1024]{2,1,0:T(8,128)}) custom-call(s32[3]{0:T(128)} %pad_add_fusion.place_ref, bf16[4,2,144,256]{3,2,1,0:T(8,128)(2,1)} %bitcast.56, bf16[4,2,144,256]{3,2,1,0:T(8,128)(2,1)} %collective-permute-done.2.refs_3_.rest_1_, bf16[4,2,144,256]{3,2,1,0:T(8,128)(2,1)} %copy-done.2, ...), custom_call_target="tpu_custom_call" | custom-call | flops 1024 | bytes 1024 | tf_op jit(solution)/shard_map/correlate/pallas_call | solution.py:289
  421.5 1.2 collective-permute-done.19.rest_4_
  422.7 14.6 %collective-permute-done.20.rest_5_ = bf16[1,2,576,256]{3,2,1,0:T(8,128)(2,1)S(1)} collective-permute-done((bf16[1,2,576,256]{3,2,1,0:T(8,128)(2,1)}, bf16[1,2,576,256]{3,2,1,0:T(8,128)(2,1)S(1)}, u32[]{:S(2)}, u32[]{:S(2)}) %collective-permute-start.20) | collective-permute-done | bytes 589856 | tf_op jit(solution)/shard_map/part5_shift3/ppermute | solution.py:352
  438.1 13.0 %correlate.9 = (bf16[2,512,1024]{2,1,0:T(8,128)(2,1)}, f32[2,512,1024]{2,1,0:T(8,128)}) custom-call(s32[3]{0:T(128)} %pad_add_fusion.place_ref, f32[2,512,1024]{2,1,0:T(8,128)} %get-tuple-element.72.rest_0_, f32[2,512,1024]{2,1,0:T(8,128)} %get-tuple-element.73.rest_1_, bf16[1,2,576,256]{3,2,1,0:T(8,128)(2,1)} %bitcast.65, ...), custom_call_target="tpu_custom_call" | custom-call | flops 1024 | bytes 1024 | tf_op jit(solution)/shard_map/correlate/pallas_call | solution.py:289
  451.8 5.3 %equalize.6.rest_0_ = f32[4,2,512,1024]{3,2,1,0:T(8,128)} custom-call(f32[1,512]{1,0:T(1,128)} %bitcast.91, f32[1,1024]{1,0:T(1,128)} %bitcast.82, f32[2,512,1024]{2,1,0:T(8,128)} %get-tuple-element.80.mine_ref, bf16[2,512,1024]{2,1,0:T(8,128)(2,1)} %collective-permute-done.22.theirs_ref, ...), custom_call_target="tpu_custom_call", output_to_operand_aliasing={{}: (4, {})} | custom-call | flops 1024 | bytes 1024 | tf_op jit(solution)/shard_map/equalize/pallas_call | solution.py:337
  457.0 5.3 %equalize.7 = f32[4,2,512,1024]{3,2,1,0:T(8,128)} custom-call(f32[1,512]{1,0:T(1,128)} %bitcast.94, f32[1,1024]{1,0:T(1,128)} %bitcast.83, f32[2,512,1024]{2,1,0:T(8,128)} %get-tuple-element.78.mine_ref, bf16[2,512,1024]{2,1,0:T(8,128)(2,1)} %collective-permute-done.21.theirs_ref, f32[4,2,512,1024]{3,2,1,0:T(8,128)} %equalize.6.rest_0_), custom_call_target="tpu_custom_call", output_to_operand_aliasing={{}: (4, {})} | custom-call | flops 1024 | bytes 1024 | tf_op jit(solution)/shard_map/equalize/pallas_call | solution.py:337
  (102 shorter events, 18.2 us)
Async XLA Ops:
  0.9 0.5 copy-start.21
  1.4 14.7 %copy-start.20 = (f32[4,144]{1,0:T(4,128)}, f32[4,144]{1,0:T(4,128)S(1)}, u32[]{:S(2)}) copy-start(f32[4,144]{1,0:T(4,128)S(1)} %convert_element_type.20) | copy-start | bytes 6916
  16.2 37.1 %collective-permute-start = (bf16[2,1584,256]{2,1,0:T(8,128)(2,1)}, bf16[2,1584,256]{2,1,0:T(8,128)(2,1)}, u32[]{:S(2)}, u32[]{:S(2)}) collective-permute-start(bf16[2,1584,256]{2,1,0:T(8,128)(2,1)} %get-tuple-element.45), channel_id=1, source_target_pairs={{0,1},{2,3},{4,5},{6,7},{8,9},{10,11},{12,13},{14,15},{16,17},{18,... | collective-permute-start | bytes 4866056 | tf_op jit(solution)/shard_map/halo/ppermute | solution.py:357
  17.5 74.0 %collective-permute-start.1 = (bf16[4,2,144,256]{3,2,1,0:T(8,128)(2,1)}, bf16[4,2,144,256]{3,2,1,0:T(8,128)(2,1)S(1)}, u32[]{:S(2)}, u32[]{:S(2)}) collective-permute-start(bf16[4,2,144,256]{3,2,1,0:T(8,128)(2,1)} %bitcast.102), channel_id=1, source_target_pairs={{0,16},{8,24},{16,0},{24,8},{1,17},{9,25},{17,1},{25,9},{2,18},{10... | collective-permute-start | bytes 1769480 | tf_op jit(solution)/shard_map/part0_shift2/ppermute | solution.py:352
  19.8 87.9 %collective-permute-start.7 = (bf16[4,2,144,256]{3,2,1,0:T(8,128)(2,1)}, bf16[4,2,144,256]{3,2,1,0:T(8,128)(2,1)S(1)}, u32[]{:S(2)}, u32[]{:S(2)}) collective-permute-start(bf16[4,2,144,256]{3,2,1,0:T(8,128)(2,1)} %bitcast.101), channel_id=1, source_target_pairs={{0,24},{8,0},{16,8},{24,16},{1,25},{9,1},{17,9},{25,17},{2,26},{10... | collective-permute-start | bytes 1769480 | tf_op jit(solution)/shard_map/part0_shift3/ppermute | solution.py:352
  20.0 126.9 %collective-permute-start.2 = (bf16[4,2,144,256]{3,2,1,0:T(8,128)(2,1)}, bf16[4,2,144,256]{3,2,1,0:T(8,128)(2,1)}, u32[]{:S(2)}, u32[]{:S(2)}) collective-permute-start(bf16[4,2,144,256]{3,2,1,0:T(8,128)(2,1)} %bitcast.100), channel_id=1, source_target_pairs={{0,8},{8,16},{16,24},{24,0},{1,9},{9,17},{17,25},{25,1},{2,10},{10... | collective-permute-start | bytes 1769480 | tf_op jit(solution)/shard_map/part0_shift1/ppermute | solution.py:352
  51.4 133.4 %collective-permute-start.5 = (bf16[4,2,432,256]{3,2,1,0:T(8,128)(2,1)}, bf16[4,2,432,256]{3,2,1,0:T(8,128)(2,1)S(1)}, u32[]{:S(2)}, u32[]{:S(2)}) collective-permute-start(bf16[4,2,432,256]{3,2,1,0:T(8,128)(2,1)} %bitcast.99), channel_id=1, source_target_pairs={{0,16},{8,24},{16,0},{24,8},{1,17},{9,25},{17,1},{25,9},{2,18},{10... | collective-permute-start | bytes 5308424 | tf_op jit(solution)/shard_map/part1_shift2/ppermute | solution.py:352
  91.5 16.2 %copy-start.2 = (bf16[4,2,144,256]{3,2,1,0:T(8,128)(2,1)}, bf16[4,2,144,256]{3,2,1,0:T(8,128)(2,1)S(1)}, u32[]{:S(2)}) copy-start(bf16[4,2,144,256]{3,2,1,0:T(8,128)(2,1)S(1)} %collective-permute-done.1.refs_2_.rest_2_) | copy-start | bytes 1769476
  107.7 0.9 copy-start.3
  108.5 125.7 %collective-permute-start.8 = (bf16[4,2,432,256]{3,2,1,0:T(8,128)(2,1)}, bf16[4,2,432,256]{3,2,1,0:T(8,128)(2,1)S(1)}, u32[]{:S(2)}, u32[]{:S(2)}) collective-permute-start(bf16[4,2,432,256]{3,2,1,0:T(8,128)(2,1)} %after.19), channel_id=1, source_target_pairs={{0,24},{8,0},{16,8},{24,16},{1,25},{9,1},{17,9},{25,17},{2,26},{10... | collective-permute-start | bytes 5308424 | tf_op jit(solution)/shard_map/part1_shift3/ppermute | solution.py:352
  146.9 4.1 copy-start.19
  146.9 101.5 %collective-permute-start.3 = (bf16[4,2,432,256]{3,2,1,0:T(8,128)(2,1)}, bf16[4,2,432,256]{3,2,1,0:T(8,128)(2,1)}, u32[]{:S(2)}, u32[]{:S(2)}) collective-permute-start(bf16[4,2,432,256]{3,2,1,0:T(8,128)(2,1)} %after.16), channel_id=1, source_target_pairs={{0,8},{8,16},{16,24},{24,0},{1,9},{9,17},{17,25},{25,1},{2,10},{10... | collective-permute-start | bytes 5308424 | tf_op jit(solution)/shard_map/part1_shift1/ppermute | solution.py:352
  184.9 1.2 copy-start
  186.1 75.2 %collective-permute-start.6 = (bf16[1168,256]{1,0:T(8,128)(2,1)}, bf16[1168,256]{1,0:T(8,128)(2,1)S(1)}, u32[]{:S(2)}, u32[]{:S(2)}) collective-permute-start(bf16[1168,256]{1,0:T(8,128)(2,1)} %after.18), channel_id=1, source_target_pairs={{0,16},{8,24},{16,0},{24,8},{1,17},{9,25},{17,1},{25,9},{2,18},{10... | collective-permute-start | bytes 1794056 | tf_op jit(solution)/shard_map/part2_shift2/ppermute | solution.py:352
  234.3 1.3 copy-start.1
  235.6 49.9 %collective-permute-start.9 = (bf16[1168,256]{1,0:T(8,128)(2,1)}, bf16[1168,256]{1,0:T(8,128)(2,1)S(1)}, u32[]{:S(2)}, u32[]{:S(2)}) collective-permute-start(bf16[1168,256]{1,0:T(8,128)(2,1)} %after.20), channel_id=1, source_target_pairs={{0,24},{8,0},{16,8},{24,16},{1,25},{9,1},{17,9},{25,17},{2,26},{10... | collective-permute-start | bytes 1794056 | tf_op jit(solution)/shard_map/part2_shift3/ppermute | solution.py:352
  248.4 51.0 %collective-permute-start.4 = (bf16[1168,256]{1,0:T(8,128)(2,1)}, bf16[1168,256]{1,0:T(8,128)(2,1)}, u32[]{:S(2)}, u32[]{:S(2)}) collective-permute-start(bf16[1168,256]{1,0:T(8,128)(2,1)} %after.17), channel_id=1, source_target_pairs={{0,8},{8,16},{16,24},{24,0},{1,9},{9,17},{17,25},{25,1},{2,10},{10... | collective-permute-start | bytes 1794056 | tf_op jit(solution)/shard_map/part2_shift1/ppermute | solution.py:352
  261.3 0.8 copy-start.10
  262.1 40.2 %copy-start.11 = (bf16[1168,256]{1,0:T(8,128)(2,1)S(1)}, bf16[1168,256]{1,0:T(8,128)(2,1)}, u32[]{:S(2)}) copy-start(bf16[1168,256]{1,0:T(8,128)(2,1)} %copy-done.10) | copy-start | bytes 1794052
  262.1 59.8 %collective-permute-start.11 = (bf16[1,2,576,256]{3,2,1,0:T(8,128)(2,1)}, bf16[1,2,576,256]{3,2,1,0:T(8,128)(2,1)S(1)}, u32[]{:S(2)}, u32[]{:S(2)}) collective-permute-start(bf16[1,2,576,256]{3,2,1,0:T(8,128)(2,1)} %after.22), channel_id=1, source_target_pairs={{0,16},{8,24},{16,0},{24,8},{1,17},{9,25},{17,1},{25,9},{2,18},{10... | collective-permute-start | bytes 1769480 | tf_op jit(solution)/shard_map/part3_shift2/ppermute | solution.py:352
  285.4 0.8 copy-start.12
  286.2 18.8 %copy-start.13 = (bf16[1168,256]{1,0:T(8,128)(2,1)S(1)}, bf16[1168,256]{1,0:T(8,128)(2,1)}, u32[]{:S(2)}) copy-start(bf16[1168,256]{1,0:T(8,128)(2,1)} %copy-done.12) | copy-start | bytes 1794052
  286.2 37.3 %collective-permute-start.12 = (bf16[1,2,576,256]{3,2,1,0:T(8,128)(2,1)}, bf16[1,2,576,256]{3,2,1,0:T(8,128)(2,1)S(1)}, u32[]{:S(2)}, u32[]{:S(2)}) collective-permute-start(bf16[1,2,576,256]{3,2,1,0:T(8,128)(2,1)} %after.23), channel_id=1, source_target_pairs={{0,24},{8,0},{16,8},{24,16},{1,25},{9,1},{17,9},{25,17},{2,26},{10... | collective-permute-start | bytes 1769480 | tf_op jit(solution)/shard_map/part3_shift3/ppermute | solution.py:352
  299.4 25.3 %collective-permute-start.10 = (bf16[1,2,576,256]{3,2,1,0:T(8,128)(2,1)}, bf16[1,2,576,256]{3,2,1,0:T(8,128)(2,1)S(1)}, u32[]{:S(2)}, u32[]{:S(2)}) collective-permute-start(bf16[1,2,576,256]{3,2,1,0:T(8,128)(2,1)} %after.21), channel_id=1, source_target_pairs={{0,8},{8,16},{16,24},{24,0},{1,9},{9,17},{17,25},{25,1},{2,10},{10... | collective-permute-start | bytes 1769480 | tf_op jit(solution)/shard_map/part3_shift1/ppermute | solution.py:352
  321.9 2.8 copy-start.4
  323.5 1.2 copy-start.5
  324.7 0.8 copy-start.6
  325.5 27.2 %collective-permute-start.17 = (bf16[2,512,1024]{2,1,0:T(8,128)(2,1)}, bf16[2,512,1024]{2,1,0:T(8,128)(2,1)}, u32[]{:S(2)}, u32[]{:S(2)}) collective-permute-start(bf16[2,512,1024]{2,1,0:T(8,128)(2,1)} %after.28), channel_id=1, source_target_pairs={{0,1},{1,0},{2,3},{3,2},{4,5},{5,4},{6,7},{7,6},{8,9},{9,8},{10,11... | collective-permute-start | bytes 6291464 | tf_op jit(solution)/shard_map/rows0/ppermute | solution.py:444
  327.6 5.2 %copy-start.18 = (f32[256]{0:T(256)S(1)}, f32[256]{0:T(256)}, u32[]{:S(2)}) copy-start(f32[256]{0:T(256)} %add_rsqrt_fusion) | copy-start | bytes 3076
  327.6 41.7 %collective-permute-start.14 = (bf16[1,2,576,256]{3,2,1,0:T(8,128)(2,1)}, bf16[1,2,576,256]{3,2,1,0:T(8,128)(2,1)S(1)}, u32[]{:S(2)}, u32[]{:S(2)}) collective-permute-start(bf16[1,2,576,256]{3,2,1,0:T(8,128)(2,1)} %after.25), channel_id=1, source_target_pairs={{0,16},{8,24},{16,0},{24,8},{1,17},{9,25},{17,1},{25,9},{2,18},{10... | collective-permute-start | bytes 1769480 | tf_op jit(solution)/shard_map/part4_shift2/ppermute | solution.py:352
  330.6 51.0 %collective-permute-start.15 = (bf16[1,2,576,256]{3,2,1,0:T(8,128)(2,1)}, bf16[1,2,576,256]{3,2,1,0:T(8,128)(2,1)S(1)}, u32[]{:S(2)}, u32[]{:S(2)}) collective-permute-start(bf16[1,2,576,256]{3,2,1,0:T(8,128)(2,1)} %after.26), channel_id=1, source_target_pairs={{0,24},{8,0},{16,8},{24,16},{1,25},{9,1},{17,9},{25,17},{2,26},{10... | collective-permute-start | bytes 1769480 | tf_op jit(solution)/shard_map/part4_shift3/ppermute | solution.py:352
  331.0 51.0 %collective-permute-start.13 = (bf16[1,2,576,256]{3,2,1,0:T(8,128)(2,1)}, bf16[1,2,576,256]{3,2,1,0:T(8,128)(2,1)S(1)}, u32[]{:S(2)}, u32[]{:S(2)}) collective-permute-start(bf16[1,2,576,256]{3,2,1,0:T(8,128)(2,1)} %after.24), channel_id=1, source_target_pairs={{0,8},{8,16},{16,24},{24,0},{1,9},{9,17},{17,25},{25,1},{2,10},{10... | collective-permute-start | bytes 1769480 | tf_op jit(solution)/shard_map/part4_shift1/ppermute | solution.py:352
  369.3 12.6 %copy-start.7 = (bf16[1,2,576,256]{3,2,1,0:T(8,128)(2,1)}, bf16[1,2,576,256]{3,2,1,0:T(8,128)(2,1)S(1)}, u32[]{:S(2)}) copy-start(bf16[1,2,576,256]{3,2,1,0:T(8,128)(2,1)S(1)} %collective-permute-done.14.refs_2_.rest_10_.refs_1_) | copy-start | bytes 1769476
  381.7 0.8 copy-start.8
  382.5 0.8 copy-start.9
  383.3 19.4 %collective-permute-start.16 = (bf16[2,512,1024]{2,1,0:T(8,128)(2,1)}, bf16[2,512,1024]{2,1,0:T(8,128)(2,1)S(1)}, u32[]{:S(2)}, u32[]{:S(2)}) collective-permute-start(bf16[2,512,1024]{2,1,0:T(8,128)(2,1)} %after.27), channel_id=1, source_target_pairs={{0,1},{1,0},{2,3},{3,2},{4,5},{5,4},{6,7},{7,6},{8,9},{9,8},{10,11... | collective-permute-start | bytes 6291464 | tf_op jit(solution)/shard_map/rows1/ppermute | solution.py:444
  384.1 38.6 %collective-permute-start.19 = (bf16[1,2,576,256]{3,2,1,0:T(8,128)(2,1)}, bf16[1,2,576,256]{3,2,1,0:T(8,128)(2,1)S(1)}, u32[]{:S(2)}, u32[]{:S(2)}) collective-permute-start(bf16[1,2,576,256]{3,2,1,0:T(8,128)(2,1)} %after.30), channel_id=1, source_target_pairs={{0,16},{8,24},{16,0},{24,8},{1,17},{9,25},{17,1},{25,9},{2,18},{10... | collective-permute-start | bytes 1769480 | tf_op jit(solution)/shard_map/part5_shift2/ppermute | solution.py:352
  384.1 53.2 %collective-permute-start.20 = (bf16[1,2,576,256]{3,2,1,0:T(8,128)(2,1)}, bf16[1,2,576,256]{3,2,1,0:T(8,128)(2,1)S(1)}, u32[]{:S(2)}, u32[]{:S(2)}) collective-permute-start(bf16[1,2,576,256]{3,2,1,0:T(8,128)(2,1)} %after.31), channel_id=1, source_target_pairs={{0,24},{8,0},{16,8},{24,16},{1,25},{9,1},{17,9},{25,17},{2,26},{10... | collective-permute-start | bytes 1769480 | tf_op jit(solution)/shard_map/part5_shift3/ppermute | solution.py:352
  386.6 50.7 %collective-permute-start.18 = (bf16[1,2,576,256]{3,2,1,0:T(8,128)(2,1)}, bf16[1,2,576,256]{3,2,1,0:T(8,128)(2,1)}, u32[]{:S(2)}, u32[]{:S(2)}) collective-permute-start(bf16[1,2,576,256]{3,2,1,0:T(8,128)(2,1)} %after.29), channel_id=1, source_target_pairs={{0,8},{8,16},{16,24},{24,0},{1,9},{9,17},{17,25},{25,1},{2,10},{10... | collective-permute-start | bytes 1769480 | tf_op jit(solution)/shard_map/part5_shift1/ppermute | solution.py:352
  402.7 1.3 copy-start.15
  404.0 5.4 %copy-start.14 = (bf16[2,512,1024]{2,1,0:T(8,128)(2,1)S(1)}, bf16[2,512,1024]{2,1,0:T(8,128)(2,1)}, u32[]{:S(2)}) copy-start(bf16[2,512,1024]{2,1,0:T(8,128)(2,1)} %get-tuple-element.71.rest_1_) | copy-start | bytes 6291460
  409.5 42.3 %collective-permute-start.22 = (bf16[2,512,1024]{2,1,0:T(8,128)(2,1)S(1)}, bf16[2,512,1024]{2,1,0:T(8,128)(2,1)}, u32[]{:S(2)}, u32[]{:S(2)}) collective-permute-start(bf16[2,512,1024]{2,1,0:T(8,128)(2,1)S(1)} %copy-done.14), channel_id=1, source_target_pairs={{0,1},{1,0},{2,3},{3,2},{4,5},{5,4},{6,7},{7,6},{8,9},{9,8},{10,11... | collective-permute-start | bytes 6291464 | tf_op jit(solution)/shard_map/rows2/ppermute | solution.py:444
  422.7 14.6 %copy-start.16 = (bf16[1,2,576,256]{3,2,1,0:T(8,128)(2,1)}, bf16[1,2,576,256]{3,2,1,0:T(8,128)(2,1)S(1)}, u32[]{:S(2)}) copy-start(bf16[1,2,576,256]{3,2,1,0:T(8,128)(2,1)S(1)} %collective-permute-done.19.rest_4_) | copy-start | bytes 1769476
  437.3 0.8 copy-start.17
  451.1 5.9 %collective-permute-start.21 = (bf16[2,512,1024]{2,1,0:T(8,128)(2,1)}, bf16[2,512,1024]{2,1,0:T(8,128)(2,1)}, u32[]{:S(2)}, u32[]{:S(2)}) collective-permute-start(bf16[2,512,1024]{2,1,0:T(8,128)(2,1)} %get-tuple-element.79.rest_1_), channel_id=1, source_target_pairs={{0,1},{1,0},{2,3},{3,2},{4,5},{5,4},{6,7},{7,6},{8,9},{9,8},{10,11... | collective-permute-start | bytes 6291464 | tf_op jit(solution)/shard_map/rows3/ppermute | solution.py:444
